TPU v7x, 32 devices: a whole 2x2x4 slice. The times are simulated.
32 devices in a mesh: parts: 2 (over y), tensor: 4 (over z), replica: 4 (over x, core).
Axes of the slice: x: 2, y: 2, z: 4, core: 2. Of those that a mesh axis runs over, the one named last changes fastest.
Arguments:
- attention_head_outputs: bfloat16 [2048, 4096], P(('parts', 'replica'), 'tensor'), parts along dimension 0, may hold values from -6 to 6
- group_owner_replica: int32 [128, 1], P(('parts', 'replica')), parts along dimension 0, may hold values from 0 to 3; in each aligned block of 16 rows (0 to 15, 16 to 31, ...) at most 4 rows name the same one
- group_adapter_slot: int32 [128], P(('parts', 'replica')), parts along dimension 0, may hold values from 0 to 7
- group_live_count: int32 [8, 16], P(('parts', 'replica')), parts along dimension 0, may hold values from 1 to 16, 224 in all within a row
- output_projection_weight: bfloat16 [4096, 8192], P('tensor'), may hold values from -0.125 to 0.125
- adapter_down_weight: bfloat16 [32, 64, 4096], P('replica', None, 'tensor'), may hold values from -0.09375 to 0.09375
- adapter_up_weight: bfloat16 [32, 64, 8192], P('replica', None, 'tensor'), may hold values from -0.75 to 0.75
Outputs:
- projected: bfloat16 [2048, 8192], P(('parts', 'replica')), parts along dimension 0
There are 2 independent parts, one for each index of `parts`. A program takes and returns all parts, laid end to end along the dimension named above; an argument that names none is the same for every part. Nothing has to cross between parts.
Inputs may be any that keep to these rules, and one draw needn't show every extreme that they name: `group_owner_replica`: among the 16 groups of one index of replica, no owner is named more than 4 times.
All inputs are finite; a program needn't handle non-finite values.
Results may differ from a plain program's by a relative error of at most 0.013.
Values may be sent and summed in bfloat16 or wider, within the bound.
No kernel may reach another device: no remote copies, remote signals or barrier semaphores. Data moves between devices by JAX's collectives and lax.ppermute only.
A program may use at most 128 MiB of HBM per device.

v0:
```python
import jax
import jax.numpy as jnp
from jax import lax
from jax.sharding import PartitionSpec as P

GROUP_ROWS = 16
CAP = 4


def on_device(
    attention_head_outputs,
    group_owner_replica,
    group_adapter_slot,
    group_live_count,
    output_projection_weight,
    adapter_down_weight,
    adapter_up_weight,
):
    rows_dev, feat_local = attention_head_outputs.shape
    groups = group_adapter_slot.shape[0]
    output_local_part = adapter_up_weight.shape[2]
    replicas = lax.axis_size("replica")
    owners = group_owner_replica[:, 0]
    group_ids = jnp.arange(groups, dtype=jnp.int32)
    same_owner = owners[:, None] == owners[None, :]
    earlier = group_ids[None, :] < group_ids[:, None]
    position = jnp.sum((same_owner & earlier).astype(jnp.int32), axis=1)
    owner_hit = owners[None, None, :] == jnp.arange(replicas, dtype=jnp.int32)[:, None, None]
    place_hit = position[None, None, :] == jnp.arange(CAP, dtype=jnp.int32)[None, :, None]
    onehot = (owner_hit & place_hit).astype(jnp.int32)
    wanted = jnp.sum(onehot * group_adapter_slot[None, None, :], axis=2)
    grouped = attention_head_outputs.reshape(groups, GROUP_ROWS, feat_local)
    requested_slots = lax.all_to_all(wanted, "replica", split_axis=0, concat_axis=0, tiled=True)
    shrink_result = jnp.take(adapter_down_weight, requested_slots, axis=0)
    expand_result = jnp.take(adapter_up_weight, requested_slots, axis=0)
    shrink_got, expand_got = (
        lax.all_to_all(shrink_result, "replica", split_axis=0, concat_axis=0, tiled=True),
        lax.all_to_all(expand_result, "replica", split_axis=0, concat_axis=0, tiled=True),
    )
    shrink_group = shrink_got[owners, position]
    expand_group = expand_got[owners, position]
    partial_value = jnp.einsum(
        "gid,grd->gir", grouped, shrink_group, preferred_element_type=jnp.float32
    )
    summed = lax.psum(partial_value.astype(jnp.bfloat16), "tensor")
    delta = jnp.einsum("gir,grn->gin", summed, expand_group, preferred_element_type=jnp.float32)
    delta = delta.reshape(rows_dev, output_local_part)
    live = (
        jnp.arange(GROUP_ROWS, dtype=jnp.int32)[None, :] < group_live_count[0][:, None]
    ).reshape(rows_dev, 1)
    term = jnp.dot(
        attention_head_outputs, output_projection_weight, preferred_element_type=jnp.float32
    )
    totals = lax.psum(term.astype(jnp.bfloat16), "tensor").astype(jnp.float32)
    delta_full = lax.all_gather(delta.astype(jnp.bfloat16), "tensor", axis=1, tiled=True).astype(
        delta.dtype
    )
    return jnp.where(live, totals + delta_full, 0.0).astype(jnp.bfloat16)


def solution(mesh):
    placed = (
        P(("parts", "replica"), "tensor"),
        P(("parts", "replica"), None),
        P(("parts", "replica")),
        P(("parts", "replica"), None),
        P("tensor", None),
        P("replica", None, "tensor"),
        P("replica", None, "tensor"),
    )
    return jax.shard_map(
        on_device,
        mesh=mesh,
        in_specs=placed,
        out_specs=P(("parts", "replica"), None),
        check_vma=False,
    )
```

profile of v0, /device:TPU:0, one launch (start us, length us, event | category | flops | bytes accessed | tf_op | source)
XLA Modules:
  0.0 294.1 jit_solution(10423031163429491733)
XLA Ops:
  6.5 1.0 convert_reduce_fusion
  7.5 0.7 iota_compare_fusion.2
  8.2 0.8 select_reduce_fusion
  9.0 7.8 %all_to_all.25 = s32[4,1,4]{2,1,0:T(1,128)S(1)} all-to-all(s32[4,1,4]{2,1,0:T(1,128)S(1)} %bitcast.33), channel_id=1, replica_groups=mesh['parts'=2,'tensor'=4,'replica'=4] {'replica'}, dimensions={0} | all-to-all | bytes 128 | tf_op jit(solution)/shard_map/all_to_all | solution.py:33
  16.8 0.1 reshape.124
  16.9 3.2 %gather_fusion = bf16[16,64,1024]{2,1,0:T(8,128)(2,1)} fusion(bf16[8,64,1024]{2,1,0:T(8,128)(2,1)} %param.12, s32[1024]{0:T(1024)S(1)} %pad_clamp_fusion), kind=kCustom, calls=%fused_computation | custom fusion | bytes 4194368 | tf_op jit(solution)/shard_map/jit(_take)/gather | solution.py:34
  20.1 3.3 %broadcast_select_fusion.1 = bf16[4,4,64,1024]{3,2,1,0:T(8,128)(2,1)} fusion(bf16[4,4,64,1024]{3,2,1,0:T(8,128)(2,1)} %bitcast.28, pred[4,4]{1,0:T(4,128)(4,1)S(1)} %compare_and_fusion), kind=kLoop, calls=%fused_computation.8 | loop fusion | flops 1048576 | bytes 4194320 | tf_op jit(solution)/shard_map/jit(_take)/select_n | solution.py:34
  23.4 4.5 %all-to-all-start.1 = ((bf16[4,4,64,1024]{3,2,1,0:T(8,128)(2,1)}), bf16[4,4,64,1024]{3,2,1,0:T(8,128)(2,1)}, u32[]{:S(2)}, u32[]{:S(2)}) async-start(bf16[4,4,64,1024]{3,2,1,0:T(8,128)(2,1)} %broadcast_select_fusion.1), calls=%async_computation.1 | async-start | bytes 4194304 | tf_op jit(solution)/shard_map/all_to_all | solution.py:37
  27.9 11.9 %convolution_convert_fusion = bf16[256,8192]{1,0:T(8,128)(2,1)} fusion(bf16[256,1024]{1,0:T(8,128)(2,1)S(1)} %copy-done.1, bf16[1024,8192]{1,0:T(8,128)(2,1)} %param.11), kind=kOutput, calls=%fused_computation.4 | convolution fusion | flops 4297064448 | bytes 21495808 | tf_op jit(solution)/shard_map/dot_general | solution.py:51
  39.8 2.8 gather_fusion.2
  42.7 4.7 %broadcast_select_fusion = bf16[4,4,64,2048]{3,2,1,0:T(8,128)(2,1)} fusion(bf16[4,4,64,2048]{3,2,1,0:T(8,128)(2,1)} %bitcast.27, pred[4,4]{1,0:T(4,128)(4,1)S(1)} %compare_and_fusion), kind=kLoop, calls=%fused_computation.6 | loop fusion | flops 2097152 | bytes 8388624 | tf_op jit(solution)/shard_map/jit(_take)/select_n | solution.py:35
  47.4 6.2 %all-to-all-done.1 = bf16[4,4,64,1024]{3,2,1,0:T(8,128)(2,1)} async-done(((bf16[4,4,64,1024]{3,2,1,0:T(8,128)(2,1)}), bf16[4,4,64,1024]{3,2,1,0:T(8,128)(2,1)}, u32[]{:S(2)}, u32[]{:S(2)}) %all-to-all-start.1) | async-done | bytes 2097184 | tf_op jit(solution)/shard_map/all_to_all | solution.py:37
  53.6 4.9 %all-to-all-start.2 = ((bf16[4,4,64,2048]{3,2,1,0:T(8,128)(2,1)}), bf16[4,4,64,2048]{3,2,1,0:T(8,128)(2,1)}, u32[]{:S(2)}, u32[]{:S(2)}) async-start(bf16[4,4,64,2048]{3,2,1,0:T(8,128)(2,1)} %broadcast_select_fusion), calls=%async_computation.2 | async-start | bytes 8388608 | tf_op jit(solution)/shard_map/all_to_all | solution.py:38
  58.6 3.6 %gather_fusion.1 = bf16[16,64,1024]{2,1,0:T(8,128)(2,1)} fusion(bf16[4,4,64,1024]{3,2,1,0:T(8,128)(2,1)} %all-to-all-done.1, s32[16]{0:T(128)S(1)} %fusion.7), kind=kCustom, calls=%fused_computation.1 | custom fusion | bytes 4194432 | tf_op jit(solution)/shard_map/gather | solution.py:40
  62.2 2.3 fusion
  64.5 22.9 %psum.15 = bf16[16,16,64]{2,1,0:T(8,128)(2,1)S(1)} all-reduce(bf16[16,16,64]{2,1,0:T(8,128)(2,1)S(1)} %fusion), channel_id=1, replica_groups=mesh['parts'=2,'tensor'=4,'replica'=4] {'tensor'}, use_global_device_ids=true, to_apply=%region_3.4 | all-reduce | flops 16384 | bytes 65536 | tf_op jit(solution)/shard_map/psum | solution.py:45
  87.4 19.4 %all-to-all-done.2 = bf16[4,4,64,2048]{3,2,1,0:T(8,128)(2,1)} async-done(((bf16[4,4,64,2048]{3,2,1,0:T(8,128)(2,1)}), bf16[4,4,64,2048]{3,2,1,0:T(8,128)(2,1)}, u32[]{:S(2)}, u32[]{:S(2)}) %all-to-all-start.2) | async-done | bytes 4194336 | tf_op jit(solution)/shard_map/all_to_all | solution.py:38
  106.8 5.0 %gather_fusion.3 = bf16[16,64,2048]{2,1,0:T(8,128)(2,1)} fusion(bf16[4,4,64,2048]{3,2,1,0:T(8,128)(2,1)} %all-to-all-done.2, s32[16]{0:T(128)S(1)} %fusion.7), kind=kCustom, calls=%fused_computation.3 | custom fusion | bytes 8388736 | tf_op jit(solution)/shard_map/gather | solution.py:41
  111.8 3.9 %convolution_convert_fusion.1 = bf16[16,16,2048]{2,1,0:T(8,128)(2,1)} fusion(bf16[16,16,64]{2,1,0:T(8,128)(2,1)S(1)} %psum.15, bf16[16,64,2048]{2,1,0:T(8,128)(2,1)} %gather_fusion.3), kind=kOutput, calls=%fused_computation.7 | convolution fusion | flops 67633152 | bytes 5275648 | tf_op jit(solution)/shard_map/gir,grn->gin/dot_general | solution.py:46
  115.7 0.1 iota_compare_fusion.1
  115.8 0.1 lt.72
  115.9 82.7 %all-reduce.2.cloned.1.call-done = bf16[256,8192]{1,0:T(8,128)(2,1)} async-done(((bf16[256,8192]{1,0:T(8,128)(2,1)}), bf16[256,8192]{1,0:T(8,128)(2,1)}) %all-reduce.2.cloned.1.call-update) | async-done | bytes 4194320 | tf_op jit(solution)/shard_map/psum | solution.py:54
  198.6 81.5 %all-gather.2.cloned.1.call-done = bf16[256,8192]{1,0:T(8,128)(2,1)} async-done(((bf16[256,2048]{1,0:T(8,128)(2,1)}), bf16[256,8192]{1,0:T(8,128)(2,1)}) %all-gather.2.cloned.1.call-update) | async-done | bytes 4194320 | tf_op jit(solution)/shard_map/all_gather | solution.py:55
  280.1 7.2 %select_convert_fusion = bf16[256,8192]{1,0:T(8,128)(2,1)} fusion(bf16[256,8192]{1,0:T(8,128)(2,1)} %all-gather.2.cloned.1.call-done, bf16[256,8192]{1,0:T(8,128)(2,1)} %all-reduce.2.cloned.1.call-done, pred[256]{0:T(512)(128)(4,1)S(1)} %lt.72), kind=kLoop, calls=%fused_computation.5 | loop fusion | flops 10485760 | bytes 12583168 | tf_op jit(solution)/shard_map/convert_element_type | solution.py:58
  (16 shorter events, 0.2 us)
Async XLA Ops:
  6.5 33.3 %copy-start = (bf16[8,64,2048]{2,1,0:T(8,128)(2,1)S(1)}, bf16[8,64,2048]{2,1,0:T(8,128)(2,1)}, u32[]{:S(2)}) copy-start(bf16[8,64,2048]{2,1,0:T(8,128)(2,1)} %param.13) | copy-start | bytes 6291460
  20.1 7.8 %copy-start.1 = (bf16[256,1024]{1,0:T(8,128)(2,1)S(1)}, bf16[256,1024]{1,0:T(8,128)(2,1)}, u32[]{:S(2)}) copy-start(bf16[256,1024]{1,0:T(8,128)(2,1)} %param.7) | copy-start | bytes 1572868
  23.4 30.2 %all-to-all-start.1 = ((bf16[4,4,64,1024]{3,2,1,0:T(8,128)(2,1)}), bf16[4,4,64,1024]{3,2,1,0:T(8,128)(2,1)}, u32[]{:S(2)}, u32[]{:S(2)}) async-start(bf16[4,4,64,1024]{3,2,1,0:T(8,128)(2,1)} %broadcast_select_fusion.1), calls=%async_computation.1 | async-start | bytes 4194304 | tf_op jit(solution)/shard_map/all_to_all | solution.py:37
  27.9 170.8 %all-reduce.2.cloned.1.call-start = ((), (), s32[]{:S(2)}) async-start(), calls=%async_computation.3 | async-start | bytes 8388608 | tf_op jit(solution)/shard_map/psum | solution.py:54
  47.4 11.2 %copy-start.3 = (s32[16,1]{0,1:T(1,128)S(1)}, s32[16,1]{0,1:T(1,128)}, u32[]{:S(2)}) copy-start(s32[16,1]{0,1:T(1,128)} %param.8) | copy-start | bytes 196
  53.6 53.2 %all-to-all-start.2 = ((bf16[4,4,64,2048]{3,2,1,0:T(8,128)(2,1)}), bf16[4,4,64,2048]{3,2,1,0:T(8,128)(2,1)}, u32[]{:S(2)}, u32[]{:S(2)}) async-start(bf16[4,4,64,2048]{3,2,1,0:T(8,128)(2,1)} %broadcast_select_fusion), calls=%async_computation.2 | async-start | bytes 8388608 | tf_op jit(solution)/shard_map/all_to_all | solution.py:38
  58.5 221.6 %all-gather.2.cloned.1.call-start = ((), (), s32[]{:S(2)}) async-start(), calls=%async_computation.4 | async-start | bytes 5242880 | tf_op jit(solution)/shard_map/all_gather | solution.py:55
  111.8 3.9 %copy-start.2 = (s32[1,16]{1,0:T(1,128)S(1)}, s32[1,16]{1,0:T(1,128)}, u32[]{:S(2)}) copy-start(s32[1,16]{1,0:T(1,128)} %param.10) | copy-start | bytes 196
Sparse Core Ops, SparseCore 0:
  40.0 158.6 all-reduce.1
  200.3 79.7 all-gather.1
where the time goes:
time: 295 us; the launch traced here: 294 us
  waiting for transfers between devices  190 us (64%)
  blocking collectives  30.6 us (10%)
  matrix products  18.1 us (6%)
  other arithmetic  17.7 us (6%)
  local copies, waits for them, and re-layouts  14.8 us (5%)
  between operations  13.5 us (5%)
  starting transfers between devices  9.47 us (3%)
    psum x1, waiting for transfers between devices, on_device(): totals = lax.psum(term.astype(jnp.bfloat16), 'tensor').astype(jnp.float32)  82.7 us
    all_gather x1, waiting for transfers between devices, on_device(): lax.all_gather(delta.astype(jnp.bfloat16), 'tensor', axis=1, tiled=True)  81.5 us
    psum x1, blocking collectives, on_device(): summed = lax.psum(partial_value.astype(jnp.bfloat16), 'tensor')  22.9 us
    all_to_all x1, waiting for transfers between devices, on_device(): lax.all_to_all(expand_result, 'replica', split_axis=0, concat_axis=0, til...  19.4 us
    dot_general x1, matrix products, on_device(): jnp.dot(attention_head_outputs, output_projection_weight, preferred_eleme...  11.9 us
    all_to_all x1, blocking collectives, on_device(): lax.all_to_all(wanted, 'replica', split_axis=0, concat_axis=0, tiled=True)  7.76 us
    convert_element_type x1, other arithmetic, on_device(): return jnp.where(live, totals + delta_full, 0.0).astype(jnp.bfloat16)  7.16 us
    all_to_all x1, waiting for transfers between devices, on_device(): lax.all_to_all(shrink_result, 'replica', split_axis=0, concat_axis=0, til...  6.22 us
  transfers between devices with their start and end apart: 4, of which 4 were waited for; matrix products, arithmetic and copies ran while one was open for 12% of the time, Pallas kernels for 0%

commit v1 on v0

v1 whole, which is shorter than its diff:
```python
import functools

import jax
import jax.numpy as jnp
from jax import lax
from jax.experimental import pallas as pl
from jax.experimental.pallas import tpu as pltpu
from jax.sharding import PartitionSpec as P

GROUP_ROWS = 16
CAP = 4
LIVE_ROWS = 224
TAG = 128
CHUNK = 512
SKEW = 2
BF16 = jnp.bfloat16
F32 = jnp.float32
VMEM_BYTES = 40 * 1024 * 1024


def dot(a, b):
    return jnp.dot(a, b, preferred_element_type=F32)


def dot_rows(a, b):
    return lax.dot_general(a, b, (((0,), (0,)), ((), ())), preferred_element_type=F32)


def dot_cols(a, b):
    return lax.dot_general(a, b, (((1,), (1,)), ((), ())), preferred_element_type=F32)


def iota(shape, dim):
    return lax.broadcasted_iota(jnp.int32, shape, dim)


def params():
    return pltpu.CompilerParams(vmem_limit_bytes=VMEM_BYTES)


def prepare_kernel(replicas, owner, slot, live, me, x, compact_x, sent, pick, place):
    rows, feat = x.shape
    groups = rows // GROUP_ROWS
    out_rows = sent.shape[0]
    lane = iota((1, rows), 1)
    lane_group, lane_slot = lane // GROUP_ROWS, lane % GROUP_ROWS
    row_group = iota((rows, TAG), 0) // GROUP_ROWS
    packed = jnp.full((1, rows), -1, jnp.int32)
    target = jnp.zeros((1, rows), jnp.int32)
    tags = jnp.zeros((rows, TAG), F32)
    owners = [owner[g] for g in range(groups)]
    offset = jnp.int32(0)
    used = [jnp.int32(0)] * replicas
    for g in range(groups):
        count = live[g]
        mine = lane_group == g
        packed = jnp.where(mine & (lane_slot < count), offset + lane_slot, packed)
        offset = offset + count
        position = jnp.int32(0)
        for o in range(replicas):
            hit = owners[g] == o
            position = jnp.where(hit, used[o], position)
            used[o] = used[o] + hit.astype(jnp.int32)
        hop = lax.rem(owners[g] - me[0] + replicas, replicas)
        start = (hop * CAP + position) * GROUP_ROWS
        target = jnp.where(mine, start + lane_slot, target)
        tags = jnp.where(row_group == g, slot[g].astype(F32), tags)
    compact = (iota((LIVE_ROWS, rows), 0) == packed).astype(BF16)
    spread = (iota((out_rows, rows), 0) == target).astype(BF16)
    pick[...] = compact
    place[...] = dot_cols(compact, spread).astype(BF16)
    compact_x[...] = dot(compact, x[...]).astype(BF16)
    sent[:, :feat] = dot(spread, x[...]).astype(BF16)
    sent[:, feat:] = dot(spread, tags.astype(BF16)).astype(BF16)


def prepare(owner, slot, live, me, x, replicas):
    rows, feat = x.shape
    out_rows = replicas * CAP * GROUP_ROWS
    smem = pl.BlockSpec(memory_space=pltpu.SMEM)
    vmem = pl.BlockSpec(memory_space=pltpu.VMEM)
    return pl.pallas_call(
        functools.partial(prepare_kernel, replicas),
        out_shape=(
            jax.ShapeDtypeStruct((LIVE_ROWS, feat), BF16),
            jax.ShapeDtypeStruct((out_rows, feat + TAG), BF16),
            jax.ShapeDtypeStruct((LIVE_ROWS, rows), BF16),
            jax.ShapeDtypeStruct((LIVE_ROWS, out_rows), BF16),
        ),
        in_specs=[smem, smem, smem, smem, vmem],
        out_specs=(vmem,) * 4,
        compiler_params=params(),
        name="prepare",
    )(owner, slot, live, me, x)


def base_kernel(first, x, w, out):
    out[...] = dot(x[...], w[...]).astype(BF16)[None]


def base_chunks(first, x, weight, number):
    feat, width = weight.shape
    return pl.pallas_call(
        base_kernel,
        out_shape=jax.ShapeDtypeStruct((number, LIVE_ROWS, CHUNK), BF16),
        grid_spec=pltpu.PrefetchScalarGridSpec(
            num_scalar_prefetch=1,
            grid=(number,),
            in_specs=[
                pl.BlockSpec((LIVE_ROWS, feat), lambda i, first: (0, 0)),
                pl.BlockSpec((feat, CHUNK), lambda i, first: (0, first[0] + i)),
            ],
            out_specs=pl.BlockSpec((1, LIVE_ROWS, CHUNK), lambda i, first: (i, 0, 0)),
        ),
        compiler_params=params(),
        cost_estimate=pl.CostEstimate(
            flops=2 * LIVE_ROWS * feat * CHUNK * number,
            bytes_accessed=2 * (feat + LIVE_ROWS) * CHUNK * number,
            transcendentals=0,
        ),
        name="base",
    )(first, x, weight)


def fold(rank, adapters, half):
    shape = (adapters * rank, 2 * rank)
    return (iota(shape, 0) % rank + half * rank == iota(shape, 1)).astype(BF16)


def slot_mask(tag, rank, adapters):
    shape = (tag.shape[0], adapters * rank)
    return (iota(shape, 1) // rank).astype(F32) == tag.astype(F32)


def low_kernel(rank, blocks, down, *refs):
    parts, low = refs[:blocks], refs[blocks]
    adapters = down.shape[0] // rank
    feat = down.shape[1]
    rows = parts[0].shape[0]
    half = blocks // 2
    maps = down[...]
    folds = [fold(rank, adapters, h) for h in range(2)]
    for k in range(half):
        total = None
        for h in range(2):
            part = parts[h * half + k]
            wide = dot_cols(part[:, :feat], maps)
            kept = jnp.where(slot_mask(part[:, feat : feat + 1], rank, adapters), wide, 0.0)
            got = dot(kept.astype(BF16), folds[h])
            total = got if total is None else total + got
        low[k * rows : (k + 1) * rows, :] = total.astype(BF16)


def low_values(parts, down, rank):
    rows, width = parts[0].shape
    blocks = len(parts)
    vmem = pl.BlockSpec(memory_space=pltpu.VMEM)
    return pl.pallas_call(
        functools.partial(low_kernel, rank, blocks),
        out_shape=jax.ShapeDtypeStruct((blocks // 2 * rows, 2 * rank), BF16),
        in_specs=[vmem] * (blocks + 1),
        out_specs=vmem,
        compiler_params=params(),
        name="low",
    )(down, *parts)


def delta_kernel(rank, blocks, sums, up, *refs):
    tags, lows, outs = refs[:blocks], refs[blocks : blocks + sums], refs[blocks + sums :]
    adapters = up.shape[0] // rank
    rows = tags[0].shape[0]
    half = blocks // 2
    total = lows[0][...].astype(F32)
    for other in lows[1:]:
        total = total + other[...].astype(F32)
    low = total.astype(BF16)
    maps = up[...]
    for h in range(2):
        spread = fold(rank, adapters, h)
        for k in range(half):
            wide = dot_cols(low[k * rows : (k + 1) * rows, :], spread)
            mask = slot_mask(tags[h * half + k][:, :1], rank, adapters)
            kept = jnp.where(mask, wide, 0.0).astype(BF16)
            outs[h * half + k][...] = dot(kept, maps).astype(BF16)


def delta_values(parts, lows, up, rank):
    rows, width = parts[0].shape
    blocks = len(parts)
    columns = up.shape[1]
    vmem = pl.BlockSpec(memory_space=pltpu.VMEM)
    tag = pl.BlockSpec((rows, TAG), lambda i: (0, width // TAG - 1))
    whole = lambda a: pl.BlockSpec(a.shape, lambda i: (0, 0))
    return pl.pallas_call(
        functools.partial(delta_kernel, rank, blocks, len(lows)),
        out_shape=[jax.ShapeDtypeStruct((rows, columns), BF16)] * blocks,
        grid=(1,),
        in_specs=[whole(up)] + [tag] * blocks + [whole(a) for a in lows],
        out_specs=[pl.BlockSpec((rows, columns), lambda i: (0, 0))] * blocks,
        compiler_params=params(),
        name="delta",
    )(up, *parts, *lows)


def add_delta_kernel(blocks, first, base, place, *refs):
    parts, out = refs[:blocks], refs[blocks]
    rows = parts[0].shape[0]
    total = base[0].astype(F32)
    for k in range(blocks):
        total = total + dot(place[:, k * rows : (k + 1) * rows], parts[k][...])
    out[0] = total.astype(BF16)


def add_delta(first, base, place, parts):
    rows, columns = parts[0].shape
    chunk = base.shape[2]
    return pl.pallas_call(
        functools.partial(add_delta_kernel, len(parts)),
        out_shape=jax.ShapeDtypeStruct((columns // chunk, LIVE_ROWS, chunk), BF16),
        grid_spec=pltpu.PrefetchScalarGridSpec(
            num_scalar_prefetch=1,
            grid=(columns // chunk,),
            in_specs=[
                pl.BlockSpec((1, LIVE_ROWS, chunk), lambda i, first: (first[0] + i, 0, 0)),
                pl.BlockSpec(place.shape, lambda i, first: (0, 0)),
            ]
            + [pl.BlockSpec((rows, chunk), lambda i, first: (0, i))] * len(parts),
            out_specs=pl.BlockSpec((1, LIVE_ROWS, chunk), lambda i, first: (i, 0, 0)),
        ),
        compiler_params=params(),
        name="add_delta",
    )(first, base, place, *parts)


def finish_kernel(at, base, left, right, pick, held, out):
    @pl.when(at[1] > 0)
    def _():
        total = base[...].astype(F32) + left[...].astype(F32) + right[...].astype(F32)
        out[...] = dot_rows(pick[...], total.astype(BF16)).astype(BF16)

    @pl.when(at[1] == 0)
    def _():
        out[...] = held[...]


def finish(at, base, left, right, pick, held):
    rows = pick.shape[1]
    whole = lambda a: pl.BlockSpec(a.shape, lambda i, at: (0,) * a.ndim)
    here = pl.BlockSpec((rows, CHUNK), lambda i, at: (0, at[0]))
    return pl.pallas_call(
        finish_kernel,
        out_shape=jax.ShapeDtypeStruct(held.shape, BF16),
        grid_spec=pltpu.PrefetchScalarGridSpec(
            num_scalar_prefetch=1,
            grid=(1,),
            in_specs=[whole(base), whole(left), whole(right), whole(pick), here],
            out_specs=here,
        ),
        input_output_aliases={5: 0},
        compiler_params=params(),
        name="finish",
    )(at, base, left, right, pick, held)


def adapter_parts(sent, down, up):
    replicas, shards = lax.axis_size("replica"), lax.axis_size("tensor")
    rank = down.shape[1]
    rows = CAP * GROUP_ROWS
    parts = [sent[:rows]]
    for k in range(1, replicas):
        hops = [(i, (i + k) % replicas) for i in range(replicas)]
        parts.append(lax.ppermute(sent[k * rows : (k + 1) * rows], "replica", hops))
    low = low_values(parts, down.reshape(-1, down.shape[2]), rank)
    if shards <= 4:
        lows = [low]
        for k in range(1, shards):
            hops = [(i, (i + k) % shards) for i in range(shards)]
            lows.append(lax.ppermute(low, "tensor", hops))
    else:
        lows = [lax.psum(low, "tensor")]
    made = delta_values(parts, lows, up.reshape(-1, up.shape[2]), rank)
    back = [made[0]]
    for k in range(1, replicas):
        hops = [(i, (i - k) % replicas) for i in range(replicas)]
        back.append(lax.ppermute(made[k], "replica", hops))
    return back


def on_device(x, owner, slot, live, weight, down, up):
    rows = x.shape[0]
    width = weight.shape[1]
    replicas, shards = lax.axis_size("replica"), lax.axis_size("tensor")
    me = lax.axis_index("replica").astype(jnp.int32).reshape(1)
    z = lax.axis_index("tensor").astype(jnp.int32)
    compact_x, sent, pick, place = prepare(owner[:, 0], slot, live[0], me, x, replicas)
    share = width // shards
    if shards != 4:
        base = dot(compact_x, weight)
        back = jnp.concatenate(adapter_parts(sent, down, up), axis=0)
        mine = lax.dynamic_slice_in_dim(base, z * share, share, 1) + dot(place, back)
        base = lax.dynamic_update_slice_in_dim(base, mine, z * share, 1).astype(BF16)
        total = lax.psum_scatter(base, "tensor", scatter_dimension=1, tiled=True)
        total = lax.all_gather(total, "tensor", axis=1, tiled=True)
        return dot_rows(pick, total).astype(BF16)

    chunks, per = width // CHUNK, share // CHUNK
    last = shards - 1
    even_right = z % 2 == 0
    right_lag, left_lag = -SKEW * z, -SKEW * (last - z)

    def chunk_of(position, right):
        return jnp.clip(jnp.where(right, chunks - 1 - position, position), 0, chunks - 1)

    def even_chunk(step):
        return chunk_of(step + jnp.where(even_right, right_lag, left_lag), even_right)

    def odd_chunk(step):
        return chunk_of(step + jnp.where(even_right, left_lag, right_lag), ~even_right)

    even = [pair for i in range(0, last, 2) for pair in ((i, i + 1), (i + 1, i))]
    odd = [pair for i in range(1, last, 2) for pair in ((i, i + 1), (i + 1, i))]
    first = base_chunks(even_chunk(0).reshape(1), compact_x, weight, 1)[0]
    base = base_chunks(jnp.zeros((1,), jnp.int32), compact_x, weight, chunks)
    back = adapter_parts(sent, down, up)
    own = add_delta((z * per).reshape(1), base, place, back)

    def term(chunk, with_delta):
        plain = lax.dynamic_index_in_dim(base, chunk, 0, keepdims=False)
        if not with_delta:
            return plain
        near = lax.dynamic_index_in_dim(own, jnp.clip(chunk - z * per, 0, per - 1), 0, keepdims=False)
        return jnp.where(chunk // per == z, near, plain)

    steps = chunks + SKEW * (shards - 2)
    ready = per + SKEW * (shards - 2)
    evens, odds = [], []
    result = jnp.zeros((rows, width), BF16)
    inner = (z > 0) & (z < last)

    def close(step, result):
        partner = chunks - 1 - step + SKEW
        got_odd = odds[partner] if 0 <= partner < len(odds) else jnp.zeros_like(evens[0])
        position = jnp.where(inner, step, step - SKEW * (shards - 2))
        chunk = chunk_of(position, ~even_right)
        valid = (position >= 0) & (position < chunks)
        at = jnp.stack([chunk, valid.astype(jnp.int32)])
        return finish(at, term(chunk, True), evens[step], got_odd, pick, result)

    for step in range(steps):
        with_delta = step >= ready
        if step == 0:
            message = first
        else:
            message = term(even_chunk(step), with_delta)
            if step >= SKEW:
                message = (message.astype(F32) + odds[step - SKEW].astype(F32)).astype(BF16)
        evens.append(lax.ppermute(message, "tensor", even))
        if step < SKEW:
            odds.append(jnp.zeros_like(first))
        elif step < chunks + SKEW:
            message = term(odd_chunk(step), with_delta)
            message = (message.astype(F32) + evens[step - SKEW].astype(F32)).astype(BF16)
            odds.append(lax.ppermute(message, "tensor", odd))
    done = set()
    for step in range(steps):
        for s in range(step + 1):
            partner = chunks - 1 - s + SKEW
            if s not in done and partner <= step:
                result = close(s, result)
                done.add(s)
    return result


def solution(mesh):
    placed = (
        P(("parts", "replica"), "tensor"),
        P(("parts", "replica"), None),
        P(("parts", "replica")),
        P(("parts", "replica"), None),
        P("tensor", None),
        P("replica", None, "tensor"),
        P("replica", None, "tensor"),
    )
    return jax.shard_map(
        on_device,
        mesh=mesh,
        in_specs=placed,
        out_specs=P(("parts", "replica"), None),
        check_vma=False,
    )
```

time: 295 us -> 319 us (1.081)
  waiting for transfers between devices: 190 us -> 67.5 us
  starting transfers between devices: 9.47 us -> 109 us
  Pallas kernels: 0 us -> 72.9 us
  other arithmetic: 17.7 us -> 51 us
  blocking collectives: 30.6 us -> 0 us
  matrix products: 18.1 us -> 0 us
  between operations: 13.5 us -> 0.73 us
    ppermute x0 -> x45, starting transfers between devices: none -> 109 us  [the longest x20 86.5 us: on_device(): evens.append(lax.ppermute(message, 'tensor', even))]
    psum x1 -> x0, waiting for transfers between devices: 82.7 us -> none  [on_device(): totals = lax.psum(term.astype(jnp.bfloat16), 'tensor').astype(jnp.float32)]
    all_gather x1 -> x0, waiting for transfers between devices: 81.5 us -> none  [on_device(): lax.all_gather(delta.astype(jnp.bfloat16), 'tensor', axis=1, tiled=True)]
    pallas_call x0 -> x26, Pallas kernels: none -> 72.9 us  [the longest x20 50.3 us: finish(): pl.pallas_call(finish_kernel, out_shape=jax.ShapeDtypeStruct(held.shape,...]
    ppermute x0 -> x45, waiting for transfers between devices: none -> 67.5 us  [the longest x20 48.1 us: on_device(): evens.append(lax.ppermute(message, 'tensor', even))]
    convert_element_type x1 -> x21, other arithmetic: 7.16 us -> 33.8 us  [the longest x11 17.3 us: on_device(): message = (message.astype(F32) + odds[step - SKEW].astype(F32)).astype(BF16)]
    all_to_all x2 -> x0, waiting for transfers between devices: 25.6 us -> none  [the longest x1 19.4 us: on_device(): lax.all_to_all(expand_result, 'replica', split_axis=0, concat_axis=0, til...]
    psum x1 -> x0, blocking collectives: 22.9 us -> none  [on_device(): summed = lax.psum(partial_value.astype(jnp.bfloat16), 'tensor')]
  transfers between devices with their start and end apart: 4 -> 45, of which waited for: 4 -> 21; matrix products, arithmetic and copies ran while one was open for 12% -> 9% of each run, Pallas kernels for 0% -> 21%
where the time goes in v1:
time: 319 us; the launch traced here: 317 us
  starting transfers between devices  109 us (34%)
  Pallas kernels  72.9 us (23%)
  waiting for transfers between devices  67.5 us (21%)
  other arithmetic  51 us (16%)
  local copies, waits for them, and re-layouts  15.9 us (5%)
    ppermute x20, starting transfers between devices, on_device(): evens.append(lax.ppermute(message, 'tensor', even))  86.5 us
    pallas_call x20, Pallas kernels, finish(): pl.pallas_call(finish_kernel, out_shape=jax.ShapeDtypeStruct(held.shape,...  50.3 us
    ppermute x20, waiting for transfers between devices, on_device(): evens.append(lax.ppermute(message, 'tensor', even))  48.1 us
    convert_element_type x11, other arithmetic, on_device(): message = (message.astype(F32) + odds[step - SKEW].astype(F32)).astype(BF16)  17.3 us
    convert_element_type x10, other arithmetic, on_device(): (message.astype(F32) + evens[step - SKEW].astype(F32)).astype(BF16)  16.5 us
    pallas_call x2, Pallas kernels, base_chunks(): pl.pallas_call(base_kernel, out_shape=jax.ShapeDtypeStruct((number, LIVE_...  15.7 us
    ppermute x16, starting transfers between devices, on_device(): odds.append(lax.ppermute(message, 'tensor', odd))  14.8 us
    unnamed x120, local copies, waits for them, and re-layouts  13.4 us
  transfers between devices with their start and end apart: 45, of which 21 were waited for; matrix products, arithmetic and copies ran while one was open for 9% of the time, Pallas kernels for 21%

profile of v1, /device:TPU:0, one launch (start us, length us, event | category | flops | bytes accessed | tf_op | source)
XLA Modules:
  0.0 317.4 jit_solution(10997695439269236794)
XLA Ops:
  5.9 3.1 collective-permute-start.36
  9.0 14.0 %base.2 = bf16[16,224,512]{2,1,0:T(8,128)(2,1)S(1)} custom-call(s32[1]{0:T(128)} %constant.749.clone.1.first, bf16[224,1024]{1,0:T(8,128)(2,1)S(1)} %get-tuple-element.13.x, bf16[1024,8192]{1,0:T(8,128)(2,1)} %w.3), custom_call_target="tpu_custom_call" | custom-call | flops 3758096384 | bytes 20447232 | tf_op jit(solution)/shard_map/base/pallas_call | solution.py:103
  28.2 9.9 %collective-permute-start.38 = (bf16[224,512]{1,0:T(8,128)(2,1)}, bf16[224,512]{1,0:T(8,128)(2,1)}, u32[]{:S(2)}, u32[]{:S(2)}) collective-permute-start(bf16[224,512]{1,0:T(8,128)(2,1)} %fusion.1), channel_id=1, source_target_pairs={{0,4},{4,0},{8,12},{12,8},{1,5},{5,1},{9,13},{13,9},{2,6},{6,2},{1... | collective-permute-start | bytes 688136 | tf_op jit(solution)/shard_map/ppermute | solution.py:357
  49.5 3.2 %collective-permute-start.4 = (bf16[128,128]{1,0:T(8,128)(2,1)S(1)}, bf16[128,128]{1,0:T(8,128)(2,1)S(1)}, u32[]{:S(2)}, u32[]{:S(2)}) collective-permute-start(bf16[128,128]{1,0:T(8,128)(2,1)S(1)} %low.1.refs_4_), channel_id=1, source_target_pairs={{0,8},{4,12},{8,0},{12,4},{1,9},{5,13},{9,1},{13,5},{2,10},{6,14},... | collective-permute-start | bytes 98312 | tf_op jit(solution)/shard_map/ppermute | solution.py:278
  64.4 4.7 %collective-permute-done.6.refs_1_ = bf16[64,2048]{1,0:T(8,128)(2,1)S(1)} collective-permute-done((bf16[64,2048]{1,0:T(8,128)(2,1)}, bf16[64,2048]{1,0:T(8,128)(2,1)S(1)}, u32[]{:S(2)}, u32[]{:S(2)}) %collective-permute-start.6) | collective-permute-done | bytes 262176 | tf_op jit(solution)/shard_map/ppermute | solution.py:285
  69.1 5.6 %collective-permute-done.7.refs_2_ = bf16[64,2048]{1,0:T(8,128)(2,1)S(1)} collective-permute-done((bf16[64,2048]{1,0:T(8,128)(2,1)}, bf16[64,2048]{1,0:T(8,128)(2,1)S(1)}, u32[]{:S(2)}, u32[]{:S(2)}) %collective-permute-start.7) | collective-permute-done | bytes 262176 | tf_op jit(solution)/shard_map/ppermute | solution.py:285
  81.4 5.3 %collective-permute-done.40.left = bf16[224,512]{1,0:T(8,128)(2,1)S(1)} collective-permute-done((bf16[224,512]{1,0:T(8,128)(2,1)S(1)}, bf16[224,512]{1,0:T(8,128)(2,1)S(1)}, u32[]{:S(2)}, u32[]{:S(2)}) %collective-permute-start.40) | collective-permute-done | bytes 229408 | tf_op jit(solution)/shard_map/ppermute | solution.py:357
  91.0 3.2 collective-permute-start.9
  100.5 4.9 %collective-permute-done.18.left = bf16[224,512]{1,0:T(8,128)(2,1)S(1)} collective-permute-done((bf16[224,512]{1,0:T(8,128)(2,1)S(1)}, bf16[224,512]{1,0:T(8,128)(2,1)S(1)}, u32[]{:S(2)}, u32[]{:S(2)}) %collective-permute-start.18) | collective-permute-done | bytes 229408 | tf_op jit(solution)/shard_map/ppermute | solution.py:357
  105.4 4.3 %collective-permute-done.27.left = bf16[224,512]{1,0:T(8,128)(2,1)S(1)} collective-permute-done((bf16[224,512]{1,0:T(8,128)(2,1)S(1)}, bf16[224,512]{1,0:T(8,128)(2,1)S(1)}, u32[]{:S(2)}, u32[]{:S(2)}) %collective-permute-start.27) | collective-permute-done | bytes 229408 | tf_op jit(solution)/shard_map/ppermute | solution.py:357
  118.9 10.0 %collective-permute-start.29 = (bf16[224,512]{1,0:T(8,128)(2,1)}, bf16[224,512]{1,0:T(8,128)(2,1)S(1)}, u32[]{:S(2)}, u32[]{:S(2)}) collective-permute-start(bf16[224,512]{1,0:T(8,128)(2,1)} %fusion.9), channel_id=1, source_target_pairs={{0,4},{4,0},{8,12},{12,8},{1,5},{5,1},{9,13},{13,9},{2,6},{6,2},{1... | collective-permute-start | bytes 688136 | tf_op jit(solution)/shard_map/ppermute | solution.py:357
  129.6 4.4 %collective-permute-done.29.left = bf16[224,512]{1,0:T(8,128)(2,1)S(1)} collective-permute-done((bf16[224,512]{1,0:T(8,128)(2,1)}, bf16[224,512]{1,0:T(8,128)(2,1)S(1)}, u32[]{:S(2)}, u32[]{:S(2)}) %collective-permute-start.29) | collective-permute-done | bytes 229408 | tf_op jit(solution)/shard_map/ppermute | solution.py:357
  139.8 2.8 collective-permute-done.11.left
  142.7 3.9 %collective-permute-done.20.left = bf16[224,512]{1,0:T(8,128)(2,1)S(1)} collective-permute-done((bf16[224,512]{1,0:T(8,128)(2,1)}, bf16[224,512]{1,0:T(8,128)(2,1)S(1)}, u32[]{:S(2)}, u32[]{:S(2)}) %collective-permute-start.20) | collective-permute-done | bytes 229408 | tf_op jit(solution)/shard_map/ppermute | solution.py:357
  151.6 4.3 %collective-permute-done.31.left = bf16[224,512]{1,0:T(8,128)(2,1)} collective-permute-done((bf16[224,512]{1,0:T(8,128)(2,1)}, bf16[224,512]{1,0:T(8,128)(2,1)}, u32[]{:S(2)}, u32[]{:S(2)}) %collective-permute-start.31) | collective-permute-done | bytes 229408 | tf_op jit(solution)/shard_map/ppermute | solution.py:357
  160.9 12.3 %collective-permute-start.33 = (bf16[224,512]{1,0:T(8,128)(2,1)}, bf16[224,512]{1,0:T(8,128)(2,1)}, u32[]{:S(2)}, u32[]{:S(2)}) collective-permute-start(bf16[224,512]{1,0:T(8,128)(2,1)} %fusion.13), channel_id=1, source_target_pairs={{0,4},{4,0},{8,12},{12,8},{1,5},{5,1},{9,13},{13,9},{2,6},{6,2},{1... | collective-permute-start | bytes 688136 | tf_op jit(solution)/shard_map/ppermute | solution.py:357
  174.5 2.9 collective-permute-done.33.left
  182.3 9.4 %collective-permute-start.22 = (bf16[224,512]{1,0:T(8,128)(2,1)}, bf16[224,512]{1,0:T(8,128)(2,1)}, u32[]{:S(2)}, u32[]{:S(2)}) collective-permute-start(bf16[224,512]{1,0:T(8,128)(2,1)} %get-tuple-element.46), channel_id=1, source_target_pairs={{0,4},{4,0},{8,12},{12,8},{1,5},{5,1},{9,13},{13,9},{2,6},{6,2},{1... | collective-permute-start | bytes 688136 | tf_op jit(solution)/shard_map/ppermute | solution.py:357
  192.9 4.1 %collective-permute-done.22.left = bf16[224,512]{1,0:T(8,128)(2,1)} collective-permute-done((bf16[224,512]{1,0:T(8,128)(2,1)}, bf16[224,512]{1,0:T(8,128)(2,1)}, u32[]{:S(2)}, u32[]{:S(2)}) %collective-permute-start.22) | collective-permute-done | bytes 229408 | tf_op jit(solution)/shard_map/ppermute | solution.py:357
  203.9 10.2 %collective-permute-start.24 = (bf16[224,512]{1,0:T(8,128)(2,1)}, bf16[224,512]{1,0:T(8,128)(2,1)}, u32[]{:S(2)}, u32[]{:S(2)}) collective-permute-start(bf16[224,512]{1,0:T(8,128)(2,1)} %fusion.21), channel_id=1, source_target_pairs={{0,4},{4,0},{8,12},{12,8},{1,5},{5,1},{9,13},{13,9},{2,6},{6,2},{1... | collective-permute-start | bytes 688136 | tf_op jit(solution)/shard_map/ppermute | solution.py:357
  230.8 11.9 %collective-permute-start.15 = (bf16[224,512]{1,0:T(8,128)(2,1)}, bf16[224,512]{1,0:T(8,128)(2,1)}, u32[]{:S(2)}, u32[]{:S(2)}) collective-permute-start(bf16[224,512]{1,0:T(8,128)(2,1)} %fusion.29), channel_id=1, source_target_pairs={{0,4},{4,0},{8,12},{12,8},{1,5},{5,1},{9,13},{13,9},{2,6},{6,2},{1... | collective-permute-start | bytes 688136 | tf_op jit(solution)/shard_map/ppermute | solution.py:357
  244.6 3.6 %collective-permute-done.15.left = bf16[224,512]{1,0:T(8,128)(2,1)} collective-permute-done((bf16[224,512]{1,0:T(8,128)(2,1)}, bf16[224,512]{1,0:T(8,128)(2,1)}, u32[]{:S(2)}, u32[]{:S(2)}) %collective-permute-start.15) | collective-permute-done | bytes 229408 | tf_op jit(solution)/shard_map/ppermute | solution.py:357
  251.5 3.6 %collective-permute-start.44 = (bf16[224,512]{1,0:T(8,128)(2,1)}, bf16[224,512]{1,0:T(8,128)(2,1)S(1)}, u32[]{:S(2)}, u32[]{:S(2)}) collective-permute-start(bf16[224,512]{1,0:T(8,128)(2,1)} %get-tuple-element.36), channel_id=1, source_target_pairs={{0,4},{4,0},{8,12},{12,8},{1,5},{5,1},{9,13},{13,9},{2,6},{6,2},{1... | collective-permute-start | bytes 688136 | tf_op jit(solution)/shard_map/ppermute | solution.py:357
  258.3 2.9 collective-permute-start.17
  (259 shorter events, 172.2 us)
Async XLA Ops:
  5.9 17.2 %collective-permute-start.36 = (bf16[224,512]{1,0:T(8,128)(2,1)S(1)}, bf16[224,512]{1,0:T(8,128)(2,1)S(1)}, u32[]{:S(2)}, u32[]{:S(2)}) collective-permute-start(bf16[224,512]{1,0:T(8,128)(2,1)S(1)} %bitcast.192), channel_id=1, source_target_pairs={{0,4},{4,0},{8,12},{12,8},{1,5},{5,1},{9,13},{13,9},{2,6},{6,2},{1... | collective-permute-start | bytes 688136 | tf_op jit(solution)/shard_map/ppermute | solution.py:357
  28.2 34.4 %collective-permute-start.38 = (bf16[224,512]{1,0:T(8,128)(2,1)}, bf16[224,512]{1,0:T(8,128)(2,1)}, u32[]{:S(2)}, u32[]{:S(2)}) collective-permute-start(bf16[224,512]{1,0:T(8,128)(2,1)} %fusion.1), channel_id=1, source_target_pairs={{0,4},{4,0},{8,12},{12,8},{1,5},{5,1},{9,13},{13,9},{2,6},{6,2},{1... | collective-permute-start | bytes 688136 | tf_op jit(solution)/shard_map/ppermute | solution.py:357
  62.1 12.6 %collective-permute-start.7 = (bf16[64,2048]{1,0:T(8,128)(2,1)}, bf16[64,2048]{1,0:T(8,128)(2,1)S(1)}, u32[]{:S(2)}, u32[]{:S(2)}) collective-permute-start(bf16[64,2048]{1,0:T(8,128)(2,1)} %get-tuple-element.18), channel_id=1, source_target_pairs={{0,2},{1,3},{2,0},{3,1},{4,6},{5,7},{6,4},{7,5},{8,10},{9,11},{10,... | collective-permute-start | bytes 786440 | tf_op jit(solution)/shard_map/ppermute | solution.py:285
  62.4 13.0 %collective-permute-start.8 = (bf16[64,2048]{1,0:T(8,128)(2,1)S(1)}, bf16[64,2048]{1,0:T(8,128)(2,1)S(1)}, u32[]{:S(2)}, u32[]{:S(2)}) collective-permute-start(bf16[64,2048]{1,0:T(8,128)(2,1)S(1)} %get-tuple-element.19), channel_id=1, source_target_pairs={{0,1},{1,2},{2,3},{3,0},{4,5},{5,6},{6,7},{7,4},{8,9},{9,10},{10,1... | collective-permute-start | bytes 786440 | tf_op jit(solution)/shard_map/ppermute | solution.py:285
  63.7 16.3 %collective-permute-start.39 = (bf16[224,512]{1,0:T(8,128)(2,1)S(1)}, bf16[224,512]{1,0:T(8,128)(2,1)S(1)}, u32[]{:S(2)}, u32[]{:S(2)}) collective-permute-start(bf16[224,512]{1,0:T(8,128)(2,1)S(1)} %fusion.2), channel_id=1, source_target_pairs={{4,8},{8,4},{5,9},{9,5},{6,10},{10,6},{7,11},{11,7},{20,24},{24,20... | collective-permute-start | bytes 688136 | tf_op jit(solution)/shard_map/ppermute | solution.py:363
  87.8 9.4 %collective-permute-start.41 = (bf16[224,512]{1,0:T(8,128)(2,1)S(1)}, bf16[224,512]{1,0:T(8,128)(2,1)S(1)}, u32[]{:S(2)}, u32[]{:S(2)}) collective-permute-start(bf16[224,512]{1,0:T(8,128)(2,1)S(1)} %fusion.4), channel_id=1, source_target_pairs={{4,8},{8,4},{5,9},{9,5},{6,10},{10,6},{7,11},{11,7},{20,24},{24,20... | collective-permute-start | bytes 688136 | tf_op jit(solution)/shard_map/ppermute | solution.py:363
  91.0 9.6 %collective-permute-start.9 = (bf16[224,512]{1,0:T(8,128)(2,1)S(1)}, bf16[224,512]{1,0:T(8,128)(2,1)S(1)}, u32[]{:S(2)}, u32[]{:S(2)}) collective-permute-start(bf16[224,512]{1,0:T(8,128)(2,1)S(1)} %get-tuple-element.52), channel_id=1, source_target_pairs={{0,4},{4,0},{8,12},{12,8},{1,5},{5,1},{9,13},{13,9},{2,6},{6,2},{1... | collective-permute-start | bytes 688136 | tf_op jit(solution)/shard_map/ppermute | solution.py:357
  95.2 10.3 %collective-permute-start.18 = (bf16[224,512]{1,0:T(8,128)(2,1)S(1)}, bf16[224,512]{1,0:T(8,128)(2,1)S(1)}, u32[]{:S(2)}, u32[]{:S(2)}) collective-permute-start(bf16[224,512]{1,0:T(8,128)(2,1)S(1)} %get-tuple-element.51), channel_id=1, source_target_pairs={{0,4},{4,0},{8,12},{12,8},{1,5},{5,1},{9,13},{13,9},{2,6},{6,2},{1... | collective-permute-start | bytes 688136 | tf_op jit(solution)/shard_map/ppermute | solution.py:357
  95.2 14.5 %collective-permute-start.27 = (bf16[224,512]{1,0:T(8,128)(2,1)S(1)}, bf16[224,512]{1,0:T(8,128)(2,1)S(1)}, u32[]{:S(2)}, u32[]{:S(2)}) collective-permute-start(bf16[224,512]{1,0:T(8,128)(2,1)S(1)} %get-tuple-element.50), channel_id=1, source_target_pairs={{0,4},{4,0},{8,12},{12,8},{1,5},{5,1},{9,13},{13,9},{2,6},{6,2},{1... | collective-permute-start | bytes 688136 | tf_op jit(solution)/shard_map/ppermute | solution.py:357
  98.0 14.2 %collective-permute-start.42 = (bf16[224,512]{1,0:T(8,128)(2,1)S(1)}, bf16[224,512]{1,0:T(8,128)(2,1)S(1)}, u32[]{:S(2)}, u32[]{:S(2)}) collective-permute-start(bf16[224,512]{1,0:T(8,128)(2,1)S(1)} %fusion.5), channel_id=1, source_target_pairs={{0,4},{4,0},{8,12},{12,8},{1,5},{5,1},{9,13},{13,9},{2,6},{6,2},{1... | collective-permute-start | bytes 688136 | tf_op jit(solution)/shard_map/ppermute | solution.py:357
  115.2 14.5 %collective-permute-start.10 = (bf16[224,512]{1,0:T(8,128)(2,1)S(1)}, bf16[224,512]{1,0:T(8,128)(2,1)S(1)}, u32[]{:S(2)}, u32[]{:S(2)}) collective-permute-start(bf16[224,512]{1,0:T(8,128)(2,1)S(1)} %get-tuple-element.56), channel_id=1, source_target_pairs={{4,8},{8,4},{5,9},{9,5},{6,10},{10,6},{7,11},{11,7},{20,24},{24,20... | collective-permute-start | bytes 688136 | tf_op jit(solution)/shard_map/ppermute | solution.py:363
  115.9 13.8 %collective-permute-start.19 = (bf16[224,512]{1,0:T(8,128)(2,1)S(1)}, bf16[224,512]{1,0:T(8,128)(2,1)S(1)}, u32[]{:S(2)}, u32[]{:S(2)}) collective-permute-start(bf16[224,512]{1,0:T(8,128)(2,1)S(1)} %get-tuple-element.55), channel_id=1, source_target_pairs={{4,8},{8,4},{5,9},{9,5},{6,10},{10,6},{7,11},{11,7},{20,24},{24,20... | collective-permute-start | bytes 688136 | tf_op jit(solution)/shard_map/ppermute | solution.py:363
  118.9 15.1 %collective-permute-start.29 = (bf16[224,512]{1,0:T(8,128)(2,1)}, bf16[224,512]{1,0:T(8,128)(2,1)S(1)}, u32[]{:S(2)}, u32[]{:S(2)}) collective-permute-start(bf16[224,512]{1,0:T(8,128)(2,1)} %fusion.9), channel_id=1, source_target_pairs={{0,4},{4,0},{8,12},{12,8},{1,5},{5,1},{9,13},{13,9},{2,6},{6,2},{1... | collective-permute-start | bytes 688136 | tf_op jit(solution)/shard_map/ppermute | solution.py:357
  128.9 10.9 %collective-permute-start.43 = (bf16[224,512]{1,0:T(8,128)(2,1)}, bf16[224,512]{1,0:T(8,128)(2,1)S(1)}, u32[]{:S(2)}, u32[]{:S(2)}) collective-permute-start(bf16[224,512]{1,0:T(8,128)(2,1)} %get-tuple-element.53), channel_id=1, source_target_pairs={{4,8},{8,4},{5,9},{9,5},{6,10},{10,6},{7,11},{11,7},{20,24},{24,20... | collective-permute-start | bytes 688136 | tf_op jit(solution)/shard_map/ppermute | solution.py:363
  138.5 8.1 %collective-permute-start.20 = (bf16[224,512]{1,0:T(8,128)(2,1)}, bf16[224,512]{1,0:T(8,128)(2,1)S(1)}, u32[]{:S(2)}, u32[]{:S(2)}) collective-permute-start(bf16[224,512]{1,0:T(8,128)(2,1)} %get-tuple-element.58), channel_id=1, source_target_pairs={{0,4},{4,0},{8,12},{12,8},{1,5},{5,1},{9,13},{13,9},{2,6},{6,2},{1... | collective-permute-start | bytes 688136 | tf_op jit(solution)/shard_map/ppermute | solution.py:357
  138.5 8.1 %collective-permute-start.30 = (bf16[224,512]{1,0:T(8,128)(2,1)}, bf16[224,512]{1,0:T(8,128)(2,1)}, u32[]{:S(2)}, u32[]{:S(2)}) collective-permute-start(bf16[224,512]{1,0:T(8,128)(2,1)} %get-tuple-element.57), channel_id=1, source_target_pairs={{4,8},{8,4},{5,9},{9,5},{6,10},{10,6},{7,11},{11,7},{20,24},{24,20... | collective-permute-start | bytes 688136 | tf_op jit(solution)/shard_map/ppermute | solution.py:363
  160.9 16.6 %collective-permute-start.33 = (bf16[224,512]{1,0:T(8,128)(2,1)}, bf16[224,512]{1,0:T(8,128)(2,1)}, u32[]{:S(2)}, u32[]{:S(2)}) collective-permute-start(bf16[224,512]{1,0:T(8,128)(2,1)} %fusion.13), channel_id=1, source_target_pairs={{0,4},{4,0},{8,12},{12,8},{1,5},{5,1},{9,13},{13,9},{2,6},{6,2},{1... | collective-permute-start | bytes 688136 | tf_op jit(solution)/shard_map/ppermute | solution.py:357
  182.3 14.7 %collective-permute-start.22 = (bf16[224,512]{1,0:T(8,128)(2,1)}, bf16[224,512]{1,0:T(8,128)(2,1)}, u32[]{:S(2)}, u32[]{:S(2)}) collective-permute-start(bf16[224,512]{1,0:T(8,128)(2,1)} %get-tuple-element.46), channel_id=1, source_target_pairs={{0,4},{4,0},{8,12},{12,8},{1,5},{5,1},{9,13},{13,9},{2,6},{6,2},{1... | collective-permute-start | bytes 688136 | tf_op jit(solution)/shard_map/ppermute | solution.py:357
  203.9 14.5 %collective-permute-start.24 = (bf16[224,512]{1,0:T(8,128)(2,1)}, bf16[224,512]{1,0:T(8,128)(2,1)}, u32[]{:S(2)}, u32[]{:S(2)}) collective-permute-start(bf16[224,512]{1,0:T(8,128)(2,1)} %fusion.21), channel_id=1, source_target_pairs={{0,4},{4,0},{8,12},{12,8},{1,5},{5,1},{9,13},{13,9},{2,6},{6,2},{1... | collective-permute-start | bytes 688136 | tf_op jit(solution)/shard_map/ppermute | solution.py:357
  230.8 17.5 %collective-permute-start.15 = (bf16[224,512]{1,0:T(8,128)(2,1)}, bf16[224,512]{1,0:T(8,128)(2,1)}, u32[]{:S(2)}, u32[]{:S(2)}) collective-permute-start(bf16[224,512]{1,0:T(8,128)(2,1)} %fusion.29), channel_id=1, source_target_pairs={{0,4},{4,0},{8,12},{12,8},{1,5},{5,1},{9,13},{13,9},{2,6},{6,2},{1... | collective-permute-start | bytes 688136 | tf_op jit(solution)/shard_map/ppermute | solution.py:357
  251.5 53.5 %collective-permute-start.44 = (bf16[224,512]{1,0:T(8,128)(2,1)}, bf16[224,512]{1,0:T(8,128)(2,1)S(1)}, u32[]{:S(2)}, u32[]{:S(2)}) collective-permute-start(bf16[224,512]{1,0:T(8,128)(2,1)} %get-tuple-element.36), channel_id=1, source_target_pairs={{0,4},{4,0},{8,12},{12,8},{1,5},{5,1},{9,13},{13,9},{2,6},{6,2},{1... | collective-permute-start | bytes 688136 | tf_op jit(solution)/shard_map/ppermute | solution.py:357
  255.1 54.8 %collective-permute-start.35 = (bf16[224,512]{1,0:T(8,128)(2,1)}, bf16[224,512]{1,0:T(8,128)(2,1)S(1)}, u32[]{:S(2)}, u32[]{:S(2)}) collective-permute-start(bf16[224,512]{1,0:T(8,128)(2,1)} %get-tuple-element.45), channel_id=1, source_target_pairs={{0,4},{4,0},{8,12},{12,8},{1,5},{5,1},{9,13},{13,9},{2,6},{6,2},{1... | collective-permute-start | bytes 688136 | tf_op jit(solution)/shard_map/ppermute | solution.py:357
  255.2 57.2 %collective-permute-start.26 = (bf16[224,512]{1,0:T(8,128)(2,1)}, bf16[224,512]{1,0:T(8,128)(2,1)S(1)}, u32[]{:S(2)}, u32[]{:S(2)}) collective-permute-start(bf16[224,512]{1,0:T(8,128)(2,1)} %get-tuple-element.48), channel_id=1, source_target_pairs={{0,4},{4,0},{8,12},{12,8},{1,5},{5,1},{9,13},{13,9},{2,6},{6,2},{1... | collective-permute-start | bytes 688136 | tf_op jit(solution)/shard_map/ppermute | solution.py:357
  258.3 56.6 %collective-permute-start.17 = (bf16[224,512]{1,0:T(8,128)(2,1)S(1)}, bf16[224,512]{1,0:T(8,128)(2,1)S(1)}, u32[]{:S(2)}, u32[]{:S(2)}) collective-permute-start(bf16[224,512]{1,0:T(8,128)(2,1)S(1)} %fusion.31), channel_id=1, source_target_pairs={{0,4},{4,0},{8,12},{12,8},{1,5},{5,1},{9,13},{13,9},{2,6},{6,2},{1... | collective-permute-start | bytes 688136 | tf_op jit(solution)/shard_map/ppermute | solution.py:357
  (81 other events, 422.8 us)

commit v2 on v1

v2 whole, which is shorter than its diff:
```python
import functools

import jax
import jax.numpy as jnp
from jax import lax
from jax.experimental import pallas as pl
from jax.experimental.pallas import tpu as pltpu
from jax.sharding import PartitionSpec as P

GROUP_ROWS = 16
CAP = 4
LIVE_ROWS = 224
TAG = 128
CHUNK = 1024
TILE = 512
BF16 = jnp.bfloat16
F32 = jnp.float32
MIB = 1024 * 1024


def dot(a, b):
    return jnp.dot(a, b, preferred_element_type=F32)


def dot_rows(a, b):
    return lax.dot_general(a, b, (((0,), (0,)), ((), ())), preferred_element_type=F32)


def dot_cols(a, b):
    return lax.dot_general(a, b, (((1,), (1,)), ((), ())), preferred_element_type=F32)


def iota(shape, dim):
    return lax.broadcasted_iota(jnp.int32, shape, dim)


def params(mib=16):
    return pltpu.CompilerParams(vmem_limit_bytes=mib * MIB)


def cost(flops, elements):
    return pl.CostEstimate(flops=flops, bytes_accessed=2 * elements, transcendentals=0)


ANY = pl.BlockSpec(memory_space=pl.ANY)
VMEM = pl.BlockSpec(memory_space=pltpu.VMEM)


def prepare_kernel(replicas, owner_in, slot_in, live_in, x, compact_x, sent, pick, place, owner, slot, live, sems):
    copies = [
        pltpu.make_async_copy(src, dst, sems.at[i])
        for i, (src, dst) in enumerate(((owner_in, owner), (slot_in, slot), (live_in, live)))
    ]
    for copy in copies:
        copy.start()
    for copy in copies:
        copy.wait()
    me = lax.axis_index("replica")
    rows, feat = x.shape
    groups = rows // GROUP_ROWS
    out_rows = sent.shape[0]
    lane = iota((1, rows), 1)
    lane_group, lane_slot = lane // GROUP_ROWS, lane % GROUP_ROWS
    row_group = iota((rows, TAG), 0) // GROUP_ROWS
    packed = jnp.full((1, rows), -1, jnp.int32)
    target = jnp.zeros((1, rows), jnp.int32)
    tags = jnp.zeros((rows, TAG), F32)
    owners = [owner[g] for g in range(groups)]
    offset = jnp.int32(0)
    used = [jnp.int32(0)] * replicas
    for g in range(groups):
        count = live[g]
        mine = lane_group == g
        packed = jnp.where(mine & (lane_slot < count), offset + lane_slot, packed)
        offset = offset + count
        position = jnp.int32(0)
        for o in range(replicas):
            hit = owners[g] == o
            position = jnp.where(hit, used[o], position)
            used[o] = used[o] + hit.astype(jnp.int32)
        hop = lax.rem(owners[g] - me + replicas, replicas)
        start = (hop * CAP + position) * GROUP_ROWS
        target = jnp.where(mine, start + lane_slot, target)
        tags = jnp.where(row_group == g, slot[g].astype(F32), tags)
    compact = (iota((LIVE_ROWS, rows), 0) == packed).astype(BF16)
    spread = (iota((out_rows, rows), 0) == target).astype(BF16)
    pick[...] = compact
    place[...] = dot_cols(compact, spread).astype(BF16)
    compact_x[...] = dot(compact, x[...]).astype(BF16)
    sent[:, :feat] = dot(spread, x[...]).astype(BF16)
    sent[:, feat:] = dot(spread, tags.astype(BF16)).astype(BF16)


def prepare(owner, slot, live, x, replicas):
    rows, feat = x.shape
    out_rows = replicas * CAP * GROUP_ROWS
    smalls = [pltpu.SMEM(a.shape, jnp.int32) for a in (owner, slot, live)]
    return pl.pallas_call(
        functools.partial(prepare_kernel, replicas),
        out_shape=(
            jax.ShapeDtypeStruct((LIVE_ROWS, feat), BF16),
            jax.ShapeDtypeStruct((out_rows, feat + TAG), BF16),
            jax.ShapeDtypeStruct((LIVE_ROWS, rows), BF16),
            jax.ShapeDtypeStruct((LIVE_ROWS, out_rows), BF16),
        ),
        in_specs=[ANY, ANY, ANY, VMEM],
        out_specs=(VMEM,) * 4,
        scratch_shapes=smalls + [pltpu.SemaphoreType.DMA((3,))],
        compiler_params=params(),
        name="prepare",
    )(owner, slot, live, x)


def first_kernel(at, x, w, out):
    out[...] = dot(x[...], w[...]).astype(BF16)


def first_chunk(at, x, weight):
    feat, _ = weight.shape
    tiles = CHUNK // TILE
    return pl.pallas_call(
        first_kernel,
        out_shape=jax.ShapeDtypeStruct((LIVE_ROWS, CHUNK), BF16),
        grid_spec=pltpu.PrefetchScalarGridSpec(
            num_scalar_prefetch=1,
            grid=(tiles,),
            in_specs=[
                pl.BlockSpec((LIVE_ROWS, feat), lambda i, at: (0, 0)),
                pl.BlockSpec((feat, TILE), lambda i, at: (0, at[0] * tiles + i)),
            ],
            out_specs=pl.BlockSpec((LIVE_ROWS, TILE), lambda i, at: (0, i)),
        ),
        compiler_params=params(48),
        cost_estimate=cost(2 * LIVE_ROWS * feat * CHUNK, (feat + LIVE_ROWS) * CHUNK),
        name="first",
    )(at, x, weight)


def base_kernel(x, w, token_in, out, token):
    wide = dot(x[...], w[...]).astype(BF16)
    for j in range(out.shape[0]):
        out[j] = wide[:, j * CHUNK : (j + 1) * CHUNK]


def base_chunks(x, weight, token, group=2):
    feat, width = weight.shape
    number = width // CHUNK
    return pl.pallas_call(
        base_kernel,
        out_shape=(
            jax.ShapeDtypeStruct((number, LIVE_ROWS, CHUNK), BF16),
            jax.ShapeDtypeStruct(token.shape, token.dtype),
        ),
        grid=(number // group,),
        in_specs=[
            pl.BlockSpec((LIVE_ROWS, feat), lambda i: (0, 0)),
            pl.BlockSpec((feat, group * CHUNK), lambda i: (0, i)),
            ANY,
        ],
        out_specs=(pl.BlockSpec((group, LIVE_ROWS, CHUNK), lambda i: (i, 0, 0)), ANY),
        input_output_aliases={2: 1},
        compiler_params=params(48),
        cost_estimate=cost(2 * LIVE_ROWS * feat * width, (feat + LIVE_ROWS) * width),
        name="base",
    )(x, weight, token)


def hop_kernel(at, base, *refs):
    out = refs[-2]
    total = base[0].astype(F32)
    if len(refs) == 4:
        total = total + refs[0][...].astype(F32)
    out[...] = total.astype(BF16)


def hop(chunk, base, got, token):
    here = pl.BlockSpec((LIVE_ROWS, TILE), lambda i, at: (0, i))
    inputs = [base] + ([got] if got is not None else []) + [token]
    return pl.pallas_call(
        hop_kernel,
        out_shape=(
            jax.ShapeDtypeStruct((LIVE_ROWS, CHUNK), BF16),
            jax.ShapeDtypeStruct(token.shape, token.dtype),
        ),
        grid_spec=pltpu.PrefetchScalarGridSpec(
            num_scalar_prefetch=1,
            grid=(CHUNK // TILE,),
            in_specs=[pl.BlockSpec((1, LIVE_ROWS, TILE), lambda i, at: (at[0], 0, i))]
            + [here] * (len(inputs) - 2)
            + [ANY],
            out_specs=(here, ANY),
        ),
        input_output_aliases={len(inputs): 1},
        compiler_params=params(),
        cost_estimate=cost(2 * LIVE_ROWS * CHUNK, 3 * LIVE_ROWS * CHUNK),
        name="hop",
    )(chunk.reshape(1), *inputs)


def fold(rank, adapters, half):
    shape = (adapters * rank, 2 * rank)
    return (iota(shape, 0) % rank + half * rank == iota(shape, 1)).astype(BF16)


def slot_mask(tag, rank, adapters):
    shape = (tag.shape[0], adapters * rank)
    return (iota(shape, 1) // rank).astype(F32) == tag.astype(F32)


def low_kernel(rank, blocks, down, *refs):
    parts, low = refs[:blocks], refs[blocks + 1]
    adapters = down.shape[0] // rank
    feat = down.shape[1]
    rows = parts[0].shape[0]
    half = blocks // 2
    maps = down[...]
    folds = [fold(rank, adapters, h) for h in range(2)]
    for k in range(half):
        total = None
        for h in range(2):
            part = parts[h * half + k]
            wide = dot_cols(part[:, :feat], maps)
            kept = jnp.where(slot_mask(part[:, feat : feat + 1], rank, adapters), wide, 0.0)
            got = dot(kept.astype(BF16), folds[h])
            total = got if total is None else total + got
        low[k * rows : (k + 1) * rows, :] = total.astype(BF16)


def low_values(parts, down, rank, token):
    rows, width = parts[0].shape
    blocks = len(parts)
    return pl.pallas_call(
        functools.partial(low_kernel, rank, blocks),
        out_shape=(
            jax.ShapeDtypeStruct((blocks // 2 * rows, 2 * rank), BF16),
            jax.ShapeDtypeStruct(token.shape, token.dtype),
        ),
        in_specs=[VMEM] * (blocks + 1) + [ANY],
        out_specs=(VMEM, ANY),
        input_output_aliases={blocks + 1: 1},
        compiler_params=params(),
        name="low",
    )(down, *parts, token)


def delta_kernel(rank, blocks, sums, up, *refs):
    tags, lows, outs = refs[:blocks], refs[blocks : blocks + sums], refs[blocks + sums + 1 :]
    adapters = up.shape[0] // rank
    rows = tags[0].shape[0]
    half = blocks // 2
    total = lows[0][...].astype(F32)
    for other in lows[1:]:
        total = total + other[...].astype(F32)
    low = total.astype(BF16)
    maps = up[...]
    for h in range(2):
        spread = fold(rank, adapters, h)
        for k in range(half):
            wide = dot_cols(low[k * rows : (k + 1) * rows, :], spread)
            mask = slot_mask(tags[h * half + k][:, :1], rank, adapters)
            kept = jnp.where(mask, wide, 0.0).astype(BF16)
            outs[h * half + k][...] = dot(kept, maps).astype(BF16)


def delta_values(parts, lows, up, rank, token):
    rows, width = parts[0].shape
    blocks = len(parts)
    columns = up.shape[1]
    tag = pl.BlockSpec((rows, TAG), lambda i: (0, width // TAG - 1))
    whole = lambda a: pl.BlockSpec(a.shape, lambda i: (0, 0))
    return pl.pallas_call(
        functools.partial(delta_kernel, rank, blocks, len(lows)),
        out_shape=[jax.ShapeDtypeStruct((rows, columns), BF16)] * blocks
        + [jax.ShapeDtypeStruct(token.shape, token.dtype)],
        grid=(1,),
        in_specs=[whole(up)] + [tag] * blocks + [whole(a) for a in lows] + [ANY],
        out_specs=[pl.BlockSpec((rows, columns), lambda i: (0, 0))] * blocks + [ANY],
        input_output_aliases={1 + blocks + len(lows): blocks},
        compiler_params=params(),
        name="delta",
    )(up, *parts, *lows, token)


def add_delta_kernel(blocks, at, base, place, *refs):
    parts, out = refs[:blocks], refs[blocks + 1]
    rows = parts[0].shape[0]
    total = base[0].astype(F32)
    for k in range(blocks):
        total = total + dot(place[:, k * rows : (k + 1) * rows], parts[k][...])
    out[0] = total.astype(BF16)


def add_delta(first, base, place, parts, token):
    rows, columns = parts[0].shape
    chunk = base.shape[2]
    here = pl.BlockSpec((1, LIVE_ROWS, chunk), lambda i, at: (at[0] + i, 0, 0))
    return pl.pallas_call(
        functools.partial(add_delta_kernel, len(parts)),
        out_shape=(
            jax.ShapeDtypeStruct(base.shape, base.dtype),
            jax.ShapeDtypeStruct(token.shape, token.dtype),
        ),
        grid_spec=pltpu.PrefetchScalarGridSpec(
            num_scalar_prefetch=1,
            grid=(columns // chunk,),
            in_specs=[here, pl.BlockSpec(place.shape, lambda i, at: (0, 0))]
            + [pl.BlockSpec((rows, chunk), lambda i, at: (0, i))] * len(parts)
            + [ANY],
            out_specs=(here, ANY),
        ),
        input_output_aliases={1: 0, 3 + len(parts): 1},
        compiler_params=params(),
        name="add_delta",
    )(first, base, place, *parts, token)


def finish_kernel(at, base, left, right, pick, held, token_in, out, token):
    @pl.when(at[1] > 0)
    def _():
        total = base[0].astype(F32) + left[...].astype(F32) + right[...].astype(F32)
        out[...] = dot_rows(pick[...], total.astype(BF16)).astype(BF16)

    @pl.when(at[1] == 0)
    def _():
        out[...] = held[...]


def finish(at, base, left, right, pick, held, token):
    rows = pick.shape[1]
    tiles = CHUNK // TILE
    got = pl.BlockSpec((LIVE_ROWS, TILE), lambda i, at: (0, i))
    here = pl.BlockSpec((rows, TILE), lambda i, at: (0, at[0] * tiles + i))
    return pl.pallas_call(
        finish_kernel,
        out_shape=(
            jax.ShapeDtypeStruct(held.shape, BF16),
            jax.ShapeDtypeStruct(token.shape, token.dtype),
        ),
        grid_spec=pltpu.PrefetchScalarGridSpec(
            num_scalar_prefetch=1,
            grid=(tiles,),
            in_specs=[
                pl.BlockSpec((1, LIVE_ROWS, TILE), lambda i, at: (at[0], 0, i)),
                got,
                got,
                pl.BlockSpec(pick.shape, lambda i, at: (0, 0)),
                here,
                ANY,
            ],
            out_specs=(here, ANY),
        ),
        input_output_aliases={5: 0, 6: 1},
        compiler_params=params(),
        cost_estimate=cost(2 * LIVE_ROWS * rows * CHUNK, 6 * LIVE_ROWS * CHUNK),
        name="finish",
    )(at, base, left, right, pick, held, token)


def send_groups(sent):
    replicas = lax.axis_size("replica")
    rows = CAP * GROUP_ROWS
    parts = [sent[:rows]]
    for k in range(1, replicas):
        hops = [(i, (i + k) % replicas) for i in range(replicas)]
        parts.append(lax.ppermute(sent[k * rows : (k + 1) * rows], "replica", hops))
    return parts


def send_lows(low):
    shards = lax.axis_size("tensor")
    if shards > 4:
        return [lax.psum(low, "tensor")]
    lows = [low]
    for k in range(1, shards):
        hops = [(i, (i + k) % shards) for i in range(shards)]
        lows.append(lax.ppermute(low, "tensor", hops))
    return lows


def send_back(made):
    replicas = lax.axis_size("replica")
    back = [made[0]]
    for k in range(1, replicas):
        hops = [(i, (i - k) % replicas) for i in range(replicas)]
        back.append(lax.ppermute(made[k], "replica", hops))
    return back


def on_device(x, owner, slot, live, weight, down, up):
    rows = x.shape[0]
    width = weight.shape[1]
    rank = down.shape[1]
    replicas, shards = lax.axis_size("replica"), lax.axis_size("tensor")
    z = lax.axis_index("tensor").astype(jnp.int32)
    compact_x, sent, pick, place = prepare(owner[:, 0], slot, live[0], x, replicas)
    share = width // shards
    down, up = down.reshape(-1, down.shape[2]), up.reshape(-1, up.shape[2])
    token = jnp.zeros((8, 128), jnp.int32)
    if shards != 4:
        base = dot(compact_x, weight)
        parts = send_groups(sent)
        low, token = low_values(parts, down, rank, token)
        *made, token = delta_values(parts, send_lows(low), up, rank, token)
        back = jnp.concatenate(send_back(made), axis=0)
        mine = lax.dynamic_slice_in_dim(base, z * share, share, 1) + dot(place, back)
        base = lax.dynamic_update_slice_in_dim(base, mine, z * share, 1).astype(BF16)
        total = lax.psum_scatter(base, "tensor", scatter_dimension=1, tiled=True)
        total = lax.all_gather(total, "tensor", axis=1, tiled=True)
        return dot_rows(pick, total).astype(BF16)

    chunks, per = width // CHUNK, share // CHUNK
    inner = (z == 1) | (z == 2)
    even_right, odd_right = z % 2 == 0, z % 2 == 1
    even = [(0, 1), (1, 0), (2, 3), (3, 2)]
    odd = [(1, 2), (2, 1)]

    def chunk_of(position, right):
        return jnp.clip(jnp.where(right, chunks - 1 - position, position), 0, chunks - 1)

    def even_chunk(step):
        return chunk_of(step - jnp.where(inner, 3, 0), even_right)

    def odd_chunk(step):
        return chunk_of(jnp.int32(step - 1), odd_right)

    evens, odds = {}, {}
    result = jnp.zeros((rows, width), BF16)
    message = first_chunk(even_chunk(0).reshape(1), compact_x, weight)
    evens[0] = lax.ppermute(message, "tensor", even)
    parts = send_groups(sent)
    base, token = base_chunks(compact_x, weight, token)
    unfinished = list(range(chunks + 3))
    seen_even, seen_odd = set(), set()

    def close(result, token, base):
        for a in list(unfinished):
            b = chunks - a
            if a not in seen_even or (1 <= b <= chunks and b not in seen_odd):
                continue
            unfinished.remove(a)
            position = jnp.where(inner, a, a - 3)
            valid = (position >= 0) & (position < chunks)
            at = jnp.stack([chunk_of(position, ~even_right), valid.astype(jnp.int32)])
            other = odds[b] if 1 <= b <= chunks else odds[1]
            result, token = finish(at, base, evens[a], other, pick, result, token)
        return result, token

    for step in range(1, chunks + 3):
        message, token = hop(even_chunk(step), base, odds.get(step - 2), token)
        evens[step] = lax.ppermute(message, "tensor", even)
        seen_odd.add(step - 2)
        if step == 1:
            low, token = low_values(parts, down, rank, token)
            lows = send_lows(low)
        if step == 2:
            *made, token = delta_values(parts, lows, up, rank, token)
            back = send_back(made)
        if step == 3 + per - 1:
            base, token = add_delta((z * per).reshape(1), base, place, back, token)
        result, token = close(result, token, base)
        if step <= chunks:
            message, token = hop(odd_chunk(step), base, evens[step - 1], token)
            odds[step] = lax.ppermute(message, "tensor", odd)
        seen_even.add(step - 1)
        result, token = close(result, token, base)
    seen_even.add(chunks + 2)
    result, token = close(result, token, base)
    return result


def solution(mesh):
    placed = (
        P(("parts", "replica"), "tensor"),
        P(("parts", "replica"), None),
        P(("parts", "replica")),
        P(("parts", "replica"), None),
        P("tensor", None),
        P("replica", None, "tensor"),
        P("replica", None, "tensor"),
    )
    return jax.shard_map(
        on_device,
        mesh=mesh,
        in_specs=placed,
        out_specs=P(("parts", "replica"), None),
        check_vma=False,
    )
```

time: 319 us -> 177 us (0.55)
  starting transfers between devices: 109 us -> 42.2 us
  other arithmetic: 51 us -> 0.82 us
  waiting for transfers between devices: 67.5 us -> 19.4 us
  local copies, waits for them, and re-layouts: 15.9 us -> 41.3 us
    ppermute x45 -> x28, starting transfers between devices: 109 us -> 42.2 us  [the longest x10 21.1 us: on_device(): evens[step] = lax.ppermute(message, 'tensor', even)]
    ppermute x45 -> x28, waiting for transfers between devices: 67.5 us -> 19.4 us  [the longest x3 9.76 us: send_back(): back.append(lax.ppermute(made[k], 'replica', hops))]
    convert_element_type x21 -> x0, other arithmetic: 33.8 us -> none  [the longest x11 17.3 us: on_device(): message = (message.astype(F32) + odds[step - SKEW].astype(F32)).astype(BF16)]
    unnamed x120 -> x70, local copies, waits for them, and re-layouts: 13.4 us -> 38.7 us
    another operation x19 -> x11, other arithmetic: 10.7 us -> 0.82 us  [close(): at = jnp.stack([chunk_of(position, ~even_right), valid.astype(jnp.int32)])]
    select_n x4 -> x0, other arithmetic: 6.52 us -> none  [term(): return jnp.where(chunk // per == z, near, plain)]
    pallas_call x23 -> x32, Pallas kernels: 67.7 us -> 65.5 us  [the longest x11 31.8 us: finish(): pl.pallas_call(finish_kernel, out_shape=(jax.ShapeDtypeStruct(held.shape,...]
  transfers between devices with their start and end apart: 45 -> 28, of which waited for: 21 -> 7; matrix products, arithmetic and copies ran while one was open for 9% -> 2% of each run, Pallas kernels for 21% -> 37%
where the time goes in v2:
time: 177 us; the launch traced here: 176 us
  Pallas kernels  71.9 us (41%)
  starting transfers between devices  42.2 us (24%)
  local copies, waits for them, and re-layouts  41.3 us (23%)
  waiting for transfers between devices  19.4 us (11%)
    unnamed x70, local copies, waits for them, and re-layouts  38.7 us
    pallas_call x11, Pallas kernels, finish(): pl.pallas_call(finish_kernel, out_shape=(jax.ShapeDtypeStruct(held.shape,...  31.8 us
    ppermute x10, starting transfers between devices, on_device(): evens[step] = lax.ppermute(message, 'tensor', even)  21.1 us
    pallas_call x18, Pallas kernels, hop(): pl.pallas_call(hop_kernel, out_shape=(jax.ShapeDtypeStruct((LIVE_ROWS, CH...  21.1 us
    ppermute x3, waiting for transfers between devices, send_back(): back.append(lax.ppermute(made[k], 'replica', hops))  9.76 us
    pallas_call x1, Pallas kernels, base_chunks(): pl.pallas_call(base_kernel, out_shape=(jax.ShapeDtypeStruct((number, LIVE...  8.15 us
    ppermute x8, starting transfers between devices, on_device(): odds[step] = lax.ppermute(message, 'tensor', odd)  7.1 us
    ppermute x3, starting transfers between devices, send_lows(): lows.append(lax.ppermute(low, 'tensor', hops))  5.52 us
  transfers between devices with their start and end apart: 28, of which 7 were waited for; matrix products, arithmetic and copies ran while one was open for 2% of the time, Pallas kernels for 37%

profile of v2, /device:TPU:0, one launch (start us, length us, event | category | flops | bytes accessed | tf_op | source)
XLA Modules:
  0.0 175.9 jit_solution(7839363747550949783)
XLA Ops:
  6.4 3.1 %collective-permute-start.6 = (bf16[224,1024]{1,0:T(8,128)(2,1)S(1)}, bf16[224,1024]{1,0:T(8,128)(2,1)S(1)}, u32[]{:S(2)}, u32[]{:S(2)}) collective-permute-start(bf16[224,1024]{1,0:T(8,128)(2,1)S(1)} %first.1), channel_id=1, source_target_pairs={{0,4},{4,0},{8,12},{12,8},{1,5},{5,1},{9,13},{13,9},{2,6},{6,2},{1... | collective-permute-start | bytes 1376264 | tf_op jit(solution)/shard_map/ppermute | solution.py:429
  9.5 8.2 %base.1 = (bf16[8,224,1024]{2,1,0:T(8,128)(2,1)S(1)}, s32[8,128]{1,0:T(8,128)S(1)}) custom-call(bf16[224,1024]{1,0:T(8,128)(2,1)S(1)} %get-tuple-element.77.x, bf16[1024,8192]{1,0:T(8,128)(2,1)} %w.3, s32[8,128]{1,0:T(8,128)S(1)} %broadcast_in_dim.6.token_in), custom_call_target="tpu_custom_call", output_to_operand_aliasing={{1}: (2, {})} | custom-call | flops 3758096384 | bytes 20447232 | tf_op jit(solution)/shard_map/base/pallas_call | solution.py:148
  29.3 2.3 %low.1 = (bf16[128,128]{1,0:T(8,128)(2,1)}, s32[8,128]{1,0:T(8,128)S(1)}) custom-call(bf16[512,1024]{1,0:T(8,128)(2,1)S(1)} %bitcast.46, bf16[64,1152]{1,0:T(8,128)(2,1)S(1)} %get-tuple-element.152.refs_0_, bf16[64,1152]{1,0:T(8,128)(2,1)S(1)} %collective-permute-done.refs_1_, ...), custom_call_target="tpu_custom_call", output_to_operand_aliasing={{1}: (5, {})} | custom-call | tf_op jit(solution)/shard_map/low/pallas_call | solution.py:232
  33.1 2.6 %collective-permute-start.4 = (bf16[128,128]{1,0:T(8,128)(2,1)}, bf16[128,128]{1,0:T(8,128)(2,1)}, u32[]{:S(2)}, u32[]{:S(2)}) collective-permute-start(bf16[128,128]{1,0:T(8,128)(2,1)} %get-tuple-element.83.refs_4_), channel_id=1, source_target_pairs={{0,8},{4,12},{8,0},{12,4},{1,9},{5,13},{9,1},{13,5},{2,10},{6,14},... | collective-permute-start | bytes 98312 | tf_op jit(solution)/shard_map/ppermute | solution.py:376
  47.6 2.9 %delta.1 = (bf16[64,2048]{1,0:T(8,128)(2,1)S(1)}, bf16[64,2048]{1,0:T(8,128)(2,1)}, bf16[64,2048]{1,0:T(8,128)(2,1)S(1)}, bf16[64,2048]{1,0:T(8,128)(2,1)S(1)}, s32[8,128]{1,0:T(8,128)S(1)}) custom-call(bf16[512,2048]{1,0:T(8,128)(2,1)S(1)} %bitcast.45, bf16[64,1152]{1,0:T(8,128)(2,1)S(1)} %get-tuple-element.152.refs_0_, ...), custom_call_target="tpu_custom_call", output_to_operand_aliasing={{4}: (9, {})} | custom-call | tf_op jit(solution)/shard_map/delta/pallas_call | solution.py:271
  60.0 2.9 %collective-permute-start.16 = (bf16[224,1024]{1,0:T(8,128)(2,1)}, bf16[224,1024]{1,0:T(8,128)(2,1)S(1)}, u32[]{:S(2)}, u32[]{:S(2)}) collective-permute-start(bf16[224,1024]{1,0:T(8,128)(2,1)} %get-tuple-element.103), channel_id=1, source_target_pairs={{0,4},{4,0},{8,12},{12,8},{1,5},{5,1},{9,13},{13,9},{2,6},{6,2},{1... | collective-permute-start | bytes 1376264 | tf_op jit(solution)/shard_map/ppermute | solution.py:450
  73.6 8.7 %collective-permute-done.8.refs_2_ = bf16[64,2048]{1,0:T(8,128)(2,1)} collective-permute-done((bf16[64,2048]{1,0:T(8,128)(2,1)}, bf16[64,2048]{1,0:T(8,128)(2,1)}, u32[]{:S(2)}, u32[]{:S(2)}) %collective-permute-start.8) | collective-permute-done | bytes 262176 | tf_op jit(solution)/shard_map/ppermute | solution.py:385
  96.9 2.7 %collective-permute-start.18 = (bf16[224,1024]{1,0:T(8,128)(2,1)}, bf16[224,1024]{1,0:T(8,128)(2,1)}, u32[]{:S(2)}, u32[]{:S(2)}) collective-permute-start(bf16[224,1024]{1,0:T(8,128)(2,1)} %get-tuple-element.108), channel_id=1, source_target_pairs={{0,4},{4,0},{8,12},{12,8},{1,5},{5,1},{9,13},{13,9},{2,6},{6,2},{1... | collective-permute-start | bytes 1376264 | tf_op jit(solution)/shard_map/ppermute | solution.py:450
  107.7 3.4 %collective-permute-start.22 = (bf16[224,1024]{1,0:T(8,128)(2,1)}, bf16[224,1024]{1,0:T(8,128)(2,1)}, u32[]{:S(2)}, u32[]{:S(2)}) collective-permute-start(bf16[224,1024]{1,0:T(8,128)(2,1)} %get-tuple-element.119), channel_id=1, source_target_pairs={{0,4},{4,0},{8,12},{12,8},{1,5},{5,1},{9,13},{13,9},{2,6},{6,2},{1... | collective-permute-start | bytes 1376264 | tf_op jit(solution)/shard_map/ppermute | solution.py:450
  111.1 2.5 %broadcast_in_dim.7.held = bf16[256,8192]{1,0:T(8,128)(2,1)} broadcast(bf16[]{:T(256)} %constant.50.clone.1), dimensions={} | broadcast | bytes 4194306 | tf_op jit(solution)/shard_map/broadcast_in_dim | solution.py:427
  113.6 3.0 %finish.11 = (bf16[256,8192]{1,0:T(8,128)(2,1)}, s32[8,128]{1,0:T(8,128)S(1)}) custom-call(s32[2]{0:T(128)S(1)} %pad_add_fusion.2.at, bf16[8,224,1024]{2,1,0:T(8,128)(2,1)S(1)} %copy-done.13, bf16[224,1024]{1,0:T(8,128)(2,1)S(1)} %copy-done.21, ...), custom_call_target="tpu_custom_call", output_to_operand_aliasing={{0}: (5, {}), {1}: (6, {})} | custom-call | flops 117440512 | bytes 2752512 | tf_op jit(solution)/shard_map/finish/pallas_call | solution.py:333
  119.9 3.0 %finish.12 = (bf16[256,8192]{1,0:T(8,128)(2,1)}, s32[8,128]{1,0:T(8,128)S(1)}) custom-call(s32[2]{0:T(128)S(1)} %pad_add_fusion.1.at, bf16[8,224,1024]{2,1,0:T(8,128)(2,1)S(1)} %copy-done.13, bf16[224,1024]{1,0:T(8,128)(2,1)} %collective-permute-done.18.refs_0_.left, ...), custom_call_target="tpu_custom_call", output_to_operand_aliasing={{0}: (5, {}), {1}: (6, {})} | custom-call | flops 117440512 | bytes 2752512 | tf_op jit(solution)/shard_map/finish/pallas_call | solution.py:333
  123.9 2.7 %collective-permute-start.20 = (bf16[224,1024]{1,0:T(8,128)(2,1)}, bf16[224,1024]{1,0:T(8,128)(2,1)S(1)}, u32[]{:S(2)}, u32[]{:S(2)}) collective-permute-start(bf16[224,1024]{1,0:T(8,128)(2,1)} %get-tuple-element.117), channel_id=1, source_target_pairs={{0,4},{4,0},{8,12},{12,8},{1,5},{5,1},{9,13},{13,9},{2,6},{6,2},{1... | collective-permute-start | bytes 1376264 | tf_op jit(solution)/shard_map/ppermute | solution.py:450
  128.9 3.2 %finish.13 = (bf16[256,8192]{1,0:T(8,128)(2,1)}, s32[8,128]{1,0:T(8,128)S(1)}) custom-call(s32[2]{0:T(128)S(1)} %pad_add_fusion.5.at, bf16[8,224,1024]{2,1,0:T(8,128)(2,1)S(1)} %copy-done.14, bf16[224,1024]{1,0:T(8,128)(2,1)S(1)} %collective-permute-done.16.refs_0_.left, ...), custom_call_target="tpu_custom_call", output_to_operand_aliasing={{0}: (5, {}), {1}: (6, {})} | custom-call | flops 117440512 | bytes 2752512 | tf_op jit(solution)/shard_map/finish/pallas_call | solution.py:333
  134.6 3.0 %finish.14 = (bf16[256,8192]{1,0:T(8,128)(2,1)}, s32[8,128]{1,0:T(8,128)S(1)}) custom-call(s32[2]{0:T(128)S(1)} %pad_add_fusion.4.at, bf16[8,224,1024]{2,1,0:T(8,128)(2,1)S(1)} %copy-done.15, bf16[224,1024]{1,0:T(8,128)(2,1)} %collective-permute-done.22.refs_0_.left, ...), custom_call_target="tpu_custom_call", output_to_operand_aliasing={{0}: (5, {}), {1}: (6, {})} | custom-call | flops 117440512 | bytes 2752512 | tf_op jit(solution)/shard_map/finish/pallas_call | solution.py:333
  139.5 2.8 %collective-permute-start.24 = (bf16[224,1024]{1,0:T(8,128)(2,1)}, bf16[224,1024]{1,0:T(8,128)(2,1)S(1)}, u32[]{:S(2)}, u32[]{:S(2)}) collective-permute-start(bf16[224,1024]{1,0:T(8,128)(2,1)} %get-tuple-element.130), channel_id=1, source_target_pairs={{0,4},{4,0},{8,12},{12,8},{1,5},{5,1},{9,13},{13,9},{2,6},{6,2},{1... | collective-permute-start | bytes 1376264 | tf_op jit(solution)/shard_map/ppermute | solution.py:450
  142.3 2.7 %finish.15 = (bf16[256,8192]{1,0:T(8,128)(2,1)}, s32[8,128]{1,0:T(8,128)S(1)}) custom-call(s32[2]{0:T(128)S(1)} %pad_add_fusion.3.at, bf16[8,224,1024]{2,1,0:T(8,128)(2,1)S(1)} %copy-done.15, bf16[224,1024]{1,0:T(8,128)(2,1)} %collective-permute-done.12.refs_0_.left, ...), custom_call_target="tpu_custom_call", output_to_operand_aliasing={{0}: (5, {}), {1}: (6, {})} | custom-call | flops 117440512 | bytes 2752512 | tf_op jit(solution)/shard_map/finish/pallas_call | solution.py:333
  149.1 3.2 %finish.16 = (bf16[256,8192]{1,0:T(8,128)(2,1)}, s32[8,128]{1,0:T(8,128)S(1)}) custom-call(s32[2]{0:T(128)S(1)} %pad_add_fusion.8.at, bf16[8,224,1024]{2,1,0:T(8,128)(2,1)S(1)} %copy-done.16, bf16[224,1024]{1,0:T(8,128)(2,1)S(1)} %collective-permute-done.20.refs_0_.left, ...), custom_call_target="tpu_custom_call", output_to_operand_aliasing={{0}: (5, {}), {1}: (6, {})} | custom-call | flops 117440512 | bytes 2752512 | tf_op jit(solution)/shard_map/finish/pallas_call | solution.py:333
  155.4 2.6 %finish.17 = (bf16[256,8192]{1,0:T(8,128)(2,1)}, s32[8,128]{1,0:T(8,128)S(1)}) custom-call(s32[2]{0:T(128)S(1)} %pad_add_fusion.7.at, bf16[8,224,1024]{2,1,0:T(8,128)(2,1)S(1)} %copy-done.17, bf16[224,1024]{1,0:T(8,128)(2,1)} %collective-permute-done.10.refs_0_.left, ...), custom_call_target="tpu_custom_call", output_to_operand_aliasing={{0}: (5, {}), {1}: (6, {})} | custom-call | flops 117440512 | bytes 2752512 | tf_op jit(solution)/shard_map/finish/pallas_call | solution.py:333
  158.0 2.9 %finish.18 = (bf16[256,8192]{1,0:T(8,128)(2,1)}, s32[8,128]{1,0:T(8,128)S(1)}) custom-call(s32[2]{0:T(128)S(1)} %pad_add_fusion.6.at, bf16[8,224,1024]{2,1,0:T(8,128)(2,1)S(1)} %copy-done.17, bf16[224,1024]{1,0:T(8,128)(2,1)S(1)} %collective-permute-done.24.left, ...), custom_call_target="tpu_custom_call", output_to_operand_aliasing={{0}: (5, {}), {1}: (6, {})} | custom-call | flops 117440512 | bytes 2752512 | tf_op jit(solution)/shard_map/finish/pallas_call | solution.py:333
  163.5 2.4 %finish.19 = (bf16[256,8192]{1,0:T(8,128)(2,1)}, s32[8,128]{1,0:T(8,128)S(1)}) custom-call(s32[2]{0:T(128)S(1)} %pad_add_fusion.10.at, bf16[8,224,1024]{2,1,0:T(8,128)(2,1)S(1)} %copy-done.18, bf16[224,1024]{1,0:T(8,128)(2,1)S(1)} %collective-permute-done.6.refs_0_.left, ...), custom_call_target="tpu_custom_call", output_to_operand_aliasing={{0}: (5, {}), {1}: (6, {})} | custom-call | flops 117440512 | bytes 2752512 | tf_op jit(solution)/shard_map/finish/pallas_call | solution.py:333
  166.7 2.9 %finish.20 = (bf16[256,8192]{1,0:T(8,128)(2,1)}, s32[8,128]{1,0:T(8,128)S(1)}) custom-call(s32[2]{0:T(128)S(1)} %pad_add_fusion.9.at, bf16[8,224,1024]{2,1,0:T(8,128)(2,1)S(1)} %copy-done.18, bf16[224,1024]{1,0:T(8,128)(2,1)S(1)} %collective-permute-done.27.left, ...), custom_call_target="tpu_custom_call", output_to_operand_aliasing={{0}: (5, {}), {1}: (6, {})} | custom-call | flops 117440512 | bytes 2752512 | tf_op jit(solution)/shard_map/finish/pallas_call | solution.py:333
  169.6 3.5 %collective-permute-done.26.left = bf16[224,1024]{1,0:T(8,128)(2,1)S(1)} collective-permute-done((bf16[224,1024]{1,0:T(8,128)(2,1)S(1)}, bf16[224,1024]{1,0:T(8,128)(2,1)S(1)}, u32[]{:S(2)}, u32[]{:S(2)}) %collective-permute-start.26) | collective-permute-done | bytes 458784 | tf_op jit(solution)/shard_map/ppermute | solution.py:450
  173.0 2.9 %finish.21 = (bf16[256,8192]{1,0:T(8,128)(2,1)}, s32[8,128]{1,0:T(8,128)S(1)}) custom-call(s32[2]{0:T(128)S(1)} %pad_add_fusion.at, bf16[8,224,1024]{2,1,0:T(8,128)(2,1)S(1)} %copy-done.18, bf16[224,1024]{1,0:T(8,128)(2,1)S(1)} %collective-permute-done.26.left, ...), custom_call_target="tpu_custom_call", output_to_operand_aliasing={{0}: (5, {}), {1}: (6, {})} | custom-call | flops 117440512 | bytes 2752512 | tf_op jit(solution)/shard_map/finish/pallas_call | solution.py:333
  (151 shorter events, 95.6 us)
Async XLA Ops:
  6.4 30.7 %collective-permute-start.6 = (bf16[224,1024]{1,0:T(8,128)(2,1)S(1)}, bf16[224,1024]{1,0:T(8,128)(2,1)S(1)}, u32[]{:S(2)}, u32[]{:S(2)}) collective-permute-start(bf16[224,1024]{1,0:T(8,128)(2,1)S(1)} %first.1), channel_id=1, source_target_pairs={{0,4},{4,0},{8,12},{12,8},{1,5},{5,1},{9,13},{13,9},{2,6},{6,2},{1... | collective-permute-start | bytes 1376264 | tf_op jit(solution)/shard_map/ppermute | solution.py:429
  20.4 30.9 %collective-permute-start.10 = (bf16[224,1024]{1,0:T(8,128)(2,1)}, bf16[224,1024]{1,0:T(8,128)(2,1)}, u32[]{:S(2)}, u32[]{:S(2)}) collective-permute-start(bf16[224,1024]{1,0:T(8,128)(2,1)} %get-tuple-element.91), channel_id=1, source_target_pairs={{0,4},{4,0},{8,12},{12,8},{1,5},{5,1},{9,13},{13,9},{2,6},{6,2},{1... | collective-permute-start | bytes 1376264 | tf_op jit(solution)/shard_map/ppermute | solution.py:450
  31.6 12.1 %collective-permute-start.3 = (bf16[128,128]{1,0:T(8,128)(2,1)}, bf16[128,128]{1,0:T(8,128)(2,1)}, u32[]{:S(2)}, u32[]{:S(2)}) collective-permute-start(bf16[128,128]{1,0:T(8,128)(2,1)} %get-tuple-element.83.refs_4_), channel_id=1, source_target_pairs={{0,4},{4,8},{8,12},{12,0},{1,5},{5,9},{9,13},{13,1},{2,6},{6,10},{... | collective-permute-start | bytes 98312 | tf_op jit(solution)/shard_map/ppermute | solution.py:376
  33.1 12.7 %collective-permute-start.4 = (bf16[128,128]{1,0:T(8,128)(2,1)}, bf16[128,128]{1,0:T(8,128)(2,1)}, u32[]{:S(2)}, u32[]{:S(2)}) collective-permute-start(bf16[128,128]{1,0:T(8,128)(2,1)} %get-tuple-element.83.refs_4_), channel_id=1, source_target_pairs={{0,8},{4,12},{8,0},{12,4},{1,9},{5,13},{9,1},{13,5},{2,10},{6,14},... | collective-permute-start | bytes 98312 | tf_op jit(solution)/shard_map/ppermute | solution.py:376
  35.7 10.1 %collective-permute-start.5 = (bf16[128,128]{1,0:T(8,128)(2,1)}, bf16[128,128]{1,0:T(8,128)(2,1)}, u32[]{:S(2)}, u32[]{:S(2)}) collective-permute-start(bf16[128,128]{1,0:T(8,128)(2,1)} %get-tuple-element.83.refs_4_), channel_id=1, source_target_pairs={{0,12},{4,0},{8,4},{12,8},{1,13},{5,1},{9,5},{13,9},{2,14},{6,2},{... | collective-permute-start | bytes 98312 | tf_op jit(solution)/shard_map/ppermute | solution.py:376
  40.1 17.0 %collective-permute-start.13 = (bf16[224,1024]{1,0:T(8,128)(2,1)}, bf16[224,1024]{1,0:T(8,128)(2,1)S(1)}, u32[]{:S(2)}, u32[]{:S(2)}) collective-permute-start(bf16[224,1024]{1,0:T(8,128)(2,1)} %get-tuple-element.95), channel_id=1, source_target_pairs={{4,8},{8,4},{5,9},{9,5},{6,10},{10,6},{7,11},{11,7},{20,24},{24,20... | collective-permute-start | bytes 1376264 | tf_op jit(solution)/shard_map/ppermute | solution.py:463
  43.7 19.2 %collective-permute-start.12 = (bf16[224,1024]{1,0:T(8,128)(2,1)}, bf16[224,1024]{1,0:T(8,128)(2,1)}, u32[]{:S(2)}, u32[]{:S(2)}) collective-permute-start(bf16[224,1024]{1,0:T(8,128)(2,1)} %get-tuple-element.94), channel_id=1, source_target_pairs={{0,4},{4,0},{8,12},{12,8},{1,5},{5,1},{9,13},{13,9},{2,6},{6,2},{1... | collective-permute-start | bytes 1376264 | tf_op jit(solution)/shard_map/ppermute | solution.py:450
  55.2 12.3 %collective-permute-start.11 = (bf16[224,1024]{1,0:T(8,128)(2,1)S(1)}, bf16[224,1024]{1,0:T(8,128)(2,1)S(1)}, u32[]{:S(2)}, u32[]{:S(2)}) collective-permute-start(bf16[224,1024]{1,0:T(8,128)(2,1)S(1)} %get-tuple-element.93), channel_id=1, source_target_pairs={{4,8},{8,4},{5,9},{9,5},{6,10},{10,6},{7,11},{11,7},{20,24},{24,20... | collective-permute-start | bytes 1376264 | tf_op jit(solution)/shard_map/ppermute | solution.py:463
  55.9 17.7 %collective-permute-start.7 = (bf16[64,2048]{1,0:T(8,128)(2,1)}, bf16[64,2048]{1,0:T(8,128)(2,1)S(1)}, u32[]{:S(2)}, u32[]{:S(2)}) collective-permute-start(bf16[64,2048]{1,0:T(8,128)(2,1)} %get-tuple-element.88), channel_id=1, source_target_pairs={{0,3},{1,0},{2,1},{3,2},{4,7},{5,4},{6,5},{7,6},{8,11},{9,8},{10,9... | collective-permute-start | bytes 786440 | tf_op jit(solution)/shard_map/ppermute | solution.py:385
  60.0 29.5 %collective-permute-start.16 = (bf16[224,1024]{1,0:T(8,128)(2,1)}, bf16[224,1024]{1,0:T(8,128)(2,1)S(1)}, u32[]{:S(2)}, u32[]{:S(2)}) collective-permute-start(bf16[224,1024]{1,0:T(8,128)(2,1)} %get-tuple-element.103), channel_id=1, source_target_pairs={{0,4},{4,0},{8,12},{12,8},{1,5},{5,1},{9,13},{13,9},{2,6},{6,2},{1... | collective-permute-start | bytes 1376264 | tf_op jit(solution)/shard_map/ppermute | solution.py:450
  66.8 27.1 %collective-permute-start.15 = (bf16[224,1024]{1,0:T(8,128)(2,1)}, bf16[224,1024]{1,0:T(8,128)(2,1)S(1)}, u32[]{:S(2)}, u32[]{:S(2)}) collective-permute-start(bf16[224,1024]{1,0:T(8,128)(2,1)} %get-tuple-element.102), channel_id=1, source_target_pairs={{4,8},{8,4},{5,9},{9,5},{6,10},{10,6},{7,11},{11,7},{20,24},{24,20... | collective-permute-start | bytes 1376264 | tf_op jit(solution)/shard_map/ppermute | solution.py:463
  70.5 29.1 %collective-permute-start.14 = (bf16[224,1024]{1,0:T(8,128)(2,1)}, bf16[224,1024]{1,0:T(8,128)(2,1)S(1)}, u32[]{:S(2)}, u32[]{:S(2)}) collective-permute-start(bf16[224,1024]{1,0:T(8,128)(2,1)} %get-tuple-element.101), channel_id=1, source_target_pairs={{0,4},{4,0},{8,12},{12,8},{1,5},{5,1},{9,13},{13,9},{2,6},{6,2},{1... | collective-permute-start | bytes 1376264 | tf_op jit(solution)/shard_map/ppermute | solution.py:450
  73.6 9.8 %collective-permute-start.9 = (bf16[64,2048]{1,0:T(8,128)(2,1)}, bf16[64,2048]{1,0:T(8,128)(2,1)}, u32[]{:S(2)}, u32[]{:S(2)}) collective-permute-start(bf16[64,2048]{1,0:T(8,128)(2,1)} %copy-done.33), channel_id=1, source_target_pairs={{0,1},{1,2},{2,3},{3,0},{4,5},{5,6},{6,7},{7,4},{8,9},{9,10},{10,1... | collective-permute-start | bytes 786440 | tf_op jit(solution)/shard_map/ppermute | solution.py:385
  92.5 11.2 %collective-permute-start.19 = (bf16[224,1024]{1,0:T(8,128)(2,1)}, bf16[224,1024]{1,0:T(8,128)(2,1)}, u32[]{:S(2)}, u32[]{:S(2)}) collective-permute-start(bf16[224,1024]{1,0:T(8,128)(2,1)} %get-tuple-element.110), channel_id=1, source_target_pairs={{4,8},{8,4},{5,9},{9,5},{6,10},{10,6},{7,11},{11,7},{20,24},{24,20... | collective-permute-start | bytes 1376264 | tf_op jit(solution)/shard_map/ppermute | solution.py:463
  96.9 19.7 %collective-permute-start.18 = (bf16[224,1024]{1,0:T(8,128)(2,1)}, bf16[224,1024]{1,0:T(8,128)(2,1)}, u32[]{:S(2)}, u32[]{:S(2)}) collective-permute-start(bf16[224,1024]{1,0:T(8,128)(2,1)} %get-tuple-element.108), channel_id=1, source_target_pairs={{0,4},{4,0},{8,12},{12,8},{1,5},{5,1},{9,13},{13,9},{2,6},{6,2},{1... | collective-permute-start | bytes 1376264 | tf_op jit(solution)/shard_map/ppermute | solution.py:450
  102.8 20.1 %collective-permute-start.17 = (bf16[224,1024]{1,0:T(8,128)(2,1)}, bf16[224,1024]{1,0:T(8,128)(2,1)S(1)}, u32[]{:S(2)}, u32[]{:S(2)}) collective-permute-start(bf16[224,1024]{1,0:T(8,128)(2,1)} %get-tuple-element.107), channel_id=1, source_target_pairs={{4,8},{8,4},{5,9},{9,5},{6,10},{10,6},{7,11},{11,7},{20,24},{24,20... | collective-permute-start | bytes 1376264 | tf_op jit(solution)/shard_map/ppermute | solution.py:463
  107.7 24.4 %collective-permute-start.22 = (bf16[224,1024]{1,0:T(8,128)(2,1)}, bf16[224,1024]{1,0:T(8,128)(2,1)}, u32[]{:S(2)}, u32[]{:S(2)}) collective-permute-start(bf16[224,1024]{1,0:T(8,128)(2,1)} %get-tuple-element.119), channel_id=1, source_target_pairs={{0,4},{4,0},{8,12},{12,8},{1,5},{5,1},{9,13},{13,9},{2,6},{6,2},{1... | collective-permute-start | bytes 1376264 | tf_op jit(solution)/shard_map/ppermute | solution.py:450
  118.5 19.2 %collective-permute-start.21 = (bf16[224,1024]{1,0:T(8,128)(2,1)}, bf16[224,1024]{1,0:T(8,128)(2,1)}, u32[]{:S(2)}, u32[]{:S(2)}) collective-permute-start(bf16[224,1024]{1,0:T(8,128)(2,1)} %get-tuple-element.118), channel_id=1, source_target_pairs={{4,8},{8,4},{5,9},{9,5},{6,10},{10,6},{7,11},{11,7},{20,24},{24,20... | collective-permute-start | bytes 1376264 | tf_op jit(solution)/shard_map/ppermute | solution.py:463
  123.9 21.1 %collective-permute-start.20 = (bf16[224,1024]{1,0:T(8,128)(2,1)}, bf16[224,1024]{1,0:T(8,128)(2,1)S(1)}, u32[]{:S(2)}, u32[]{:S(2)}) collective-permute-start(bf16[224,1024]{1,0:T(8,128)(2,1)} %get-tuple-element.117), channel_id=1, source_target_pairs={{0,4},{4,0},{8,12},{12,8},{1,5},{5,1},{9,13},{13,9},{2,6},{6,2},{1... | collective-permute-start | bytes 1376264 | tf_op jit(solution)/shard_map/ppermute | solution.py:450
  134.0 18.4 %collective-permute-start.25 = (bf16[224,1024]{1,0:T(8,128)(2,1)}, bf16[224,1024]{1,0:T(8,128)(2,1)S(1)}, u32[]{:S(2)}, u32[]{:S(2)}) collective-permute-start(bf16[224,1024]{1,0:T(8,128)(2,1)} %get-tuple-element.131), channel_id=1, source_target_pairs={{4,8},{8,4},{5,9},{9,5},{6,10},{10,6},{7,11},{11,7},{20,24},{24,20... | collective-permute-start | bytes 1376264 | tf_op jit(solution)/shard_map/ppermute | solution.py:463
  139.5 18.5 %collective-permute-start.24 = (bf16[224,1024]{1,0:T(8,128)(2,1)}, bf16[224,1024]{1,0:T(8,128)(2,1)S(1)}, u32[]{:S(2)}, u32[]{:S(2)}) collective-permute-start(bf16[224,1024]{1,0:T(8,128)(2,1)} %get-tuple-element.130), channel_id=1, source_target_pairs={{0,4},{4,0},{8,12},{12,8},{1,5},{5,1},{9,13},{13,9},{2,6},{6,2},{1... | collective-permute-start | bytes 1376264 | tf_op jit(solution)/shard_map/ppermute | solution.py:450
  145.9 14.9 %collective-permute-start.23 = (bf16[224,1024]{1,0:T(8,128)(2,1)}, bf16[224,1024]{1,0:T(8,128)(2,1)S(1)}, u32[]{:S(2)}, u32[]{:S(2)}) collective-permute-start(bf16[224,1024]{1,0:T(8,128)(2,1)} %get-tuple-element.129), channel_id=1, source_target_pairs={{4,8},{8,4},{5,9},{9,5},{6,10},{10,6},{7,11},{11,7},{20,24},{24,20... | collective-permute-start | bytes 1376264 | tf_op jit(solution)/shard_map/ppermute | solution.py:463
  153.3 13.4 %collective-permute-start.27 = (bf16[224,1024]{1,0:T(8,128)(2,1)}, bf16[224,1024]{1,0:T(8,128)(2,1)S(1)}, u32[]{:S(2)}, u32[]{:S(2)}) collective-permute-start(bf16[224,1024]{1,0:T(8,128)(2,1)} %get-tuple-element.141), channel_id=1, source_target_pairs={{0,4},{4,0},{8,12},{12,8},{1,5},{5,1},{9,13},{13,9},{2,6},{6,2},{1... | collective-permute-start | bytes 1376264 | tf_op jit(solution)/shard_map/ppermute | solution.py:450
  161.1 11.9 %collective-permute-start.26 = (bf16[224,1024]{1,0:T(8,128)(2,1)S(1)}, bf16[224,1024]{1,0:T(8,128)(2,1)S(1)}, u32[]{:S(2)}, u32[]{:S(2)}) collective-permute-start(bf16[224,1024]{1,0:T(8,128)(2,1)S(1)} %get-tuple-element.140), channel_id=1, source_target_pairs={{0,4},{4,0},{8,12},{12,8},{1,5},{5,1},{9,13},{13,9},{2,6},{6,2},{1... | collective-permute-start | bytes 1376264 | tf_op jit(solution)/shard_map/ppermute | solution.py:450
  (39 other events, 142.7 us)

commit v3 on v2

--- a/solution.py
+++ b/solution.py
@@ -22,10 +22,6 @@
     return jnp.dot(a, b, preferred_element_type=F32)
 
 
-def dot_rows(a, b):
-    return lax.dot_general(a, b, (((0,), (0,)), ((), ())), preferred_element_type=F32)
-
-
 def dot_cols(a, b):
     return lax.dot_general(a, b, (((1,), (1,)), ((), ())), preferred_element_type=F32)
 
@@ -34,7 +30,7 @@
     return lax.broadcasted_iota(jnp.int32, shape, dim)
 
 
-def params(mib=16):
+def params(mib=50):
     return pltpu.CompilerParams(vmem_limit_bytes=mib * MIB)
 
 
@@ -84,7 +80,7 @@
         tags = jnp.where(row_group == g, slot[g].astype(F32), tags)
     compact = (iota((LIVE_ROWS, rows), 0) == packed).astype(BF16)
     spread = (iota((out_rows, rows), 0) == target).astype(BF16)
-    pick[...] = compact
+    pick[...] = compact.astype(F32).T.astype(BF16)
     place[...] = dot_cols(compact, spread).astype(BF16)
     compact_x[...] = dot(compact, x[...]).astype(BF16)
     sent[:, :feat] = dot(spread, x[...]).astype(BF16)
@@ -100,13 +96,13 @@
         out_shape=(
             jax.ShapeDtypeStruct((LIVE_ROWS, feat), BF16),
             jax.ShapeDtypeStruct((out_rows, feat + TAG), BF16),
-            jax.ShapeDtypeStruct((LIVE_ROWS, rows), BF16),
+            jax.ShapeDtypeStruct((rows, LIVE_ROWS), BF16),
             jax.ShapeDtypeStruct((LIVE_ROWS, out_rows), BF16),
         ),
         in_specs=[ANY, ANY, ANY, VMEM],
         out_specs=(VMEM,) * 4,
         scratch_shapes=smalls + [pltpu.SemaphoreType.DMA((3,))],
-        compiler_params=params(),
+        compiler_params=params(60),
         name="prepare",
     )(owner, slot, live, x)
 
@@ -130,7 +126,7 @@
             ],
             out_specs=pl.BlockSpec((LIVE_ROWS, TILE), lambda i, at: (0, i)),
         ),
-        compiler_params=params(48),
+        compiler_params=params(),
         cost_estimate=cost(2 * LIVE_ROWS * feat * CHUNK, (feat + LIVE_ROWS) * CHUNK),
         name="first",
     )(at, x, weight)
@@ -159,7 +155,7 @@
         ],
         out_specs=(pl.BlockSpec((group, LIVE_ROWS, CHUNK), lambda i: (i, 0, 0)), ANY),
         input_output_aliases={2: 1},
-        compiler_params=params(48),
+        compiler_params=params(),
         cost_estimate=cost(2 * LIVE_ROWS * feat * width, (feat + LIVE_ROWS) * width),
         name="base",
     )(x, weight, token)
@@ -314,26 +310,38 @@
     )(first, base, place, *parts, token)
 
 
-def finish_kernel(at, base, left, right, pick, held, token_in, out, token):
+def finish_kernel(at, base, left, right, pick, *refs):
+    out, _, made, sems = refs[-4:]
+    tile, tiles = pl.program_id(0), pl.num_programs(0)
+
+    def copy(i):
+        column = pl.multiple_of(at[0] * CHUNK + i * TILE, TILE)
+        return pltpu.make_async_copy(made.at[i], out.at[:, pl.ds(column, TILE)], sems.at[i])
+
     @pl.when(at[1] > 0)
     def _():
         total = base[0].astype(F32) + left[...].astype(F32) + right[...].astype(F32)
-        out[...] = dot_rows(pick[...], total.astype(BF16)).astype(BF16)
-
-    @pl.when(at[1] == 0)
-    def _():
-        out[...] = held[...]
+        made[tile] = dot(pick[...], total.astype(BF16)).astype(BF16)
+        copy(tile).start()
+
+        @pl.when(tile == tiles - 1)
+        def _():
+            for i in range(CHUNK // TILE):
+                copy(i).wait()
 
 
 def finish(at, base, left, right, pick, held, token):
-    rows = pick.shape[1]
+    rows, width = pick.shape[0], base.shape[0] * CHUNK
     tiles = CHUNK // TILE
     got = pl.BlockSpec((LIVE_ROWS, TILE), lambda i, at: (0, i))
-    here = pl.BlockSpec((rows, TILE), lambda i, at: (0, at[0] * tiles + i))
+    last = [token] if held is None else [held, token]
+    aliases = {6: 1} if held is not None else {5: 1}
+    if held is not None:
+        aliases[5] = 0
     return pl.pallas_call(
         finish_kernel,
         out_shape=(
-            jax.ShapeDtypeStruct(held.shape, BF16),
+            jax.ShapeDtypeStruct((rows, width), BF16),
             jax.ShapeDtypeStruct(token.shape, token.dtype),
         ),
         grid_spec=pltpu.PrefetchScalarGridSpec(
@@ -344,16 +352,16 @@
                 got,
                 got,
                 pl.BlockSpec(pick.shape, lambda i, at: (0, 0)),
-                here,
-                ANY,
-            ],
-            out_specs=(here, ANY),
-        ),
-        input_output_aliases={5: 0, 6: 1},
+            ]
+            + [ANY] * len(last),
+            out_specs=(ANY, ANY),
+            scratch_shapes=[pltpu.VMEM((tiles, rows, TILE), BF16), pltpu.SemaphoreType.DMA((tiles,))],
+        ),
+        input_output_aliases=aliases,
         compiler_params=params(),
         cost_estimate=cost(2 * LIVE_ROWS * rows * CHUNK, 6 * LIVE_ROWS * CHUNK),
         name="finish",
-    )(at, base, left, right, pick, held, token)
+    )(at, base, left, right, pick, *last)
 
 
 def send_groups(sent):
@@ -406,7 +414,7 @@
         base = lax.dynamic_update_slice_in_dim(base, mine, z * share, 1).astype(BF16)
         total = lax.psum_scatter(base, "tensor", scatter_dimension=1, tiled=True)
         total = lax.all_gather(total, "tensor", axis=1, tiled=True)
-        return dot_rows(pick, total).astype(BF16)
+        return dot(pick, total).astype(BF16)
 
     chunks, per = width // CHUNK, share // CHUNK
     inner = (z == 1) | (z == 2)
@@ -424,11 +432,13 @@
         return chunk_of(jnp.int32(step - 1), odd_right)
 
     evens, odds = {}, {}
-    result = jnp.zeros((rows, width), BF16)
+    result = None
     message = first_chunk(even_chunk(0).reshape(1), compact_x, weight)
     evens[0] = lax.ppermute(message, "tensor", even)
     parts = send_groups(sent)
     base, token = base_chunks(compact_x, weight, token)
+    low, token = low_values(parts, down, rank, token)
+    lows = send_lows(low)
     unfinished = list(range(chunks + 3))
     seen_even, seen_odd = set(), set()
 
@@ -449,9 +459,6 @@
         message, token = hop(even_chunk(step), base, odds.get(step - 2), token)
         evens[step] = lax.ppermute(message, "tensor", even)
         seen_odd.add(step - 2)
-        if step == 1:
-            low, token = low_values(parts, down, rank, token)
-            lows = send_lows(low)
         if step == 2:
             *made, token = delta_values(parts, lows, up, rank, token)
             back = send_back(made)

time: 177 us -> 156 us (0.88)
  local copies, waits for them, and re-layouts: 41.3 us -> 4.73 us
  Pallas kernels: 71.9 us -> 84.7 us
  starting transfers between devices: 42.2 us -> 45.3 us
    unnamed x70 -> x28, local copies, waits for them, and re-layouts: 38.7 us -> 3.56 us
    pallas_call x18, Pallas kernels: 21.1 us -> 33.2 us  [hop(): pl.pallas_call(hop_kernel, out_shape=(jax.ShapeDtypeStruct((LIVE_ROWS, CH...]
    ppermute x3, waiting for transfers between devices: 5.36 us -> 0.01 us  [send_groups(): parts.append(lax.ppermute(sent[k * rows:(k + 1) * rows], 'replica', hops))]
    ppermute x3, waiting for transfers between devices: 0.01 us -> 4.82 us  [send_lows(): lows.append(lax.ppermute(low, 'tensor', hops))]
    pallas_call x11, Pallas kernels: 31.8 us -> 28.2 us  [finish(): pl.pallas_call(finish_kernel, out_shape=(jax.ShapeDtypeStruct((rows, widt...]
    ppermute x10, starting transfers between devices: 21.1 us -> 24.7 us  [on_device(): evens[step] = lax.ppermute(message, 'tensor', even)]
    broadcast_in_dim x1 -> x0, local copies, waits for them, and re-layouts: 2.49 us -> none  [on_device(): result = jnp.zeros((rows, width), BF16)]
    pallas_call x1, Pallas kernels: 1.26 us -> 3.25 us  [prepare(): pl.pallas_call(functools.partial(prepare_kernel, replicas), out_shape=(ja...]
  transfers between devices with their start and end apart: 28 -> 28, of which waited for: 7 -> 5; matrix products, arithmetic and copies ran while one was open for 2% -> 1% of each run, Pallas kernels for 37% -> 51%
where the time goes in v3:
time: 156 us; the launch traced here: 155 us
  Pallas kernels  84.7 us (54%)
  starting transfers between devices  45.3 us (29%)
  waiting for transfers between devices  19.1 us (12%)
  local copies, waits for them, and re-layouts  4.73 us (3%)
    pallas_call x18, Pallas kernels, hop(): pl.pallas_call(hop_kernel, out_shape=(jax.ShapeDtypeStruct((LIVE_ROWS, CH...  33.2 us
    pallas_call x11, Pallas kernels, finish(): pl.pallas_call(finish_kernel, out_shape=(jax.ShapeDtypeStruct((rows, widt...  28.2 us
    ppermute x10, starting transfers between devices, on_device(): evens[step] = lax.ppermute(message, 'tensor', even)  24.7 us
    pallas_call x1, Pallas kernels, base_chunks(): pl.pallas_call(base_kernel, out_shape=(jax.ShapeDtypeStruct((number, LIVE...  9.69 us
    ppermute x3, waiting for transfers between devices, send_back(): back.append(lax.ppermute(made[k], 'replica', hops))  8.4 us
    ppermute x8, starting transfers between devices, on_device(): odds[step] = lax.ppermute(message, 'tensor', odd)  6.96 us
    ppermute x10, waiting for transfers between devices, on_device(): evens[step] = lax.ppermute(message, 'tensor', even)  5.86 us
    ppermute x3, starting transfers between devices, send_lows(): lows.append(lax.ppermute(low, 'tensor', hops))  5.52 us
  transfers between devices with their start and end apart: 28, of which 5 were waited for; matrix products, arithmetic and copies ran while one was open for 1% of the time, Pallas kernels for 51%

profile of v3, /device:TPU:0, one launch (start us, length us, event | category | flops | bytes accessed | tf_op | source)
XLA Modules:
  0.0 155.2 jit_solution(7292312742406402481)
XLA Ops:
  0.0 3.3 %prepare.1 = (bf16[224,1024]{1,0:T(8,128)(2,1)}, bf16[256,1152]{1,0:T(8,128)(2,1)}, bf16[256,224]{1,0:T(8,128)(2,1)}, bf16[224,256]{1,0:T(8,128)(2,1)}) custom-call(s32[16]{0:T(128)} %bitcast.47, s32[16]{0:T(128)} %slot_in.1, s32[16]{0:T(128)} %bitcast.48, bf16[256,1024]{1,0:T(8,128)(2,1)} %x.1), custom_call_target="tpu_custom_call" | custom-call | tf_op jit(solution)/shard_map/prepare/pallas_call | solution.py:94
  4.9 2.6 %collective-permute-start.1 = (bf16[64,1152]{1,0:T(8,128)(2,1)S(1)}, bf16[64,1152]{1,0:T(8,128)(2,1)S(1)}, u32[]{:S(2)}, u32[]{:S(2)}) collective-permute-start(bf16[64,1152]{1,0:T(8,128)(2,1)S(1)} %get-tuple-element.150), channel_id=1, source_target_pairs={{0,2},{1,3},{2,0},{3,1},{4,6},{5,7},{6,4},{7,5},{8,10},{9,11},{10,... | collective-permute-start | bytes 442376 | tf_op jit(solution)/shard_map/ppermute | solution.py:373
  9.9 2.8 %first.1 = bf16[224,1024]{1,0:T(8,128)(2,1)} custom-call(s32[1]{0:T(128)} %bitcast.9.at, bf16[224,1024]{1,0:T(8,128)(2,1)S(1)} %copy-done.2, bf16[1024,8192]{1,0:T(8,128)(2,1)} %w.3), custom_call_target="tpu_custom_call" | custom-call | flops 469762048 | bytes 2555904 | tf_op jit(solution)/shard_map/first/pallas_call | solution.py:117
  14.3 9.7 %base.1 = (bf16[8,224,1024]{2,1,0:T(8,128)(2,1)}, s32[8,128]{1,0:T(8,128)S(1)}) custom-call(bf16[224,1024]{1,0:T(8,128)(2,1)S(1)} %copy-done.2, bf16[1024,8192]{1,0:T(8,128)(2,1)} %w.3, s32[8,128]{1,0:T(8,128)S(1)} %broadcast_in_dim.3.token_in), custom_call_target="tpu_custom_call", output_to_operand_aliasing={{1}: (2, {})} | custom-call | flops 3758096384 | bytes 20447232 | tf_op jit(solution)/shard_map/base/pallas_call | solution.py:144
  29.5 2.6 %collective-permute-start.4 = (bf16[128,128]{1,0:T(8,128)(2,1)S(1)}, bf16[128,128]{1,0:T(8,128)(2,1)S(1)}, u32[]{:S(2)}, u32[]{:S(2)}) collective-permute-start(bf16[128,128]{1,0:T(8,128)(2,1)S(1)} %get-tuple-element.82.refs_4_), channel_id=1, source_target_pairs={{0,8},{4,12},{8,0},{12,4},{1,9},{5,13},{9,1},{13,5},{2,10},{6,14},... | collective-permute-start | bytes 98312 | tf_op jit(solution)/shard_map/ppermute | solution.py:384
  37.8 4.8 %collective-permute-done.3.refs_5_ = bf16[128,128]{1,0:T(8,128)(2,1)S(1)} collective-permute-done((bf16[128,128]{1,0:T(8,128)(2,1)S(1)}, bf16[128,128]{1,0:T(8,128)(2,1)S(1)}, u32[]{:S(2)}, u32[]{:S(2)}) %collective-permute-start.3) | collective-permute-done | bytes 32800 | tf_op jit(solution)/shard_map/ppermute | solution.py:384
  44.4 2.8 %delta.1 = (bf16[64,2048]{1,0:T(8,128)(2,1)S(1)}, bf16[64,2048]{1,0:T(8,128)(2,1)}, bf16[64,2048]{1,0:T(8,128)(2,1)S(1)}, bf16[64,2048]{1,0:T(8,128)(2,1)S(1)}, s32[8,128]{1,0:T(8,128)S(1)}) custom-call(bf16[512,2048]{1,0:T(8,128)(2,1)S(1)} %bitcast.45, bf16[64,1152]{1,0:T(8,128)(2,1)S(1)} %get-tuple-element.152.refs_0_, ...), custom_call_target="tpu_custom_call", output_to_operand_aliasing={{4}: (9, {})} | custom-call | tf_op jit(solution)/shard_map/delta/pallas_call | solution.py:267
  52.2 3.8 %collective-permute-start.16 = (bf16[224,1024]{1,0:T(8,128)(2,1)}, bf16[224,1024]{1,0:T(8,128)(2,1)S(1)}, u32[]{:S(2)}, u32[]{:S(2)}) collective-permute-start(bf16[224,1024]{1,0:T(8,128)(2,1)} %get-tuple-element.103), channel_id=1, source_target_pairs={{0,4},{4,0},{8,12},{12,8},{1,5},{5,1},{9,13},{13,9},{2,6},{6,2},{1... | collective-permute-start | bytes 1376264 | tf_op jit(solution)/shard_map/ppermute | solution.py:460
  61.3 2.9 %collective-permute-start.14 = (bf16[224,1024]{1,0:T(8,128)(2,1)}, bf16[224,1024]{1,0:T(8,128)(2,1)S(1)}, u32[]{:S(2)}, u32[]{:S(2)}) collective-permute-start(bf16[224,1024]{1,0:T(8,128)(2,1)} %get-tuple-element.101), channel_id=1, source_target_pairs={{0,4},{4,0},{8,12},{12,8},{1,5},{5,1},{9,13},{13,9},{2,6},{6,2},{1... | collective-permute-start | bytes 1376264 | tf_op jit(solution)/shard_map/ppermute | solution.py:460
  66.3 7.4 %collective-permute-done.8.refs_2_ = bf16[64,2048]{1,0:T(8,128)(2,1)S(1)} collective-permute-done((bf16[64,2048]{1,0:T(8,128)(2,1)}, bf16[64,2048]{1,0:T(8,128)(2,1)S(1)}, u32[]{:S(2)}, u32[]{:S(2)}) %collective-permute-start.8) | collective-permute-done | bytes 262176 | tf_op jit(solution)/shard_map/ppermute | solution.py:393
  74.7 3.1 %add_delta.1 = (bf16[8,224,1024]{2,1,0:T(8,128)(2,1)}, s32[8,128]{1,0:T(8,128)S(1)}) custom-call(s32[1]{0:T(128)} %bitcast.2.at, bf16[8,224,1024]{2,1,0:T(8,128)(2,1)} %get-tuple-element.78.base, bf16[224,256]{1,0:T(8,128)(2,1)S(1)} %copy-done.10, bf16[64,2048]{1,0:T(8,128)(2,1)S(1)} %copy-done.9, ...), custom_call_target="tpu_custom_call", output_to_operand_aliasing={{0}: (1, {}), {1}: (7, {})} | custom-call | tf_op jit(solution)/shard_map/add_delta/pallas_call | solution.py:293
  82.4 2.7 %collective-permute-start.18 = (bf16[224,1024]{1,0:T(8,128)(2,1)}, bf16[224,1024]{1,0:T(8,128)(2,1)}, u32[]{:S(2)}, u32[]{:S(2)}) collective-permute-start(bf16[224,1024]{1,0:T(8,128)(2,1)} %get-tuple-element.108), channel_id=1, source_target_pairs={{0,4},{4,0},{8,12},{12,8},{1,5},{5,1},{9,13},{13,9},{2,6},{6,2},{1... | collective-permute-start | bytes 1376264 | tf_op jit(solution)/shard_map/ppermute | solution.py:460
  90.3 7.0 %collective-permute-start.22 = (bf16[224,1024]{1,0:T(8,128)(2,1)}, bf16[224,1024]{1,0:T(8,128)(2,1)}, u32[]{:S(2)}, u32[]{:S(2)}) collective-permute-start(bf16[224,1024]{1,0:T(8,128)(2,1)} %get-tuple-element.119), channel_id=1, source_target_pairs={{0,4},{4,0},{8,12},{12,8},{1,5},{5,1},{9,13},{13,9},{2,6},{6,2},{1... | collective-permute-start | bytes 1376264 | tf_op jit(solution)/shard_map/ppermute | solution.py:460
  97.3 2.8 %finish.11 = (bf16[256,8192]{1,0:T(8,128)(2,1)}, s32[8,128]{1,0:T(8,128)S(1)}) custom-call(s32[2]{0:T(128)S(1)} %pad_add_fusion.2.at, bf16[8,224,1024]{2,1,0:T(8,128)(2,1)} %get-tuple-element.100.base, bf16[224,1024]{1,0:T(8,128)(2,1)S(1)} %collective-permute-done.14.refs_0_.left, ...), custom_call_target="tpu_custom_call", output_to_operand_aliasing={{1}: (5, {})} | custom-call | flops 117440512 | bytes 2752512 | tf_op jit(solution)/shard_map/finish/pallas_call | solution.py:341
  102.8 3.0 %finish.12 = (bf16[256,8192]{1,0:T(8,128)(2,1)}, s32[8,128]{1,0:T(8,128)S(1)}) custom-call(s32[2]{0:T(128)S(1)} %pad_add_fusion.1.at, bf16[8,224,1024]{2,1,0:T(8,128)(2,1)} %get-tuple-element.100.base, bf16[224,1024]{1,0:T(8,128)(2,1)} %collective-permute-done.18.refs_0_.left, ...), custom_call_target="tpu_custom_call", output_to_operand_aliasing={{1}: (6, {}), {0}: (5, {})} | custom-call | flops 117440512 | bytes 2752512 | tf_op jit(solution)/shard_map/finish/pallas_call | solution.py:341
  110.5 2.9 %finish.13 = (bf16[256,8192]{1,0:T(8,128)(2,1)}, s32[8,128]{1,0:T(8,128)S(1)}) custom-call(s32[2]{0:T(128)S(1)} %pad_add_fusion.5.at, bf16[8,224,1024]{2,1,0:T(8,128)(2,1)} %get-tuple-element.100.base, bf16[224,1024]{1,0:T(8,128)(2,1)S(1)} %collective-permute-done.16.refs_0_.left, ...), custom_call_target="tpu_custom_call", output_to_operand_aliasing={{1}: (6, {}), {0}: (5, {})} | custom-call | flops 117440512 | bytes 2752512 | tf_op jit(solution)/shard_map/finish/pallas_call | solution.py:341
  116.2 2.9 %finish.14 = (bf16[256,8192]{1,0:T(8,128)(2,1)}, s32[8,128]{1,0:T(8,128)S(1)}) custom-call(s32[2]{0:T(128)S(1)} %pad_add_fusion.4.at, bf16[8,224,1024]{2,1,0:T(8,128)(2,1)} %get-tuple-element.100.base, bf16[224,1024]{1,0:T(8,128)(2,1)} %collective-permute-done.22.refs_0_.left, ...), custom_call_target="tpu_custom_call", output_to_operand_aliasing={{1}: (6, {}), {0}: (5, {})} | custom-call | flops 117440512 | bytes 2752512 | tf_op jit(solution)/shard_map/finish/pallas_call | solution.py:341
  127.9 2.8 %finish.16 = (bf16[256,8192]{1,0:T(8,128)(2,1)}, s32[8,128]{1,0:T(8,128)S(1)}) custom-call(s32[2]{0:T(128)S(1)} %pad_add_fusion.8.at, bf16[8,224,1024]{2,1,0:T(8,128)(2,1)} %get-tuple-element.100.base, bf16[224,1024]{1,0:T(8,128)(2,1)S(1)} %collective-permute-done.20.refs_0_.left, ...), custom_call_target="tpu_custom_call", output_to_operand_aliasing={{1}: (6, {}), {0}: (5, {})} | custom-call | flops 117440512 | bytes 2752512 | tf_op jit(solution)/shard_map/finish/pallas_call | solution.py:341
  132.5 3.4 %collective-permute-start.27 = (bf16[224,1024]{1,0:T(8,128)(2,1)}, bf16[224,1024]{1,0:T(8,128)(2,1)S(1)}, u32[]{:S(2)}, u32[]{:S(2)}) collective-permute-start(bf16[224,1024]{1,0:T(8,128)(2,1)} %get-tuple-element.141), channel_id=1, source_target_pairs={{0,4},{4,0},{8,12},{12,8},{1,5},{5,1},{9,13},{13,9},{2,6},{6,2},{1... | collective-permute-start | bytes 1376264 | tf_op jit(solution)/shard_map/ppermute | solution.py:460
  137.8 2.8 %finish.18 = (bf16[256,8192]{1,0:T(8,128)(2,1)}, s32[8,128]{1,0:T(8,128)S(1)}) custom-call(s32[2]{0:T(128)S(1)} %pad_add_fusion.6.at, bf16[8,224,1024]{2,1,0:T(8,128)(2,1)} %get-tuple-element.100.base, bf16[224,1024]{1,0:T(8,128)(2,1)S(1)} %collective-permute-done.24.left, ...), custom_call_target="tpu_custom_call", output_to_operand_aliasing={{1}: (6, {}), {0}: (5, {})} | custom-call | flops 117440512 | bytes 2752512 | tf_op jit(solution)/shard_map/finish/pallas_call | solution.py:341
  143.8 2.8 %collective-permute-done.27.left = bf16[224,1024]{1,0:T(8,128)(2,1)S(1)} collective-permute-done((bf16[224,1024]{1,0:T(8,128)(2,1)}, bf16[224,1024]{1,0:T(8,128)(2,1)S(1)}, u32[]{:S(2)}, u32[]{:S(2)}) %collective-permute-start.27) | collective-permute-done | bytes 458784 | tf_op jit(solution)/shard_map/ppermute | solution.py:460
  146.6 2.8 %finish.20 = (bf16[256,8192]{1,0:T(8,128)(2,1)}, s32[8,128]{1,0:T(8,128)S(1)}) custom-call(s32[2]{0:T(128)S(1)} %pad_add_fusion.9.at, bf16[8,224,1024]{2,1,0:T(8,128)(2,1)} %get-tuple-element.100.base, bf16[224,1024]{1,0:T(8,128)(2,1)S(1)} %collective-permute-done.27.left, ...), custom_call_target="tpu_custom_call", output_to_operand_aliasing={{1}: (6, {}), {0}: (5, {})} | custom-call | flops 117440512 | bytes 2752512 | tf_op jit(solution)/shard_map/finish/pallas_call | solution.py:341
  149.4 3.0 %collective-permute-done.26.left = bf16[224,1024]{1,0:T(8,128)(2,1)S(1)} collective-permute-done((bf16[224,1024]{1,0:T(8,128)(2,1)S(1)}, bf16[224,1024]{1,0:T(8,128)(2,1)S(1)}, u32[]{:S(2)}, u32[]{:S(2)}) %collective-permute-start.26) | collective-permute-done | bytes 458784 | tf_op jit(solution)/shard_map/ppermute | solution.py:460
  152.4 2.8 %finish.21 = (bf16[256,8192]{1,0:T(8,128)(2,1)}, s32[8,128]{1,0:T(8,128)S(1)}) custom-call(s32[2]{0:T(128)S(1)} %pad_add_fusion.at, bf16[8,224,1024]{2,1,0:T(8,128)(2,1)} %get-tuple-element.100.base, bf16[224,1024]{1,0:T(8,128)(2,1)S(1)} %collective-permute-done.26.left, ...), custom_call_target="tpu_custom_call", output_to_operand_aliasing={{1}: (6, {}), {0}: (5, {})} | custom-call | flops 117440512 | bytes 2752512 | tf_op jit(solution)/shard_map/finish/pallas_call | solution.py:341
  (108 shorter events, 67.3 us)
Async XLA Ops:
  4.4 19.5 %collective-permute-start = (bf16[64,1152]{1,0:T(8,128)(2,1)S(1)}, bf16[64,1152]{1,0:T(8,128)(2,1)S(1)}, u32[]{:S(2)}, u32[]{:S(2)}) collective-permute-start(bf16[64,1152]{1,0:T(8,128)(2,1)S(1)} %get-tuple-element.151), channel_id=1, source_target_pairs={{0,1},{1,2},{2,3},{3,0},{4,5},{5,6},{6,7},{7,4},{8,9},{9,10},{10,1... | collective-permute-start | bytes 442376 | tf_op jit(solution)/shard_map/ppermute | solution.py:373
  4.9 19.0 %collective-permute-start.1 = (bf16[64,1152]{1,0:T(8,128)(2,1)S(1)}, bf16[64,1152]{1,0:T(8,128)(2,1)S(1)}, u32[]{:S(2)}, u32[]{:S(2)}) collective-permute-start(bf16[64,1152]{1,0:T(8,128)(2,1)S(1)} %get-tuple-element.150), channel_id=1, source_target_pairs={{0,2},{1,3},{2,0},{3,1},{4,6},{5,7},{6,4},{7,5},{8,10},{9,11},{10,... | collective-permute-start | bytes 442376 | tf_op jit(solution)/shard_map/ppermute | solution.py:373
  7.5 16.5 %collective-permute-start.2 = (bf16[64,1152]{1,0:T(8,128)(2,1)S(1)}, bf16[64,1152]{1,0:T(8,128)(2,1)S(1)}, u32[]{:S(2)}, u32[]{:S(2)}) collective-permute-start(bf16[64,1152]{1,0:T(8,128)(2,1)S(1)} %get-tuple-element.149), channel_id=1, source_target_pairs={{0,3},{1,0},{2,1},{3,2},{4,7},{5,4},{6,5},{7,6},{8,11},{9,8},{10,9... | collective-permute-start | bytes 442376 | tf_op jit(solution)/shard_map/ppermute | solution.py:373
  12.7 20.8 %collective-permute-start.6 = (bf16[224,1024]{1,0:T(8,128)(2,1)}, bf16[224,1024]{1,0:T(8,128)(2,1)S(1)}, u32[]{:S(2)}, u32[]{:S(2)}) collective-permute-start(bf16[224,1024]{1,0:T(8,128)(2,1)} %first.1), channel_id=1, source_target_pairs={{0,4},{4,0},{8,12},{12,8},{1,5},{5,1},{9,13},{13,9},{2,6},{6,2},{1... | collective-permute-start | bytes 1376264 | tf_op jit(solution)/shard_map/ppermute | solution.py:437
  27.5 20.5 %collective-permute-start.10 = (bf16[224,1024]{1,0:T(8,128)(2,1)}, bf16[224,1024]{1,0:T(8,128)(2,1)}, u32[]{:S(2)}, u32[]{:S(2)}) collective-permute-start(bf16[224,1024]{1,0:T(8,128)(2,1)} %get-tuple-element.91), channel_id=1, source_target_pairs={{0,4},{4,0},{8,12},{12,8},{1,5},{5,1},{9,13},{13,9},{2,6},{6,2},{1... | collective-permute-start | bytes 1376264 | tf_op jit(solution)/shard_map/ppermute | solution.py:460
  27.9 14.7 %collective-permute-start.3 = (bf16[128,128]{1,0:T(8,128)(2,1)S(1)}, bf16[128,128]{1,0:T(8,128)(2,1)S(1)}, u32[]{:S(2)}, u32[]{:S(2)}) collective-permute-start(bf16[128,128]{1,0:T(8,128)(2,1)S(1)} %get-tuple-element.82.refs_4_), channel_id=1, source_target_pairs={{0,4},{4,8},{8,12},{12,0},{1,5},{5,9},{9,13},{13,1},{2,6},{6,10},{... | collective-permute-start | bytes 98312 | tf_op jit(solution)/shard_map/ppermute | solution.py:384
  29.5 13.1 %collective-permute-start.4 = (bf16[128,128]{1,0:T(8,128)(2,1)S(1)}, bf16[128,128]{1,0:T(8,128)(2,1)S(1)}, u32[]{:S(2)}, u32[]{:S(2)}) collective-permute-start(bf16[128,128]{1,0:T(8,128)(2,1)S(1)} %get-tuple-element.82.refs_4_), channel_id=1, source_target_pairs={{0,8},{4,12},{8,0},{12,4},{1,9},{5,13},{9,1},{13,5},{2,10},{6,14},... | collective-permute-start | bytes 98312 | tf_op jit(solution)/shard_map/ppermute | solution.py:384
  32.1 10.5 %collective-permute-start.5 = (bf16[128,128]{1,0:T(8,128)(2,1)S(1)}, bf16[128,128]{1,0:T(8,128)(2,1)}, u32[]{:S(2)}, u32[]{:S(2)}) collective-permute-start(bf16[128,128]{1,0:T(8,128)(2,1)S(1)} %get-tuple-element.82.refs_4_), channel_id=1, source_target_pairs={{0,12},{4,0},{8,4},{12,8},{1,13},{5,1},{9,5},{13,9},{2,14},{6,2},{... | collective-permute-start | bytes 98312 | tf_op jit(solution)/shard_map/ppermute | solution.py:384
  35.3 15.1 %collective-permute-start.13 = (bf16[224,1024]{1,0:T(8,128)(2,1)}, bf16[224,1024]{1,0:T(8,128)(2,1)S(1)}, u32[]{:S(2)}, u32[]{:S(2)}) collective-permute-start(bf16[224,1024]{1,0:T(8,128)(2,1)} %get-tuple-element.95), channel_id=1, source_target_pairs={{4,8},{8,4},{5,9},{9,5},{6,10},{10,6},{7,11},{11,7},{20,24},{24,20... | collective-permute-start | bytes 1376264 | tf_op jit(solution)/shard_map/ppermute | solution.py:470
  42.6 13.4 %collective-permute-start.12 = (bf16[224,1024]{1,0:T(8,128)(2,1)}, bf16[224,1024]{1,0:T(8,128)(2,1)}, u32[]{:S(2)}, u32[]{:S(2)}) collective-permute-start(bf16[224,1024]{1,0:T(8,128)(2,1)} %get-tuple-element.94), channel_id=1, source_target_pairs={{0,4},{4,0},{8,12},{12,8},{1,5},{5,1},{9,13},{13,9},{2,6},{6,2},{1... | collective-permute-start | bytes 1376264 | tf_op jit(solution)/shard_map/ppermute | solution.py:460
  50.3 16.0 %collective-permute-start.7 = (bf16[64,2048]{1,0:T(8,128)(2,1)}, bf16[64,2048]{1,0:T(8,128)(2,1)S(1)}, u32[]{:S(2)}, u32[]{:S(2)}) collective-permute-start(bf16[64,2048]{1,0:T(8,128)(2,1)} %get-tuple-element.88), channel_id=1, source_target_pairs={{0,3},{1,0},{2,1},{3,2},{4,7},{5,4},{6,5},{7,6},{8,11},{9,8},{10,9... | collective-permute-start | bytes 786440 | tf_op jit(solution)/shard_map/ppermute | solution.py:393
  52.2 25.6 %collective-permute-start.16 = (bf16[224,1024]{1,0:T(8,128)(2,1)}, bf16[224,1024]{1,0:T(8,128)(2,1)S(1)}, u32[]{:S(2)}, u32[]{:S(2)}) collective-permute-start(bf16[224,1024]{1,0:T(8,128)(2,1)} %get-tuple-element.103), channel_id=1, source_target_pairs={{0,4},{4,0},{8,12},{12,8},{1,5},{5,1},{9,13},{13,9},{2,6},{6,2},{1... | collective-permute-start | bytes 1376264 | tf_op jit(solution)/shard_map/ppermute | solution.py:460
  58.0 22.3 %collective-permute-start.15 = (bf16[224,1024]{1,0:T(8,128)(2,1)}, bf16[224,1024]{1,0:T(8,128)(2,1)}, u32[]{:S(2)}, u32[]{:S(2)}) collective-permute-start(bf16[224,1024]{1,0:T(8,128)(2,1)} %get-tuple-element.102), channel_id=1, source_target_pairs={{4,8},{8,4},{5,9},{9,5},{6,10},{10,6},{7,11},{11,7},{20,24},{24,20... | collective-permute-start | bytes 1376264 | tf_op jit(solution)/shard_map/ppermute | solution.py:470
  61.3 23.7 %collective-permute-start.14 = (bf16[224,1024]{1,0:T(8,128)(2,1)}, bf16[224,1024]{1,0:T(8,128)(2,1)S(1)}, u32[]{:S(2)}, u32[]{:S(2)}) collective-permute-start(bf16[224,1024]{1,0:T(8,128)(2,1)} %get-tuple-element.101), channel_id=1, source_target_pairs={{0,4},{4,0},{8,12},{12,8},{1,5},{5,1},{9,13},{13,9},{2,6},{6,2},{1... | collective-permute-start | bytes 1376264 | tf_op jit(solution)/shard_map/ppermute | solution.py:460
  82.4 17.7 %collective-permute-start.18 = (bf16[224,1024]{1,0:T(8,128)(2,1)}, bf16[224,1024]{1,0:T(8,128)(2,1)}, u32[]{:S(2)}, u32[]{:S(2)}) collective-permute-start(bf16[224,1024]{1,0:T(8,128)(2,1)} %get-tuple-element.108), channel_id=1, source_target_pairs={{0,4},{4,0},{8,12},{12,8},{1,5},{5,1},{9,13},{13,9},{2,6},{6,2},{1... | collective-permute-start | bytes 1376264 | tf_op jit(solution)/shard_map/ppermute | solution.py:460
  86.9 19.0 %collective-permute-start.17 = (bf16[224,1024]{1,0:T(8,128)(2,1)}, bf16[224,1024]{1,0:T(8,128)(2,1)}, u32[]{:S(2)}, u32[]{:S(2)}) collective-permute-start(bf16[224,1024]{1,0:T(8,128)(2,1)} %get-tuple-element.107), channel_id=1, source_target_pairs={{4,8},{8,4},{5,9},{9,5},{6,10},{10,6},{7,11},{11,7},{20,24},{24,20... | collective-permute-start | bytes 1376264 | tf_op jit(solution)/shard_map/ppermute | solution.py:470
  90.3 23.2 %collective-permute-start.22 = (bf16[224,1024]{1,0:T(8,128)(2,1)}, bf16[224,1024]{1,0:T(8,128)(2,1)}, u32[]{:S(2)}, u32[]{:S(2)}) collective-permute-start(bf16[224,1024]{1,0:T(8,128)(2,1)} %get-tuple-element.119), channel_id=1, source_target_pairs={{0,4},{4,0},{8,12},{12,8},{1,5},{5,1},{9,13},{13,9},{2,6},{6,2},{1... | collective-permute-start | bytes 1376264 | tf_op jit(solution)/shard_map/ppermute | solution.py:460
  102.2 17.0 %collective-permute-start.21 = (bf16[224,1024]{1,0:T(8,128)(2,1)}, bf16[224,1024]{1,0:T(8,128)(2,1)S(1)}, u32[]{:S(2)}, u32[]{:S(2)}) collective-permute-start(bf16[224,1024]{1,0:T(8,128)(2,1)} %get-tuple-element.118), channel_id=1, source_target_pairs={{4,8},{8,4},{5,9},{9,5},{6,10},{10,6},{7,11},{11,7},{20,24},{24,20... | collective-permute-start | bytes 1376264 | tf_op jit(solution)/shard_map/ppermute | solution.py:470
  108.0 17.1 %collective-permute-start.20 = (bf16[224,1024]{1,0:T(8,128)(2,1)}, bf16[224,1024]{1,0:T(8,128)(2,1)S(1)}, u32[]{:S(2)}, u32[]{:S(2)}) collective-permute-start(bf16[224,1024]{1,0:T(8,128)(2,1)} %get-tuple-element.117), channel_id=1, source_target_pairs={{0,4},{4,0},{8,12},{12,8},{1,5},{5,1},{9,13},{13,9},{2,6},{6,2},{1... | collective-permute-start | bytes 1376264 | tf_op jit(solution)/shard_map/ppermute | solution.py:460
  115.6 15.1 %collective-permute-start.25 = (bf16[224,1024]{1,0:T(8,128)(2,1)}, bf16[224,1024]{1,0:T(8,128)(2,1)S(1)}, u32[]{:S(2)}, u32[]{:S(2)}) collective-permute-start(bf16[224,1024]{1,0:T(8,128)(2,1)} %get-tuple-element.131), channel_id=1, source_target_pairs={{4,8},{8,4},{5,9},{9,5},{6,10},{10,6},{7,11},{11,7},{20,24},{24,20... | collective-permute-start | bytes 1376264 | tf_op jit(solution)/shard_map/ppermute | solution.py:470
  121.0 16.8 %collective-permute-start.24 = (bf16[224,1024]{1,0:T(8,128)(2,1)}, bf16[224,1024]{1,0:T(8,128)(2,1)S(1)}, u32[]{:S(2)}, u32[]{:S(2)}) collective-permute-start(bf16[224,1024]{1,0:T(8,128)(2,1)} %get-tuple-element.130), channel_id=1, source_target_pairs={{0,4},{4,0},{8,12},{12,8},{1,5},{5,1},{9,13},{13,9},{2,6},{6,2},{1... | collective-permute-start | bytes 1376264 | tf_op jit(solution)/shard_map/ppermute | solution.py:460
  126.9 13.7 %collective-permute-start.23 = (bf16[224,1024]{1,0:T(8,128)(2,1)}, bf16[224,1024]{1,0:T(8,128)(2,1)S(1)}, u32[]{:S(2)}, u32[]{:S(2)}) collective-permute-start(bf16[224,1024]{1,0:T(8,128)(2,1)} %get-tuple-element.129), channel_id=1, source_target_pairs={{4,8},{8,4},{5,9},{9,5},{6,10},{10,6},{7,11},{11,7},{20,24},{24,20... | collective-permute-start | bytes 1376264 | tf_op jit(solution)/shard_map/ppermute | solution.py:470
  132.5 14.1 %collective-permute-start.27 = (bf16[224,1024]{1,0:T(8,128)(2,1)}, bf16[224,1024]{1,0:T(8,128)(2,1)S(1)}, u32[]{:S(2)}, u32[]{:S(2)}) collective-permute-start(bf16[224,1024]{1,0:T(8,128)(2,1)} %get-tuple-element.141), channel_id=1, source_target_pairs={{0,4},{4,0},{8,12},{12,8},{1,5},{5,1},{9,13},{13,9},{2,6},{6,2},{1... | collective-permute-start | bytes 1376264 | tf_op jit(solution)/shard_map/ppermute | solution.py:460
  141.8 10.6 %collective-permute-start.26 = (bf16[224,1024]{1,0:T(8,128)(2,1)S(1)}, bf16[224,1024]{1,0:T(8,128)(2,1)S(1)}, u32[]{:S(2)}, u32[]{:S(2)}) collective-permute-start(bf16[224,1024]{1,0:T(8,128)(2,1)S(1)} %get-tuple-element.140), channel_id=1, source_target_pairs={{0,4},{4,0},{8,12},{12,8},{1,5},{5,1},{9,13},{13,9},{2,6},{6,2},{1... | collective-permute-start | bytes 1376264 | tf_op jit(solution)/shard_map/ppermute | solution.py:460
  (18 other events, 165.5 us)

commit v4 on v3

v4 whole, which is shorter than its diff:
```python
import functools

import jax
import jax.numpy as jnp
from jax import lax
from jax.experimental import pallas as pl
from jax.experimental.pallas import tpu as pltpu
from jax.sharding import PartitionSpec as P

GROUP_ROWS = 16
CAP = 4
LIVE_ROWS = 224
TAG = 128
CHUNK = 1024
TILE = 512
BF16 = jnp.bfloat16
F32 = jnp.float32
MIB = 1024 * 1024
PREPARE_MIB = 60
DELTA_AT = 2


def dot(a, b):
    return jnp.dot(a, b, preferred_element_type=F32)


def dot_cols(a, b):
    return lax.dot_general(a, b, (((1,), (1,)), ((), ())), preferred_element_type=F32)


def iota(shape, dim):
    return lax.broadcasted_iota(jnp.int32, shape, dim)


def params(mib=50):
    return pltpu.CompilerParams(vmem_limit_bytes=mib * MIB)


def cost(flops, elements):
    return pl.CostEstimate(flops=flops, bytes_accessed=2 * elements, transcendentals=0)


ANY = pl.BlockSpec(memory_space=pl.ANY)
VMEM = pl.BlockSpec(memory_space=pltpu.VMEM)


def is_inner():
    z = lax.axis_index("tensor")
    return (z == 1) | (z == 2)


def chunk_at(q, chunks):
    return jnp.where(lax.axis_index("tensor") % 2 == 0, chunks - 1 - q, q)


def weight_copy(w, q, into, sem):
    column = pl.multiple_of(chunk_at(q, w.shape[1] // CHUNK) * CHUNK, CHUNK)
    return pltpu.make_async_copy(w.at[:, pl.ds(column, CHUNK)], into, sem)


def prepare_kernel(replicas, line, owner_in, slot_in, live_in, x_in, *refs):
    refs = list(refs)
    w = refs.pop(0) if line else None
    compact_x, pick, place = refs[:3]
    blocks = refs[3 : 3 + replicas]
    message = refs[3 + replicas] if line else None
    owner, slot, live, x, sems = refs[-5:]
    wide, wide_sem = (refs[-7], refs[-6]) if line else (None, None)
    copies = [
        pltpu.make_async_copy(src, dst, sems.at[i])
        for i, (src, dst) in enumerate(((owner_in, owner), (slot_in, slot), (live_in, live), (x_in, x)))
    ]
    for copy in copies:
        copy.start()
    if line:
        weights = weight_copy(w, 0, wide, wide_sem.at[0])
        weights.start()
    for copy in copies:
        copy.wait()
    me = lax.axis_index("replica")
    rows, feat = x.shape
    groups = rows // GROUP_ROWS
    out_rows = replicas * CAP * GROUP_ROWS
    lane = iota((1, rows), 1)
    lane_group, lane_slot = lane // GROUP_ROWS, lane % GROUP_ROWS
    row_group = iota((rows, TAG), 0) // GROUP_ROWS
    packed = jnp.full((1, rows), -1, jnp.int32)
    target = jnp.zeros((1, rows), jnp.int32)
    tags = jnp.zeros((rows, TAG), F32)
    owners = [owner[g] for g in range(groups)]
    offset = jnp.int32(0)
    used = [jnp.int32(0)] * replicas
    for g in range(groups):
        count = live[g]
        mine = lane_group == g
        packed = jnp.where(mine & (lane_slot < count), offset + lane_slot, packed)
        offset = offset + count
        position = jnp.int32(0)
        for o in range(replicas):
            hit = owners[g] == o
            position = jnp.where(hit, used[o], position)
            used[o] = used[o] + hit.astype(jnp.int32)
        hop = lax.rem(owners[g] - me + replicas, replicas)
        start = (hop * CAP + position) * GROUP_ROWS
        target = jnp.where(mine, start + lane_slot, target)
        tags = jnp.where(row_group == g, slot[g].astype(F32), tags)
    compact = (iota((LIVE_ROWS, rows), 0) == packed).astype(BF16)
    spread = (iota((out_rows, rows), 0) == target).astype(BF16)
    pick[...] = compact.astype(F32).T.astype(BF16)
    place[...] = dot_cols(compact, spread).astype(BF16)
    packed_x = dot(compact, x[...]).astype(BF16)
    compact_x[...] = packed_x
    sent = dot(spread, x[...]).astype(BF16)
    sent_tags = dot(spread, tags.astype(BF16)).astype(BF16)
    for k, block in enumerate(blocks):
        here = slice(k * block.shape[0], (k + 1) * block.shape[0])
        block[:, :feat] = sent[here]
        block[:, feat:] = sent_tags[here]
    if line:
        weights.wait()
        message[...] = dot(packed_x, wide[...]).astype(BF16)


def prepare(owner, slot, live, x, replicas, weight=None):
    rows, feat = x.shape
    block = CAP * GROUP_ROWS
    line = weight is not None
    shape = lambda *dims: jax.ShapeDtypeStruct(dims, BF16)
    outs = [shape(LIVE_ROWS, feat), shape(rows, LIVE_ROWS), shape(LIVE_ROWS, replicas * block)]
    outs += [shape(block, feat + TAG)] * replicas
    scratch = [pltpu.SMEM(a.shape, jnp.int32) for a in (owner, slot, live)]
    scratch += [pltpu.VMEM(x.shape, BF16), pltpu.SemaphoreType.DMA((4,))]
    if line:
        outs.append(shape(LIVE_ROWS, CHUNK))
        scratch = [pltpu.VMEM((feat, CHUNK), BF16), pltpu.SemaphoreType.DMA((1,))] + scratch
    return pl.pallas_call(
        functools.partial(prepare_kernel, replicas, line),
        out_shape=outs,
        in_specs=[ANY] * (5 if line else 4),
        out_specs=[VMEM] * len(outs),
        scratch_shapes=scratch,
        compiler_params=params(PREPARE_MIB),
        name="prepare",
    )(owner, slot, live, x, *([weight] if line else []))


def base_kernel(places, x, w, token_in, *refs):
    outs, wide, sems = refs[: len(places)], refs[-2], refs[-1]
    slots = wide.shape[0]
    copies = [weight_copy(w, q, wide.at[i % slots], sems.at[i % slots]) for i, q in enumerate(places)]
    for copy in copies[: slots - 1]:
        copy.start()
    for i, copy in enumerate(copies):
        if i + slots - 1 < len(copies):
            copies[i + slots - 1].start()
        copy.wait()
        outs[i][...] = dot(x[...], wide[i % slots]).astype(BF16)


def base_chunks(places, x, weight, token):
    feat, _ = weight.shape
    elements = (feat + LIVE_ROWS) * CHUNK * len(places)
    return pl.pallas_call(
        functools.partial(base_kernel, places),
        out_shape=[jax.ShapeDtypeStruct((LIVE_ROWS, CHUNK), BF16)] * len(places)
        + [jax.ShapeDtypeStruct(token.shape, token.dtype)],
        in_specs=[VMEM, ANY, ANY],
        out_specs=[VMEM] * len(places) + [ANY],
        input_output_aliases={2: len(places)},
        scratch_shapes=[pltpu.VMEM((3, feat, CHUNK), BF16), pltpu.SemaphoreType.DMA((3,))],
        compiler_params=params(),
        cost_estimate=cost(2 * feat * LIVE_ROWS * CHUNK * len(places), elements),
        name="base",
    )(x, weight, token)


def odd_hop_kernel(base, got, token_in, out, token):
    out[...] = (base[...].astype(F32) + got[...].astype(F32)).astype(BF16)


def even_hop_kernel(near, far, got, token_in, out, token):
    @pl.when(is_inner())
    def _():
        out[...] = (near[...].astype(F32) + got[...].astype(F32)).astype(BF16)

    @pl.when(jnp.logical_not(is_inner()))
    def _():
        out[...] = far[...]


def hop(kernel, inputs, token):
    return pl.pallas_call(
        kernel,
        out_shape=(
            jax.ShapeDtypeStruct((LIVE_ROWS, CHUNK), BF16),
            jax.ShapeDtypeStruct(token.shape, token.dtype),
        ),
        in_specs=[VMEM] * len(inputs) + [ANY],
        out_specs=(VMEM, ANY),
        input_output_aliases={len(inputs): 1},
        compiler_params=params(),
        cost_estimate=cost(2 * LIVE_ROWS * CHUNK, 3 * LIVE_ROWS * CHUNK),
        name="hop",
    )(*inputs, token)


def fold(rank, adapters, half):
    shape = (adapters * rank, 2 * rank)
    return (iota(shape, 0) % rank + half * rank == iota(shape, 1)).astype(BF16)


def slot_mask(tag, rank, adapters):
    shape = (tag.shape[0], adapters * rank)
    return (iota(shape, 1) // rank).astype(F32) == tag.astype(F32)


def low_kernel(rank, blocks, down, *refs):
    parts, low = refs[:blocks], refs[blocks + 1]
    adapters = down.shape[0] // rank
    feat = down.shape[1]
    rows = parts[0].shape[0]
    half = blocks // 2
    maps = down[...]
    folds = [fold(rank, adapters, h) for h in range(2)]
    for k in range(half):
        total = None
        for h in range(2):
            part = parts[h * half + k]
            wide = dot_cols(part[:, :feat], maps)
            kept = jnp.where(slot_mask(part[:, feat : feat + 1], rank, adapters), wide, 0.0)
            got = dot(kept.astype(BF16), folds[h])
            total = got if total is None else total + got
        low[k * rows : (k + 1) * rows, :] = total.astype(BF16)


def low_values(parts, down, rank, token):
    rows, width = parts[0].shape
    blocks = len(parts)
    return pl.pallas_call(
        functools.partial(low_kernel, rank, blocks),
        out_shape=(
            jax.ShapeDtypeStruct((blocks // 2 * rows, 2 * rank), BF16),
            jax.ShapeDtypeStruct(token.shape, token.dtype),
        ),
        in_specs=[VMEM] * (blocks + 1) + [ANY],
        out_specs=(VMEM, ANY),
        input_output_aliases={blocks + 1: 1},
        compiler_params=params(),
        name="low",
    )(down, *parts, token)


def delta_kernel(rank, blocks, sums, up, *refs):
    tags, lows, outs = refs[:blocks], refs[blocks : blocks + sums], refs[blocks + sums + 1 :]
    adapters = up.shape[0] // rank
    rows = tags[0].shape[0]
    half = blocks // 2
    total = lows[0][...].astype(F32)
    for other in lows[1:]:
        total = total + other[...].astype(F32)
    low = total.astype(BF16)
    maps = up[...]
    for h in range(2):
        spread = fold(rank, adapters, h)
        for k in range(half):
            wide = dot_cols(low[k * rows : (k + 1) * rows, :], spread)
            mask = slot_mask(tags[h * half + k][:, :1], rank, adapters)
            kept = jnp.where(mask, wide, 0.0).astype(BF16)
            outs[h * half + k][...] = dot(kept, maps).astype(BF16)


def delta_values(parts, lows, up, rank, token):
    rows, width = parts[0].shape
    blocks = len(parts)
    columns = up.shape[1]
    tag = pl.BlockSpec((rows, TAG), lambda i: (0, width // TAG - 1))
    whole = lambda a: pl.BlockSpec(a.shape, lambda i: (0, 0))
    return pl.pallas_call(
        functools.partial(delta_kernel, rank, blocks, len(lows)),
        out_shape=[jax.ShapeDtypeStruct((rows, columns), BF16)] * blocks
        + [jax.ShapeDtypeStruct(token.shape, token.dtype)],
        grid=(1,),
        in_specs=[whole(up)] + [tag] * blocks + [whole(a) for a in lows] + [ANY],
        out_specs=[pl.BlockSpec((rows, columns), lambda i: (0, 0))] * blocks + [ANY],
        input_output_aliases={1 + blocks + len(lows): blocks},
        compiler_params=params(),
        name="delta",
    )(up, *parts, *lows, token)


def add_delta_kernel(per, chunks, place, *refs):
    bases, refs = refs[: 2 * per], refs[2 * per :]
    outs, parts = refs[-2 * per - 1 : -1], refs[: -2 * per - 2]
    rows = parts[0].shape[0]
    inner = is_inner()
    z = lax.axis_index("tensor")
    for j in range(per):
        chunk = chunk_at(jnp.where(inner, per, 3 * per) + j, chunks)
        column = pl.multiple_of((chunk - z * per) * CHUNK, CHUNK)
        total = None
        for k, part in enumerate(parts):
            got = dot(place[:, k * rows : (k + 1) * rows], part[:, pl.ds(column, CHUNK)])
            total = got if total is None else total + got
        for i, mine in ((j, inner), (per + j, jnp.logical_not(inner))):
            wide = bases[i][...].astype(F32)
            outs[i][...] = (wide + jnp.where(mine, total, 0.0)).astype(BF16)


def add_delta(bases, place, parts, chunks, token):
    per = len(bases) // 2
    inputs = [place, *bases, *parts]
    return pl.pallas_call(
        functools.partial(add_delta_kernel, per, chunks),
        out_shape=[jax.ShapeDtypeStruct(bases[0].shape, BF16)] * len(bases)
        + [jax.ShapeDtypeStruct(token.shape, token.dtype)],
        in_specs=[VMEM] * len(inputs) + [ANY],
        out_specs=[VMEM] * len(bases) + [ANY],
        input_output_aliases={len(inputs): len(bases)},
        compiler_params=params(),
        name="add_delta",
    )(*inputs, token)


def finish_kernel(chunks, near_q, far_q, *refs):
    refs = list(refs)
    near = refs.pop(0) if near_q is not None else None
    far = refs.pop(0) if far_q is not None else None
    even, odd = refs.pop(0), refs.pop(0) if near_q is not None else None
    pick = refs.pop(0)
    out, _, made, sems = refs[-4:]
    tiles = CHUNK // TILE

    def write(q, terms):
        column = chunk_at(q, chunks) * CHUNK
        copies = []
        for i in range(tiles):
            total = sum(term[:, i * TILE : (i + 1) * TILE].astype(F32) for term in terms)
            made[i] = dot(pick[...], total.astype(BF16)).astype(BF16)
            here = pl.ds(pl.multiple_of(column + i * TILE, TILE), TILE)
            copies.append(pltpu.make_async_copy(made.at[i], out.at[:, here], sems.at[i]))
            copies[-1].start()
        for copy in copies:
            copy.wait()

    if near_q is not None:

        @pl.when(is_inner())
        def _():
            write(near_q, [near, even, odd])

    if far_q is not None:

        @pl.when(jnp.logical_not(is_inner()))
        def _():
            write(far_q, [far, even])


def finish(near_q, far_q, bases, even, odd, pick, held, token):
    rows, chunks = pick.shape[0], len(bases)
    inputs = [bases[q] for q in (near_q, far_q) if q is not None] + [even]
    inputs += [odd] if near_q is not None else []
    inputs += [pick]
    last = [token] if held is None else [held, token]
    aliases = {len(inputs) + len(last) - 1: 1}
    if held is not None:
        aliases[len(inputs)] = 0
    return pl.pallas_call(
        functools.partial(finish_kernel, chunks, near_q, far_q),
        out_shape=(
            jax.ShapeDtypeStruct((rows, chunks * CHUNK), BF16),
            jax.ShapeDtypeStruct(token.shape, token.dtype),
        ),
        in_specs=[VMEM] * len(inputs) + [ANY] * len(last),
        out_specs=(ANY, ANY),
        scratch_shapes=[pltpu.VMEM((CHUNK // TILE, rows, TILE), BF16), pltpu.SemaphoreType.DMA((CHUNK // TILE,))],
        input_output_aliases=aliases,
        compiler_params=params(),
        cost_estimate=cost(2 * LIVE_ROWS * rows * CHUNK, 6 * LIVE_ROWS * CHUNK),
        name="finish",
    )(*inputs, *last)


def send_groups(blocks):
    replicas = lax.axis_size("replica")
    parts = [blocks[0]]
    for k in range(1, replicas):
        hops = [(i, (i + k) % replicas) for i in range(replicas)]
        parts.append(lax.ppermute(blocks[k], "replica", hops))
    return parts


def send_lows(low):
    shards = lax.axis_size("tensor")
    if shards > 4:
        return [lax.psum(low, "tensor")]
    lows = [low]
    for k in range(1, shards):
        hops = [(i, (i + k) % shards) for i in range(shards)]
        lows.append(lax.ppermute(low, "tensor", hops))
    return lows


def send_back(made):
    replicas = lax.axis_size("replica")
    back = [made[0]]
    for k in range(1, replicas):
        hops = [(i, (i - k) % replicas) for i in range(replicas)]
        back.append(lax.ppermute(made[k], "replica", hops))
    return back


def on_device(x, owner, slot, live, weight, down, up):
    width = weight.shape[1]
    rank = down.shape[1]
    replicas, shards = lax.axis_size("replica"), lax.axis_size("tensor")
    share = width // shards
    down, up = down.reshape(-1, down.shape[2]), up.reshape(-1, up.shape[2])
    token = jnp.zeros((8, 128), jnp.int32)
    if shards != 4:
        compact_x, pick, place, *blocks = prepare(owner[:, 0], slot, live[0], x, replicas)
        z = lax.axis_index("tensor").astype(jnp.int32)
        base = dot(compact_x, weight)
        parts = send_groups(blocks)
        low, token = low_values(parts, down, rank, token)
        *made, token = delta_values(parts, send_lows(low), up, rank, token)
        back = jnp.concatenate(send_back(made), axis=0)
        mine = lax.dynamic_slice_in_dim(base, z * share, share, 1) + dot(place, back)
        base = lax.dynamic_update_slice_in_dim(base, mine, z * share, 1).astype(BF16)
        total = lax.psum_scatter(base, "tensor", scatter_dimension=1, tiled=True)
        total = lax.all_gather(total, "tensor", axis=1, tiled=True)
        return dot(pick, total).astype(BF16)

    chunks, per = width // CHUNK, share // CHUNK
    even = [(0, 1), (1, 0), (2, 3), (3, 2)]
    odd = [(1, 2), (2, 1)]
    compact_x, pick, place, *rest = prepare(owner[:, 0], slot, live[0], x, replicas, weight)
    blocks, message = rest[:-1], rest[-1]
    evens, odds = {0: lax.ppermute(message, "tensor", even)}, {}
    parts = send_groups(blocks)
    *early, token = base_chunks((1, 2), compact_x, weight, token)
    bases = [message, *early]
    for step in (1, 2):
        evens[step] = lax.ppermute(bases[step], "tensor", even)
    *late, token = base_chunks(tuple(range(3, chunks)), compact_x, weight, token)
    bases += late
    low, token = low_values(parts, down, rank, token)
    lows = send_lows(low)
    steps = chunks + 3
    result = None
    unfinished = list(range(steps))
    seen_even, seen_odd = set(), set()

    def close(result, token):
        for a in list(unfinished):
            b = chunks - a
            if a not in seen_even or (1 <= b <= chunks and b not in seen_odd):
                continue
            unfinished.remove(a)
            near_q = chunks - 1 - a if a < chunks else None
            far_q = chunks + 2 - a if a >= 3 else None
            result, token = finish(near_q, far_q, bases, evens[a], odds.get(b), pick, result, token)
        return result, token

    for step in range(1, steps):
        if step >= 3:
            far = bases[min(step, chunks - 1)]
            inputs = [bases[step - 3], far, odds[step - 2]]
            message, token = hop(even_hop_kernel, inputs, token)
            evens[step] = lax.ppermute(message, "tensor", even)
            seen_odd.add(step - 2)
            result, token = close(result, token)
        if step <= chunks:
            message, token = hop(odd_hop_kernel, [bases[chunks - step], evens[step - 1]], token)
            odds[step] = lax.ppermute(message, "tensor", odd)
        seen_even.add(step - 1)
        if step == DELTA_AT:
            *made, token = delta_values(parts, lows, up, rank, token)
            back = send_back(made)
        if step == per + 2:
            own = list(range(per, 2 * per)) + list(range(3 * per, 4 * per))
            *summed, token = add_delta([bases[q] for q in own], place, back, chunks, token)
            for q, value in zip(own, summed):
                bases[q] = value
        result, token = close(result, token)
    seen_even.add(steps - 1)
    result, token = close(result, token)
    return result


def solution(mesh):
    placed = (
        P(("parts", "replica"), "tensor"),
        P(("parts", "replica"), None),
        P(("parts", "replica")),
        P(("parts", "replica"), None),
        P("tensor", None),
        P("replica", None, "tensor"),
        P("replica", None, "tensor"),
    )
    return jax.shard_map(
        on_device,
        mesh=mesh,
        in_specs=placed,
        out_specs=P(("parts", "replica"), None),
        check_vma=False,
    )
```

time: 156 us -> 137 us (0.88)
  Pallas kernels: 84.7 us -> 28 us
  starting transfers between devices: 45.3 us -> 66.8 us
  waiting for transfers between devices: 19.1 us -> 39.8 us
  local copies, waits for them, and re-layouts: 4.73 us -> 1.06 us
    pallas_call x33 -> x31, Pallas kernels: 80.2 us -> 24.2 us  [the longest x11 8.86 us: finish(): pl.pallas_call(functools.partial(finish_kernel, chunks, near_q, far_q), o...]
    ppermute x10 -> x8, waiting for transfers between devices: 5.86 us -> 29.1 us  [on_device(): evens[step] = lax.ppermute(message, 'tensor', even)]
    ppermute x3, starting transfers between devices: 5.52 us -> 16.9 us  [send_lows(): lows.append(lax.ppermute(low, 'tensor', hops))]
    ppermute x10 -> x8, starting transfers between devices: 24.7 us -> 32 us  [on_device(): evens[step] = lax.ppermute(message, 'tensor', even)]
    ppermute x4 -> x6, starting transfers between devices: 6.03 us -> 11 us  [the longest x2 4.95 us: on_device(): evens[step] = lax.ppermute(bases[step], 'tensor', even)]
    ppermute x3, waiting for transfers between devices: 8.4 us -> 4.96 us  [send_back(): back.append(lax.ppermute(made[k], 'replica', hops))]
    unnamed x28 -> x18, local copies, waits for them, and re-layouts: 3.56 us -> 1.05 us
    ppermute x4 -> x6, waiting for transfers between devices: 0.01 us -> 1.57 us  [the longest x2 1.56 us: on_device(): evens[step] = lax.ppermute(bases[step], 'tensor', even)]
  transfers between devices with their start and end apart: 28 -> 28, of which waited for: 5 -> 12; matrix products, arithmetic and copies ran while one was open for 1% -> 0% of each run, Pallas kernels for 51% -> 17%
where the time goes in v4:
time: 137 us; the launch traced here: 136 us
  starting transfers between devices  66.8 us (49%)
  waiting for transfers between devices  39.8 us (29%)
  Pallas kernels  28 us (20%)
    ppermute x8, starting transfers between devices, on_device(): evens[step] = lax.ppermute(message, 'tensor', even)  32 us
    ppermute x8, waiting for transfers between devices, on_device(): evens[step] = lax.ppermute(message, 'tensor', even)  29.1 us
    ppermute x3, starting transfers between devices, send_lows(): lows.append(lax.ppermute(low, 'tensor', hops))  16.9 us
    pallas_call x11, Pallas kernels, finish(): pl.pallas_call(functools.partial(finish_kernel, chunks, near_q, far_q), o...  8.86 us
    pallas_call x2, Pallas kernels, base_chunks(): pl.pallas_call(functools.partial(base_kernel, places), out_shape=[jax.Sha...  8.26 us
    ppermute x8, starting transfers between devices, on_device(): odds[step] = lax.ppermute(message, 'tensor', odd)  5.52 us
    ppermute x3, waiting for transfers between devices, send_back(): back.append(lax.ppermute(made[k], 'replica', hops))  4.96 us
    ppermute x2, starting transfers between devices, on_device(): evens[step] = lax.ppermute(bases[step], 'tensor', even)  4.95 us
  transfers between devices with their start and end apart: 28, of which 12 were waited for; matrix products, arithmetic and copies ran while one was open for 0% of the time, Pallas kernels for 17%

profile of v4, /device:TPU:0, one launch (start us, length us, event | category | flops | bytes accessed | tf_op | source)
XLA Modules:
  0.0 136.2 jit_solution(14884063975682060843)
XLA Ops:
  0.0 3.3 %prepare.1 = (bf16[224,1024]{1,0:T(8,128)(2,1)}, bf16[256,224]{1,0:T(8,128)(2,1)}, bf16[224,256]{1,0:T(8,128)(2,1)}, bf16[64,1152]{1,0:T(8,128)(2,1)}, bf16[64,1...) custom-call(s32[16]{0:T(128)} %bitcast.6, s32[16]{0:T(128)} %slot_in.1, ...), custom_call_target="tpu_custom_call" | custom-call | tf_op jit(solution)/shard_map/prepare/pallas_call | solution.py:136
  3.3 3.1 %collective-permute-start.7 = (bf16[224,1024]{1,0:T(8,128)(2,1)}, bf16[224,1024]{1,0:T(8,128)(2,1)S(1)}, u32[]{:S(2)}, u32[]{:S(2)}) collective-permute-start(bf16[224,1024]{1,0:T(8,128)(2,1)} %get-tuple-element.87.near.base.refs_0_), channel_id=1, source_target_pairs={{0,4},{4,0},{8,12},{12,8},{1,5},{5,1},{9,13},{13,9},{2,6},{6,2},{1... | collective-permute-start | bytes 1376264 | tf_op jit(solution)/shard_map/ppermute | solution.py:438
  10.3 2.9 %base.2 = (bf16[224,1024]{1,0:T(8,128)(2,1)S(1)}, bf16[224,1024]{1,0:T(8,128)(2,1)S(1)}, s32[8,128]{1,0:T(8,128)S(1)}) custom-call(bf16[224,1024]{1,0:T(8,128)(2,1)S(1)} %copy-done.5, bf16[1024,8192]{1,0:T(8,128)(2,1)} %w.3, s32[8,128]{1,0:T(8,128)S(1)} %broadcast_in_dim.3.token_in), custom_call_target="tpu_custom_call", output_to_operand_aliasing={{2}: (2, {})} | custom-call | flops 939524096 | bytes 5111808 | tf_op jit(solution)/shard_map/base/pallas_call | solution.py:163
  13.8 5.4 %base.3 = (bf16[224,1024]{1,0:T(8,128)(2,1)S(1)}, bf16[224,1024]{1,0:T(8,128)(2,1)S(1)}, bf16[224,1024]{1,0:T(8,128)(2,1)S(1)}, bf16[224,1024]{1,0:T(8,128)(2,1)...) custom-call(bf16[224,1024]{1,0:T(8,128)(2,1)S(1)} %copy-done.5, ...), custom_call_target="tpu_custom_call", output_to_operand_aliasing={{5}: (2, {})} | custom-call | flops 2348810240 | bytes 12779520 | tf_op jit(solution)/shard_map/base/pallas_call | solution.py:163
  21.7 4.4 %collective-permute-start.14 = (bf16[224,1024]{1,0:T(8,128)(2,1)S(1)}, bf16[224,1024]{1,0:T(8,128)(2,1)S(1)}, u32[]{:S(2)}, u32[]{:S(2)}) collective-permute-start(bf16[224,1024]{1,0:T(8,128)(2,1)S(1)} %get-tuple-element.90.refs_0_), channel_id=1, source_target_pairs={{0,4},{4,0},{8,12},{12,8},{1,5},{5,1},{9,13},{13,9},{2,6},{6,2},{1... | collective-permute-start | bytes 1376264 | tf_op jit(solution)/shard_map/ppermute | solution.py:443
  28.6 4.1 %collective-permute-start.5 = (bf16[128,128]{1,0:T(8,128)(2,1)S(1)}, bf16[128,128]{1,0:T(8,128)(2,1)S(1)}, u32[]{:S(2)}, u32[]{:S(2)}) collective-permute-start(bf16[128,128]{1,0:T(8,128)(2,1)S(1)} %get-tuple-element.100.refs_4_), channel_id=1, source_target_pairs={{0,12},{4,0},{8,4},{12,8},{1,13},{5,1},{9,5},{13,9},{2,14},{6,2},{... | collective-permute-start | bytes 98312 | tf_op jit(solution)/shard_map/ppermute | solution.py:399
  32.7 2.2 %collective-permute-start.4 = (bf16[128,128]{1,0:T(8,128)(2,1)S(1)}, bf16[128,128]{1,0:T(8,128)(2,1)S(1)}, u32[]{:S(2)}, u32[]{:S(2)}) collective-permute-start(bf16[128,128]{1,0:T(8,128)(2,1)S(1)} %get-tuple-element.100.refs_4_), channel_id=1, source_target_pairs={{0,8},{4,12},{8,0},{12,4},{1,9},{5,13},{9,1},{13,5},{2,10},{6,14},... | collective-permute-start | bytes 98312 | tf_op jit(solution)/shard_map/ppermute | solution.py:399
  34.9 2.5 %collective-permute-done.5.refs_7_ = bf16[128,128]{1,0:T(8,128)(2,1)S(1)} collective-permute-done((bf16[128,128]{1,0:T(8,128)(2,1)S(1)}, bf16[128,128]{1,0:T(8,128)(2,1)S(1)}, u32[]{:S(2)}, u32[]{:S(2)}) %collective-permute-start.5) | collective-permute-done | bytes 32800 | tf_op jit(solution)/shard_map/ppermute | solution.py:399
  37.5 10.6 %collective-permute-start.3 = (bf16[128,128]{1,0:T(8,128)(2,1)S(1)}, bf16[128,128]{1,0:T(8,128)(2,1)S(1)}, u32[]{:S(2)}, u32[]{:S(2)}) collective-permute-start(bf16[128,128]{1,0:T(8,128)(2,1)S(1)} %get-tuple-element.100.refs_4_), channel_id=1, source_target_pairs={{0,4},{4,8},{8,12},{12,0},{1,5},{5,9},{9,13},{13,1},{2,6},{6,10},{... | collective-permute-start | bytes 98312 | tf_op jit(solution)/shard_map/ppermute | solution.py:399
  51.8 2.5 %collective-permute-start.12 = (bf16[224,1024]{1,0:T(8,128)(2,1)S(1)}, bf16[224,1024]{1,0:T(8,128)(2,1)S(1)}, u32[]{:S(2)}, u32[]{:S(2)}) collective-permute-start(bf16[224,1024]{1,0:T(8,128)(2,1)S(1)} %get-tuple-element.112), channel_id=1, source_target_pairs={{0,4},{4,0},{8,12},{12,8},{1,5},{5,1},{9,13},{13,9},{2,6},{6,2},{1... | collective-permute-start | bytes 1376264 | tf_op jit(solution)/shard_map/ppermute | solution.py:469
  57.9 7.8 %collective-permute-done.12.got.refs_2_ = bf16[224,1024]{1,0:T(8,128)(2,1)S(1)} collective-permute-done((bf16[224,1024]{1,0:T(8,128)(2,1)S(1)}, bf16[224,1024]{1,0:T(8,128)(2,1)S(1)}, u32[]{:S(2)}, u32[]{:S(2)}) %collective-permute-start.12) | collective-permute-done | bytes 458784 | tf_op jit(solution)/shard_map/ppermute | solution.py:469
  67.9 3.6 %collective-permute-done.10.refs_7_ = bf16[64,2048]{1,0:T(8,128)(2,1)S(1)} collective-permute-done((bf16[64,2048]{1,0:T(8,128)(2,1)S(1)}, bf16[64,2048]{1,0:T(8,128)(2,1)S(1)}, u32[]{:S(2)}, u32[]{:S(2)}) %collective-permute-start.10) | collective-permute-done | bytes 262176 | tf_op jit(solution)/shard_map/ppermute | solution.py:408
  71.5 2.5 %add_delta.1 = (bf16[224,1024]{1,0:T(8,128)(2,1)S(1)}, bf16[224,1024]{1,0:T(8,128)(2,1)S(1)}, bf16[224,1024]{1,0:T(8,128)(2,1)S(1)}, bf16[224,1024]{1,0:T(8,128)(2,1)S(1)}, s32[8,128]{1,0:T(8,128)S(1)}) custom-call(bf16[224,256]{1,0:T(8,128)(2,1)S(1)} %copy-done.8, bf16[224,1024]{1,0:T(8,128)(2,1)S(1)} %get-tuple-element.90.refs_0_, ...), custom_call_target="tpu_custom_call", output_to_operand_aliasing={{4}: (9, {})} | custom-call | tf_op jit(solution)/shard_map/add_delta/pallas_call | solution.py:312
  77.1 5.8 %collective-permute-start.22 = (bf16[224,1024]{1,0:T(8,128)(2,1)S(1)}, bf16[224,1024]{1,0:T(8,128)(2,1)S(1)}, u32[]{:S(2)}, u32[]{:S(2)}) collective-permute-start(bf16[224,1024]{1,0:T(8,128)(2,1)S(1)} %get-tuple-element.139), channel_id=1, source_target_pairs={{0,4},{4,0},{8,12},{12,8},{1,5},{5,1},{9,13},{13,9},{2,6},{6,2},{1... | collective-permute-start | bytes 1376264 | tf_op jit(solution)/shard_map/ppermute | solution.py:469
  84.0 3.0 %collective-permute-done.18.got.refs_2_ = bf16[224,1024]{1,0:T(8,128)(2,1)S(1)} collective-permute-done((bf16[224,1024]{1,0:T(8,128)(2,1)S(1)}, bf16[224,1024]{1,0:T(8,128)(2,1)S(1)}, u32[]{:S(2)}, u32[]{:S(2)}) %collective-permute-start.18) | collective-permute-done | bytes 458784 | tf_op jit(solution)/shard_map/ppermute | solution.py:469
  89.1 3.9 %collective-permute-start.20 = (bf16[224,1024]{1,0:T(8,128)(2,1)S(1)}, bf16[224,1024]{1,0:T(8,128)(2,1)S(1)}, u32[]{:S(2)}, u32[]{:S(2)}) collective-permute-start(bf16[224,1024]{1,0:T(8,128)(2,1)S(1)} %get-tuple-element.137), channel_id=1, source_target_pairs={{0,4},{4,0},{8,12},{12,8},{1,5},{5,1},{9,13},{13,9},{2,6},{6,2},{1... | collective-permute-start | bytes 1376264 | tf_op jit(solution)/shard_map/ppermute | solution.py:469
  94.2 2.6 %collective-permute-done.22.got.refs_2_ = bf16[224,1024]{1,0:T(8,128)(2,1)S(1)} collective-permute-done((bf16[224,1024]{1,0:T(8,128)(2,1)S(1)}, bf16[224,1024]{1,0:T(8,128)(2,1)S(1)}, u32[]{:S(2)}, u32[]{:S(2)}) %collective-permute-start.22) | collective-permute-done | bytes 458784 | tf_op jit(solution)/shard_map/ppermute | solution.py:469
  98.8 5.6 %collective-permute-start.24 = (bf16[224,1024]{1,0:T(8,128)(2,1)S(1)}, bf16[224,1024]{1,0:T(8,128)(2,1)S(1)}, u32[]{:S(2)}, u32[]{:S(2)}) collective-permute-start(bf16[224,1024]{1,0:T(8,128)(2,1)S(1)} %get-tuple-element.150), channel_id=1, source_target_pairs={{0,4},{4,0},{8,12},{12,8},{1,5},{5,1},{9,13},{13,9},{2,6},{6,2},{1... | collective-permute-start | bytes 1376264 | tf_op jit(solution)/shard_map/ppermute | solution.py:469
  104.4 2.2 %collective-permute-done.20.got.refs_2_ = bf16[224,1024]{1,0:T(8,128)(2,1)S(1)} collective-permute-done((bf16[224,1024]{1,0:T(8,128)(2,1)S(1)}, bf16[224,1024]{1,0:T(8,128)(2,1)S(1)}, u32[]{:S(2)}, u32[]{:S(2)}) %collective-permute-start.20) | collective-permute-done | bytes 458784 | tf_op jit(solution)/shard_map/ppermute | solution.py:469
  108.6 5.6 %collective-permute-start.27 = (bf16[224,1024]{1,0:T(8,128)(2,1)S(1)}, bf16[224,1024]{1,0:T(8,128)(2,1)S(1)}, u32[]{:S(2)}, u32[]{:S(2)}) collective-permute-start(bf16[224,1024]{1,0:T(8,128)(2,1)S(1)} %get-tuple-element.161), channel_id=1, source_target_pairs={{0,4},{4,0},{8,12},{12,8},{1,5},{5,1},{9,13},{13,9},{2,6},{6,2},{1... | collective-permute-start | bytes 1376264 | tf_op jit(solution)/shard_map/ppermute | solution.py:469
  114.2 2.2 %collective-permute-done.24.refs_1_ = bf16[224,1024]{1,0:T(8,128)(2,1)S(1)} collective-permute-done((bf16[224,1024]{1,0:T(8,128)(2,1)S(1)}, bf16[224,1024]{1,0:T(8,128)(2,1)S(1)}, u32[]{:S(2)}, u32[]{:S(2)}) %collective-permute-start.24) | collective-permute-done | bytes 458784 | tf_op jit(solution)/shard_map/ppermute | solution.py:469
  117.6 5.0 %collective-permute-start.26 = (bf16[224,1024]{1,0:T(8,128)(2,1)S(1)}, bf16[224,1024]{1,0:T(8,128)(2,1)S(1)}, u32[]{:S(2)}, u32[]{:S(2)}) collective-permute-start(bf16[224,1024]{1,0:T(8,128)(2,1)S(1)} %get-tuple-element.160), channel_id=1, source_target_pairs={{0,4},{4,0},{8,12},{12,8},{1,5},{5,1},{9,13},{13,9},{2,6},{6,2},{1... | collective-permute-start | bytes 1376264 | tf_op jit(solution)/shard_map/ppermute | solution.py:469
  122.7 3.6 %collective-permute-done.27.refs_1_ = bf16[224,1024]{1,0:T(8,128)(2,1)S(1)} collective-permute-done((bf16[224,1024]{1,0:T(8,128)(2,1)S(1)}, bf16[224,1024]{1,0:T(8,128)(2,1)S(1)}, u32[]{:S(2)}, u32[]{:S(2)}) %collective-permute-start.27) | collective-permute-done | bytes 458784 | tf_op jit(solution)/shard_map/ppermute | solution.py:469
  127.4 7.6 %collective-permute-done.26.refs_1_ = bf16[224,1024]{1,0:T(8,128)(2,1)S(1)} collective-permute-done((bf16[224,1024]{1,0:T(8,128)(2,1)S(1)}, bf16[224,1024]{1,0:T(8,128)(2,1)S(1)}, u32[]{:S(2)}, u32[]{:S(2)}) %collective-permute-start.26) | collective-permute-done | bytes 458784 | tf_op jit(solution)/shard_map/ppermute | solution.py:469
  (84 shorter events, 33.4 us)
Async XLA Ops:
  3.3 17.7 %collective-permute-start.7 = (bf16[224,1024]{1,0:T(8,128)(2,1)}, bf16[224,1024]{1,0:T(8,128)(2,1)S(1)}, u32[]{:S(2)}, u32[]{:S(2)}) collective-permute-start(bf16[224,1024]{1,0:T(8,128)(2,1)} %get-tuple-element.87.near.base.refs_0_), channel_id=1, source_target_pairs={{0,4},{4,0},{8,12},{12,8},{1,5},{5,1},{9,13},{13,9},{2,6},{6,2},{1... | collective-permute-start | bytes 1376264 | tf_op jit(solution)/shard_map/ppermute | solution.py:438
  6.4 12.8 %collective-permute-start = (bf16[64,1152]{1,0:T(8,128)(2,1)}, bf16[64,1152]{1,0:T(8,128)(2,1)S(1)}, u32[]{:S(2)}, u32[]{:S(2)}) collective-permute-start(bf16[64,1152]{1,0:T(8,128)(2,1)} %get-tuple-element.96), channel_id=1, source_target_pairs={{0,1},{1,2},{2,3},{3,0},{4,5},{5,6},{6,7},{7,4},{8,9},{9,10},{10,1... | collective-permute-start | bytes 442376 | tf_op jit(solution)/shard_map/ppermute | solution.py:388
  6.4 12.8 %collective-permute-start.1 = (bf16[64,1152]{1,0:T(8,128)(2,1)}, bf16[64,1152]{1,0:T(8,128)(2,1)S(1)}, u32[]{:S(2)}, u32[]{:S(2)}) collective-permute-start(bf16[64,1152]{1,0:T(8,128)(2,1)} %get-tuple-element.97), channel_id=1, source_target_pairs={{0,2},{1,3},{2,0},{3,1},{4,6},{5,7},{6,4},{7,5},{8,10},{9,11},{10,... | collective-permute-start | bytes 442376 | tf_op jit(solution)/shard_map/ppermute | solution.py:388
  7.9 11.3 %collective-permute-start.2 = (bf16[64,1152]{1,0:T(8,128)(2,1)}, bf16[64,1152]{1,0:T(8,128)(2,1)S(1)}, u32[]{:S(2)}, u32[]{:S(2)}) collective-permute-start(bf16[64,1152]{1,0:T(8,128)(2,1)} %get-tuple-element.98), channel_id=1, source_target_pairs={{0,3},{1,0},{2,1},{3,2},{4,7},{5,4},{6,5},{7,6},{8,11},{9,8},{10,9... | collective-permute-start | bytes 442376 | tf_op jit(solution)/shard_map/ppermute | solution.py:388
  13.3 14.5 %collective-permute-start.6 = (bf16[224,1024]{1,0:T(8,128)(2,1)S(1)}, bf16[224,1024]{1,0:T(8,128)(2,1)S(1)}, u32[]{:S(2)}, u32[]{:S(2)}) collective-permute-start(bf16[224,1024]{1,0:T(8,128)(2,1)S(1)} %get-tuple-element.101.near.base.refs_0_), channel_id=1, source_target_pairs={{0,4},{4,0},{8,12},{12,8},{1,5},{5,1},{9,13},{13,9},{2,6},{6,2},{1... | collective-permute-start | bytes 1376264 | tf_op jit(solution)/shard_map/ppermute | solution.py:443
  21.1 30.7 %collective-permute-start.11 = (bf16[224,1024]{1,0:T(8,128)(2,1)S(1)}, bf16[224,1024]{1,0:T(8,128)(2,1)S(1)}, u32[]{:S(2)}, u32[]{:S(2)}) collective-permute-start(bf16[224,1024]{1,0:T(8,128)(2,1)S(1)} %get-tuple-element.110), channel_id=1, source_target_pairs={{4,8},{8,4},{5,9},{9,5},{6,10},{10,6},{7,11},{11,7},{20,24},{24,20... | collective-permute-start | bytes 1376264 | tf_op jit(solution)/shard_map/ppermute | solution.py:474
  21.7 32.5 %collective-permute-start.14 = (bf16[224,1024]{1,0:T(8,128)(2,1)S(1)}, bf16[224,1024]{1,0:T(8,128)(2,1)S(1)}, u32[]{:S(2)}, u32[]{:S(2)}) collective-permute-start(bf16[224,1024]{1,0:T(8,128)(2,1)S(1)} %get-tuple-element.90.refs_0_), channel_id=1, source_target_pairs={{0,4},{4,0},{8,12},{12,8},{1,5},{5,1},{9,13},{13,9},{2,6},{6,2},{1... | collective-permute-start | bytes 1376264 | tf_op jit(solution)/shard_map/ppermute | solution.py:443
  27.9 27.2 %collective-permute-start.13 = (bf16[224,1024]{1,0:T(8,128)(2,1)S(1)}, bf16[224,1024]{1,0:T(8,128)(2,1)S(1)}, u32[]{:S(2)}, u32[]{:S(2)}) collective-permute-start(bf16[224,1024]{1,0:T(8,128)(2,1)S(1)} %get-tuple-element.113), channel_id=1, source_target_pairs={{4,8},{8,4},{5,9},{9,5},{6,10},{10,6},{7,11},{11,7},{20,24},{24,20... | collective-permute-start | bytes 1376264 | tf_op jit(solution)/shard_map/ppermute | solution.py:474
  32.7 15.3 %collective-permute-start.4 = (bf16[128,128]{1,0:T(8,128)(2,1)S(1)}, bf16[128,128]{1,0:T(8,128)(2,1)S(1)}, u32[]{:S(2)}, u32[]{:S(2)}) collective-permute-start(bf16[128,128]{1,0:T(8,128)(2,1)S(1)} %get-tuple-element.100.refs_4_), channel_id=1, source_target_pairs={{0,8},{4,12},{8,0},{12,4},{1,9},{5,13},{9,1},{13,5},{2,10},{6,14},... | collective-permute-start | bytes 98312 | tf_op jit(solution)/shard_map/ppermute | solution.py:399
  37.5 12.2 %collective-permute-start.3 = (bf16[128,128]{1,0:T(8,128)(2,1)S(1)}, bf16[128,128]{1,0:T(8,128)(2,1)S(1)}, u32[]{:S(2)}, u32[]{:S(2)}) collective-permute-start(bf16[128,128]{1,0:T(8,128)(2,1)S(1)} %get-tuple-element.100.refs_4_), channel_id=1, source_target_pairs={{0,4},{4,8},{8,12},{12,0},{1,5},{5,9},{9,13},{13,1},{2,6},{6,10},{... | collective-permute-start | bytes 98312 | tf_op jit(solution)/shard_map/ppermute | solution.py:399
  51.8 13.9 %collective-permute-start.12 = (bf16[224,1024]{1,0:T(8,128)(2,1)S(1)}, bf16[224,1024]{1,0:T(8,128)(2,1)S(1)}, u32[]{:S(2)}, u32[]{:S(2)}) collective-permute-start(bf16[224,1024]{1,0:T(8,128)(2,1)S(1)} %get-tuple-element.112), channel_id=1, source_target_pairs={{0,4},{4,0},{8,12},{12,8},{1,5},{5,1},{9,13},{13,9},{2,6},{6,2},{1... | collective-permute-start | bytes 1376264 | tf_op jit(solution)/shard_map/ppermute | solution.py:469
  54.4 19.6 %collective-permute-start.16 = (bf16[224,1024]{1,0:T(8,128)(2,1)S(1)}, bf16[224,1024]{1,0:T(8,128)(2,1)S(1)}, u32[]{:S(2)}, u32[]{:S(2)}) collective-permute-start(bf16[224,1024]{1,0:T(8,128)(2,1)S(1)} %get-tuple-element.123), channel_id=1, source_target_pairs={{4,8},{8,4},{5,9},{9,5},{6,10},{10,6},{7,11},{11,7},{20,24},{24,20... | collective-permute-start | bytes 1376264 | tf_op jit(solution)/shard_map/ppermute | solution.py:474
  55.2 21.1 %collective-permute-start.15 = (bf16[224,1024]{1,0:T(8,128)(2,1)S(1)}, bf16[224,1024]{1,0:T(8,128)(2,1)S(1)}, u32[]{:S(2)}, u32[]{:S(2)}) collective-permute-start(bf16[224,1024]{1,0:T(8,128)(2,1)S(1)} %get-tuple-element.121), channel_id=1, source_target_pairs={{0,4},{4,0},{8,12},{12,8},{1,5},{5,1},{9,13},{13,9},{2,6},{6,2},{1... | collective-permute-start | bytes 1376264 | tf_op jit(solution)/shard_map/ppermute | solution.py:469
  56.6 11.3 %collective-permute-start.9 = (bf16[64,2048]{1,0:T(8,128)(2,1)S(1)}, bf16[64,2048]{1,0:T(8,128)(2,1)S(1)}, u32[]{:S(2)}, u32[]{:S(2)}) collective-permute-start(bf16[64,2048]{1,0:T(8,128)(2,1)S(1)} %get-tuple-element.107), channel_id=1, source_target_pairs={{0,2},{1,3},{2,0},{3,1},{4,6},{5,7},{6,4},{7,5},{8,10},{9,11},{10,... | collective-permute-start | bytes 786440 | tf_op jit(solution)/shard_map/ppermute | solution.py:408
  65.8 11.2 %collective-permute-start.19 = (bf16[224,1024]{1,0:T(8,128)(2,1)S(1)}, bf16[224,1024]{1,0:T(8,128)(2,1)S(1)}, u32[]{:S(2)}, u32[]{:S(2)}) collective-permute-start(bf16[224,1024]{1,0:T(8,128)(2,1)S(1)} %get-tuple-element.130), channel_id=1, source_target_pairs={{4,8},{8,4},{5,9},{9,5},{6,10},{10,6},{7,11},{11,7},{20,24},{24,20... | collective-permute-start | bytes 1376264 | tf_op jit(solution)/shard_map/ppermute | solution.py:474
  74.1 12.9 %collective-permute-start.18 = (bf16[224,1024]{1,0:T(8,128)(2,1)S(1)}, bf16[224,1024]{1,0:T(8,128)(2,1)S(1)}, u32[]{:S(2)}, u32[]{:S(2)}) collective-permute-start(bf16[224,1024]{1,0:T(8,128)(2,1)S(1)} %get-tuple-element.127), channel_id=1, source_target_pairs={{0,4},{4,0},{8,12},{12,8},{1,5},{5,1},{9,13},{13,9},{2,6},{6,2},{1... | collective-permute-start | bytes 1376264 | tf_op jit(solution)/shard_map/ppermute | solution.py:469
  76.4 12.7 %collective-permute-start.17 = (bf16[224,1024]{1,0:T(8,128)(2,1)S(1)}, bf16[224,1024]{1,0:T(8,128)(2,1)S(1)}, u32[]{:S(2)}, u32[]{:S(2)}) collective-permute-start(bf16[224,1024]{1,0:T(8,128)(2,1)S(1)} %get-tuple-element.126), channel_id=1, source_target_pairs={{4,8},{8,4},{5,9},{9,5},{6,10},{10,6},{7,11},{11,7},{20,24},{24,20... | collective-permute-start | bytes 1376264 | tf_op jit(solution)/shard_map/ppermute | solution.py:474
  77.1 19.7 %collective-permute-start.22 = (bf16[224,1024]{1,0:T(8,128)(2,1)S(1)}, bf16[224,1024]{1,0:T(8,128)(2,1)S(1)}, u32[]{:S(2)}, u32[]{:S(2)}) collective-permute-start(bf16[224,1024]{1,0:T(8,128)(2,1)S(1)} %get-tuple-element.139), channel_id=1, source_target_pairs={{0,4},{4,0},{8,12},{12,8},{1,5},{5,1},{9,13},{13,9},{2,6},{6,2},{1... | collective-permute-start | bytes 1376264 | tf_op jit(solution)/shard_map/ppermute | solution.py:469
  87.1 11.6 %collective-permute-start.21 = (bf16[224,1024]{1,0:T(8,128)(2,1)S(1)}, bf16[224,1024]{1,0:T(8,128)(2,1)S(1)}, u32[]{:S(2)}, u32[]{:S(2)}) collective-permute-start(bf16[224,1024]{1,0:T(8,128)(2,1)S(1)} %get-tuple-element.138), channel_id=1, source_target_pairs={{4,8},{8,4},{5,9},{9,5},{6,10},{10,6},{7,11},{11,7},{20,24},{24,20... | collective-permute-start | bytes 1376264 | tf_op jit(solution)/shard_map/ppermute | solution.py:474
  89.1 17.5 %collective-permute-start.20 = (bf16[224,1024]{1,0:T(8,128)(2,1)S(1)}, bf16[224,1024]{1,0:T(8,128)(2,1)S(1)}, u32[]{:S(2)}, u32[]{:S(2)}) collective-permute-start(bf16[224,1024]{1,0:T(8,128)(2,1)S(1)} %get-tuple-element.137), channel_id=1, source_target_pairs={{0,4},{4,0},{8,12},{12,8},{1,5},{5,1},{9,13},{13,9},{2,6},{6,2},{1... | collective-permute-start | bytes 1376264 | tf_op jit(solution)/shard_map/ppermute | solution.py:469
  96.9 11.6 %collective-permute-start.25 = (bf16[224,1024]{1,0:T(8,128)(2,1)S(1)}, bf16[224,1024]{1,0:T(8,128)(2,1)S(1)}, u32[]{:S(2)}, u32[]{:S(2)}) collective-permute-start(bf16[224,1024]{1,0:T(8,128)(2,1)S(1)} %get-tuple-element.151), channel_id=1, source_target_pairs={{4,8},{8,4},{5,9},{9,5},{6,10},{10,6},{7,11},{11,7},{20,24},{24,20... | collective-permute-start | bytes 1376264 | tf_op jit(solution)/shard_map/ppermute | solution.py:474
  98.8 17.7 %collective-permute-start.24 = (bf16[224,1024]{1,0:T(8,128)(2,1)S(1)}, bf16[224,1024]{1,0:T(8,128)(2,1)S(1)}, u32[]{:S(2)}, u32[]{:S(2)}) collective-permute-start(bf16[224,1024]{1,0:T(8,128)(2,1)S(1)} %get-tuple-element.150), channel_id=1, source_target_pairs={{0,4},{4,0},{8,12},{12,8},{1,5},{5,1},{9,13},{13,9},{2,6},{6,2},{1... | collective-permute-start | bytes 1376264 | tf_op jit(solution)/shard_map/ppermute | solution.py:469
  108.6 17.7 %collective-permute-start.27 = (bf16[224,1024]{1,0:T(8,128)(2,1)S(1)}, bf16[224,1024]{1,0:T(8,128)(2,1)S(1)}, u32[]{:S(2)}, u32[]{:S(2)}) collective-permute-start(bf16[224,1024]{1,0:T(8,128)(2,1)S(1)} %get-tuple-element.161), channel_id=1, source_target_pairs={{0,4},{4,0},{8,12},{12,8},{1,5},{5,1},{9,13},{13,9},{2,6},{6,2},{1... | collective-permute-start | bytes 1376264 | tf_op jit(solution)/shard_map/ppermute | solution.py:469
  117.6 17.4 %collective-permute-start.26 = (bf16[224,1024]{1,0:T(8,128)(2,1)S(1)}, bf16[224,1024]{1,0:T(8,128)(2,1)S(1)}, u32[]{:S(2)}, u32[]{:S(2)}) collective-permute-start(bf16[224,1024]{1,0:T(8,128)(2,1)S(1)} %get-tuple-element.160), channel_id=1, source_target_pairs={{0,4},{4,0},{8,12},{12,8},{1,5},{5,1},{9,13},{13,9},{2,6},{6,2},{1... | collective-permute-start | bytes 1376264 | tf_op jit(solution)/shard_map/ppermute | solution.py:469
  (13 other events, 251.7 us)

commit v5 on v4

--- a/solution.py
+++ b/solution.py
@@ -11,13 +11,16 @@
 CAP = 4
 LIVE_ROWS = 224
 TAG = 128
-CHUNK = 1024
-TILE = 512
+LANES = 128
+CUTS = 3
 BF16 = jnp.bfloat16
 F32 = jnp.float32
 MIB = 1024 * 1024
+HOP_WORK = 14000
+FIRST_HOP_WORK = 8000
+BASE_WORK = 400000
 PREPARE_MIB = 60
-DELTA_AT = 2
+DELTA_AT = 1
 
 
 def dot(a, b):
@@ -49,21 +52,32 @@
     return (z == 1) | (z == 2)
 
 
-def chunk_at(q, chunks):
-    return jnp.where(lax.axis_index("tensor") % 2 == 0, chunks - 1 - q, q)
-
-
-def weight_copy(w, q, into, sem):
-    column = pl.multiple_of(chunk_at(q, w.shape[1] // CHUNK) * CHUNK, CHUNK)
-    return pltpu.make_async_copy(w.at[:, pl.ds(column, CHUNK)], into, sem)
-
-
-def prepare_kernel(replicas, line, owner_in, slot_in, live_in, x_in, *refs):
+def widths_of(width, shards):
+    tiles = width // shards // LANES
+    if CUTS == 3:
+        side = tiles // 3
+        cuts = (side, tiles - 2 * side, side)
+    else:
+        cuts = (tiles // CUTS,) * CUTS
+    return tuple(cut * LANES for cut in cuts) * shards
+
+
+def column_at(q, widths):
+    left, right = sum(widths[:q]), sum(widths[: len(widths) - 1 - q])
+    column = jnp.where(lax.axis_index("tensor") % 2 == 0, right, left)
+    return pl.multiple_of(column, LANES)
+
+
+def weight_copy(w, q, widths, into, sem):
+    return pltpu.make_async_copy(w.at[:, pl.ds(column_at(q, widths), widths[q])], into, sem)
+
+
+def prepare_kernel(replicas, widths, owner_in, slot_in, live_in, x_in, *refs):
     refs = list(refs)
+    line = widths is not None
     w = refs.pop(0) if line else None
-    compact_x, pick, place = refs[:3]
-    blocks = refs[3 : 3 + replicas]
-    message = refs[3 + replicas] if line else None
+    compact_x, pick, place, spread_out, tags_out = refs[:5]
+    message = refs[5] if line else None
     owner, slot, live, x, sems = refs[-5:]
     wide, wide_sem = (refs[-7], refs[-6]) if line else (None, None)
     copies = [
@@ -73,7 +87,7 @@
     for copy in copies:
         copy.start()
     if line:
-        weights = weight_copy(w, 0, wide, wide_sem.at[0])
+        weights = weight_copy(w, 0, widths, wide, wide_sem.at[0])
         weights.start()
     for copy in copies:
         copy.wait()
@@ -110,31 +124,27 @@
     place[...] = dot_cols(compact, spread).astype(BF16)
     packed_x = dot(compact, x[...]).astype(BF16)
     compact_x[...] = packed_x
-    sent = dot(spread, x[...]).astype(BF16)
-    sent_tags = dot(spread, tags.astype(BF16)).astype(BF16)
-    for k, block in enumerate(blocks):
-        here = slice(k * block.shape[0], (k + 1) * block.shape[0])
-        block[:, :feat] = sent[here]
-        block[:, feat:] = sent_tags[here]
+    spread_out[...] = spread
+    tags_out[...] = tags.astype(BF16)
     if line:
         weights.wait()
         message[...] = dot(packed_x, wide[...]).astype(BF16)
 
 
-def prepare(owner, slot, live, x, replicas, weight=None):
+def prepare(owner, slot, live, x, replicas, weight=None, widths=None):
     rows, feat = x.shape
     block = CAP * GROUP_ROWS
     line = weight is not None
     shape = lambda *dims: jax.ShapeDtypeStruct(dims, BF16)
     outs = [shape(LIVE_ROWS, feat), shape(rows, LIVE_ROWS), shape(LIVE_ROWS, replicas * block)]
-    outs += [shape(block, feat + TAG)] * replicas
+    outs += [shape(replicas * block, rows), shape(rows, TAG)]
     scratch = [pltpu.SMEM(a.shape, jnp.int32) for a in (owner, slot, live)]
     scratch += [pltpu.VMEM(x.shape, BF16), pltpu.SemaphoreType.DMA((4,))]
     if line:
-        outs.append(shape(LIVE_ROWS, CHUNK))
-        scratch = [pltpu.VMEM((feat, CHUNK), BF16), pltpu.SemaphoreType.DMA((1,))] + scratch
-    return pl.pallas_call(
-        functools.partial(prepare_kernel, replicas, line),
+        outs.append(shape(LIVE_ROWS, widths[0]))
+        scratch = [pltpu.VMEM((feat, widths[0]), BF16), pltpu.SemaphoreType.DMA((1,))] + scratch
+    return pl.pallas_call(
+        functools.partial(prepare_kernel, replicas, widths),
         out_shape=outs,
         in_specs=[ANY] * (5 if line else 4),
         out_specs=[VMEM] * len(outs),
@@ -144,32 +154,59 @@
     )(owner, slot, live, x, *([weight] if line else []))
 
 
-def base_kernel(places, x, w, token_in, *refs):
+def spread_kernel(spread, tags, x, token_in, *blocks):
+    feat = x.shape[1]
+    sent = dot(spread[...], x[...]).astype(BF16)
+    sent_tags = dot(spread[...], tags[...]).astype(BF16)
+    for k, block in enumerate(blocks[:-1]):
+        here = slice(k * block.shape[0], (k + 1) * block.shape[0])
+        block[:, :feat] = sent[here]
+        block[:, feat:] = sent_tags[here]
+
+
+def spread_groups(spread, tags, x, token):
+    rows = CAP * GROUP_ROWS
+    blocks = spread.shape[0] // rows
+    return pl.pallas_call(
+        spread_kernel,
+        out_shape=[jax.ShapeDtypeStruct((rows, x.shape[1] + TAG), BF16)] * blocks
+        + [jax.ShapeDtypeStruct(token.shape, token.dtype)],
+        in_specs=[VMEM] * 3 + [ANY],
+        out_specs=[VMEM] * blocks + [ANY],
+        input_output_aliases={3: blocks},
+        compiler_params=params(),
+        name="spread",
+    )(spread, tags, x, token)
+
+
+def base_kernel(places, widths, x, w, token_in, *refs):
     outs, wide, sems = refs[: len(places)], refs[-2], refs[-1]
     slots = wide.shape[0]
-    copies = [weight_copy(w, q, wide.at[i % slots], sems.at[i % slots]) for i, q in enumerate(places)]
+    copies = [
+        weight_copy(w, q, widths, wide.at[i % slots, :, : widths[q]], sems.at[i % slots]) for i, q in enumerate(places)
+    ]
     for copy in copies[: slots - 1]:
         copy.start()
-    for i, copy in enumerate(copies):
+    for i, (q, copy) in enumerate(zip(places, copies)):
         if i + slots - 1 < len(copies):
             copies[i + slots - 1].start()
         copy.wait()
-        outs[i][...] = dot(x[...], wide[i % slots]).astype(BF16)
-
-
-def base_chunks(places, x, weight, token):
+        outs[i][...] = dot(x[...], wide[i % slots, :, : widths[q]]).astype(BF16)
+
+
+def base_chunks(places, widths, x, weight, token):
     feat, _ = weight.shape
-    elements = (feat + LIVE_ROWS) * CHUNK * len(places)
-    return pl.pallas_call(
-        functools.partial(base_kernel, places),
-        out_shape=[jax.ShapeDtypeStruct((LIVE_ROWS, CHUNK), BF16)] * len(places)
+    columns = sum(widths[q] for q in places)
+    return pl.pallas_call(
+        functools.partial(base_kernel, places, widths),
+        out_shape=[jax.ShapeDtypeStruct((LIVE_ROWS, widths[q]), BF16) for q in places]
         + [jax.ShapeDtypeStruct(token.shape, token.dtype)],
         in_specs=[VMEM, ANY, ANY],
         out_specs=[VMEM] * len(places) + [ANY],
         input_output_aliases={2: len(places)},
-        scratch_shapes=[pltpu.VMEM((3, feat, CHUNK), BF16), pltpu.SemaphoreType.DMA((3,))],
-        compiler_params=params(),
-        cost_estimate=cost(2 * feat * LIVE_ROWS * CHUNK * len(places), elements),
+        scratch_shapes=[pltpu.VMEM((3, feat, max(widths)), BF16), pltpu.SemaphoreType.DMA((3,))],
+        compiler_params=params(),
+        cost_estimate=cost(BASE_WORK * columns, columns),
         name="base",
     )(x, weight, token)
 
@@ -188,18 +225,18 @@
         out[...] = far[...]
 
 
-def hop(kernel, inputs, token):
+def hop(kernel, inputs, token, work=HOP_WORK):
     return pl.pallas_call(
         kernel,
         out_shape=(
-            jax.ShapeDtypeStruct((LIVE_ROWS, CHUNK), BF16),
+            jax.ShapeDtypeStruct(inputs[0].shape, BF16),
             jax.ShapeDtypeStruct(token.shape, token.dtype),
         ),
         in_specs=[VMEM] * len(inputs) + [ANY],
         out_specs=(VMEM, ANY),
         input_output_aliases={len(inputs): 1},
         compiler_params=params(),
-        cost_estimate=cost(2 * LIVE_ROWS * CHUNK, 3 * LIVE_ROWS * CHUNK),
+        cost_estimate=cost(work * inputs[0].size, 3 * inputs[0].size),
         name="hop",
     )(*inputs, token)
 
@@ -288,30 +325,29 @@
     )(up, *parts, *lows, token)
 
 
-def add_delta_kernel(per, chunks, place, *refs):
+def add_delta_kernel(per, place, *refs):
     bases, refs = refs[: 2 * per], refs[2 * per :]
     outs, parts = refs[-2 * per - 1 : -1], refs[: -2 * per - 2]
     rows = parts[0].shape[0]
     inner = is_inner()
-    z = lax.axis_index("tensor")
+    widths = tuple(base.shape[1] for base in bases[:per])
     for j in range(per):
-        chunk = chunk_at(jnp.where(inner, per, 3 * per) + j, chunks)
-        column = pl.multiple_of((chunk - z * per) * CHUNK, CHUNK)
+        column = column_at(j, widths)
         total = None
         for k, part in enumerate(parts):
-            got = dot(place[:, k * rows : (k + 1) * rows], part[:, pl.ds(column, CHUNK)])
+            got = dot(place[:, k * rows : (k + 1) * rows], part[:, pl.ds(column, widths[j])])
             total = got if total is None else total + got
         for i, mine in ((j, inner), (per + j, jnp.logical_not(inner))):
             wide = bases[i][...].astype(F32)
             outs[i][...] = (wide + jnp.where(mine, total, 0.0)).astype(BF16)
 
 
-def add_delta(bases, place, parts, chunks, token):
+def add_delta(bases, place, parts, token):
     per = len(bases) // 2
     inputs = [place, *bases, *parts]
     return pl.pallas_call(
-        functools.partial(add_delta_kernel, per, chunks),
-        out_shape=[jax.ShapeDtypeStruct(bases[0].shape, BF16)] * len(bases)
+        functools.partial(add_delta_kernel, per),
+        out_shape=[jax.ShapeDtypeStruct(base.shape, BF16) for base in bases]
         + [jax.ShapeDtypeStruct(token.shape, token.dtype)],
         in_specs=[VMEM] * len(inputs) + [ANY],
         out_specs=[VMEM] * len(bases) + [ANY],
@@ -321,23 +357,23 @@
     )(*inputs, token)
 
 
-def finish_kernel(chunks, near_q, far_q, *refs):
+def finish_kernel(widths, near_q, far_q, *refs):
     refs = list(refs)
     near = refs.pop(0) if near_q is not None else None
     far = refs.pop(0) if far_q is not None else None
     even, odd = refs.pop(0), refs.pop(0) if near_q is not None else None
     pick = refs.pop(0)
     out, _, made, sems = refs[-4:]
-    tiles = CHUNK // TILE
 
     def write(q, terms):
-        column = chunk_at(q, chunks) * CHUNK
+        column, width = column_at(q, widths), widths[q]
+        cut = width // LANES // 2 * LANES
         copies = []
-        for i in range(tiles):
-            total = sum(term[:, i * TILE : (i + 1) * TILE].astype(F32) for term in terms)
-            made[i] = dot(pick[...], total.astype(BF16)).astype(BF16)
-            here = pl.ds(pl.multiple_of(column + i * TILE, TILE), TILE)
-            copies.append(pltpu.make_async_copy(made.at[i], out.at[:, here], sems.at[i]))
+        for i, here in enumerate((slice(0, cut), slice(cut, width))):
+            total = sum(term[:, here].astype(F32) for term in terms)
+            made[:, here] = dot(pick[...], total.astype(BF16)).astype(BF16)
+            there = pl.ds(pl.multiple_of(column + here.start, LANES), here.stop - here.start)
+            copies.append(pltpu.make_async_copy(made.at[:, here], out.at[:, there], sems.at[i]))
             copies[-1].start()
         for copy in copies:
             copy.wait()
@@ -355,8 +391,8 @@
             write(far_q, [far, even])
 
 
-def finish(near_q, far_q, bases, even, odd, pick, held, token):
-    rows, chunks = pick.shape[0], len(bases)
+def finish(near_q, far_q, widths, bases, even, odd, pick, held, token):
+    rows, width = pick.shape[0], even.shape[1]
     inputs = [bases[q] for q in (near_q, far_q) if q is not None] + [even]
     inputs += [odd] if near_q is not None else []
     inputs += [pick]
@@ -365,17 +401,17 @@
     if held is not None:
         aliases[len(inputs)] = 0
     return pl.pallas_call(
-        functools.partial(finish_kernel, chunks, near_q, far_q),
+        functools.partial(finish_kernel, widths, near_q, far_q),
         out_shape=(
-            jax.ShapeDtypeStruct((rows, chunks * CHUNK), BF16),
+            jax.ShapeDtypeStruct((rows, sum(widths)), BF16),
             jax.ShapeDtypeStruct(token.shape, token.dtype),
         ),
         in_specs=[VMEM] * len(inputs) + [ANY] * len(last),
         out_specs=(ANY, ANY),
-        scratch_shapes=[pltpu.VMEM((CHUNK // TILE, rows, TILE), BF16), pltpu.SemaphoreType.DMA((CHUNK // TILE,))],
+        scratch_shapes=[pltpu.VMEM((rows, width), BF16), pltpu.SemaphoreType.DMA((2,))],
         input_output_aliases=aliases,
         compiler_params=params(),
-        cost_estimate=cost(2 * LIVE_ROWS * rows * CHUNK, 6 * LIVE_ROWS * CHUNK),
+        cost_estimate=cost(2 * LIVE_ROWS * rows * width, 6 * LIVE_ROWS * width),
         name="finish",
     )(*inputs, *last)
 
@@ -413,12 +449,12 @@
     width = weight.shape[1]
     rank = down.shape[1]
     replicas, shards = lax.axis_size("replica"), lax.axis_size("tensor")
-    share = width // shards
     down, up = down.reshape(-1, down.shape[2]), up.reshape(-1, up.shape[2])
     token = jnp.zeros((8, 128), jnp.int32)
     if shards != 4:
-        compact_x, pick, place, *blocks = prepare(owner[:, 0], slot, live[0], x, replicas)
-        z = lax.axis_index("tensor").astype(jnp.int32)
+        compact_x, pick, place, spread, tags = prepare(owner[:, 0], slot, live[0], x, replicas)
+        *blocks, token = spread_groups(spread, tags, x, token)
+        z, share = lax.axis_index("tensor").astype(jnp.int32), width // shards
         base = dot(compact_x, weight)
         parts = send_groups(blocks)
         low, token = low_values(parts, down, rank, token)
@@ -430,18 +466,20 @@
         total = lax.all_gather(total, "tensor", axis=1, tiled=True)
         return dot(pick, total).astype(BF16)
 
-    chunks, per = width // CHUNK, share // CHUNK
+    widths = widths_of(width, shards)
+    chunks, per = len(widths), len(widths) // shards
     even = [(0, 1), (1, 0), (2, 3), (3, 2)]
     odd = [(1, 2), (2, 1)]
-    compact_x, pick, place, *rest = prepare(owner[:, 0], slot, live[0], x, replicas, weight)
-    blocks, message = rest[:-1], rest[-1]
+    opened = prepare(owner[:, 0], slot, live[0], x, replicas, weight, widths)
+    compact_x, pick, place, spread, tags, message = opened
     evens, odds = {0: lax.ppermute(message, "tensor", even)}, {}
+    *blocks, token = spread_groups(spread, tags, x, token)
     parts = send_groups(blocks)
-    *early, token = base_chunks((1, 2), compact_x, weight, token)
+    *early, token = base_chunks((1, 2), widths, compact_x, weight, token)
     bases = [message, *early]
     for step in (1, 2):
         evens[step] = lax.ppermute(bases[step], "tensor", even)
-    *late, token = base_chunks(tuple(range(3, chunks)), compact_x, weight, token)
+    *late, token = base_chunks(tuple(range(3, chunks)), widths, compact_x, weight, token)
     bases += late
     low, token = low_values(parts, down, rank, token)
     lows = send_lows(low)
@@ -458,19 +496,20 @@
             unfinished.remove(a)
             near_q = chunks - 1 - a if a < chunks else None
             far_q = chunks + 2 - a if a >= 3 else None
-            result, token = finish(near_q, far_q, bases, evens[a], odds.get(b), pick, result, token)
+            result, token = finish(near_q, far_q, widths, bases, evens[a], odds.get(b), pick, result, token)
         return result, token
 
     for step in range(1, steps):
         if step >= 3:
-            far = bases[min(step, chunks - 1)]
+            far = bases[step] if step < chunks else bases[step - 3]
             inputs = [bases[step - 3], far, odds[step - 2]]
             message, token = hop(even_hop_kernel, inputs, token)
             evens[step] = lax.ppermute(message, "tensor", even)
             seen_odd.add(step - 2)
             result, token = close(result, token)
         if step <= chunks:
-            message, token = hop(odd_hop_kernel, [bases[chunks - step], evens[step - 1]], token)
+            work = FIRST_HOP_WORK if step == 1 else HOP_WORK
+            message, token = hop(odd_hop_kernel, [bases[chunks - step], evens[step - 1]], token, work)
             odds[step] = lax.ppermute(message, "tensor", odd)
         seen_even.add(step - 1)
         if step == DELTA_AT:
@@ -478,7 +517,7 @@
             back = send_back(made)
         if step == per + 2:
             own = list(range(per, 2 * per)) + list(range(3 * per, 4 * per))
-            *summed, token = add_delta([bases[q] for q in own], place, back, chunks, token)
+            *summed, token = add_delta([bases[q] for q in own], place, back, token)
             for q, value in zip(own, summed):
                 bases[q] = value
         result, token = close(result, token)

time: 137 us -> 140 us (1.022)
  waiting for transfers between devices: 39.8 us -> 21.8 us
  starting transfers between devices: 66.8 us -> 80.5 us
  Pallas kernels: 28 us -> 33.4 us
  local copies, waits for them, and re-layouts: 1.06 us -> 2.97 us
    ppermute x8 -> x12, starting transfers between devices: 32 us -> 50.9 us  [on_device(): evens[step] = lax.ppermute(message, 'tensor', even)]
    ppermute x3, starting transfers between devices: 16.9 us -> 6.35 us  [send_lows(): lows.append(lax.ppermute(low, 'tensor', hops))]
    ppermute x8 -> x12, waiting for transfers between devices: 29.1 us -> 21.5 us  [on_device(): evens[step] = lax.ppermute(message, 'tensor', even)]
    pallas_call x31 -> x44, Pallas kernels: 24.2 us -> 29.6 us  [the longest x15 12 us: finish(): pl.pallas_call(functools.partial(finish_kernel, widths, near_q, far_q), o...]
    ppermute x3, waiting for transfers between devices: 4.96 us -> 0.01 us  [send_back(): back.append(lax.ppermute(made[k], 'replica', hops))]
    ppermute x3, waiting for transfers between devices: 4.12 us -> 0.01 us  [send_lows(): lows.append(lax.ppermute(low, 'tensor', hops))]
    ppermute x8 -> x12, starting transfers between devices: 5.52 us -> 8.61 us  [on_device(): odds[step] = lax.ppermute(message, 'tensor', odd)]
    ppermute x2, starting transfers between devices: 4.95 us -> 6.99 us  [on_device(): evens[step] = lax.ppermute(bases[step], 'tensor', even)]
  transfers between devices with their start and end apart: 28 -> 36, of which waited for: 12 -> 7; matrix products, arithmetic and copies ran while one was open for 0% -> 0% of each run, Pallas kernels for 17% -> 21%
where the time goes in v5:
time: 140 us; the launch traced here: 139 us
  starting transfers between devices  80.5 us (58%)
  Pallas kernels  33.4 us (24%)
  waiting for transfers between devices  21.8 us (16%)
  local copies, waits for them, and re-layouts  2.97 us (2%)
    ppermute x12, starting transfers between devices, on_device(): evens[step] = lax.ppermute(message, 'tensor', even)  50.9 us
    ppermute x12, waiting for transfers between devices, on_device(): evens[step] = lax.ppermute(message, 'tensor', even)  21.5 us
    pallas_call x15, Pallas kernels, finish(): pl.pallas_call(functools.partial(finish_kernel, widths, near_q, far_q), o...  12 us
    pallas_call x2, Pallas kernels, base_chunks(): pl.pallas_call(functools.partial(base_kernel, places, widths), out_shape=...  9.9 us
    ppermute x12, starting transfers between devices, on_device(): odds[step] = lax.ppermute(message, 'tensor', odd)  8.61 us
    ppermute x2, starting transfers between devices, on_device(): evens[step] = lax.ppermute(bases[step], 'tensor', even)  6.99 us
    ppermute x3, starting transfers between devices, send_lows(): lows.append(lax.ppermute(low, 'tensor', hops))  6.35 us
    ppermute x1, starting transfers between devices, on_device(): evens, odds = ({0: lax.ppermute(message, 'tensor', even)}, {})  3.09 us
  transfers between devices with their start and end apart: 36, of which 7 were waited for; matrix products, arithmetic and copies ran while one was open for 0% of the time, Pallas kernels for 21%

profile of v5, /device:TPU:0, one launch (start us, length us, event | category | flops | bytes accessed | tf_op | source)
XLA Modules:
  0.0 139.5 jit_solution(3439367709664313880)
XLA Ops:
  0.0 2.9 %prepare.1 = (bf16[224,1024]{1,0:T(8,128)(2,1)}, bf16[256,224]{1,0:T(8,128)(2,1)}, bf16[224,256]{1,0:T(8,128)(2,1)}, bf16[256,256]{1,0:T(8,128)(2,1)}, bf16[256,...) custom-call(s32[16]{0:T(128)} %bitcast.6, s32[16]{0:T(128)} %slot_in.1, s32[16]{0:T(128)} %bitcast.7, bf16[256,1024]{1,0:T(8,128)(2,1)} %x.1, ...), custom_call_target="tpu_custom_call" | custom-call | tf_op jit(solution)/shard_map/prepare/pallas_call | solution.py:146
  2.9 3.1 %collective-permute-start.6 = (bf16[224,640]{1,0:T(8,128)(2,1)}, bf16[224,640]{1,0:T(8,128)(2,1)S(1)}, u32[]{:S(2)}, u32[]{:S(2)}) collective-permute-start(bf16[224,640]{1,0:T(8,128)(2,1)} %get-tuple-element.120.near.base.refs_0_), channel_id=1, source_target_pairs={{0,4},{4,0},{8,12},{12,8},{1,5},{5,1},{9,13},{13,9},{2,6},{6,2},{1... | collective-permute-start | bytes 860168 | tf_op jit(solution)/shard_map/ppermute | solution.py:475
  12.1 2.7 %base.2 = (bf16[224,768]{1,0:T(8,128)(2,1)S(1)}, bf16[224,640]{1,0:T(8,128)(2,1)S(1)}, s32[8,128]{1,0:T(8,128)S(1)}) custom-call(bf16[224,1024]{1,0:T(8,128)(2,1)S(1)} %copy-done.3, bf16[1024,8192]{1,0:T(8,128)(2,1)} %w.3, s32[8,128]{1,0:T(8,128)S(1)} %get-tuple-element.125.token_in), custom_call_target="tpu_custom_call", output_to_operand_aliasing={{2}: (2, {})} | custom-call | flops 563200000 | bytes 2816 | tf_op jit(solution)/shard_map/base/pallas_call | solution.py:200
  15.4 7.2 %base.3 = (bf16[224,640]{1,0:T(8,128)(2,1)S(1)}, bf16[224,768]{1,0:T(8,128)(2,1)S(1)}, bf16[224,640]{1,0:T(8,128)(2,1)S(1)}, bf16[224,640]{1,0:T(8,128)(2,1)S(1)...) custom-call(bf16[224,1024]{1,0:T(8,128)(2,1)S(1)} %copy-done.3, ...), custom_call_target="tpu_custom_call", output_to_operand_aliasing={{9}: (2, {})} | custom-call | flops 2457600000 | bytes 12288 | tf_op jit(solution)/shard_map/base/pallas_call | solution.py:200
  25.1 3.7 %collective-permute-start.5 = (bf16[128,128]{1,0:T(8,128)(2,1)S(1)}, bf16[128,128]{1,0:T(8,128)(2,1)S(1)}, u32[]{:S(2)}, u32[]{:S(2)}) collective-permute-start(bf16[128,128]{1,0:T(8,128)(2,1)S(1)} %get-tuple-element.138.refs_4_), channel_id=1, source_target_pairs={{0,12},{4,0},{8,4},{12,8},{1,13},{5,1},{9,5},{13,9},{2,14},{6,2},{... | collective-permute-start | bytes 98312 | tf_op jit(solution)/shard_map/ppermute | solution.py:435
  28.8 2.2 %collective-permute-start.4 = (bf16[128,128]{1,0:T(8,128)(2,1)S(1)}, bf16[128,128]{1,0:T(8,128)(2,1)S(1)}, u32[]{:S(2)}, u32[]{:S(2)}) collective-permute-start(bf16[128,128]{1,0:T(8,128)(2,1)S(1)} %get-tuple-element.138.refs_4_), channel_id=1, source_target_pairs={{0,8},{4,12},{8,0},{12,4},{1,9},{5,13},{9,1},{13,5},{2,10},{6,14},... | collective-permute-start | bytes 98312 | tf_op jit(solution)/shard_map/ppermute | solution.py:435
  31.5 6.5 %collective-permute-start.12 = (bf16[224,640]{1,0:T(8,128)(2,1)S(1)}, bf16[224,640]{1,0:T(8,128)(2,1)S(1)}, u32[]{:S(2)}, u32[]{:S(2)}) collective-permute-start(bf16[224,640]{1,0:T(8,128)(2,1)S(1)} %get-tuple-element.149.near.base.refs_0_), channel_id=1, source_target_pairs={{0,4},{4,0},{8,12},{12,8},{1,5},{5,1},{9,13},{13,9},{2,6},{6,2},{1... | collective-permute-start | bytes 860168 | tf_op jit(solution)/shard_map/ppermute | solution.py:481
  37.9 2.1 %delta.1 = (bf16[64,2048]{1,0:T(8,128)(2,1)S(1)}, bf16[64,2048]{1,0:T(8,128)(2,1)S(1)}, bf16[64,2048]{1,0:T(8,128)(2,1)S(1)}, bf16[64,2048]{1,0:T(8,128)(2,1)S(1)}, s32[8,128]{1,0:T(8,128)S(1)}) custom-call(bf16[512,2048]{1,0:T(8,128)(2,1)S(1)} %bitcast.4, bf16[64,1152]{1,0:T(8,128)(2,1)S(1)} %get-tuple-element.133.refs_0_, ...), custom_call_target="tpu_custom_call", output_to_operand_aliasing={{4}: (9, {})} | custom-call | tf_op jit(solution)/shard_map/delta/pallas_call | solution.py:315
  42.8 2.9 %collective-permute-start.16 = (bf16[224,640]{1,0:T(8,128)(2,1)S(1)}, bf16[224,640]{1,0:T(8,128)(2,1)S(1)}, u32[]{:S(2)}, u32[]{:S(2)}) collective-permute-start(bf16[224,640]{1,0:T(8,128)(2,1)S(1)} %get-tuple-element.157), channel_id=1, source_target_pairs={{0,4},{4,0},{8,12},{12,8},{1,5},{5,1},{9,13},{13,9},{2,6},{6,2},{1... | collective-permute-start | bytes 860168 | tf_op jit(solution)/shard_map/ppermute | solution.py:507
  46.6 6.6 %collective-permute-done.16.got.refs_2_ = bf16[224,640]{1,0:T(8,128)(2,1)S(1)} collective-permute-done((bf16[224,640]{1,0:T(8,128)(2,1)S(1)}, bf16[224,640]{1,0:T(8,128)(2,1)S(1)}, u32[]{:S(2)}, u32[]{:S(2)}) %collective-permute-start.16) | collective-permute-done | bytes 286752 | tf_op jit(solution)/shard_map/ppermute | solution.py:507
  53.1 5.1 %collective-permute-start.14 = (bf16[224,768]{1,0:T(8,128)(2,1)S(1)}, bf16[224,768]{1,0:T(8,128)(2,1)S(1)}, u32[]{:S(2)}, u32[]{:S(2)}) collective-permute-start(bf16[224,768]{1,0:T(8,128)(2,1)S(1)} %get-tuple-element.154), channel_id=1, source_target_pairs={{0,4},{4,0},{8,12},{12,8},{1,5},{5,1},{9,13},{13,9},{2,6},{6,2},{1... | collective-permute-start | bytes 1032200 | tf_op jit(solution)/shard_map/ppermute | solution.py:507
  59.1 7.0 %collective-permute-done.14.got.refs_2_ = bf16[224,768]{1,0:T(8,128)(2,1)S(1)} collective-permute-done((bf16[224,768]{1,0:T(8,128)(2,1)S(1)}, bf16[224,768]{1,0:T(8,128)(2,1)S(1)}, u32[]{:S(2)}, u32[]{:S(2)}) %collective-permute-start.14) | collective-permute-done | bytes 344096 | tf_op jit(solution)/shard_map/ppermute | solution.py:507
  66.1 2.7 %collective-permute-start.17 = (bf16[224,640]{1,0:T(8,128)(2,1)S(1)}, bf16[224,640]{1,0:T(8,128)(2,1)S(1)}, u32[]{:S(2)}, u32[]{:S(2)}) collective-permute-start(bf16[224,640]{1,0:T(8,128)(2,1)S(1)} %get-tuple-element.166), channel_id=1, source_target_pairs={{0,4},{4,0},{8,12},{12,8},{1,5},{5,1},{9,13},{13,9},{2,6},{6,2},{1... | collective-permute-start | bytes 860168 | tf_op jit(solution)/shard_map/ppermute | solution.py:507
  69.7 3.1 %add_delta.1 = (bf16[224,640]{1,0:T(8,128)(2,1)S(1)}, bf16[224,768]{1,0:T(8,128)(2,1)S(1)}, bf16[224,640]{1,0:T(8,128)(2,1)S(1)}, bf16[224,640]{1,0:T(8,128)(2,1...) custom-call(bf16[224,256]{1,0:T(8,128)(2,1)S(1)} %copy-done.10, ...), custom_call_target="tpu_custom_call", output_to_operand_aliasing={{6}: (11, {})} | custom-call | tf_op jit(solution)/shard_map/add_delta/pallas_call | solution.py:348
  72.8 4.1 %collective-permute-start.20 = (bf16[224,640]{1,0:T(8,128)(2,1)S(1)}, bf16[224,640]{1,0:T(8,128)(2,1)S(1)}, u32[]{:S(2)}, u32[]{:S(2)}) collective-permute-start(bf16[224,640]{1,0:T(8,128)(2,1)S(1)} %get-tuple-element.171), channel_id=1, source_target_pairs={{0,4},{4,0},{8,12},{12,8},{1,5},{5,1},{9,13},{13,9},{2,6},{6,2},{1... | collective-permute-start | bytes 860168 | tf_op jit(solution)/shard_map/ppermute | solution.py:507
  77.7 6.5 %collective-permute-start.24 = (bf16[224,768]{1,0:T(8,128)(2,1)S(1)}, bf16[224,768]{1,0:T(8,128)(2,1)S(1)}, u32[]{:S(2)}, u32[]{:S(2)}) collective-permute-start(bf16[224,768]{1,0:T(8,128)(2,1)S(1)} %get-tuple-element.181), channel_id=1, source_target_pairs={{0,4},{4,0},{8,12},{12,8},{1,5},{5,1},{9,13},{13,9},{2,6},{6,2},{1... | collective-permute-start | bytes 1032200 | tf_op jit(solution)/shard_map/ppermute | solution.py:507
  85.2 5.1 %collective-permute-start.22 = (bf16[224,640]{1,0:T(8,128)(2,1)S(1)}, bf16[224,640]{1,0:T(8,128)(2,1)S(1)}, u32[]{:S(2)}, u32[]{:S(2)}) collective-permute-start(bf16[224,640]{1,0:T(8,128)(2,1)S(1)} %get-tuple-element.177), channel_id=1, source_target_pairs={{0,4},{4,0},{8,12},{12,8},{1,5},{5,1},{9,13},{13,9},{2,6},{6,2},{1... | collective-permute-start | bytes 860168 | tf_op jit(solution)/shard_map/ppermute | solution.py:507
  93.3 5.6 %collective-permute-start.26 = (bf16[224,640]{1,0:T(8,128)(2,1)S(1)}, bf16[224,640]{1,0:T(8,128)(2,1)S(1)}, u32[]{:S(2)}, u32[]{:S(2)}) collective-permute-start(bf16[224,640]{1,0:T(8,128)(2,1)S(1)} %get-tuple-element.191), channel_id=1, source_target_pairs={{0,4},{4,0},{8,12},{12,8},{1,5},{5,1},{9,13},{13,9},{2,6},{6,2},{1... | collective-permute-start | bytes 860168 | tf_op jit(solution)/shard_map/ppermute | solution.py:507
  101.8 4.1 %collective-permute-start.30 = (bf16[224,768]{1,0:T(8,128)(2,1)S(1)}, bf16[224,768]{1,0:T(8,128)(2,1)S(1)}, u32[]{:S(2)}, u32[]{:S(2)}) collective-permute-start(bf16[224,768]{1,0:T(8,128)(2,1)S(1)} %get-tuple-element.205), channel_id=1, source_target_pairs={{0,4},{4,0},{8,12},{12,8},{1,5},{5,1},{9,13},{13,9},{2,6},{6,2},{1... | collective-permute-start | bytes 1032200 | tf_op jit(solution)/shard_map/ppermute | solution.py:507
  108.8 3.9 %collective-permute-start.28 = (bf16[224,640]{1,0:T(8,128)(2,1)S(1)}, bf16[224,640]{1,0:T(8,128)(2,1)S(1)}, u32[]{:S(2)}, u32[]{:S(2)}) collective-permute-start(bf16[224,640]{1,0:T(8,128)(2,1)S(1)} %get-tuple-element.203), channel_id=1, source_target_pairs={{0,4},{4,0},{8,12},{12,8},{1,5},{5,1},{9,13},{13,9},{2,6},{6,2},{1... | collective-permute-start | bytes 860168 | tf_op jit(solution)/shard_map/ppermute | solution.py:507
  116.4 4.3 %collective-permute-start.32 = (bf16[224,640]{1,0:T(8,128)(2,1)S(1)}, bf16[224,640]{1,0:T(8,128)(2,1)S(1)}, u32[]{:S(2)}, u32[]{:S(2)}) collective-permute-start(bf16[224,640]{1,0:T(8,128)(2,1)S(1)} %get-tuple-element.216), channel_id=1, source_target_pairs={{0,4},{4,0},{8,12},{12,8},{1,5},{5,1},{9,13},{13,9},{2,6},{6,2},{1... | collective-permute-start | bytes 860168 | tf_op jit(solution)/shard_map/ppermute | solution.py:507
  122.5 5.0 %collective-permute-start.35 = (bf16[224,768]{1,0:T(8,128)(2,1)S(1)}, bf16[224,768]{1,0:T(8,128)(2,1)S(1)}, u32[]{:S(2)}, u32[]{:S(2)}) collective-permute-start(bf16[224,768]{1,0:T(8,128)(2,1)S(1)} %get-tuple-element.227), channel_id=1, source_target_pairs={{0,4},{4,0},{8,12},{12,8},{1,5},{5,1},{9,13},{13,9},{2,6},{6,2},{1... | collective-permute-start | bytes 1032200 | tf_op jit(solution)/shard_map/ppermute | solution.py:507
  130.9 4.4 %collective-permute-done.35.refs_1_ = bf16[224,768]{1,0:T(8,128)(2,1)S(1)} collective-permute-done((bf16[224,768]{1,0:T(8,128)(2,1)S(1)}, bf16[224,768]{1,0:T(8,128)(2,1)S(1)}, u32[]{:S(2)}, u32[]{:S(2)}) %collective-permute-start.35) | collective-permute-done | bytes 344096 | tf_op jit(solution)/shard_map/ppermute | solution.py:507
  136.3 2.0 %collective-permute-done.34.refs_1_ = bf16[224,640]{1,0:T(8,128)(2,1)S(1)} collective-permute-done((bf16[224,640]{1,0:T(8,128)(2,1)S(1)}, bf16[224,640]{1,0:T(8,128)(2,1)S(1)}, u32[]{:S(2)}, u32[]{:S(2)}) %collective-permute-start.34) | collective-permute-done | bytes 286752 | tf_op jit(solution)/shard_map/ppermute | solution.py:507
  (119 shorter events, 35.8 us)
Async XLA Ops:
  2.9 21.4 %collective-permute-start.6 = (bf16[224,640]{1,0:T(8,128)(2,1)}, bf16[224,640]{1,0:T(8,128)(2,1)S(1)}, u32[]{:S(2)}, u32[]{:S(2)}) collective-permute-start(bf16[224,640]{1,0:T(8,128)(2,1)} %get-tuple-element.120.near.base.refs_0_), channel_id=1, source_target_pairs={{0,4},{4,0},{8,12},{12,8},{1,5},{5,1},{9,13},{13,9},{2,6},{6,2},{1... | collective-permute-start | bytes 860168 | tf_op jit(solution)/shard_map/ppermute | solution.py:475
  8.1 14.5 %collective-permute-start = (bf16[64,1152]{1,0:T(8,128)(2,1)S(1)}, bf16[64,1152]{1,0:T(8,128)(2,1)S(1)}, u32[]{:S(2)}, u32[]{:S(2)}) collective-permute-start(bf16[64,1152]{1,0:T(8,128)(2,1)S(1)} %get-tuple-element.134), channel_id=1, source_target_pairs={{0,1},{1,2},{2,3},{3,0},{4,5},{5,6},{6,7},{7,4},{8,9},{9,10},{10,1... | collective-permute-start | bytes 442376 | tf_op jit(solution)/shard_map/ppermute | solution.py:424
  8.2 14.4 %collective-permute-start.1 = (bf16[64,1152]{1,0:T(8,128)(2,1)S(1)}, bf16[64,1152]{1,0:T(8,128)(2,1)S(1)}, u32[]{:S(2)}, u32[]{:S(2)}) collective-permute-start(bf16[64,1152]{1,0:T(8,128)(2,1)S(1)} %get-tuple-element.135), channel_id=1, source_target_pairs={{0,2},{1,3},{2,0},{3,1},{4,6},{5,7},{6,4},{7,5},{8,10},{9,11},{10,... | collective-permute-start | bytes 442376 | tf_op jit(solution)/shard_map/ppermute | solution.py:424
  9.7 12.9 %collective-permute-start.2 = (bf16[64,1152]{1,0:T(8,128)(2,1)S(1)}, bf16[64,1152]{1,0:T(8,128)(2,1)S(1)}, u32[]{:S(2)}, u32[]{:S(2)}) collective-permute-start(bf16[64,1152]{1,0:T(8,128)(2,1)S(1)} %get-tuple-element.136), channel_id=1, source_target_pairs={{0,3},{1,0},{2,1},{3,2},{4,7},{5,4},{6,5},{7,6},{8,11},{9,8},{10,9... | collective-permute-start | bytes 442376 | tf_op jit(solution)/shard_map/ppermute | solution.py:424
  14.9 26.6 %collective-permute-start.10 = (bf16[224,768]{1,0:T(8,128)(2,1)S(1)}, bf16[224,768]{1,0:T(8,128)(2,1)S(1)}, u32[]{:S(2)}, u32[]{:S(2)}) collective-permute-start(bf16[224,768]{1,0:T(8,128)(2,1)S(1)} %get-tuple-element.146.near.base.refs_0_), channel_id=1, source_target_pairs={{0,4},{4,0},{8,12},{12,8},{1,5},{5,1},{9,13},{13,9},{2,6},{6,2},{1... | collective-permute-start | bytes 1032200 | tf_op jit(solution)/shard_map/ppermute | solution.py:481
  24.4 17.3 %collective-permute-start.13 = (bf16[224,640]{1,0:T(8,128)(2,1)S(1)}, bf16[224,640]{1,0:T(8,128)(2,1)S(1)}, u32[]{:S(2)}, u32[]{:S(2)}) collective-permute-start(bf16[224,640]{1,0:T(8,128)(2,1)S(1)} %get-tuple-element.150), channel_id=1, source_target_pairs={{4,8},{8,4},{5,9},{9,5},{6,10},{10,6},{7,11},{11,7},{20,24},{24,20... | collective-permute-start | bytes 860168 | tf_op jit(solution)/shard_map/ppermute | solution.py:513
  31.5 11.4 %collective-permute-start.12 = (bf16[224,640]{1,0:T(8,128)(2,1)S(1)}, bf16[224,640]{1,0:T(8,128)(2,1)S(1)}, u32[]{:S(2)}, u32[]{:S(2)}) collective-permute-start(bf16[224,640]{1,0:T(8,128)(2,1)S(1)} %get-tuple-element.149.near.base.refs_0_), channel_id=1, source_target_pairs={{0,4},{4,0},{8,12},{12,8},{1,5},{5,1},{9,13},{13,9},{2,6},{6,2},{1... | collective-permute-start | bytes 860168 | tf_op jit(solution)/shard_map/ppermute | solution.py:481
  40.0 28.8 %collective-permute-start.7 = (bf16[64,2048]{1,0:T(8,128)(2,1)S(1)}, bf16[64,2048]{1,0:T(8,128)(2,1)S(1)}, u32[]{:S(2)}, u32[]{:S(2)}) collective-permute-start(bf16[64,2048]{1,0:T(8,128)(2,1)S(1)} %get-tuple-element.142), channel_id=1, source_target_pairs={{0,3},{1,0},{2,1},{3,2},{4,7},{5,4},{6,5},{7,6},{8,11},{9,8},{10,9... | collective-permute-start | bytes 786440 | tf_op jit(solution)/shard_map/ppermute | solution.py:444
  40.1 29.6 %collective-permute-start.8 = (bf16[64,2048]{1,0:T(8,128)(2,1)S(1)}, bf16[64,2048]{1,0:T(8,128)(2,1)S(1)}, u32[]{:S(2)}, u32[]{:S(2)}) collective-permute-start(bf16[64,2048]{1,0:T(8,128)(2,1)S(1)} %get-tuple-element.143), channel_id=1, source_target_pairs={{0,2},{1,3},{2,0},{3,1},{4,6},{5,7},{6,4},{7,5},{8,10},{9,11},{10,... | collective-permute-start | bytes 786440 | tf_op jit(solution)/shard_map/ppermute | solution.py:444
  41.4 28.3 %collective-permute-start.9 = (bf16[64,2048]{1,0:T(8,128)(2,1)S(1)}, bf16[64,2048]{1,0:T(8,128)(2,1)S(1)}, u32[]{:S(2)}, u32[]{:S(2)}) collective-permute-start(bf16[64,2048]{1,0:T(8,128)(2,1)S(1)} %get-tuple-element.144), channel_id=1, source_target_pairs={{0,1},{1,2},{2,3},{3,0},{4,5},{5,6},{6,7},{7,4},{8,9},{9,10},{10,1... | collective-permute-start | bytes 786440 | tf_op jit(solution)/shard_map/ppermute | solution.py:444
  42.8 10.3 %collective-permute-start.16 = (bf16[224,640]{1,0:T(8,128)(2,1)S(1)}, bf16[224,640]{1,0:T(8,128)(2,1)S(1)}, u32[]{:S(2)}, u32[]{:S(2)}) collective-permute-start(bf16[224,640]{1,0:T(8,128)(2,1)S(1)} %get-tuple-element.157), channel_id=1, source_target_pairs={{0,4},{4,0},{8,12},{12,8},{1,5},{5,1},{9,13},{13,9},{2,6},{6,2},{1... | collective-permute-start | bytes 860168 | tf_op jit(solution)/shard_map/ppermute | solution.py:507
  45.8 12.5 %collective-permute-start.15 = (bf16[224,640]{1,0:T(8,128)(2,1)S(1)}, bf16[224,640]{1,0:T(8,128)(2,1)S(1)}, u32[]{:S(2)}, u32[]{:S(2)}) collective-permute-start(bf16[224,640]{1,0:T(8,128)(2,1)S(1)} %get-tuple-element.155), channel_id=1, source_target_pairs={{4,8},{8,4},{5,9},{9,5},{6,10},{10,6},{7,11},{11,7},{20,24},{24,20... | collective-permute-start | bytes 860168 | tf_op jit(solution)/shard_map/ppermute | solution.py:513
  53.1 12.9 %collective-permute-start.14 = (bf16[224,768]{1,0:T(8,128)(2,1)S(1)}, bf16[224,768]{1,0:T(8,128)(2,1)S(1)}, u32[]{:S(2)}, u32[]{:S(2)}) collective-permute-start(bf16[224,768]{1,0:T(8,128)(2,1)S(1)} %get-tuple-element.154), channel_id=1, source_target_pairs={{0,4},{4,0},{8,12},{12,8},{1,5},{5,1},{9,13},{13,9},{2,6},{6,2},{1... | collective-permute-start | bytes 1032200 | tf_op jit(solution)/shard_map/ppermute | solution.py:507
  58.4 14.4 %collective-permute-start.18 = (bf16[224,640]{1,0:T(8,128)(2,1)S(1)}, bf16[224,640]{1,0:T(8,128)(2,1)S(1)}, u32[]{:S(2)}, u32[]{:S(2)}) collective-permute-start(bf16[224,640]{1,0:T(8,128)(2,1)S(1)} %get-tuple-element.167), channel_id=1, source_target_pairs={{4,8},{8,4},{5,9},{9,5},{6,10},{10,6},{7,11},{11,7},{20,24},{24,20... | collective-permute-start | bytes 860168 | tf_op jit(solution)/shard_map/ppermute | solution.py:513
  66.1 10.8 %collective-permute-start.17 = (bf16[224,640]{1,0:T(8,128)(2,1)S(1)}, bf16[224,640]{1,0:T(8,128)(2,1)S(1)}, u32[]{:S(2)}, u32[]{:S(2)}) collective-permute-start(bf16[224,640]{1,0:T(8,128)(2,1)S(1)} %get-tuple-element.166), channel_id=1, source_target_pairs={{0,4},{4,0},{8,12},{12,8},{1,5},{5,1},{9,13},{13,9},{2,6},{6,2},{1... | collective-permute-start | bytes 860168 | tf_op jit(solution)/shard_map/ppermute | solution.py:507
  72.8 11.4 %collective-permute-start.20 = (bf16[224,640]{1,0:T(8,128)(2,1)S(1)}, bf16[224,640]{1,0:T(8,128)(2,1)S(1)}, u32[]{:S(2)}, u32[]{:S(2)}) collective-permute-start(bf16[224,640]{1,0:T(8,128)(2,1)S(1)} %get-tuple-element.171), channel_id=1, source_target_pairs={{0,4},{4,0},{8,12},{12,8},{1,5},{5,1},{9,13},{13,9},{2,6},{6,2},{1... | collective-permute-start | bytes 860168 | tf_op jit(solution)/shard_map/ppermute | solution.py:507
  77.7 13.7 %collective-permute-start.24 = (bf16[224,768]{1,0:T(8,128)(2,1)S(1)}, bf16[224,768]{1,0:T(8,128)(2,1)S(1)}, u32[]{:S(2)}, u32[]{:S(2)}) collective-permute-start(bf16[224,768]{1,0:T(8,128)(2,1)S(1)} %get-tuple-element.181), channel_id=1, source_target_pairs={{0,4},{4,0},{8,12},{12,8},{1,5},{5,1},{9,13},{13,9},{2,6},{6,2},{1... | collective-permute-start | bytes 1032200 | tf_op jit(solution)/shard_map/ppermute | solution.py:507
  85.2 14.6 %collective-permute-start.22 = (bf16[224,640]{1,0:T(8,128)(2,1)S(1)}, bf16[224,640]{1,0:T(8,128)(2,1)S(1)}, u32[]{:S(2)}, u32[]{:S(2)}) collective-permute-start(bf16[224,640]{1,0:T(8,128)(2,1)S(1)} %get-tuple-element.177), channel_id=1, source_target_pairs={{0,4},{4,0},{8,12},{12,8},{1,5},{5,1},{9,13},{13,9},{2,6},{6,2},{1... | collective-permute-start | bytes 860168 | tf_op jit(solution)/shard_map/ppermute | solution.py:507
  91.5 10.3 %collective-permute-start.27 = (bf16[224,768]{1,0:T(8,128)(2,1)S(1)}, bf16[224,768]{1,0:T(8,128)(2,1)S(1)}, u32[]{:S(2)}, u32[]{:S(2)}) collective-permute-start(bf16[224,768]{1,0:T(8,128)(2,1)S(1)} %get-tuple-element.193), channel_id=1, source_target_pairs={{4,8},{8,4},{5,9},{9,5},{6,10},{10,6},{7,11},{11,7},{20,24},{24,20... | collective-permute-start | bytes 1032200 | tf_op jit(solution)/shard_map/ppermute | solution.py:513
  93.3 13.7 %collective-permute-start.26 = (bf16[224,640]{1,0:T(8,128)(2,1)S(1)}, bf16[224,640]{1,0:T(8,128)(2,1)S(1)}, u32[]{:S(2)}, u32[]{:S(2)}) collective-permute-start(bf16[224,640]{1,0:T(8,128)(2,1)S(1)} %get-tuple-element.191), channel_id=1, source_target_pairs={{0,4},{4,0},{8,12},{12,8},{1,5},{5,1},{9,13},{13,9},{2,6},{6,2},{1... | collective-permute-start | bytes 860168 | tf_op jit(solution)/shard_map/ppermute | solution.py:507
  101.8 12.7 %collective-permute-start.30 = (bf16[224,768]{1,0:T(8,128)(2,1)S(1)}, bf16[224,768]{1,0:T(8,128)(2,1)S(1)}, u32[]{:S(2)}, u32[]{:S(2)}) collective-permute-start(bf16[224,768]{1,0:T(8,128)(2,1)S(1)} %get-tuple-element.205), channel_id=1, source_target_pairs={{0,4},{4,0},{8,12},{12,8},{1,5},{5,1},{9,13},{13,9},{2,6},{6,2},{1... | collective-permute-start | bytes 1032200 | tf_op jit(solution)/shard_map/ppermute | solution.py:507
  108.8 11.9 %collective-permute-start.28 = (bf16[224,640]{1,0:T(8,128)(2,1)S(1)}, bf16[224,640]{1,0:T(8,128)(2,1)S(1)}, u32[]{:S(2)}, u32[]{:S(2)}) collective-permute-start(bf16[224,640]{1,0:T(8,128)(2,1)S(1)} %get-tuple-element.203), channel_id=1, source_target_pairs={{0,4},{4,0},{8,12},{12,8},{1,5},{5,1},{9,13},{13,9},{2,6},{6,2},{1... | collective-permute-start | bytes 860168 | tf_op jit(solution)/shard_map/ppermute | solution.py:507
  116.4 11.9 %collective-permute-start.32 = (bf16[224,640]{1,0:T(8,128)(2,1)S(1)}, bf16[224,640]{1,0:T(8,128)(2,1)S(1)}, u32[]{:S(2)}, u32[]{:S(2)}) collective-permute-start(bf16[224,640]{1,0:T(8,128)(2,1)S(1)} %get-tuple-element.216), channel_id=1, source_target_pairs={{0,4},{4,0},{8,12},{12,8},{1,5},{5,1},{9,13},{13,9},{2,6},{6,2},{1... | collective-permute-start | bytes 860168 | tf_op jit(solution)/shard_map/ppermute | solution.py:507
  122.5 12.8 %collective-permute-start.35 = (bf16[224,768]{1,0:T(8,128)(2,1)S(1)}, bf16[224,768]{1,0:T(8,128)(2,1)S(1)}, u32[]{:S(2)}, u32[]{:S(2)}) collective-permute-start(bf16[224,768]{1,0:T(8,128)(2,1)S(1)} %get-tuple-element.227), channel_id=1, source_target_pairs={{0,4},{4,0},{8,12},{12,8},{1,5},{5,1},{9,13},{13,9},{2,6},{6,2},{1... | collective-permute-start | bytes 1032200 | tf_op jit(solution)/shard_map/ppermute | solution.py:507
  (24 other events, 180.1 us)

commit v6 on v5

--- a/solution.py
+++ b/solution.py
@@ -20,7 +20,7 @@
 FIRST_HOP_WORK = 8000
 BASE_WORK = 400000
 PREPARE_MIB = 60
-DELTA_AT = 1
+DELTA_AT = 3
 
 
 def dot(a, b):

time: 140 us -> 129 us (0.921)
  starting transfers between devices: 80.5 us -> 70.7 us
    ppermute x3, starting transfers between devices: 6.35 us -> 2.03 us  [send_lows(): lows.append(lax.ppermute(low, 'tensor', hops))]
    ppermute x12, waiting for transfers between devices: 21.5 us -> 17.3 us  [on_device(): evens[step] = lax.ppermute(message, 'tensor', even)]
    ppermute x12, starting transfers between devices: 50.9 us -> 47.5 us  [on_device(): evens[step] = lax.ppermute(message, 'tensor', even)]
    ppermute x2, waiting for transfers between devices: 0.26 us -> 3.58 us  [on_device(): evens[step] = lax.ppermute(bases[step], 'tensor', even)]
    ppermute x2, starting transfers between devices: 6.99 us -> 4.97 us  [on_device(): evens[step] = lax.ppermute(bases[step], 'tensor', even)]
  transfers between devices with their start and end apart: 36 -> 36, of which waited for: 7 -> 9; matrix products, arithmetic and copies ran while one was open for 0% -> 0% of each run, Pallas kernels for 21% -> 23%
where the time goes in v6:
time: 129 us
  starting transfers between devices  70.7 us (55%)
  Pallas kernels  33.4 us (26%)
  waiting for transfers between devices  20.9 us (16%)
  local copies, waits for them, and re-layouts  2.96 us (2%)
    ppermute x12, starting transfers between devices, on_device(): evens[step] = lax.ppermute(message, 'tensor', even)  47.5 us
    ppermute x12, waiting for transfers between devices, on_device(): evens[step] = lax.ppermute(message, 'tensor', even)  17.3 us
    pallas_call x15, Pallas kernels, finish(): pl.pallas_call(functools.partial(finish_kernel, widths, near_q, far_q), o...  12 us
    pallas_call x2, Pallas kernels, base_chunks(): pl.pallas_call(functools.partial(base_kernel, places, widths), out_shape=...  9.9 us
    ppermute x12, starting transfers between devices, on_device(): odds[step] = lax.ppermute(message, 'tensor', odd)  8.61 us
    ppermute x2, starting transfers between devices, on_device(): evens[step] = lax.ppermute(bases[step], 'tensor', even)  4.97 us
    ppermute x2, waiting for transfers between devices, on_device(): evens[step] = lax.ppermute(bases[step], 'tensor', even)  3.58 us
    ppermute x1, starting transfers between devices, on_device(): evens, odds = ({0: lax.ppermute(message, 'tensor', even)}, {})  3.09 us
  transfers between devices with their start and end apart: 36, of which 9 were waited for; matrix products, arithmetic and copies ran while one was open for 0% of the time, Pallas kernels for 23%

profile of v6, /device:TPU:0, one launch (start us, length us, event | category | flops | bytes accessed | tf_op | source)
XLA Modules:
  0.0 128.8 jit_solution(8701032480410099514)
XLA Ops:
  0.0 2.9 %prepare.1 = (bf16[224,1024]{1,0:T(8,128)(2,1)}, bf16[256,224]{1,0:T(8,128)(2,1)}, bf16[224,256]{1,0:T(8,128)(2,1)}, bf16[256,256]{1,0:T(8,128)(2,1)}, bf16[256,...) custom-call(s32[16]{0:T(128)} %bitcast.6, s32[16]{0:T(128)} %slot_in.1, s32[16]{0:T(128)} %bitcast.7, bf16[256,1024]{1,0:T(8,128)(2,1)} %x.1, ...), custom_call_target="tpu_custom_call" | custom-call | tf_op jit(solution)/shard_map/prepare/pallas_call | solution.py:146
  2.9 3.1 %collective-permute-start.7 = (bf16[224,640]{1,0:T(8,128)(2,1)}, bf16[224,640]{1,0:T(8,128)(2,1)S(1)}, u32[]{:S(2)}, u32[]{:S(2)}) collective-permute-start(bf16[224,640]{1,0:T(8,128)(2,1)} %get-tuple-element.120.near.base.refs_0_), channel_id=1, source_target_pairs={{0,4},{4,0},{8,12},{12,8},{1,5},{5,1},{9,13},{13,9},{2,6},{6,2},{1... | collective-permute-start | bytes 860168 | tf_op jit(solution)/shard_map/ppermute | solution.py:475
  12.1 2.7 %base.2 = (bf16[224,768]{1,0:T(8,128)(2,1)S(1)}, bf16[224,640]{1,0:T(8,128)(2,1)S(1)}, s32[8,128]{1,0:T(8,128)S(1)}) custom-call(bf16[224,1024]{1,0:T(8,128)(2,1)S(1)} %copy-done.3, bf16[1024,8192]{1,0:T(8,128)(2,1)} %w.3, s32[8,128]{1,0:T(8,128)S(1)} %get-tuple-element.125.token_in), custom_call_target="tpu_custom_call", output_to_operand_aliasing={{2}: (2, {})} | custom-call | flops 563200000 | bytes 2816 | tf_op jit(solution)/shard_map/base/pallas_call | solution.py:200
  15.4 7.2 %base.3 = (bf16[224,640]{1,0:T(8,128)(2,1)S(1)}, bf16[224,768]{1,0:T(8,128)(2,1)S(1)}, bf16[224,640]{1,0:T(8,128)(2,1)S(1)}, bf16[224,640]{1,0:T(8,128)(2,1)S(1)...) custom-call(bf16[224,1024]{1,0:T(8,128)(2,1)S(1)} %copy-done.3, ...), custom_call_target="tpu_custom_call", output_to_operand_aliasing={{9}: (2, {})} | custom-call | flops 2457600000 | bytes 12288 | tf_op jit(solution)/shard_map/base/pallas_call | solution.py:200
  22.6 1.7 %low.1 = (bf16[128,128]{1,0:T(8,128)(2,1)S(1)}, s32[8,128]{1,0:T(8,128)S(1)}) custom-call(bf16[512,1024]{1,0:T(8,128)(2,1)S(1)} %bitcast.5, bf16[64,1152]{1,0:T(8,128)(2,1)S(1)} %get-tuple-element.133.refs_0_, bf16[64,1152]{1,0:T(8,128)(2,1)S(1)} %collective-permute-done.refs_1_, ...), custom_call_target="tpu_custom_call", output_to_operand_aliasing={{1}: (5, {})} | custom-call | tf_op jit(solution)/shard_map/low/pallas_call | solution.py:276
  25.1 4.4 %collective-permute-start.6 = (bf16[224,640]{1,0:T(8,128)(2,1)S(1)}, bf16[224,640]{1,0:T(8,128)(2,1)S(1)}, u32[]{:S(2)}, u32[]{:S(2)}) collective-permute-start(bf16[224,640]{1,0:T(8,128)(2,1)S(1)} %get-tuple-element.139.near.base.refs_0_), channel_id=1, source_target_pairs={{0,4},{4,0},{8,12},{12,8},{1,5},{5,1},{9,13},{13,9},{2,6},{6,2},{1... | collective-permute-start | bytes 860168 | tf_op jit(solution)/shard_map/ppermute | solution.py:481
  32.6 3.6 %collective-permute-done.6.got.refs_1_ = bf16[224,640]{1,0:T(8,128)(2,1)S(1)} collective-permute-done((bf16[224,640]{1,0:T(8,128)(2,1)S(1)}, bf16[224,640]{1,0:T(8,128)(2,1)S(1)}, u32[]{:S(2)}, u32[]{:S(2)}) %collective-permute-start.6) | collective-permute-done | bytes 286752 | tf_op jit(solution)/shard_map/ppermute | solution.py:481
  36.2 4.4 %collective-permute-start.16 = (bf16[224,640]{1,0:T(8,128)(2,1)S(1)}, bf16[224,640]{1,0:T(8,128)(2,1)S(1)}, u32[]{:S(2)}, u32[]{:S(2)}) collective-permute-start(bf16[224,640]{1,0:T(8,128)(2,1)S(1)} %get-tuple-element.157), channel_id=1, source_target_pairs={{0,4},{4,0},{8,12},{12,8},{1,5},{5,1},{9,13},{13,9},{2,6},{6,2},{1... | collective-permute-start | bytes 860168 | tf_op jit(solution)/shard_map/ppermute | solution.py:507
  41.4 2.1 %delta.1 = (bf16[64,2048]{1,0:T(8,128)(2,1)S(1)}, bf16[64,2048]{1,0:T(8,128)(2,1)S(1)}, bf16[64,2048]{1,0:T(8,128)(2,1)S(1)}, bf16[64,2048]{1,0:T(8,128)(2,1)S(1)}, s32[8,128]{1,0:T(8,128)S(1)}) custom-call(bf16[512,2048]{1,0:T(8,128)(2,1)S(1)} %bitcast.4, bf16[64,1152]{1,0:T(8,128)(2,1)S(1)} %get-tuple-element.133.refs_0_, ...), custom_call_target="tpu_custom_call", output_to_operand_aliasing={{4}: (9, {})} | custom-call | tf_op jit(solution)/shard_map/delta/pallas_call | solution.py:315
  45.2 4.0 %collective-permute-start.14 = (bf16[224,768]{1,0:T(8,128)(2,1)S(1)}, bf16[224,768]{1,0:T(8,128)(2,1)S(1)}, u32[]{:S(2)}, u32[]{:S(2)}) collective-permute-start(bf16[224,768]{1,0:T(8,128)(2,1)S(1)} %get-tuple-element.154), channel_id=1, source_target_pairs={{0,4},{4,0},{8,12},{12,8},{1,5},{5,1},{9,13},{13,9},{2,6},{6,2},{1... | collective-permute-start | bytes 1032200 | tf_op jit(solution)/shard_map/ppermute | solution.py:507
  50.0 7.1 %collective-permute-done.14.got.refs_2_ = bf16[224,768]{1,0:T(8,128)(2,1)S(1)} collective-permute-done((bf16[224,768]{1,0:T(8,128)(2,1)S(1)}, bf16[224,768]{1,0:T(8,128)(2,1)S(1)}, u32[]{:S(2)}, u32[]{:S(2)}) %collective-permute-start.14) | collective-permute-done | bytes 344096 | tf_op jit(solution)/shard_map/ppermute | solution.py:507
  57.1 2.3 %collective-permute-start.17 = (bf16[224,640]{1,0:T(8,128)(2,1)S(1)}, bf16[224,640]{1,0:T(8,128)(2,1)S(1)}, u32[]{:S(2)}, u32[]{:S(2)}) collective-permute-start(bf16[224,640]{1,0:T(8,128)(2,1)S(1)} %get-tuple-element.166), channel_id=1, source_target_pairs={{0,4},{4,0},{8,12},{12,8},{1,5},{5,1},{9,13},{13,9},{2,6},{6,2},{1... | collective-permute-start | bytes 860168 | tf_op jit(solution)/shard_map/ppermute | solution.py:507
  60.5 3.1 %add_delta.1 = (bf16[224,640]{1,0:T(8,128)(2,1)S(1)}, bf16[224,768]{1,0:T(8,128)(2,1)S(1)}, bf16[224,640]{1,0:T(8,128)(2,1)S(1)}, bf16[224,640]{1,0:T(8,128)(2,1...) custom-call(bf16[224,256]{1,0:T(8,128)(2,1)S(1)} %copy-done.10, ...), custom_call_target="tpu_custom_call", output_to_operand_aliasing={{6}: (11, {})} | custom-call | tf_op jit(solution)/shard_map/add_delta/pallas_call | solution.py:348
  63.6 3.0 %collective-permute-start.20 = (bf16[224,640]{1,0:T(8,128)(2,1)S(1)}, bf16[224,640]{1,0:T(8,128)(2,1)S(1)}, u32[]{:S(2)}, u32[]{:S(2)}) collective-permute-start(bf16[224,640]{1,0:T(8,128)(2,1)S(1)} %get-tuple-element.171), channel_id=1, source_target_pairs={{0,4},{4,0},{8,12},{12,8},{1,5},{5,1},{9,13},{13,9},{2,6},{6,2},{1... | collective-permute-start | bytes 860168 | tf_op jit(solution)/shard_map/ppermute | solution.py:507
  67.9 5.1 %collective-permute-start.24 = (bf16[224,768]{1,0:T(8,128)(2,1)S(1)}, bf16[224,768]{1,0:T(8,128)(2,1)S(1)}, u32[]{:S(2)}, u32[]{:S(2)}) collective-permute-start(bf16[224,768]{1,0:T(8,128)(2,1)S(1)} %get-tuple-element.181), channel_id=1, source_target_pairs={{0,4},{4,0},{8,12},{12,8},{1,5},{5,1},{9,13},{13,9},{2,6},{6,2},{1... | collective-permute-start | bytes 1032200 | tf_op jit(solution)/shard_map/ppermute | solution.py:507
  75.2 4.6 %collective-permute-start.22 = (bf16[224,640]{1,0:T(8,128)(2,1)S(1)}, bf16[224,640]{1,0:T(8,128)(2,1)S(1)}, u32[]{:S(2)}, u32[]{:S(2)}) collective-permute-start(bf16[224,640]{1,0:T(8,128)(2,1)S(1)} %get-tuple-element.177), channel_id=1, source_target_pairs={{0,4},{4,0},{8,12},{12,8},{1,5},{5,1},{9,13},{13,9},{2,6},{6,2},{1... | collective-permute-start | bytes 860168 | tf_op jit(solution)/shard_map/ppermute | solution.py:507
  83.8 4.3 %collective-permute-start.26 = (bf16[224,640]{1,0:T(8,128)(2,1)S(1)}, bf16[224,640]{1,0:T(8,128)(2,1)S(1)}, u32[]{:S(2)}, u32[]{:S(2)}) collective-permute-start(bf16[224,640]{1,0:T(8,128)(2,1)S(1)} %get-tuple-element.191), channel_id=1, source_target_pairs={{0,4},{4,0},{8,12},{12,8},{1,5},{5,1},{9,13},{13,9},{2,6},{6,2},{1... | collective-permute-start | bytes 860168 | tf_op jit(solution)/shard_map/ppermute | solution.py:507
  91.1 4.3 %collective-permute-start.30 = (bf16[224,768]{1,0:T(8,128)(2,1)S(1)}, bf16[224,768]{1,0:T(8,128)(2,1)S(1)}, u32[]{:S(2)}, u32[]{:S(2)}) collective-permute-start(bf16[224,768]{1,0:T(8,128)(2,1)S(1)} %get-tuple-element.205), channel_id=1, source_target_pairs={{0,4},{4,0},{8,12},{12,8},{1,5},{5,1},{9,13},{13,9},{2,6},{6,2},{1... | collective-permute-start | bytes 1032200 | tf_op jit(solution)/shard_map/ppermute | solution.py:507
  98.2 3.3 %collective-permute-start.28 = (bf16[224,640]{1,0:T(8,128)(2,1)S(1)}, bf16[224,640]{1,0:T(8,128)(2,1)S(1)}, u32[]{:S(2)}, u32[]{:S(2)}) collective-permute-start(bf16[224,640]{1,0:T(8,128)(2,1)S(1)} %get-tuple-element.203), channel_id=1, source_target_pairs={{0,4},{4,0},{8,12},{12,8},{1,5},{5,1},{9,13},{13,9},{2,6},{6,2},{1... | collective-permute-start | bytes 860168 | tf_op jit(solution)/shard_map/ppermute | solution.py:507
  104.3 3.5 %collective-permute-start.32 = (bf16[224,640]{1,0:T(8,128)(2,1)S(1)}, bf16[224,640]{1,0:T(8,128)(2,1)S(1)}, u32[]{:S(2)}, u32[]{:S(2)}) collective-permute-start(bf16[224,640]{1,0:T(8,128)(2,1)S(1)} %get-tuple-element.216), channel_id=1, source_target_pairs={{0,4},{4,0},{8,12},{12,8},{1,5},{5,1},{9,13},{13,9},{2,6},{6,2},{1... | collective-permute-start | bytes 860168 | tf_op jit(solution)/shard_map/ppermute | solution.py:507
  110.2 6.2 %collective-permute-start.35 = (bf16[224,768]{1,0:T(8,128)(2,1)S(1)}, bf16[224,768]{1,0:T(8,128)(2,1)S(1)}, u32[]{:S(2)}, u32[]{:S(2)}) collective-permute-start(bf16[224,768]{1,0:T(8,128)(2,1)S(1)} %get-tuple-element.227), channel_id=1, source_target_pairs={{0,4},{4,0},{8,12},{12,8},{1,5},{5,1},{9,13},{13,9},{2,6},{6,2},{1... | collective-permute-start | bytes 1032200 | tf_op jit(solution)/shard_map/ppermute | solution.py:507
  117.4 2.7 %collective-permute-start.34 = (bf16[224,640]{1,0:T(8,128)(2,1)S(1)}, bf16[224,640]{1,0:T(8,128)(2,1)S(1)}, u32[]{:S(2)}, u32[]{:S(2)}) collective-permute-start(bf16[224,640]{1,0:T(8,128)(2,1)S(1)} %get-tuple-element.226), channel_id=1, source_target_pairs={{0,4},{4,0},{8,12},{12,8},{1,5},{5,1},{9,13},{13,9},{2,6},{6,2},{1... | collective-permute-start | bytes 860168 | tf_op jit(solution)/shard_map/ppermute | solution.py:507
  120.1 4.4 %collective-permute-done.35.refs_1_ = bf16[224,768]{1,0:T(8,128)(2,1)S(1)} collective-permute-done((bf16[224,768]{1,0:T(8,128)(2,1)S(1)}, bf16[224,768]{1,0:T(8,128)(2,1)S(1)}, u32[]{:S(2)}, u32[]{:S(2)}) %collective-permute-start.35) | collective-permute-done | bytes 344096 | tf_op jit(solution)/shard_map/ppermute | solution.py:507
  125.5 2.2 %collective-permute-done.34.refs_1_ = bf16[224,640]{1,0:T(8,128)(2,1)S(1)} collective-permute-done((bf16[224,640]{1,0:T(8,128)(2,1)S(1)}, bf16[224,640]{1,0:T(8,128)(2,1)S(1)}, u32[]{:S(2)}, u32[]{:S(2)}) %collective-permute-start.34) | collective-permute-done | bytes 286752 | tf_op jit(solution)/shard_map/ppermute | solution.py:507
  (119 shorter events, 36.0 us)
Async XLA Ops:
  2.9 21.4 %collective-permute-start.7 = (bf16[224,640]{1,0:T(8,128)(2,1)}, bf16[224,640]{1,0:T(8,128)(2,1)S(1)}, u32[]{:S(2)}, u32[]{:S(2)}) collective-permute-start(bf16[224,640]{1,0:T(8,128)(2,1)} %get-tuple-element.120.near.base.refs_0_), channel_id=1, source_target_pairs={{0,4},{4,0},{8,12},{12,8},{1,5},{5,1},{9,13},{13,9},{2,6},{6,2},{1... | collective-permute-start | bytes 860168 | tf_op jit(solution)/shard_map/ppermute | solution.py:475
  8.1 14.5 %collective-permute-start = (bf16[64,1152]{1,0:T(8,128)(2,1)S(1)}, bf16[64,1152]{1,0:T(8,128)(2,1)S(1)}, u32[]{:S(2)}, u32[]{:S(2)}) collective-permute-start(bf16[64,1152]{1,0:T(8,128)(2,1)S(1)} %get-tuple-element.134), channel_id=1, source_target_pairs={{0,1},{1,2},{2,3},{3,0},{4,5},{5,6},{6,7},{7,4},{8,9},{9,10},{10,1... | collective-permute-start | bytes 442376 | tf_op jit(solution)/shard_map/ppermute | solution.py:424
  8.2 14.4 %collective-permute-start.1 = (bf16[64,1152]{1,0:T(8,128)(2,1)S(1)}, bf16[64,1152]{1,0:T(8,128)(2,1)S(1)}, u32[]{:S(2)}, u32[]{:S(2)}) collective-permute-start(bf16[64,1152]{1,0:T(8,128)(2,1)S(1)} %get-tuple-element.135), channel_id=1, source_target_pairs={{0,2},{1,3},{2,0},{3,1},{4,6},{5,7},{6,4},{7,5},{8,10},{9,11},{10,... | collective-permute-start | bytes 442376 | tf_op jit(solution)/shard_map/ppermute | solution.py:424
  9.7 12.9 %collective-permute-start.2 = (bf16[64,1152]{1,0:T(8,128)(2,1)S(1)}, bf16[64,1152]{1,0:T(8,128)(2,1)S(1)}, u32[]{:S(2)}, u32[]{:S(2)}) collective-permute-start(bf16[64,1152]{1,0:T(8,128)(2,1)S(1)} %get-tuple-element.136), channel_id=1, source_target_pairs={{0,3},{1,0},{2,1},{3,2},{4,7},{5,4},{6,5},{7,6},{8,11},{9,8},{10,9... | collective-permute-start | bytes 442376 | tf_op jit(solution)/shard_map/ppermute | solution.py:424
  14.9 16.2 %collective-permute-start.9 = (bf16[224,768]{1,0:T(8,128)(2,1)S(1)}, bf16[224,768]{1,0:T(8,128)(2,1)S(1)}, u32[]{:S(2)}, u32[]{:S(2)}) collective-permute-start(bf16[224,768]{1,0:T(8,128)(2,1)S(1)} %get-tuple-element.142.near.base.refs_0_), channel_id=1, source_target_pairs={{0,4},{4,0},{8,12},{12,8},{1,5},{5,1},{9,13},{13,9},{2,6},{6,2},{1... | collective-permute-start | bytes 1032200 | tf_op jit(solution)/shard_map/ppermute | solution.py:481
  25.1 11.1 %collective-permute-start.6 = (bf16[224,640]{1,0:T(8,128)(2,1)S(1)}, bf16[224,640]{1,0:T(8,128)(2,1)S(1)}, u32[]{:S(2)}, u32[]{:S(2)}) collective-permute-start(bf16[224,640]{1,0:T(8,128)(2,1)S(1)} %get-tuple-element.139.near.base.refs_0_), channel_id=1, source_target_pairs={{0,4},{4,0},{8,12},{12,8},{1,5},{5,1},{9,13},{13,9},{2,6},{6,2},{1... | collective-permute-start | bytes 860168 | tf_op jit(solution)/shard_map/ppermute | solution.py:481
  29.5 11.1 %collective-permute-start.5 = (bf16[128,128]{1,0:T(8,128)(2,1)S(1)}, bf16[128,128]{1,0:T(8,128)(2,1)S(1)}, u32[]{:S(2)}, u32[]{:S(2)}) collective-permute-start(bf16[128,128]{1,0:T(8,128)(2,1)S(1)} %get-tuple-element.138.refs_4_), channel_id=1, source_target_pairs={{0,12},{4,0},{8,4},{12,8},{1,13},{5,1},{9,5},{13,9},{2,14},{6,2},{... | collective-permute-start | bytes 98312 | tf_op jit(solution)/shard_map/ppermute | solution.py:435
  30.9 10.4 %collective-permute-start.4 = (bf16[128,128]{1,0:T(8,128)(2,1)S(1)}, bf16[128,128]{1,0:T(8,128)(2,1)S(1)}, u32[]{:S(2)}, u32[]{:S(2)}) collective-permute-start(bf16[128,128]{1,0:T(8,128)(2,1)S(1)} %get-tuple-element.138.refs_4_), channel_id=1, source_target_pairs={{0,8},{4,12},{8,0},{12,4},{1,9},{5,13},{9,1},{13,5},{2,10},{6,14},... | collective-permute-start | bytes 98312 | tf_op jit(solution)/shard_map/ppermute | solution.py:435
  31.1 10.3 %collective-permute-start.3 = (bf16[128,128]{1,0:T(8,128)(2,1)S(1)}, bf16[128,128]{1,0:T(8,128)(2,1)S(1)}, u32[]{:S(2)}, u32[]{:S(2)}) collective-permute-start(bf16[128,128]{1,0:T(8,128)(2,1)S(1)} %get-tuple-element.138.refs_4_), channel_id=1, source_target_pairs={{0,4},{4,8},{8,12},{12,0},{1,5},{5,9},{9,13},{13,1},{2,6},{6,10},{... | collective-permute-start | bytes 98312 | tf_op jit(solution)/shard_map/ppermute | solution.py:435
  31.7 13.2 %collective-permute-start.13 = (bf16[224,768]{1,0:T(8,128)(2,1)S(1)}, bf16[224,768]{1,0:T(8,128)(2,1)S(1)}, u32[]{:S(2)}, u32[]{:S(2)}) collective-permute-start(bf16[224,768]{1,0:T(8,128)(2,1)S(1)} %get-tuple-element.152), channel_id=1, source_target_pairs={{4,8},{8,4},{5,9},{9,5},{6,10},{10,6},{7,11},{11,7},{20,24},{24,20... | collective-permute-start | bytes 1032200 | tf_op jit(solution)/shard_map/ppermute | solution.py:513
  43.4 16.1 %collective-permute-start.10 = (bf16[64,2048]{1,0:T(8,128)(2,1)S(1)}, bf16[64,2048]{1,0:T(8,128)(2,1)S(1)}, u32[]{:S(2)}, u32[]{:S(2)}) collective-permute-start(bf16[64,2048]{1,0:T(8,128)(2,1)S(1)} %get-tuple-element.148), channel_id=1, source_target_pairs={{0,3},{1,0},{2,1},{3,2},{4,7},{5,4},{6,5},{7,6},{8,11},{9,8},{10,9... | collective-permute-start | bytes 786440 | tf_op jit(solution)/shard_map/ppermute | solution.py:444
  43.5 16.9 %collective-permute-start.11 = (bf16[64,2048]{1,0:T(8,128)(2,1)S(1)}, bf16[64,2048]{1,0:T(8,128)(2,1)S(1)}, u32[]{:S(2)}, u32[]{:S(2)}) collective-permute-start(bf16[64,2048]{1,0:T(8,128)(2,1)S(1)} %get-tuple-element.149), channel_id=1, source_target_pairs={{0,2},{1,3},{2,0},{3,1},{4,6},{5,7},{6,4},{7,5},{8,10},{9,11},{10,... | collective-permute-start | bytes 786440 | tf_op jit(solution)/shard_map/ppermute | solution.py:444
  44.8 15.6 %collective-permute-start.12 = (bf16[64,2048]{1,0:T(8,128)(2,1)S(1)}, bf16[64,2048]{1,0:T(8,128)(2,1)S(1)}, u32[]{:S(2)}, u32[]{:S(2)}) collective-permute-start(bf16[64,2048]{1,0:T(8,128)(2,1)S(1)} %get-tuple-element.150), channel_id=1, source_target_pairs={{0,1},{1,2},{2,3},{3,0},{4,5},{5,6},{6,7},{7,4},{8,9},{9,10},{10,1... | collective-permute-start | bytes 786440 | tf_op jit(solution)/shard_map/ppermute | solution.py:444
  45.2 12.0 %collective-permute-start.14 = (bf16[224,768]{1,0:T(8,128)(2,1)S(1)}, bf16[224,768]{1,0:T(8,128)(2,1)S(1)}, u32[]{:S(2)}, u32[]{:S(2)}) collective-permute-start(bf16[224,768]{1,0:T(8,128)(2,1)S(1)} %get-tuple-element.154), channel_id=1, source_target_pairs={{0,4},{4,0},{8,12},{12,8},{1,5},{5,1},{9,13},{13,9},{2,6},{6,2},{1... | collective-permute-start | bytes 1032200 | tf_op jit(solution)/shard_map/ppermute | solution.py:507
  49.3 14.3 %collective-permute-start.18 = (bf16[224,640]{1,0:T(8,128)(2,1)S(1)}, bf16[224,640]{1,0:T(8,128)(2,1)S(1)}, u32[]{:S(2)}, u32[]{:S(2)}) collective-permute-start(bf16[224,640]{1,0:T(8,128)(2,1)S(1)} %get-tuple-element.167), channel_id=1, source_target_pairs={{4,8},{8,4},{5,9},{9,5},{6,10},{10,6},{7,11},{11,7},{20,24},{24,20... | collective-permute-start | bytes 860168 | tf_op jit(solution)/shard_map/ppermute | solution.py:513
  63.6 10.6 %collective-permute-start.20 = (bf16[224,640]{1,0:T(8,128)(2,1)S(1)}, bf16[224,640]{1,0:T(8,128)(2,1)S(1)}, u32[]{:S(2)}, u32[]{:S(2)}) collective-permute-start(bf16[224,640]{1,0:T(8,128)(2,1)S(1)} %get-tuple-element.171), channel_id=1, source_target_pairs={{0,4},{4,0},{8,12},{12,8},{1,5},{5,1},{9,13},{13,9},{2,6},{6,2},{1... | collective-permute-start | bytes 860168 | tf_op jit(solution)/shard_map/ppermute | solution.py:507
  67.9 14.0 %collective-permute-start.24 = (bf16[224,768]{1,0:T(8,128)(2,1)S(1)}, bf16[224,768]{1,0:T(8,128)(2,1)S(1)}, u32[]{:S(2)}, u32[]{:S(2)}) collective-permute-start(bf16[224,768]{1,0:T(8,128)(2,1)S(1)} %get-tuple-element.181), channel_id=1, source_target_pairs={{0,4},{4,0},{8,12},{12,8},{1,5},{5,1},{9,13},{13,9},{2,6},{6,2},{1... | collective-permute-start | bytes 1032200 | tf_op jit(solution)/shard_map/ppermute | solution.py:507
  75.2 13.9 %collective-permute-start.22 = (bf16[224,640]{1,0:T(8,128)(2,1)S(1)}, bf16[224,640]{1,0:T(8,128)(2,1)S(1)}, u32[]{:S(2)}, u32[]{:S(2)}) collective-permute-start(bf16[224,640]{1,0:T(8,128)(2,1)S(1)} %get-tuple-element.177), channel_id=1, source_target_pairs={{0,4},{4,0},{8,12},{12,8},{1,5},{5,1},{9,13},{13,9},{2,6},{6,2},{1... | collective-permute-start | bytes 860168 | tf_op jit(solution)/shard_map/ppermute | solution.py:507
  83.8 12.5 %collective-permute-start.26 = (bf16[224,640]{1,0:T(8,128)(2,1)S(1)}, bf16[224,640]{1,0:T(8,128)(2,1)S(1)}, u32[]{:S(2)}, u32[]{:S(2)}) collective-permute-start(bf16[224,640]{1,0:T(8,128)(2,1)S(1)} %get-tuple-element.191), channel_id=1, source_target_pairs={{0,4},{4,0},{8,12},{12,8},{1,5},{5,1},{9,13},{13,9},{2,6},{6,2},{1... | collective-permute-start | bytes 860168 | tf_op jit(solution)/shard_map/ppermute | solution.py:507
  91.1 11.4 %collective-permute-start.30 = (bf16[224,768]{1,0:T(8,128)(2,1)S(1)}, bf16[224,768]{1,0:T(8,128)(2,1)S(1)}, u32[]{:S(2)}, u32[]{:S(2)}) collective-permute-start(bf16[224,768]{1,0:T(8,128)(2,1)S(1)} %get-tuple-element.205), channel_id=1, source_target_pairs={{0,4},{4,0},{8,12},{12,8},{1,5},{5,1},{9,13},{13,9},{2,6},{6,2},{1... | collective-permute-start | bytes 1032200 | tf_op jit(solution)/shard_map/ppermute | solution.py:507
  98.2 10.1 %collective-permute-start.28 = (bf16[224,640]{1,0:T(8,128)(2,1)S(1)}, bf16[224,640]{1,0:T(8,128)(2,1)S(1)}, u32[]{:S(2)}, u32[]{:S(2)}) collective-permute-start(bf16[224,640]{1,0:T(8,128)(2,1)S(1)} %get-tuple-element.203), channel_id=1, source_target_pairs={{0,4},{4,0},{8,12},{12,8},{1,5},{5,1},{9,13},{13,9},{2,6},{6,2},{1... | collective-permute-start | bytes 860168 | tf_op jit(solution)/shard_map/ppermute | solution.py:507
  104.3 12.1 %collective-permute-start.32 = (bf16[224,640]{1,0:T(8,128)(2,1)S(1)}, bf16[224,640]{1,0:T(8,128)(2,1)S(1)}, u32[]{:S(2)}, u32[]{:S(2)}) collective-permute-start(bf16[224,640]{1,0:T(8,128)(2,1)S(1)} %get-tuple-element.216), channel_id=1, source_target_pairs={{0,4},{4,0},{8,12},{12,8},{1,5},{5,1},{9,13},{13,9},{2,6},{6,2},{1... | collective-permute-start | bytes 860168 | tf_op jit(solution)/shard_map/ppermute | solution.py:507
  110.2 14.4 %collective-permute-start.35 = (bf16[224,768]{1,0:T(8,128)(2,1)S(1)}, bf16[224,768]{1,0:T(8,128)(2,1)S(1)}, u32[]{:S(2)}, u32[]{:S(2)}) collective-permute-start(bf16[224,768]{1,0:T(8,128)(2,1)S(1)} %get-tuple-element.227), channel_id=1, source_target_pairs={{0,4},{4,0},{8,12},{12,8},{1,5},{5,1},{9,13},{13,9},{2,6},{6,2},{1... | collective-permute-start | bytes 1032200 | tf_op jit(solution)/shard_map/ppermute | solution.py:507
  117.4 10.3 %collective-permute-start.34 = (bf16[224,640]{1,0:T(8,128)(2,1)S(1)}, bf16[224,640]{1,0:T(8,128)(2,1)S(1)}, u32[]{:S(2)}, u32[]{:S(2)}) collective-permute-start(bf16[224,640]{1,0:T(8,128)(2,1)S(1)} %get-tuple-element.226), channel_id=1, source_target_pairs={{0,4},{4,0},{8,12},{12,8},{1,5},{5,1},{9,13},{13,9},{2,6},{6,2},{1... | collective-permute-start | bytes 860168 | tf_op jit(solution)/shard_map/ppermute | solution.py:507
  (24 other events, 168.4 us)

commit v7 on v6

--- a/solution.py
+++ b/solution.py
@@ -16,7 +16,7 @@
 BF16 = jnp.bfloat16
 F32 = jnp.float32
 MIB = 1024 * 1024
-HOP_WORK = 14000
+HOP_WORK = 8000
 FIRST_HOP_WORK = 8000
 BASE_WORK = 400000
 PREPARE_MIB = 60
@@ -76,8 +76,9 @@
     refs = list(refs)
     line = widths is not None
     w = refs.pop(0) if line else None
-    compact_x, pick, place, spread_out, tags_out = refs[:5]
-    message = refs[5] if line else None
+    compact_x, pick, place = refs[:3]
+    blocks = refs[3 : 3 + replicas]
+    message = refs[3 + replicas] if line else None
     owner, slot, live, x, sems = refs[-5:]
     wide, wide_sem = (refs[-7], refs[-6]) if line else (None, None)
     copies = [
@@ -124,8 +125,12 @@
     place[...] = dot_cols(compact, spread).astype(BF16)
     packed_x = dot(compact, x[...]).astype(BF16)
     compact_x[...] = packed_x
-    spread_out[...] = spread
-    tags_out[...] = tags.astype(BF16)
+    sent = dot(spread, x[...]).astype(BF16)
+    sent_tags = dot(spread, tags.astype(BF16)).astype(BF16)
+    for k, block in enumerate(blocks):
+        here = slice(k * block.shape[0], (k + 1) * block.shape[0])
+        block[:, :feat] = sent[here]
+        block[:, feat:] = sent_tags[here]
     if line:
         weights.wait()
         message[...] = dot(packed_x, wide[...]).astype(BF16)
@@ -137,7 +142,7 @@
     line = weight is not None
     shape = lambda *dims: jax.ShapeDtypeStruct(dims, BF16)
     outs = [shape(LIVE_ROWS, feat), shape(rows, LIVE_ROWS), shape(LIVE_ROWS, replicas * block)]
-    outs += [shape(replicas * block, rows), shape(rows, TAG)]
+    outs += [shape(block, feat + TAG)] * replicas
     scratch = [pltpu.SMEM(a.shape, jnp.int32) for a in (owner, slot, live)]
     scratch += [pltpu.VMEM(x.shape, BF16), pltpu.SemaphoreType.DMA((4,))]
     if line:
@@ -152,31 +157,6 @@
         compiler_params=params(PREPARE_MIB),
         name="prepare",
     )(owner, slot, live, x, *([weight] if line else []))
-
-
-def spread_kernel(spread, tags, x, token_in, *blocks):
-    feat = x.shape[1]
-    sent = dot(spread[...], x[...]).astype(BF16)
-    sent_tags = dot(spread[...], tags[...]).astype(BF16)
-    for k, block in enumerate(blocks[:-1]):
-        here = slice(k * block.shape[0], (k + 1) * block.shape[0])
-        block[:, :feat] = sent[here]
-        block[:, feat:] = sent_tags[here]
-
-
-def spread_groups(spread, tags, x, token):
-    rows = CAP * GROUP_ROWS
-    blocks = spread.shape[0] // rows
-    return pl.pallas_call(
-        spread_kernel,
-        out_shape=[jax.ShapeDtypeStruct((rows, x.shape[1] + TAG), BF16)] * blocks
-        + [jax.ShapeDtypeStruct(token.shape, token.dtype)],
-        in_specs=[VMEM] * 3 + [ANY],
-        out_specs=[VMEM] * blocks + [ANY],
-        input_output_aliases={3: blocks},
-        compiler_params=params(),
-        name="spread",
-    )(spread, tags, x, token)
 
 
 def base_kernel(places, widths, x, w, token_in, *refs):
@@ -452,8 +432,7 @@
     down, up = down.reshape(-1, down.shape[2]), up.reshape(-1, up.shape[2])
     token = jnp.zeros((8, 128), jnp.int32)
     if shards != 4:
-        compact_x, pick, place, spread, tags = prepare(owner[:, 0], slot, live[0], x, replicas)
-        *blocks, token = spread_groups(spread, tags, x, token)
+        compact_x, pick, place, *blocks = prepare(owner[:, 0], slot, live[0], x, replicas)
         z, share = lax.axis_index("tensor").astype(jnp.int32), width // shards
         base = dot(compact_x, weight)
         parts = send_groups(blocks)
@@ -471,16 +450,19 @@
     even = [(0, 1), (1, 0), (2, 3), (3, 2)]
     odd = [(1, 2), (2, 1)]
     opened = prepare(owner[:, 0], slot, live[0], x, replicas, weight, widths)
-    compact_x, pick, place, spread, tags, message = opened
+    compact_x, pick, place, *blocks, message = opened
     evens, odds = {0: lax.ppermute(message, "tensor", even)}, {}
-    *blocks, token = spread_groups(spread, tags, x, token)
     parts = send_groups(blocks)
-    *early, token = base_chunks((1, 2), widths, compact_x, weight, token)
-    bases = [message, *early]
+    first = (1, 2, chunks - 1)
+    *early, token = base_chunks(first, widths, compact_x, weight, token)
+    bases = {0: message, **dict(zip(first, early))}
     for step in (1, 2):
         evens[step] = lax.ppermute(bases[step], "tensor", even)
-    *late, token = base_chunks(tuple(range(3, chunks)), widths, compact_x, weight, token)
-    bases += late
+    message, token = hop(odd_hop_kernel, [bases[chunks - 1], evens[0]], token, FIRST_HOP_WORK)
+    odds[1] = lax.ppermute(message, "tensor", odd)
+    rest = tuple(range(3, chunks - 1))
+    *late, token = base_chunks(rest, widths, compact_x, weight, token)
+    bases.update(zip(rest, late))
     low, token = low_values(parts, down, rank, token)
     lows = send_lows(low)
     steps = chunks + 3
@@ -507,9 +489,8 @@
             evens[step] = lax.ppermute(message, "tensor", even)
             seen_odd.add(step - 2)
             result, token = close(result, token)
-        if step <= chunks:
-            work = FIRST_HOP_WORK if step == 1 else HOP_WORK
-            message, token = hop(odd_hop_kernel, [bases[chunks - step], evens[step - 1]], token, work)
+        if 2 <= step <= chunks:
+            message, token = hop(odd_hop_kernel, [bases[chunks - step], evens[step - 1]], token)
             odds[step] = lax.ppermute(message, "tensor", odd)
         seen_even.add(step - 1)
         if step == DELTA_AT:

time: 129 us -> 125 us (0.969)
  starting transfers between devices: 70.7 us -> 62.5 us
  waiting for transfers between devices: 20.9 us -> 26.6 us
  local copies, waits for them, and re-layouts: 2.96 us -> 1.08 us
    ppermute x12, starting transfers between devices: 47.5 us -> 36.8 us  [on_device(): evens[step] = lax.ppermute(message, 'tensor', even)]
    ppermute x3, waiting for transfers between devices: 0.01 us -> 5.84 us  [send_back(): back.append(lax.ppermute(made[k], 'replica', hops))]
    ppermute x3, waiting for transfers between devices: 0.01 us -> 5.53 us  [send_lows(): lows.append(lax.ppermute(low, 'tensor', hops))]
    ppermute x2, waiting for transfers between devices: 3.58 us -> 0.01 us  [on_device(): evens[step] = lax.ppermute(bases[step], 'tensor', even)]
    ppermute x3, starting transfers between devices: 2.03 us -> 4.8 us  [send_lows(): lows.append(lax.ppermute(low, 'tensor', hops))]
    ppermute x12, waiting for transfers between devices: 17.3 us -> 15.1 us  [on_device(): evens[step] = lax.ppermute(message, 'tensor', even)]
    unnamed x24 -> x28, local copies, waits for them, and re-layouts: 2.96 us -> 1.08 us
    ppermute x12 -> x11, starting transfers between devices: 8.61 us -> 7.8 us  [on_device(): odds[step] = lax.ppermute(message, 'tensor', odd)]
  transfers between devices with their start and end apart: 36 -> 36, of which waited for: 9 -> 10; matrix products, arithmetic and copies ran while one was open for 0% -> 0% of each run, Pallas kernels for 23% -> 24%
where the time goes in v7:
time: 125 us; the launch traced here: 124 us
  starting transfers between devices  62.5 us (50%)
  Pallas kernels  33.3 us (27%)
  waiting for transfers between devices  26.6 us (21%)
    ppermute x12, starting transfers between devices, on_device(): evens[step] = lax.ppermute(message, 'tensor', even)  36.8 us
    ppermute x12, waiting for transfers between devices, on_device(): evens[step] = lax.ppermute(message, 'tensor', even)  15.1 us
    pallas_call x15, Pallas kernels, finish(): pl.pallas_call(functools.partial(finish_kernel, widths, near_q, far_q), o...  12 us
    pallas_call x2, Pallas kernels, base_chunks(): pl.pallas_call(functools.partial(base_kernel, places, widths), out_shape=...  10 us
    ppermute x11, starting transfers between devices, on_device(): odds[step] = lax.ppermute(message, 'tensor', odd)  7.8 us
    ppermute x3, waiting for transfers between devices, send_back(): back.append(lax.ppermute(made[k], 'replica', hops))  5.84 us
    ppermute x3, waiting for transfers between devices, send_lows(): lows.append(lax.ppermute(low, 'tensor', hops))  5.53 us
    ppermute x3, starting transfers between devices, send_lows(): lows.append(lax.ppermute(low, 'tensor', hops))  4.8 us
  transfers between devices with their start and end apart: 36, of which 10 were waited for; matrix products, arithmetic and copies ran while one was open for 0% of the time, Pallas kernels for 24%

profile of v7, /device:TPU:0, one launch (start us, length us, event | category | flops | bytes accessed | tf_op | source)
XLA Modules:
  0.0 124.3 jit_solution(14233686186800449645)
XLA Ops:
  0.0 3.0 %prepare.1 = (bf16[224,1024]{1,0:T(8,128)(2,1)}, bf16[256,224]{1,0:T(8,128)(2,1)}, bf16[224,256]{1,0:T(8,128)(2,1)}, bf16[64,1152]{1,0:T(8,128)(2,1)}, bf16[64,1...) custom-call(s32[16]{0:T(128)} %bitcast.6, s32[16]{0:T(128)} %slot_in.1, ...), custom_call_target="tpu_custom_call" | custom-call | tf_op jit(solution)/shard_map/prepare/pallas_call | solution.py:151
  3.0 3.1 %collective-permute-start = (bf16[224,640]{1,0:T(8,128)(2,1)}, bf16[224,640]{1,0:T(8,128)(2,1)S(1)}, u32[]{:S(2)}, u32[]{:S(2)}) collective-permute-start(bf16[224,640]{1,0:T(8,128)(2,1)} %get-tuple-element.117.near.base.refs_0_), channel_id=1, source_target_pairs={{0,4},{4,0},{8,12},{12,8},{1,5},{5,1},{9,13},{13,9},{2,6},{6,2},{1... | collective-permute-start | bytes 860168 | tf_op jit(solution)/shard_map/ppermute | solution.py:454
  7.2 3.3 %base.2 = (bf16[224,768]{1,0:T(8,128)(2,1)S(1)}, bf16[224,640]{1,0:T(8,128)(2,1)S(1)}, bf16[224,640]{1,0:T(8,128)(2,1)S(1)}, s32[8,128]{1,0:T(8,128)S(1)}) custom-call(bf16[224,1024]{1,0:T(8,128)(2,1)S(1)} %copy-done.2, bf16[1024,8192]{1,0:T(8,128)(2,1)} %w.3, s32[8,128]{1,0:T(8,128)S(1)} %broadcast_in_dim.3.token_in), custom_call_target="tpu_custom_call", output_to_operand_aliasing={{3}: (2, {})} | custom-call | flops 819200000 | bytes 4096 | tf_op jit(solution)/shard_map/base/pallas_call | solution.py:180
  14.8 6.7 %base.3 = (bf16[224,640]{1,0:T(8,128)(2,1)S(1)}, bf16[224,768]{1,0:T(8,128)(2,1)S(1)}, bf16[224,640]{1,0:T(8,128)(2,1)S(1)}, bf16[224,640]{1,0:T(8,128)(2,1)S(1)...) custom-call(bf16[224,1024]{1,0:T(8,128)(2,1)S(1)} %copy-done.3, ...), custom_call_target="tpu_custom_call", output_to_operand_aliasing={{8}: (2, {})} | custom-call | flops 2201600000 | bytes 11008 | tf_op jit(solution)/shard_map/base/pallas_call | solution.py:180
  21.5 4.4 %collective-permute-start.7 = (bf16[224,640]{1,0:T(8,128)(2,1)S(1)}, bf16[224,640]{1,0:T(8,128)(2,1)S(1)}, u32[]{:S(2)}, u32[]{:S(2)}) collective-permute-start(bf16[224,640]{1,0:T(8,128)(2,1)S(1)} %get-tuple-element.134.near.base.refs_0_), channel_id=1, source_target_pairs={{0,4},{4,0},{8,12},{12,8},{1,5},{5,1},{9,13},{13,9},{2,6},{6,2},{1... | collective-permute-start | bytes 860168 | tf_op jit(solution)/shard_map/ppermute | solution.py:460
  28.5 1.9 %collective-permute-start.6 = (bf16[128,128]{1,0:T(8,128)(2,1)S(1)}, bf16[128,128]{1,0:T(8,128)(2,1)S(1)}, u32[]{:S(2)}, u32[]{:S(2)}) collective-permute-start(bf16[128,128]{1,0:T(8,128)(2,1)S(1)} %get-tuple-element.133.refs_4_), channel_id=1, source_target_pairs={{0,12},{4,0},{8,4},{12,8},{1,13},{5,1},{9,5},{13,9},{2,14},{6,2},{... | collective-permute-start | bytes 98312 | tf_op jit(solution)/shard_map/ppermute | solution.py:415
  35.3 5.5 %collective-permute-done.5.refs_6_ = bf16[128,128]{1,0:T(8,128)(2,1)S(1)} collective-permute-done((bf16[128,128]{1,0:T(8,128)(2,1)S(1)}, bf16[128,128]{1,0:T(8,128)(2,1)S(1)}, u32[]{:S(2)}, u32[]{:S(2)}) %collective-permute-start.5) | collective-permute-done | bytes 32800 | tf_op jit(solution)/shard_map/ppermute | solution.py:415
  40.9 2.1 %delta.1 = (bf16[64,2048]{1,0:T(8,128)(2,1)S(1)}, bf16[64,2048]{1,0:T(8,128)(2,1)S(1)}, bf16[64,2048]{1,0:T(8,128)(2,1)S(1)}, bf16[64,2048]{1,0:T(8,128)(2,1)S(1)}, s32[8,128]{1,0:T(8,128)S(1)}) custom-call(bf16[512,2048]{1,0:T(8,128)(2,1)S(1)} %bitcast.4, bf16[64,1152]{1,0:T(8,128)(2,1)S(1)} %copy-done.7, ...), custom_call_target="tpu_custom_call", output_to_operand_aliasing={{4}: (9, {})} | custom-call | tf_op jit(solution)/shard_map/delta/pallas_call | solution.py:295
  43.0 2.2 %collective-permute-start.14 = (bf16[224,768]{1,0:T(8,128)(2,1)S(1)}, bf16[224,768]{1,0:T(8,128)(2,1)S(1)}, u32[]{:S(2)}, u32[]{:S(2)}) collective-permute-start(bf16[224,768]{1,0:T(8,128)(2,1)S(1)} %get-tuple-element.148), channel_id=1, source_target_pairs={{0,4},{4,0},{8,12},{12,8},{1,5},{5,1},{9,13},{13,9},{2,6},{6,2},{1... | collective-permute-start | bytes 1032200 | tf_op jit(solution)/shard_map/ppermute | solution.py:489
  47.5 3.2 %collective-permute-done.14.got.refs_2_ = bf16[224,768]{1,0:T(8,128)(2,1)S(1)} collective-permute-done((bf16[224,768]{1,0:T(8,128)(2,1)S(1)}, bf16[224,768]{1,0:T(8,128)(2,1)S(1)}, u32[]{:S(2)}, u32[]{:S(2)}) %collective-permute-start.14) | collective-permute-done | bytes 344096 | tf_op jit(solution)/shard_map/ppermute | solution.py:489
  53.4 5.6 %collective-permute-done.11.refs_8_ = bf16[64,2048]{1,0:T(8,128)(2,1)S(1)} collective-permute-done((bf16[64,2048]{1,0:T(8,128)(2,1)S(1)}, bf16[64,2048]{1,0:T(8,128)(2,1)S(1)}, u32[]{:S(2)}, u32[]{:S(2)}) %collective-permute-start.11) | collective-permute-done | bytes 262176 | tf_op jit(solution)/shard_map/ppermute | solution.py:424
  59.3 3.1 %add_delta.1 = (bf16[224,640]{1,0:T(8,128)(2,1)S(1)}, bf16[224,768]{1,0:T(8,128)(2,1)S(1)}, bf16[224,640]{1,0:T(8,128)(2,1)S(1)}, bf16[224,640]{1,0:T(8,128)(2,1...) custom-call(bf16[224,256]{1,0:T(8,128)(2,1)S(1)} %copy-done.10, ...), custom_call_target="tpu_custom_call", output_to_operand_aliasing={{6}: (11, {})} | custom-call | tf_op jit(solution)/shard_map/add_delta/pallas_call | solution.py:328
  63.4 5.3 %collective-permute-start.24 = (bf16[224,768]{1,0:T(8,128)(2,1)S(1)}, bf16[224,768]{1,0:T(8,128)(2,1)S(1)}, u32[]{:S(2)}, u32[]{:S(2)}) collective-permute-start(bf16[224,768]{1,0:T(8,128)(2,1)S(1)} %get-tuple-element.175), channel_id=1, source_target_pairs={{0,4},{4,0},{8,12},{12,8},{1,5},{5,1},{9,13},{13,9},{2,6},{6,2},{1... | collective-permute-start | bytes 1032200 | tf_op jit(solution)/shard_map/ppermute | solution.py:489
  68.7 3.0 %collective-permute-done.20.got.refs_2_ = bf16[224,640]{1,0:T(8,128)(2,1)S(1)} collective-permute-done((bf16[224,640]{1,0:T(8,128)(2,1)S(1)}, bf16[224,640]{1,0:T(8,128)(2,1)S(1)}, u32[]{:S(2)}, u32[]{:S(2)}) %collective-permute-start.20) | collective-permute-done | bytes 286752 | tf_op jit(solution)/shard_map/ppermute | solution.py:489
  72.5 3.4 %collective-permute-start.22 = (bf16[224,640]{1,0:T(8,128)(2,1)S(1)}, bf16[224,640]{1,0:T(8,128)(2,1)S(1)}, u32[]{:S(2)}, u32[]{:S(2)}) collective-permute-start(bf16[224,640]{1,0:T(8,128)(2,1)S(1)} %get-tuple-element.171), channel_id=1, source_target_pairs={{0,4},{4,0},{8,12},{12,8},{1,5},{5,1},{9,13},{13,9},{2,6},{6,2},{1... | collective-permute-start | bytes 860168 | tf_op jit(solution)/shard_map/ppermute | solution.py:489
  76.9 2.2 %collective-permute-done.24.got.refs_2_ = bf16[224,768]{1,0:T(8,128)(2,1)S(1)} collective-permute-done((bf16[224,768]{1,0:T(8,128)(2,1)S(1)}, bf16[224,768]{1,0:T(8,128)(2,1)S(1)}, u32[]{:S(2)}, u32[]{:S(2)}) %collective-permute-start.24) | collective-permute-done | bytes 344096 | tf_op jit(solution)/shard_map/ppermute | solution.py:489
  80.9 3.4 %collective-permute-start.26 = (bf16[224,640]{1,0:T(8,128)(2,1)S(1)}, bf16[224,640]{1,0:T(8,128)(2,1)S(1)}, u32[]{:S(2)}, u32[]{:S(2)}) collective-permute-start(bf16[224,640]{1,0:T(8,128)(2,1)S(1)} %get-tuple-element.185), channel_id=1, source_target_pairs={{0,4},{4,0},{8,12},{12,8},{1,5},{5,1},{9,13},{13,9},{2,6},{6,2},{1... | collective-permute-start | bytes 860168 | tf_op jit(solution)/shard_map/ppermute | solution.py:489
  87.3 3.5 %collective-permute-start.30 = (bf16[224,768]{1,0:T(8,128)(2,1)S(1)}, bf16[224,768]{1,0:T(8,128)(2,1)S(1)}, u32[]{:S(2)}, u32[]{:S(2)}) collective-permute-start(bf16[224,768]{1,0:T(8,128)(2,1)S(1)} %get-tuple-element.199), channel_id=1, source_target_pairs={{0,4},{4,0},{8,12},{12,8},{1,5},{5,1},{9,13},{13,9},{2,6},{6,2},{1... | collective-permute-start | bytes 1032200 | tf_op jit(solution)/shard_map/ppermute | solution.py:489
  93.7 3.6 %collective-permute-start.28 = (bf16[224,640]{1,0:T(8,128)(2,1)S(1)}, bf16[224,640]{1,0:T(8,128)(2,1)S(1)}, u32[]{:S(2)}, u32[]{:S(2)}) collective-permute-start(bf16[224,640]{1,0:T(8,128)(2,1)S(1)} %get-tuple-element.197), channel_id=1, source_target_pairs={{0,4},{4,0},{8,12},{12,8},{1,5},{5,1},{9,13},{13,9},{2,6},{6,2},{1... | collective-permute-start | bytes 860168 | tf_op jit(solution)/shard_map/ppermute | solution.py:489
  101.1 4.1 %collective-permute-start.32 = (bf16[224,640]{1,0:T(8,128)(2,1)S(1)}, bf16[224,640]{1,0:T(8,128)(2,1)S(1)}, u32[]{:S(2)}, u32[]{:S(2)}) collective-permute-start(bf16[224,640]{1,0:T(8,128)(2,1)S(1)} %get-tuple-element.210), channel_id=1, source_target_pairs={{0,4},{4,0},{8,12},{12,8},{1,5},{5,1},{9,13},{13,9},{2,6},{6,2},{1... | collective-permute-start | bytes 860168 | tf_op jit(solution)/shard_map/ppermute | solution.py:489
  107.2 6.1 %collective-permute-start.35 = (bf16[224,768]{1,0:T(8,128)(2,1)S(1)}, bf16[224,768]{1,0:T(8,128)(2,1)S(1)}, u32[]{:S(2)}, u32[]{:S(2)}) collective-permute-start(bf16[224,768]{1,0:T(8,128)(2,1)S(1)} %get-tuple-element.221), channel_id=1, source_target_pairs={{0,4},{4,0},{8,12},{12,8},{1,5},{5,1},{9,13},{13,9},{2,6},{6,2},{1... | collective-permute-start | bytes 1032200 | tf_op jit(solution)/shard_map/ppermute | solution.py:489
  114.4 2.0 %collective-permute-start.34 = (bf16[224,640]{1,0:T(8,128)(2,1)S(1)}, bf16[224,640]{1,0:T(8,128)(2,1)S(1)}, u32[]{:S(2)}, u32[]{:S(2)}) collective-permute-start(bf16[224,640]{1,0:T(8,128)(2,1)S(1)} %get-tuple-element.220), channel_id=1, source_target_pairs={{0,4},{4,0},{8,12},{12,8},{1,5},{5,1},{9,13},{13,9},{2,6},{6,2},{1... | collective-permute-start | bytes 860168 | tf_op jit(solution)/shard_map/ppermute | solution.py:489
  116.4 3.7 %collective-permute-done.35.refs_1_ = bf16[224,768]{1,0:T(8,128)(2,1)S(1)} collective-permute-done((bf16[224,768]{1,0:T(8,128)(2,1)S(1)}, bf16[224,768]{1,0:T(8,128)(2,1)S(1)}, u32[]{:S(2)}, u32[]{:S(2)}) %collective-permute-start.35) | collective-permute-done | bytes 344096 | tf_op jit(solution)/shard_map/ppermute | solution.py:489
  121.1 2.1 %collective-permute-done.34.refs_1_ = bf16[224,640]{1,0:T(8,128)(2,1)S(1)} collective-permute-done((bf16[224,640]{1,0:T(8,128)(2,1)S(1)}, bf16[224,640]{1,0:T(8,128)(2,1)S(1)}, u32[]{:S(2)}, u32[]{:S(2)}) %collective-permute-start.34) | collective-permute-done | bytes 286752 | tf_op jit(solution)/shard_map/ppermute | solution.py:489
  (122 shorter events, 37.0 us)
Async XLA Ops:
  3.0 10.9 %collective-permute-start = (bf16[224,640]{1,0:T(8,128)(2,1)}, bf16[224,640]{1,0:T(8,128)(2,1)S(1)}, u32[]{:S(2)}, u32[]{:S(2)}) collective-permute-start(bf16[224,640]{1,0:T(8,128)(2,1)} %get-tuple-element.117.near.base.refs_0_), channel_id=1, source_target_pairs={{0,4},{4,0},{8,12},{12,8},{1,5},{5,1},{9,13},{13,9},{2,6},{6,2},{1... | collective-permute-start | bytes 860168 | tf_op jit(solution)/shard_map/ppermute | solution.py:454
  10.5 17.2 %collective-permute-start.9 = (bf16[224,768]{1,0:T(8,128)(2,1)S(1)}, bf16[224,768]{1,0:T(8,128)(2,1)S(1)}, u32[]{:S(2)}, u32[]{:S(2)}) collective-permute-start(bf16[224,768]{1,0:T(8,128)(2,1)S(1)} %get-tuple-element.136.near.base.refs_0_), channel_id=1, source_target_pairs={{0,4},{4,0},{8,12},{12,8},{1,5},{5,1},{9,13},{13,9},{2,6},{6,2},{1... | collective-permute-start | bytes 1032200 | tf_op jit(solution)/shard_map/ppermute | solution.py:460
  10.6 10.9 %collective-permute-start.1 = (bf16[64,1152]{1,0:T(8,128)(2,1)S(1)}, bf16[64,1152]{1,0:T(8,128)(2,1)S(1)}, u32[]{:S(2)}, u32[]{:S(2)}) collective-permute-start(bf16[64,1152]{1,0:T(8,128)(2,1)S(1)} %copy-done.13), channel_id=1, source_target_pairs={{0,1},{1,2},{2,3},{3,0},{4,5},{5,6},{6,7},{7,4},{8,9},{9,10},{10,1... | collective-permute-start | bytes 442376 | tf_op jit(solution)/shard_map/ppermute | solution.py:404
  10.7 15.3 %collective-permute-start.2 = (bf16[64,1152]{1,0:T(8,128)(2,1)S(1)}, bf16[64,1152]{1,0:T(8,128)(2,1)S(1)}, u32[]{:S(2)}, u32[]{:S(2)}) collective-permute-start(bf16[64,1152]{1,0:T(8,128)(2,1)S(1)} %copy-done.12), channel_id=1, source_target_pairs={{0,2},{1,3},{2,0},{3,1},{4,6},{5,7},{6,4},{7,5},{8,10},{9,11},{10,... | collective-permute-start | bytes 442376 | tf_op jit(solution)/shard_map/ppermute | solution.py:404
  12.6 13.4 %collective-permute-start.3 = (bf16[64,1152]{1,0:T(8,128)(2,1)S(1)}, bf16[64,1152]{1,0:T(8,128)(2,1)S(1)}, u32[]{:S(2)}, u32[]{:S(2)}) collective-permute-start(bf16[64,1152]{1,0:T(8,128)(2,1)S(1)} %copy-done.11), channel_id=1, source_target_pairs={{0,3},{1,0},{2,1},{3,2},{4,7},{5,4},{6,5},{7,6},{8,11},{9,8},{10,9... | collective-permute-start | bytes 442376 | tf_op jit(solution)/shard_map/ppermute | solution.py:404
  14.1 18.2 %collective-permute-start.8 = (bf16[224,640]{1,0:T(8,128)(2,1)S(1)}, bf16[224,640]{1,0:T(8,128)(2,1)S(1)}, u32[]{:S(2)}, u32[]{:S(2)}) collective-permute-start(bf16[224,640]{1,0:T(8,128)(2,1)S(1)} %get-tuple-element.135), channel_id=1, source_target_pairs={{4,8},{8,4},{5,9},{9,5},{6,10},{10,6},{7,11},{11,7},{20,24},{24,20... | collective-permute-start | bytes 860168 | tf_op jit(solution)/shard_map/ppermute | solution.py:462
  21.5 11.8 %collective-permute-start.7 = (bf16[224,640]{1,0:T(8,128)(2,1)S(1)}, bf16[224,640]{1,0:T(8,128)(2,1)S(1)}, u32[]{:S(2)}, u32[]{:S(2)}) collective-permute-start(bf16[224,640]{1,0:T(8,128)(2,1)S(1)} %get-tuple-element.134.near.base.refs_0_), channel_id=1, source_target_pairs={{0,4},{4,0},{8,12},{12,8},{1,5},{5,1},{9,13},{13,9},{2,6},{6,2},{1... | collective-permute-start | bytes 860168 | tf_op jit(solution)/shard_map/ppermute | solution.py:460
  27.8 15.2 %collective-permute-start.13 = (bf16[224,768]{1,0:T(8,128)(2,1)S(1)}, bf16[224,768]{1,0:T(8,128)(2,1)S(1)}, u32[]{:S(2)}, u32[]{:S(2)}) collective-permute-start(bf16[224,768]{1,0:T(8,128)(2,1)S(1)} %get-tuple-element.146), channel_id=1, source_target_pairs={{4,8},{8,4},{5,9},{9,5},{6,10},{10,6},{7,11},{11,7},{20,24},{24,20... | collective-permute-start | bytes 1032200 | tf_op jit(solution)/shard_map/ppermute | solution.py:494
  30.4 10.5 %collective-permute-start.5 = (bf16[128,128]{1,0:T(8,128)(2,1)S(1)}, bf16[128,128]{1,0:T(8,128)(2,1)S(1)}, u32[]{:S(2)}, u32[]{:S(2)}) collective-permute-start(bf16[128,128]{1,0:T(8,128)(2,1)S(1)} %get-tuple-element.133.refs_4_), channel_id=1, source_target_pairs={{0,8},{4,12},{8,0},{12,4},{1,9},{5,13},{9,1},{13,5},{2,10},{6,14},... | collective-permute-start | bytes 98312 | tf_op jit(solution)/shard_map/ppermute | solution.py:415
  33.3 13.2 %collective-permute-start.16 = (bf16[224,640]{1,0:T(8,128)(2,1)S(1)}, bf16[224,640]{1,0:T(8,128)(2,1)S(1)}, u32[]{:S(2)}, u32[]{:S(2)}) collective-permute-start(bf16[224,640]{1,0:T(8,128)(2,1)S(1)} %get-tuple-element.151), channel_id=1, source_target_pairs={{0,4},{4,0},{8,12},{12,8},{1,5},{5,1},{9,13},{13,9},{2,6},{6,2},{1... | collective-permute-start | bytes 860168 | tf_op jit(solution)/shard_map/ppermute | solution.py:489
  34.6 12.1 %collective-permute-start.15 = (bf16[224,640]{1,0:T(8,128)(2,1)S(1)}, bf16[224,640]{1,0:T(8,128)(2,1)S(1)}, u32[]{:S(2)}, u32[]{:S(2)}) collective-permute-start(bf16[224,640]{1,0:T(8,128)(2,1)S(1)} %get-tuple-element.149), channel_id=1, source_target_pairs={{4,8},{8,4},{5,9},{9,5},{6,10},{10,6},{7,11},{11,7},{20,24},{24,20... | collective-permute-start | bytes 860168 | tf_op jit(solution)/shard_map/ppermute | solution.py:494
  45.2 13.8 %collective-permute-start.11 = (bf16[64,2048]{1,0:T(8,128)(2,1)S(1)}, bf16[64,2048]{1,0:T(8,128)(2,1)S(1)}, u32[]{:S(2)}, u32[]{:S(2)}) collective-permute-start(bf16[64,2048]{1,0:T(8,128)(2,1)S(1)} %get-tuple-element.143), channel_id=1, source_target_pairs={{0,2},{1,3},{2,0},{3,1},{4,6},{5,7},{6,4},{7,5},{8,10},{9,11},{10,... | collective-permute-start | bytes 786440 | tf_op jit(solution)/shard_map/ppermute | solution.py:424
  46.5 12.8 %collective-permute-start.12 = (bf16[64,2048]{1,0:T(8,128)(2,1)S(1)}, bf16[64,2048]{1,0:T(8,128)(2,1)S(1)}, u32[]{:S(2)}, u32[]{:S(2)}) collective-permute-start(bf16[64,2048]{1,0:T(8,128)(2,1)S(1)} %get-tuple-element.144), channel_id=1, source_target_pairs={{0,1},{1,2},{2,3},{3,0},{4,5},{5,6},{6,7},{7,4},{8,9},{9,10},{10,1... | collective-permute-start | bytes 786440 | tf_op jit(solution)/shard_map/ppermute | solution.py:424
  46.8 15.5 %collective-permute-start.18 = (bf16[224,640]{1,0:T(8,128)(2,1)S(1)}, bf16[224,640]{1,0:T(8,128)(2,1)S(1)}, u32[]{:S(2)}, u32[]{:S(2)}) collective-permute-start(bf16[224,640]{1,0:T(8,128)(2,1)S(1)} %get-tuple-element.161), channel_id=1, source_target_pairs={{4,8},{8,4},{5,9},{9,5},{6,10},{10,6},{7,11},{11,7},{20,24},{24,20... | collective-permute-start | bytes 860168 | tf_op jit(solution)/shard_map/ppermute | solution.py:494
  50.7 11.8 %collective-permute-start.17 = (bf16[224,640]{1,0:T(8,128)(2,1)S(1)}, bf16[224,640]{1,0:T(8,128)(2,1)S(1)}, u32[]{:S(2)}, u32[]{:S(2)}) collective-permute-start(bf16[224,640]{1,0:T(8,128)(2,1)S(1)} %get-tuple-element.160), channel_id=1, source_target_pairs={{0,4},{4,0},{8,12},{12,8},{1,5},{5,1},{9,13},{13,9},{2,6},{6,2},{1... | collective-permute-start | bytes 860168 | tf_op jit(solution)/shard_map/ppermute | solution.py:489
  52.5 10.8 %collective-permute-start.21 = (bf16[224,768]{1,0:T(8,128)(2,1)S(1)}, bf16[224,768]{1,0:T(8,128)(2,1)S(1)}, u32[]{:S(2)}, u32[]{:S(2)}) collective-permute-start(bf16[224,768]{1,0:T(8,128)(2,1)S(1)} %get-tuple-element.167), channel_id=1, source_target_pairs={{4,8},{8,4},{5,9},{9,5},{6,10},{10,6},{7,11},{11,7},{20,24},{24,20... | collective-permute-start | bytes 1032200 | tf_op jit(solution)/shard_map/ppermute | solution.py:494
  62.6 9.8 %collective-permute-start.19 = (bf16[224,640]{1,0:T(8,128)(2,1)S(1)}, bf16[224,640]{1,0:T(8,128)(2,1)S(1)}, u32[]{:S(2)}, u32[]{:S(2)}) collective-permute-start(bf16[224,640]{1,0:T(8,128)(2,1)S(1)} %get-tuple-element.164), channel_id=1, source_target_pairs={{4,8},{8,4},{5,9},{9,5},{6,10},{10,6},{7,11},{11,7},{20,24},{24,20... | collective-permute-start | bytes 860168 | tf_op jit(solution)/shard_map/ppermute | solution.py:494
  63.4 15.7 %collective-permute-start.24 = (bf16[224,768]{1,0:T(8,128)(2,1)S(1)}, bf16[224,768]{1,0:T(8,128)(2,1)S(1)}, u32[]{:S(2)}, u32[]{:S(2)}) collective-permute-start(bf16[224,768]{1,0:T(8,128)(2,1)S(1)} %get-tuple-element.175), channel_id=1, source_target_pairs={{0,4},{4,0},{8,12},{12,8},{1,5},{5,1},{9,13},{13,9},{2,6},{6,2},{1... | collective-permute-start | bytes 1032200 | tf_op jit(solution)/shard_map/ppermute | solution.py:489
  72.5 12.8 %collective-permute-start.22 = (bf16[224,640]{1,0:T(8,128)(2,1)S(1)}, bf16[224,640]{1,0:T(8,128)(2,1)S(1)}, u32[]{:S(2)}, u32[]{:S(2)}) collective-permute-start(bf16[224,640]{1,0:T(8,128)(2,1)S(1)} %get-tuple-element.171), channel_id=1, source_target_pairs={{0,4},{4,0},{8,12},{12,8},{1,5},{5,1},{9,13},{13,9},{2,6},{6,2},{1... | collective-permute-start | bytes 860168 | tf_op jit(solution)/shard_map/ppermute | solution.py:489
  80.9 11.0 %collective-permute-start.26 = (bf16[224,640]{1,0:T(8,128)(2,1)S(1)}, bf16[224,640]{1,0:T(8,128)(2,1)S(1)}, u32[]{:S(2)}, u32[]{:S(2)}) collective-permute-start(bf16[224,640]{1,0:T(8,128)(2,1)S(1)} %get-tuple-element.185), channel_id=1, source_target_pairs={{0,4},{4,0},{8,12},{12,8},{1,5},{5,1},{9,13},{13,9},{2,6},{6,2},{1... | collective-permute-start | bytes 860168 | tf_op jit(solution)/shard_map/ppermute | solution.py:489
  87.3 11.9 %collective-permute-start.30 = (bf16[224,768]{1,0:T(8,128)(2,1)S(1)}, bf16[224,768]{1,0:T(8,128)(2,1)S(1)}, u32[]{:S(2)}, u32[]{:S(2)}) collective-permute-start(bf16[224,768]{1,0:T(8,128)(2,1)S(1)} %get-tuple-element.199), channel_id=1, source_target_pairs={{0,4},{4,0},{8,12},{12,8},{1,5},{5,1},{9,13},{13,9},{2,6},{6,2},{1... | collective-permute-start | bytes 1032200 | tf_op jit(solution)/shard_map/ppermute | solution.py:489
  93.7 11.7 %collective-permute-start.28 = (bf16[224,640]{1,0:T(8,128)(2,1)S(1)}, bf16[224,640]{1,0:T(8,128)(2,1)S(1)}, u32[]{:S(2)}, u32[]{:S(2)}) collective-permute-start(bf16[224,640]{1,0:T(8,128)(2,1)S(1)} %get-tuple-element.197), channel_id=1, source_target_pairs={{0,4},{4,0},{8,12},{12,8},{1,5},{5,1},{9,13},{13,9},{2,6},{6,2},{1... | collective-permute-start | bytes 860168 | tf_op jit(solution)/shard_map/ppermute | solution.py:489
  101.1 12.2 %collective-permute-start.32 = (bf16[224,640]{1,0:T(8,128)(2,1)S(1)}, bf16[224,640]{1,0:T(8,128)(2,1)S(1)}, u32[]{:S(2)}, u32[]{:S(2)}) collective-permute-start(bf16[224,640]{1,0:T(8,128)(2,1)S(1)} %get-tuple-element.210), channel_id=1, source_target_pairs={{0,4},{4,0},{8,12},{12,8},{1,5},{5,1},{9,13},{13,9},{2,6},{6,2},{1... | collective-permute-start | bytes 860168 | tf_op jit(solution)/shard_map/ppermute | solution.py:489
  107.2 12.8 %collective-permute-start.35 = (bf16[224,768]{1,0:T(8,128)(2,1)S(1)}, bf16[224,768]{1,0:T(8,128)(2,1)S(1)}, u32[]{:S(2)}, u32[]{:S(2)}) collective-permute-start(bf16[224,768]{1,0:T(8,128)(2,1)S(1)} %get-tuple-element.221), channel_id=1, source_target_pairs={{0,4},{4,0},{8,12},{12,8},{1,5},{5,1},{9,13},{13,9},{2,6},{6,2},{1... | collective-permute-start | bytes 1032200 | tf_op jit(solution)/shard_map/ppermute | solution.py:489
  (26 other events, 209.8 us)

commit v8 on v7

--- a/solution.py
+++ b/solution.py
@@ -18,8 +18,9 @@
 MIB = 1024 * 1024
 HOP_WORK = 8000
 FIRST_HOP_WORK = 8000
-BASE_WORK = 400000
+BASE_WORK = 50000
 PREPARE_MIB = 60
+SPLIT = 3
 DELTA_AT = 3
 
 
@@ -237,17 +238,13 @@
     feat = down.shape[1]
     rows = parts[0].shape[0]
     half = blocks // 2
-    maps = down[...]
-    folds = [fold(rank, adapters, h) for h in range(2)]
-    for k in range(half):
-        total = None
-        for h in range(2):
-            part = parts[h * half + k]
-            wide = dot_cols(part[:, :feat], maps)
-            kept = jnp.where(slot_mask(part[:, feat : feat + 1], rank, adapters), wide, 0.0)
-            got = dot(kept.astype(BF16), folds[h])
-            total = got if total is None else total + got
-        low[k * rows : (k + 1) * rows, :] = total.astype(BF16)
+    tall = jnp.concatenate([part[:, :feat] for part in parts], axis=0)
+    tags = jnp.concatenate([part[:, feat:] for part in parts], axis=0)
+    wide = dot_cols(tall, down[...])
+    kept = jnp.where(slot_mask(tags[:, :1], rank, adapters), wide, 0.0).astype(BF16)
+    cut = half * rows
+    total = dot(kept[:cut], fold(rank, adapters, 0)) + dot(kept[cut:], fold(rank, adapters, 1))
+    low[...] = total.astype(BF16)
 
 
 def low_values(parts, down, rank, token):
@@ -267,59 +264,60 @@
     )(down, *parts, token)
 
 
-def delta_kernel(rank, blocks, sums, up, *refs):
+def delta_kernel(rank, blocks, sums, pieces, up, *refs):
     tags, lows, outs = refs[:blocks], refs[blocks : blocks + sums], refs[blocks + sums + 1 :]
     adapters = up.shape[0] // rank
     rows = tags[0].shape[0]
-    half = blocks // 2
+    widths = sum(pieces, ())
     total = lows[0][...].astype(F32)
     for other in lows[1:]:
         total = total + other[...].astype(F32)
     low = total.astype(BF16)
-    maps = up[...]
-    for h in range(2):
-        spread = fold(rank, adapters, h)
-        for k in range(half):
-            wide = dot_cols(low[k * rows : (k + 1) * rows, :], spread)
-            mask = slot_mask(tags[h * half + k][:, :1], rank, adapters)
-            kept = jnp.where(mask, wide, 0.0).astype(BF16)
-            outs[h * half + k][...] = dot(kept, maps).astype(BF16)
-
-
-def delta_values(parts, lows, up, rank, token):
+    wide = jnp.concatenate([dot_cols(low, fold(rank, adapters, h)) for h in range(2)], axis=0)
+    tag = jnp.concatenate([block[...] for block in tags], axis=0)
+    kept = jnp.where(slot_mask(tag[:, :1], rank, adapters), wide, 0.0).astype(BF16)
+    j = 0
+    for i, piece in enumerate(pieces):
+        at = 0
+        for width in piece:
+            made = dot(kept, up[:, pl.ds(column_at(j, widths), width)]).astype(BF16)
+            for k in range(blocks):
+                outs[i * blocks + k][:, at : at + width] = made[k * rows : (k + 1) * rows]
+            j, at = j + 1, at + width
+
+
+def delta_values(parts, lows, up, rank, pieces, token):
     rows, width = parts[0].shape
     blocks = len(parts)
-    columns = up.shape[1]
     tag = pl.BlockSpec((rows, TAG), lambda i: (0, width // TAG - 1))
     whole = lambda a: pl.BlockSpec(a.shape, lambda i: (0, 0))
-    return pl.pallas_call(
-        functools.partial(delta_kernel, rank, blocks, len(lows)),
-        out_shape=[jax.ShapeDtypeStruct((rows, columns), BF16)] * blocks
+    sizes = [sum(piece) for piece in pieces for _ in range(blocks)]
+    *made, token = pl.pallas_call(
+        functools.partial(delta_kernel, rank, blocks, len(lows), pieces),
+        out_shape=[jax.ShapeDtypeStruct((rows, size), BF16) for size in sizes]
         + [jax.ShapeDtypeStruct(token.shape, token.dtype)],
         grid=(1,),
         in_specs=[whole(up)] + [tag] * blocks + [whole(a) for a in lows] + [ANY],
-        out_specs=[pl.BlockSpec((rows, columns), lambda i: (0, 0))] * blocks + [ANY],
-        input_output_aliases={1 + blocks + len(lows): blocks},
+        out_specs=[pl.BlockSpec((rows, size), lambda i: (0, 0)) for size in sizes] + [ANY],
+        input_output_aliases={1 + blocks + len(lows): len(sizes)},
         compiler_params=params(),
         name="delta",
     )(up, *parts, *lows, token)
+    return [made[i * blocks : (i + 1) * blocks] for i in range(len(pieces))], token
 
 
 def add_delta_kernel(per, place, *refs):
     bases, refs = refs[: 2 * per], refs[2 * per :]
     outs, parts = refs[-2 * per - 1 : -1], refs[: -2 * per - 2]
-    rows = parts[0].shape[0]
     inner = is_inner()
-    widths = tuple(base.shape[1] for base in bases[:per])
+    column = 0
     for j in range(per):
-        column = column_at(j, widths)
-        total = None
-        for k, part in enumerate(parts):
-            got = dot(place[:, k * rows : (k + 1) * rows], part[:, pl.ds(column, widths[j])])
-            total = got if total is None else total + got
+        width = bases[j].shape[1]
+        total = dot(place[...], jnp.concatenate([part[:, column : column + width] for part in parts], axis=0))
         for i, mine in ((j, inner), (per + j, jnp.logical_not(inner))):
             wide = bases[i][...].astype(F32)
             outs[i][...] = (wide + jnp.where(mine, total, 0.0)).astype(BF16)
+        column = column + width
 
 
 def add_delta(bases, place, parts, token):
@@ -437,7 +435,7 @@
         base = dot(compact_x, weight)
         parts = send_groups(blocks)
         low, token = low_values(parts, down, rank, token)
-        *made, token = delta_values(parts, send_lows(low), up, rank, token)
+        (made,), token = delta_values(parts, send_lows(low), up, rank, ((share,),), token)
         back = jnp.concatenate(send_back(made), axis=0)
         mine = lax.dynamic_slice_in_dim(base, z * share, share, 1) + dot(place, back)
         base = lax.dynamic_update_slice_in_dim(base, mine, z * share, 1).astype(BF16)
@@ -460,9 +458,11 @@
         evens[step] = lax.ppermute(bases[step], "tensor", even)
     message, token = hop(odd_hop_kernel, [bases[chunks - 1], evens[0]], token, FIRST_HOP_WORK)
     odds[1] = lax.ppermute(message, "tensor", odd)
-    rest = tuple(range(3, chunks - 1))
-    *late, token = base_chunks(rest, widths, compact_x, weight, token)
-    bases.update(zip(rest, late))
+    second = tuple(q for q in range(chunks) if q not in bases and (q <= DELTA_AT or q >= chunks - DELTA_AT))
+    *late, token = base_chunks(second, widths, compact_x, weight, token)
+    bases.update(zip(second, late))
+    rest = tuple(q for q in range(chunks) if q not in bases)
+    pieces = (widths[:SPLIT], widths[SPLIT:per]) if SPLIT < per else (widths[:per],)
     low, token = low_values(parts, down, rank, token)
     lows = send_lows(low)
     steps = chunks + 3
@@ -494,11 +494,15 @@
             odds[step] = lax.ppermute(message, "tensor", odd)
         seen_even.add(step - 1)
         if step == DELTA_AT:
-            *made, token = delta_values(parts, lows, up, rank, token)
-            back = send_back(made)
-        if step == per + 2:
-            own = list(range(per, 2 * per)) + list(range(3 * per, 4 * per))
-            *summed, token = add_delta([bases[q] for q in own], place, back, token)
+            *late, token = base_chunks(rest, widths, compact_x, weight, token)
+            bases.update(zip(rest, late))
+            made, token = delta_values(parts, lows, up, rank, pieces, token)
+            back = [send_back(blocks) for blocks in made]
+        if 0 <= step - (per + 2) < len(pieces):
+            i = step - (per + 2)
+            here = range(sum(map(len, pieces[:i])), sum(map(len, pieces[: i + 1])))
+            own = [per + j for j in here] + [3 * per + j for j in here]
+            *summed, token = add_delta([bases[q] for q in own], place, back[i], token)
             for q, value in zip(own, summed):
                 bases[q] = value
         result, token = close(result, token)

time: 125 us -> 120 us (0.960)
  starting transfers between devices: 62.5 us -> 58.1 us
  Pallas kernels: 33.3 us -> 31.8 us
    ppermute x12, waiting for transfers between devices: 15.1 us -> 21.8 us  [on_device(): evens[step] = lax.ppermute(message, 'tensor', even)]
    ppermute x3, waiting for transfers between devices: 5.53 us -> 0.24 us  [send_lows(): lows.append(lax.ppermute(low, 'tensor', hops))]
    ppermute x12, starting transfers between devices: 36.8 us -> 32.3 us  [on_device(): evens[step] = lax.ppermute(message, 'tensor', even)]
    pallas_call x2 -> x3, Pallas kernels: 10 us -> 11.5 us  [base_chunks(): pl.pallas_call(functools.partial(base_kernel, places, widths), out_shape=...]
  transfers between devices with their start and end apart: 36 -> 36, of which waited for: 10 -> 11; matrix products, arithmetic and copies ran while one was open for 0% -> 0% of each run, Pallas kernels for 24% -> 23%
where the time goes in v8:
time: 120 us; the launch traced here: 119 us
  starting transfers between devices  58.1 us (48%)
  Pallas kernels  31.8 us (26%)
  waiting for transfers between devices  27.3 us (23%)
    ppermute x12, starting transfers between devices, on_device(): evens[step] = lax.ppermute(message, 'tensor', even)  32.3 us
    ppermute x12, waiting for transfers between devices, on_device(): evens[step] = lax.ppermute(message, 'tensor', even)  21.8 us
    pallas_call x15, Pallas kernels, finish(): pl.pallas_call(functools.partial(finish_kernel, widths, near_q, far_q), o...  12 us
    pallas_call x3, Pallas kernels, base_chunks(): pl.pallas_call(functools.partial(base_kernel, places, widths), out_shape=...  11.5 us
    ppermute x11, starting transfers between devices, on_device(): odds[step] = lax.ppermute(message, 'tensor', odd)  7.61 us
    ppermute x3, waiting for transfers between devices, send_back(): back.append(lax.ppermute(made[k], 'replica', hops))  5.19 us
    ppermute x3, starting transfers between devices, send_lows(): lows.append(lax.ppermute(low, 'tensor', hops))  4.8 us
    ppermute x2, starting transfers between devices, on_device(): evens[step] = lax.ppermute(bases[step], 'tensor', even)  4.53 us
  transfers between devices with their start and end apart: 36, of which 11 were waited for; matrix products, arithmetic and copies ran while one was open for 0% of the time, Pallas kernels for 23%

profile of v8, /device:TPU:0, one launch (start us, length us, event | category | flops | bytes accessed | tf_op | source)
XLA Modules:
  0.0 119.1 jit_solution(16856656275621269842)
XLA Ops:
  0.0 3.0 %prepare.1 = (bf16[224,1024]{1,0:T(8,128)(2,1)}, bf16[256,224]{1,0:T(8,128)(2,1)}, bf16[224,256]{1,0:T(8,128)(2,1)}, bf16[64,1152]{1,0:T(8,128)(2,1)}, bf16[64,1...) custom-call(s32[16]{0:T(128)} %bitcast.6, s32[16]{0:T(128)} %slot_in.1, ...), custom_call_target="tpu_custom_call" | custom-call | tf_op jit(solution)/shard_map/prepare/pallas_call | solution.py:152
  3.0 3.1 %collective-permute-start = (bf16[224,640]{1,0:T(8,128)(2,1)}, bf16[224,640]{1,0:T(8,128)(2,1)S(1)}, u32[]{:S(2)}, u32[]{:S(2)}) collective-permute-start(bf16[224,640]{1,0:T(8,128)(2,1)} %get-tuple-element.118.near.base.refs_0_), channel_id=1, source_target_pairs={{0,4},{4,0},{8,12},{12,8},{1,5},{5,1},{9,13},{13,9},{2,6},{6,2},{1... | collective-permute-start | bytes 860168 | tf_op jit(solution)/shard_map/ppermute | solution.py:452
  7.2 3.3 %base.3 = (bf16[224,768]{1,0:T(8,128)(2,1)S(1)}, bf16[224,640]{1,0:T(8,128)(2,1)S(1)}, bf16[224,640]{1,0:T(8,128)(2,1)S(1)}, s32[8,128]{1,0:T(8,128)S(1)}) custom-call(bf16[224,1024]{1,0:T(8,128)(2,1)S(1)} %copy-done.1, bf16[1024,8192]{1,0:T(8,128)(2,1)} %w.5, s32[8,128]{1,0:T(8,128)S(1)} %broadcast_in_dim.3.token_in), custom_call_target="tpu_custom_call", output_to_operand_aliasing={{3}: (2, {})} | custom-call | flops 102400000 | bytes 4096 | tf_op jit(solution)/shard_map/base/pallas_call | solution.py:181
  14.8 3.3 %base.4 = (bf16[224,640]{1,0:T(8,128)(2,1)S(1)}, bf16[224,640]{1,0:T(8,128)(2,1)S(1)}, bf16[224,768]{1,0:T(8,128)(2,1)S(1)}, s32[8,128]{1,0:T(8,128)S(1)}) custom-call(bf16[224,1024]{1,0:T(8,128)(2,1)S(1)} %copy-done.2, bf16[1024,8192]{1,0:T(8,128)(2,1)} %w.5, s32[8,128]{1,0:T(8,128)S(1)} %get-tuple-element.123.token_in), custom_call_target="tpu_custom_call", output_to_operand_aliasing={{3}: (2, {})} | custom-call | flops 102400000 | bytes 4096 | tf_op jit(solution)/shard_map/base/pallas_call | solution.py:181
  18.1 4.4 %collective-permute-start.1 = (bf16[224,640]{1,0:T(8,128)(2,1)S(1)}, bf16[224,640]{1,0:T(8,128)(2,1)S(1)}, u32[]{:S(2)}, u32[]{:S(2)}) collective-permute-start(bf16[224,640]{1,0:T(8,128)(2,1)S(1)} %get-tuple-element.126.near.base.refs_0_), channel_id=1, source_target_pairs={{0,4},{4,0},{8,12},{12,8},{1,5},{5,1},{9,13},{13,9},{2,6},{6,2},{1... | collective-permute-start | bytes 860168 | tf_op jit(solution)/shard_map/ppermute | solution.py:458
  24.0 1.9 %collective-permute-start.9 = (bf16[128,128]{1,0:T(8,128)(2,1)S(1)}, bf16[128,128]{1,0:T(8,128)(2,1)S(1)}, u32[]{:S(2)}, u32[]{:S(2)}) collective-permute-start(bf16[128,128]{1,0:T(8,128)(2,1)S(1)} %get-tuple-element.141.refs_4_), channel_id=1, source_target_pairs={{0,12},{4,0},{8,4},{12,8},{1,13},{5,1},{9,5},{13,9},{2,14},{6,2},{... | collective-permute-start | bytes 98312 | tf_op jit(solution)/shard_map/ppermute | solution.py:413
  28.9 2.2 %collective-permute-start.16 = (bf16[224,640]{1,0:T(8,128)(2,1)S(1)}, bf16[224,640]{1,0:T(8,128)(2,1)S(1)}, u32[]{:S(2)}, u32[]{:S(2)}) collective-permute-start(bf16[224,640]{1,0:T(8,128)(2,1)S(1)} %get-tuple-element.153), channel_id=1, source_target_pairs={{0,4},{4,0},{8,12},{12,8},{1,5},{5,1},{9,13},{13,9},{2,6},{6,2},{1... | collective-permute-start | bytes 860168 | tf_op jit(solution)/shard_map/ppermute | solution.py:489
  31.2 4.8 %base.5 = (bf16[224,768]{1,0:T(8,128)(2,1)S(1)}, bf16[224,640]{1,0:T(8,128)(2,1)S(1)}, bf16[224,640]{1,0:T(8,128)(2,1)S(1)}, bf16[224,768]{1,0:T(8,128)(2,1)S(1)...) custom-call(bf16[224,1024]{1,0:T(8,128)(2,1)S(1)} %copy-done.2, ...), custom_call_target="tpu_custom_call", output_to_operand_aliasing={{5}: (2, {})} | custom-call | flops 172800000 | bytes 6912 | tf_op jit(solution)/shard_map/base/pallas_call | solution.py:181
  38.0 2.9 %collective-permute-start.14 = (bf16[224,768]{1,0:T(8,128)(2,1)S(1)}, bf16[224,768]{1,0:T(8,128)(2,1)S(1)}, u32[]{:S(2)}, u32[]{:S(2)}) collective-permute-start(bf16[224,768]{1,0:T(8,128)(2,1)S(1)} %get-tuple-element.150), channel_id=1, source_target_pairs={{0,4},{4,0},{8,12},{12,8},{1,5},{5,1},{9,13},{13,9},{2,6},{6,2},{1... | collective-permute-start | bytes 1032200 | tf_op jit(solution)/shard_map/ppermute | solution.py:489
  43.4 4.0 %collective-permute-done.14.got.refs_2_ = bf16[224,768]{1,0:T(8,128)(2,1)S(1)} collective-permute-done((bf16[224,768]{1,0:T(8,128)(2,1)S(1)}, bf16[224,768]{1,0:T(8,128)(2,1)S(1)}, u32[]{:S(2)}, u32[]{:S(2)}) %collective-permute-start.14) | collective-permute-done | bytes 344096 | tf_op jit(solution)/shard_map/ppermute | solution.py:489
  50.0 5.1 %collective-permute-done.11.refs_8_ = bf16[64,2048]{1,0:T(8,128)(2,1)S(1)} collective-permute-done((bf16[64,2048]{1,0:T(8,128)(2,1)S(1)}, bf16[64,2048]{1,0:T(8,128)(2,1)S(1)}, u32[]{:S(2)}, u32[]{:S(2)}) %collective-permute-start.11) | collective-permute-done | bytes 262176 | tf_op jit(solution)/shard_map/ppermute | solution.py:422
  55.1 2.4 %add_delta.1 = (bf16[224,640]{1,0:T(8,128)(2,1)S(1)}, bf16[224,768]{1,0:T(8,128)(2,1)S(1)}, bf16[224,640]{1,0:T(8,128)(2,1)S(1)}, bf16[224,640]{1,0:T(8,128)(2,1...) custom-call(bf16[224,256]{1,0:T(8,128)(2,1)S(1)} %copy-done.10, ...), custom_call_target="tpu_custom_call", output_to_operand_aliasing={{6}: (11, {})} | custom-call | tf_op jit(solution)/shard_map/add_delta/pallas_call | solution.py:326
  58.6 4.5 %collective-permute-start.24 = (bf16[224,768]{1,0:T(8,128)(2,1)S(1)}, bf16[224,768]{1,0:T(8,128)(2,1)S(1)}, u32[]{:S(2)}, u32[]{:S(2)}) collective-permute-start(bf16[224,768]{1,0:T(8,128)(2,1)S(1)} %get-tuple-element.177), channel_id=1, source_target_pairs={{0,4},{4,0},{8,12},{12,8},{1,5},{5,1},{9,13},{13,9},{2,6},{6,2},{1... | collective-permute-start | bytes 1032200 | tf_op jit(solution)/shard_map/ppermute | solution.py:489
  63.1 3.8 %collective-permute-done.20.got.refs_2_ = bf16[224,640]{1,0:T(8,128)(2,1)S(1)} collective-permute-done((bf16[224,640]{1,0:T(8,128)(2,1)S(1)}, bf16[224,640]{1,0:T(8,128)(2,1)S(1)}, u32[]{:S(2)}, u32[]{:S(2)}) %collective-permute-start.20) | collective-permute-done | bytes 286752 | tf_op jit(solution)/shard_map/ppermute | solution.py:489
  67.7 2.0 %collective-permute-start.22 = (bf16[224,640]{1,0:T(8,128)(2,1)S(1)}, bf16[224,640]{1,0:T(8,128)(2,1)S(1)}, u32[]{:S(2)}, u32[]{:S(2)}) collective-permute-start(bf16[224,640]{1,0:T(8,128)(2,1)S(1)} %get-tuple-element.173), channel_id=1, source_target_pairs={{0,4},{4,0},{8,12},{12,8},{1,5},{5,1},{9,13},{13,9},{2,6},{6,2},{1... | collective-permute-start | bytes 860168 | tf_op jit(solution)/shard_map/ppermute | solution.py:489
  70.7 3.5 %collective-permute-done.24.got.refs_2_ = bf16[224,768]{1,0:T(8,128)(2,1)S(1)} collective-permute-done((bf16[224,768]{1,0:T(8,128)(2,1)S(1)}, bf16[224,768]{1,0:T(8,128)(2,1)S(1)}, u32[]{:S(2)}, u32[]{:S(2)}) %collective-permute-start.24) | collective-permute-done | bytes 344096 | tf_op jit(solution)/shard_map/ppermute | solution.py:489
  76.1 1.9 %collective-permute-start.26 = (bf16[224,640]{1,0:T(8,128)(2,1)S(1)}, bf16[224,640]{1,0:T(8,128)(2,1)S(1)}, u32[]{:S(2)}, u32[]{:S(2)}) collective-permute-start(bf16[224,640]{1,0:T(8,128)(2,1)S(1)} %get-tuple-element.187), channel_id=1, source_target_pairs={{0,4},{4,0},{8,12},{12,8},{1,5},{5,1},{9,13},{13,9},{2,6},{6,2},{1... | collective-permute-start | bytes 860168 | tf_op jit(solution)/shard_map/ppermute | solution.py:489
  81.9 3.5 %collective-permute-start.30 = (bf16[224,768]{1,0:T(8,128)(2,1)S(1)}, bf16[224,768]{1,0:T(8,128)(2,1)S(1)}, u32[]{:S(2)}, u32[]{:S(2)}) collective-permute-start(bf16[224,768]{1,0:T(8,128)(2,1)S(1)} %get-tuple-element.201), channel_id=1, source_target_pairs={{0,4},{4,0},{8,12},{12,8},{1,5},{5,1},{9,13},{13,9},{2,6},{6,2},{1... | collective-permute-start | bytes 1032200 | tf_op jit(solution)/shard_map/ppermute | solution.py:489
  88.3 3.3 %collective-permute-start.28 = (bf16[224,640]{1,0:T(8,128)(2,1)S(1)}, bf16[224,640]{1,0:T(8,128)(2,1)S(1)}, u32[]{:S(2)}, u32[]{:S(2)}) collective-permute-start(bf16[224,640]{1,0:T(8,128)(2,1)S(1)} %get-tuple-element.199), channel_id=1, source_target_pairs={{0,4},{4,0},{8,12},{12,8},{1,5},{5,1},{9,13},{13,9},{2,6},{6,2},{1... | collective-permute-start | bytes 860168 | tf_op jit(solution)/shard_map/ppermute | solution.py:489
  96.3 3.1 %collective-permute-start.32 = (bf16[224,640]{1,0:T(8,128)(2,1)S(1)}, bf16[224,640]{1,0:T(8,128)(2,1)S(1)}, u32[]{:S(2)}, u32[]{:S(2)}) collective-permute-start(bf16[224,640]{1,0:T(8,128)(2,1)S(1)} %get-tuple-element.212), channel_id=1, source_target_pairs={{0,4},{4,0},{8,12},{12,8},{1,5},{5,1},{9,13},{13,9},{2,6},{6,2},{1... | collective-permute-start | bytes 860168 | tf_op jit(solution)/shard_map/ppermute | solution.py:489
  102.4 5.0 %collective-permute-start.35 = (bf16[224,768]{1,0:T(8,128)(2,1)S(1)}, bf16[224,768]{1,0:T(8,128)(2,1)S(1)}, u32[]{:S(2)}, u32[]{:S(2)}) collective-permute-start(bf16[224,768]{1,0:T(8,128)(2,1)S(1)} %get-tuple-element.223), channel_id=1, source_target_pairs={{0,4},{4,0},{8,12},{12,8},{1,5},{5,1},{9,13},{13,9},{2,6},{6,2},{1... | collective-permute-start | bytes 1032200 | tf_op jit(solution)/shard_map/ppermute | solution.py:489
  108.5 2.0 %collective-permute-start.34 = (bf16[224,640]{1,0:T(8,128)(2,1)S(1)}, bf16[224,640]{1,0:T(8,128)(2,1)S(1)}, u32[]{:S(2)}, u32[]{:S(2)}) collective-permute-start(bf16[224,640]{1,0:T(8,128)(2,1)S(1)} %get-tuple-element.222), channel_id=1, source_target_pairs={{0,4},{4,0},{8,12},{12,8},{1,5},{5,1},{9,13},{13,9},{2,6},{6,2},{1... | collective-permute-start | bytes 860168 | tf_op jit(solution)/shard_map/ppermute | solution.py:489
  110.5 4.5 %collective-permute-done.35.refs_1_ = bf16[224,768]{1,0:T(8,128)(2,1)S(1)} collective-permute-done((bf16[224,768]{1,0:T(8,128)(2,1)S(1)}, bf16[224,768]{1,0:T(8,128)(2,1)S(1)}, u32[]{:S(2)}, u32[]{:S(2)}) %collective-permute-start.35) | collective-permute-done | bytes 344096 | tf_op jit(solution)/shard_map/ppermute | solution.py:489
  116.0 2.0 %collective-permute-done.34.refs_1_ = bf16[224,640]{1,0:T(8,128)(2,1)S(1)} collective-permute-done((bf16[224,640]{1,0:T(8,128)(2,1)S(1)}, bf16[224,640]{1,0:T(8,128)(2,1)S(1)}, u32[]{:S(2)}, u32[]{:S(2)}) %collective-permute-start.34) | collective-permute-done | bytes 286752 | tf_op jit(solution)/shard_map/ppermute | solution.py:489
  (123 shorter events, 38.7 us)
Async XLA Ops:
  3.0 10.9 %collective-permute-start = (bf16[224,640]{1,0:T(8,128)(2,1)}, bf16[224,640]{1,0:T(8,128)(2,1)S(1)}, u32[]{:S(2)}, u32[]{:S(2)}) collective-permute-start(bf16[224,640]{1,0:T(8,128)(2,1)} %get-tuple-element.118.near.base.refs_0_), channel_id=1, source_target_pairs={{0,4},{4,0},{8,12},{12,8},{1,5},{5,1},{9,13},{13,9},{2,6},{6,2},{1... | collective-permute-start | bytes 860168 | tf_op jit(solution)/shard_map/ppermute | solution.py:452
  10.5 12.7 %collective-permute-start.3 = (bf16[224,768]{1,0:T(8,128)(2,1)S(1)}, bf16[224,768]{1,0:T(8,128)(2,1)S(1)}, u32[]{:S(2)}, u32[]{:S(2)}) collective-permute-start(bf16[224,768]{1,0:T(8,128)(2,1)S(1)} %get-tuple-element.129.near.base.refs_0_), channel_id=1, source_target_pairs={{0,4},{4,0},{8,12},{12,8},{1,5},{5,1},{9,13},{13,9},{2,6},{6,2},{1... | collective-permute-start | bytes 1032200 | tf_op jit(solution)/shard_map/ppermute | solution.py:458
  10.6 11.9 %collective-permute-start.5 = (bf16[64,1152]{1,0:T(8,128)(2,1)S(1)}, bf16[64,1152]{1,0:T(8,128)(2,1)S(1)}, u32[]{:S(2)}, u32[]{:S(2)}) collective-permute-start(bf16[64,1152]{1,0:T(8,128)(2,1)S(1)} %copy-done.12), channel_id=1, source_target_pairs={{0,2},{1,3},{2,0},{3,1},{4,6},{5,7},{6,4},{7,5},{8,10},{9,11},{10,... | collective-permute-start | bytes 442376 | tf_op jit(solution)/shard_map/ppermute | solution.py:402
  12.6 10.0 %collective-permute-start.6 = (bf16[64,1152]{1,0:T(8,128)(2,1)S(1)}, bf16[64,1152]{1,0:T(8,128)(2,1)S(1)}, u32[]{:S(2)}, u32[]{:S(2)}) collective-permute-start(bf16[64,1152]{1,0:T(8,128)(2,1)S(1)} %copy-done.11), channel_id=1, source_target_pairs={{0,3},{1,0},{2,1},{3,2},{4,7},{5,4},{6,5},{7,6},{8,11},{9,8},{10,9... | collective-permute-start | bytes 442376 | tf_op jit(solution)/shard_map/ppermute | solution.py:402
  14.0 13.7 %collective-permute-start.2 = (bf16[224,640]{1,0:T(8,128)(2,1)S(1)}, bf16[224,640]{1,0:T(8,128)(2,1)S(1)}, u32[]{:S(2)}, u32[]{:S(2)}) collective-permute-start(bf16[224,640]{1,0:T(8,128)(2,1)S(1)} %get-tuple-element.127), channel_id=1, source_target_pairs={{4,8},{8,4},{5,9},{9,5},{6,10},{10,6},{7,11},{11,7},{20,24},{24,20... | collective-permute-start | bytes 860168 | tf_op jit(solution)/shard_map/ppermute | solution.py:460
  18.1 10.8 %collective-permute-start.1 = (bf16[224,640]{1,0:T(8,128)(2,1)S(1)}, bf16[224,640]{1,0:T(8,128)(2,1)S(1)}, u32[]{:S(2)}, u32[]{:S(2)}) collective-permute-start(bf16[224,640]{1,0:T(8,128)(2,1)S(1)} %get-tuple-element.126.near.base.refs_0_), channel_id=1, source_target_pairs={{0,4},{4,0},{8,12},{12,8},{1,5},{5,1},{9,13},{13,9},{2,6},{6,2},{1... | collective-permute-start | bytes 860168 | tf_op jit(solution)/shard_map/ppermute | solution.py:458
  23.3 14.6 %collective-permute-start.13 = (bf16[224,768]{1,0:T(8,128)(2,1)S(1)}, bf16[224,768]{1,0:T(8,128)(2,1)S(1)}, u32[]{:S(2)}, u32[]{:S(2)}) collective-permute-start(bf16[224,768]{1,0:T(8,128)(2,1)S(1)} %get-tuple-element.148), channel_id=1, source_target_pairs={{4,8},{8,4},{5,9},{9,5},{6,10},{10,6},{7,11},{11,7},{20,24},{24,20... | collective-permute-start | bytes 1032200 | tf_op jit(solution)/shard_map/ppermute | solution.py:494
  24.0 12.0 %collective-permute-start.9 = (bf16[128,128]{1,0:T(8,128)(2,1)S(1)}, bf16[128,128]{1,0:T(8,128)(2,1)S(1)}, u32[]{:S(2)}, u32[]{:S(2)}) collective-permute-start(bf16[128,128]{1,0:T(8,128)(2,1)S(1)} %get-tuple-element.141.refs_4_), channel_id=1, source_target_pairs={{0,12},{4,0},{8,4},{12,8},{1,13},{5,1},{9,5},{13,9},{2,14},{6,2},{... | collective-permute-start | bytes 98312 | tf_op jit(solution)/shard_map/ppermute | solution.py:413
  25.9 11.0 %collective-permute-start.8 = (bf16[128,128]{1,0:T(8,128)(2,1)S(1)}, bf16[128,128]{1,0:T(8,128)(2,1)S(1)}, u32[]{:S(2)}, u32[]{:S(2)}) collective-permute-start(bf16[128,128]{1,0:T(8,128)(2,1)S(1)} %get-tuple-element.141.refs_4_), channel_id=1, source_target_pairs={{0,8},{4,12},{8,0},{12,4},{1,9},{5,13},{9,1},{13,5},{2,10},{6,14},... | collective-permute-start | bytes 98312 | tf_op jit(solution)/shard_map/ppermute | solution.py:413
  28.9 13.5 %collective-permute-start.16 = (bf16[224,640]{1,0:T(8,128)(2,1)S(1)}, bf16[224,640]{1,0:T(8,128)(2,1)S(1)}, u32[]{:S(2)}, u32[]{:S(2)}) collective-permute-start(bf16[224,640]{1,0:T(8,128)(2,1)S(1)} %get-tuple-element.153), channel_id=1, source_target_pairs={{0,4},{4,0},{8,12},{12,8},{1,5},{5,1},{9,13},{13,9},{2,6},{6,2},{1... | collective-permute-start | bytes 860168 | tf_op jit(solution)/shard_map/ppermute | solution.py:489
  40.9 14.2 %collective-permute-start.11 = (bf16[64,2048]{1,0:T(8,128)(2,1)S(1)}, bf16[64,2048]{1,0:T(8,128)(2,1)S(1)}, u32[]{:S(2)}, u32[]{:S(2)}) collective-permute-start(bf16[64,2048]{1,0:T(8,128)(2,1)S(1)} %get-tuple-element.145), channel_id=1, source_target_pairs={{0,2},{1,3},{2,0},{3,1},{4,6},{5,7},{6,4},{7,5},{8,10},{9,11},{10,... | collective-permute-start | bytes 786440 | tf_op jit(solution)/shard_map/ppermute | solution.py:422
  42.4 12.8 %collective-permute-start.12 = (bf16[64,2048]{1,0:T(8,128)(2,1)S(1)}, bf16[64,2048]{1,0:T(8,128)(2,1)S(1)}, u32[]{:S(2)}, u32[]{:S(2)}) collective-permute-start(bf16[64,2048]{1,0:T(8,128)(2,1)S(1)} %get-tuple-element.146), channel_id=1, source_target_pairs={{0,1},{1,2},{2,3},{3,0},{4,5},{5,6},{6,7},{7,4},{8,9},{9,10},{10,1... | collective-permute-start | bytes 786440 | tf_op jit(solution)/shard_map/ppermute | solution.py:422
  42.7 14.8 %collective-permute-start.18 = (bf16[224,640]{1,0:T(8,128)(2,1)S(1)}, bf16[224,640]{1,0:T(8,128)(2,1)S(1)}, u32[]{:S(2)}, u32[]{:S(2)}) collective-permute-start(bf16[224,640]{1,0:T(8,128)(2,1)S(1)} %get-tuple-element.163), channel_id=1, source_target_pairs={{4,8},{8,4},{5,9},{9,5},{6,10},{10,6},{7,11},{11,7},{20,24},{24,20... | collective-permute-start | bytes 860168 | tf_op jit(solution)/shard_map/ppermute | solution.py:494
  47.4 10.3 %collective-permute-start.17 = (bf16[224,640]{1,0:T(8,128)(2,1)S(1)}, bf16[224,640]{1,0:T(8,128)(2,1)S(1)}, u32[]{:S(2)}, u32[]{:S(2)}) collective-permute-start(bf16[224,640]{1,0:T(8,128)(2,1)S(1)} %get-tuple-element.162), channel_id=1, source_target_pairs={{0,4},{4,0},{8,12},{12,8},{1,5},{5,1},{9,13},{13,9},{2,6},{6,2},{1... | collective-permute-start | bytes 860168 | tf_op jit(solution)/shard_map/ppermute | solution.py:489
  57.8 9.9 %collective-permute-start.19 = (bf16[224,640]{1,0:T(8,128)(2,1)S(1)}, bf16[224,640]{1,0:T(8,128)(2,1)S(1)}, u32[]{:S(2)}, u32[]{:S(2)}) collective-permute-start(bf16[224,640]{1,0:T(8,128)(2,1)S(1)} %get-tuple-element.166), channel_id=1, source_target_pairs={{4,8},{8,4},{5,9},{9,5},{6,10},{10,6},{7,11},{11,7},{20,24},{24,20... | collective-permute-start | bytes 860168 | tf_op jit(solution)/shard_map/ppermute | solution.py:494
  58.6 15.7 %collective-permute-start.24 = (bf16[224,768]{1,0:T(8,128)(2,1)S(1)}, bf16[224,768]{1,0:T(8,128)(2,1)S(1)}, u32[]{:S(2)}, u32[]{:S(2)}) collective-permute-start(bf16[224,768]{1,0:T(8,128)(2,1)S(1)} %get-tuple-element.177), channel_id=1, source_target_pairs={{0,4},{4,0},{8,12},{12,8},{1,5},{5,1},{9,13},{13,9},{2,6},{6,2},{1... | collective-permute-start | bytes 1032200 | tf_op jit(solution)/shard_map/ppermute | solution.py:489
  67.7 12.3 %collective-permute-start.22 = (bf16[224,640]{1,0:T(8,128)(2,1)S(1)}, bf16[224,640]{1,0:T(8,128)(2,1)S(1)}, u32[]{:S(2)}, u32[]{:S(2)}) collective-permute-start(bf16[224,640]{1,0:T(8,128)(2,1)S(1)} %get-tuple-element.173), channel_id=1, source_target_pairs={{0,4},{4,0},{8,12},{12,8},{1,5},{5,1},{9,13},{13,9},{2,6},{6,2},{1... | collective-permute-start | bytes 860168 | tf_op jit(solution)/shard_map/ppermute | solution.py:489
  76.1 10.3 %collective-permute-start.26 = (bf16[224,640]{1,0:T(8,128)(2,1)S(1)}, bf16[224,640]{1,0:T(8,128)(2,1)S(1)}, u32[]{:S(2)}, u32[]{:S(2)}) collective-permute-start(bf16[224,640]{1,0:T(8,128)(2,1)S(1)} %get-tuple-element.187), channel_id=1, source_target_pairs={{0,4},{4,0},{8,12},{12,8},{1,5},{5,1},{9,13},{13,9},{2,6},{6,2},{1... | collective-permute-start | bytes 860168 | tf_op jit(solution)/shard_map/ppermute | solution.py:489
  81.9 12.5 %collective-permute-start.30 = (bf16[224,768]{1,0:T(8,128)(2,1)S(1)}, bf16[224,768]{1,0:T(8,128)(2,1)S(1)}, u32[]{:S(2)}, u32[]{:S(2)}) collective-permute-start(bf16[224,768]{1,0:T(8,128)(2,1)S(1)} %get-tuple-element.201), channel_id=1, source_target_pairs={{0,4},{4,0},{8,12},{12,8},{1,5},{5,1},{9,13},{13,9},{2,6},{6,2},{1... | collective-permute-start | bytes 1032200 | tf_op jit(solution)/shard_map/ppermute | solution.py:489
  86.5 9.7 %collective-permute-start.29 = (bf16[224,640]{1,0:T(8,128)(2,1)S(1)}, bf16[224,640]{1,0:T(8,128)(2,1)S(1)}, u32[]{:S(2)}, u32[]{:S(2)}) collective-permute-start(bf16[224,640]{1,0:T(8,128)(2,1)S(1)} %get-tuple-element.200), channel_id=1, source_target_pairs={{4,8},{8,4},{5,9},{9,5},{6,10},{10,6},{7,11},{11,7},{20,24},{24,20... | collective-permute-start | bytes 860168 | tf_op jit(solution)/shard_map/ppermute | solution.py:494
  88.3 12.3 %collective-permute-start.28 = (bf16[224,640]{1,0:T(8,128)(2,1)S(1)}, bf16[224,640]{1,0:T(8,128)(2,1)S(1)}, u32[]{:S(2)}, u32[]{:S(2)}) collective-permute-start(bf16[224,640]{1,0:T(8,128)(2,1)S(1)} %get-tuple-element.199), channel_id=1, source_target_pairs={{0,4},{4,0},{8,12},{12,8},{1,5},{5,1},{9,13},{13,9},{2,6},{6,2},{1... | collective-permute-start | bytes 860168 | tf_op jit(solution)/shard_map/ppermute | solution.py:489
  96.3 11.1 %collective-permute-start.32 = (bf16[224,640]{1,0:T(8,128)(2,1)S(1)}, bf16[224,640]{1,0:T(8,128)(2,1)S(1)}, u32[]{:S(2)}, u32[]{:S(2)}) collective-permute-start(bf16[224,640]{1,0:T(8,128)(2,1)S(1)} %get-tuple-element.212), channel_id=1, source_target_pairs={{0,4},{4,0},{8,12},{12,8},{1,5},{5,1},{9,13},{13,9},{2,6},{6,2},{1... | collective-permute-start | bytes 860168 | tf_op jit(solution)/shard_map/ppermute | solution.py:489
  102.4 12.6 %collective-permute-start.35 = (bf16[224,768]{1,0:T(8,128)(2,1)S(1)}, bf16[224,768]{1,0:T(8,128)(2,1)S(1)}, u32[]{:S(2)}, u32[]{:S(2)}) collective-permute-start(bf16[224,768]{1,0:T(8,128)(2,1)S(1)} %get-tuple-element.223), channel_id=1, source_target_pairs={{0,4},{4,0},{8,12},{12,8},{1,5},{5,1},{9,13},{13,9},{2,6},{6,2},{1... | collective-permute-start | bytes 1032200 | tf_op jit(solution)/shard_map/ppermute | solution.py:489
  108.5 9.6 %collective-permute-start.34 = (bf16[224,640]{1,0:T(8,128)(2,1)S(1)}, bf16[224,640]{1,0:T(8,128)(2,1)S(1)}, u32[]{:S(2)}, u32[]{:S(2)}) collective-permute-start(bf16[224,640]{1,0:T(8,128)(2,1)S(1)} %get-tuple-element.222), channel_id=1, source_target_pairs={{0,4},{4,0},{8,12},{12,8},{1,5},{5,1},{9,13},{13,9},{2,6},{6,2},{1... | collective-permute-start | bytes 860168 | tf_op jit(solution)/shard_map/ppermute | solution.py:489
  (26 other events, 183.9 us)

commit v9 on v8

--- a/solution.py
+++ b/solution.py
@@ -20,7 +20,6 @@
 FIRST_HOP_WORK = 8000
 BASE_WORK = 50000
 PREPARE_MIB = 60
-SPLIT = 3
 DELTA_AT = 3
 
 
@@ -306,30 +305,37 @@
     return [made[i * blocks : (i + 1) * blocks] for i in range(len(pieces))], token
 
 
-def add_delta_kernel(per, place, *refs):
-    bases, refs = refs[: 2 * per], refs[2 * per :]
-    outs, parts = refs[-2 * per - 1 : -1], refs[: -2 * per - 2]
-    inner = is_inner()
-    column = 0
-    for j in range(per):
-        width = bases[j].shape[1]
-        total = dot(place[...], jnp.concatenate([part[:, column : column + width] for part in parts], axis=0))
-        for i, mine in ((j, inner), (per + j, jnp.logical_not(inner))):
-            wide = bases[i][...].astype(F32)
-            outs[i][...] = (wide + jnp.where(mine, total, 0.0)).astype(BF16)
-        column = column + width
-
-
-def add_delta(bases, place, parts, token):
-    per = len(bases) // 2
+def add_delta_kernel(start, place, *refs):
+    count = len(start) * 2
+    bases, parts, outs = refs[:count], refs[count : -count - 2], refs[-count - 1 : -1]
+
+    def add(i, j):
+        base, out = bases[i], outs[i]
+        here = slice(start[j], start[j] + base.shape[1])
+        delta = dot(place[...], jnp.concatenate([part[:, here] for part in parts], axis=0))
+        out[...] = (base[...].astype(F32) + delta).astype(BF16)
+
+    @pl.when(is_inner())
+    def _():
+        for j in range(len(start)):
+            add(j, j)
+
+    @pl.when(jnp.logical_not(is_inner()))
+    def _():
+        for j in range(len(start)):
+            add(len(start) + j, j)
+
+
+def add_delta(bases, start, place, parts, token):
     inputs = [place, *bases, *parts]
+    aliases = {1 + i: i for i in range(len(bases))}
     return pl.pallas_call(
-        functools.partial(add_delta_kernel, per),
+        functools.partial(add_delta_kernel, start),
         out_shape=[jax.ShapeDtypeStruct(base.shape, BF16) for base in bases]
         + [jax.ShapeDtypeStruct(token.shape, token.dtype)],
         in_specs=[VMEM] * len(inputs) + [ANY],
         out_specs=[VMEM] * len(bases) + [ANY],
-        input_output_aliases={len(inputs): len(bases)},
+        input_output_aliases=aliases | {len(inputs): len(bases)},
         compiler_params=params(),
         name="add_delta",
     )(*inputs, token)
@@ -459,10 +465,11 @@
     message, token = hop(odd_hop_kernel, [bases[chunks - 1], evens[0]], token, FIRST_HOP_WORK)
     odds[1] = lax.ppermute(message, "tensor", odd)
     second = tuple(q for q in range(chunks) if q not in bases and (q <= DELTA_AT or q >= chunks - DELTA_AT))
-    *late, token = base_chunks(second, widths, compact_x, weight, token)
-    bases.update(zip(second, late))
+    if second:
+        *late, token = base_chunks(second, widths, compact_x, weight, token)
+        bases.update(zip(second, late))
     rest = tuple(q for q in range(chunks) if q not in bases)
-    pieces = (widths[:SPLIT], widths[SPLIT:per]) if SPLIT < per else (widths[:per],)
+    pieces = (widths[:per],)
     low, token = low_values(parts, down, rank, token)
     lows = send_lows(low)
     steps = chunks + 3
@@ -498,13 +505,11 @@
             bases.update(zip(rest, late))
             made, token = delta_values(parts, lows, up, rank, pieces, token)
             back = [send_back(blocks) for blocks in made]
-        if 0 <= step - (per + 2) < len(pieces):
-            i = step - (per + 2)
-            here = range(sum(map(len, pieces[:i])), sum(map(len, pieces[: i + 1])))
-            own = [per + j for j in here] + [3 * per + j for j in here]
-            *summed, token = add_delta([bases[q] for q in own], place, back[i], token)
-            for q, value in zip(own, summed):
-                bases[q] = value
+        if step == per + 2:
+            own = list(range(per, 2 * per)) + list(range(3 * per, 4 * per))
+            start = tuple(sum(widths[:j]) for j in range(per))
+            *summed, token = add_delta([bases[q] for q in own], start, place, back[0], token)
+            bases.update(zip(own, summed))
         result, token = close(result, token)
     seen_even.add(steps - 1)
     result, token = close(result, token)

time: 120 us -> 118 us (0.983)
  starting transfers between devices: 58.1 us -> 67.9 us
  waiting for transfers between devices: 27.3 us -> 17.9 us
  Pallas kernels: 31.8 us -> 30.1 us
    ppermute x12, starting transfers between devices: 32.3 us -> 42.2 us  [on_device(): evens[step] = lax.ppermute(message, 'tensor', even)]
    ppermute x12, waiting for transfers between devices: 21.8 us -> 12.4 us  [on_device(): evens[step] = lax.ppermute(message, 'tensor', even)]
    pallas_call x1, Pallas kernels: 2.36 us -> 0.48 us  [add_delta(): pl.pallas_call(functools.partial(add_delta_kernel, start), out_shape=[jax...]
  transfers between devices with their start and end apart: 36 -> 36, of which waited for: 11 -> 11; matrix products, arithmetic and copies ran while one was open for 0% -> 0% of each run, Pallas kernels for 23% -> 22%
where the time goes in v9:
time: 118 us
  starting transfers between devices  67.9 us (58%)
  Pallas kernels  30.1 us (26%)
  waiting for transfers between devices  17.9 us (15%)
    ppermute x12, starting transfers between devices, on_device(): evens[step] = lax.ppermute(message, 'tensor', even)  42.2 us
    ppermute x12, waiting for transfers between devices, on_device(): evens[step] = lax.ppermute(message, 'tensor', even)  12.4 us
    pallas_call x15, Pallas kernels, finish(): pl.pallas_call(functools.partial(finish_kernel, widths, near_q, far_q), o...  12 us
    pallas_call x3, Pallas kernels, base_chunks(): pl.pallas_call(functools.partial(base_kernel, places, widths), out_shape=...  11.4 us
    ppermute x11, starting transfers between devices, on_device(): odds[step] = lax.ppermute(message, 'tensor', odd)  7.48 us
    ppermute x3, waiting for transfers between devices, send_back(): back.append(lax.ppermute(made[k], 'replica', hops))  5.16 us
    ppermute x3, starting transfers between devices, send_lows(): lows.append(lax.ppermute(low, 'tensor', hops))  4.8 us
    ppermute x2, starting transfers between devices, on_device(): evens[step] = lax.ppermute(bases[step], 'tensor', even)  4.54 us
  transfers between devices with their start and end apart: 36, of which 11 were waited for; matrix products, arithmetic and copies ran while one was open for 0% of the time, Pallas kernels for 22%

profile of v9, /device:TPU:0, one launch (start us, length us, event | category | flops | bytes accessed | tf_op | source)
XLA Modules:
  0.0 117.7 jit_solution(3581007975466225985)
XLA Ops:
  0.0 3.1 %prepare.1 = (bf16[224,1024]{1,0:T(8,128)(2,1)}, bf16[256,224]{1,0:T(8,128)(2,1)}, bf16[224,256]{1,0:T(8,128)(2,1)}, bf16[64,1152]{1,0:T(8,128)(2,1)}, bf16[64,1...) custom-call(s32[16]{0:T(128)} %bitcast.6, s32[16]{0:T(128)} %slot_in.1, ...), custom_call_target="tpu_custom_call" | custom-call | tf_op jit(solution)/shard_map/prepare/pallas_call | solution.py:151
  3.1 3.1 %collective-permute-start = (bf16[224,640]{1,0:T(8,128)(2,1)}, bf16[224,640]{1,0:T(8,128)(2,1)S(1)}, u32[]{:S(2)}, u32[]{:S(2)}) collective-permute-start(bf16[224,640]{1,0:T(8,128)(2,1)} %get-tuple-element.118.near.base.refs_0_), channel_id=1, source_target_pairs={{0,4},{4,0},{8,12},{12,8},{1,5},{5,1},{9,13},{13,9},{2,6},{6,2},{1... | collective-permute-start | bytes 860168 | tf_op jit(solution)/shard_map/ppermute | solution.py:458
  7.2 3.3 %base.3 = (bf16[224,768]{1,0:T(8,128)(2,1)S(1)}, bf16[224,640]{1,0:T(8,128)(2,1)S(1)}, bf16[224,640]{1,0:T(8,128)(2,1)S(1)}, s32[8,128]{1,0:T(8,128)S(1)}) custom-call(bf16[224,1024]{1,0:T(8,128)(2,1)S(1)} %copy-done.1, bf16[1024,8192]{1,0:T(8,128)(2,1)} %w.5, s32[8,128]{1,0:T(8,128)S(1)} %broadcast_in_dim.3.token_in), custom_call_target="tpu_custom_call", output_to_operand_aliasing={{3}: (2, {})} | custom-call | flops 102400000 | bytes 4096 | tf_op jit(solution)/shard_map/base/pallas_call | solution.py:180
  10.7 1.9 %collective-permute-start.5 = (bf16[64,1152]{1,0:T(8,128)(2,1)S(1)}, bf16[64,1152]{1,0:T(8,128)(2,1)S(1)}, u32[]{:S(2)}, u32[]{:S(2)}) collective-permute-start(bf16[64,1152]{1,0:T(8,128)(2,1)S(1)} %copy-done.9), channel_id=1, source_target_pairs={{0,2},{1,3},{2,0},{3,1},{4,6},{5,7},{6,4},{7,5},{8,10},{9,11},{10,... | collective-permute-start | bytes 442376 | tf_op jit(solution)/shard_map/ppermute | solution.py:408
  14.8 3.3 %base.4 = (bf16[224,640]{1,0:T(8,128)(2,1)S(1)}, bf16[224,640]{1,0:T(8,128)(2,1)S(1)}, bf16[224,768]{1,0:T(8,128)(2,1)S(1)}, s32[8,128]{1,0:T(8,128)S(1)}) custom-call(bf16[224,1024]{1,0:T(8,128)(2,1)S(1)} %copy-done.2, bf16[1024,8192]{1,0:T(8,128)(2,1)} %w.5, s32[8,128]{1,0:T(8,128)S(1)} %get-tuple-element.123.token_in), custom_call_target="tpu_custom_call", output_to_operand_aliasing={{3}: (2, {})} | custom-call | flops 102400000 | bytes 4096 | tf_op jit(solution)/shard_map/base/pallas_call | solution.py:180
  18.1 4.5 %collective-permute-start.1 = (bf16[224,640]{1,0:T(8,128)(2,1)S(1)}, bf16[224,640]{1,0:T(8,128)(2,1)S(1)}, u32[]{:S(2)}, u32[]{:S(2)}) collective-permute-start(bf16[224,640]{1,0:T(8,128)(2,1)S(1)} %get-tuple-element.126.near.base.refs_0_), channel_id=1, source_target_pairs={{0,4},{4,0},{8,12},{12,8},{1,5},{5,1},{9,13},{13,9},{2,6},{6,2},{1... | collective-permute-start | bytes 860168 | tf_op jit(solution)/shard_map/ppermute | solution.py:464
  24.0 1.9 %collective-permute-start.9 = (bf16[128,128]{1,0:T(8,128)(2,1)S(1)}, bf16[128,128]{1,0:T(8,128)(2,1)S(1)}, u32[]{:S(2)}, u32[]{:S(2)}) collective-permute-start(bf16[128,128]{1,0:T(8,128)(2,1)S(1)} %get-tuple-element.141.refs_4_), channel_id=1, source_target_pairs={{0,12},{4,0},{8,4},{12,8},{1,13},{5,1},{9,5},{13,9},{2,14},{6,2},{... | collective-permute-start | bytes 98312 | tf_op jit(solution)/shard_map/ppermute | solution.py:419
  25.9 1.8 %collective-permute-start.8 = (bf16[128,128]{1,0:T(8,128)(2,1)S(1)}, bf16[128,128]{1,0:T(8,128)(2,1)S(1)}, u32[]{:S(2)}, u32[]{:S(2)}) collective-permute-start(bf16[128,128]{1,0:T(8,128)(2,1)S(1)} %get-tuple-element.141.refs_4_), channel_id=1, source_target_pairs={{0,8},{4,12},{8,0},{12,4},{1,9},{5,13},{9,1},{13,5},{2,10},{6,14},... | collective-permute-start | bytes 98312 | tf_op jit(solution)/shard_map/ppermute | solution.py:419
  28.9 2.2 %collective-permute-start.16 = (bf16[224,640]{1,0:T(8,128)(2,1)S(1)}, bf16[224,640]{1,0:T(8,128)(2,1)S(1)}, u32[]{:S(2)}, u32[]{:S(2)}) collective-permute-start(bf16[224,640]{1,0:T(8,128)(2,1)S(1)} %get-tuple-element.153), channel_id=1, source_target_pairs={{0,4},{4,0},{8,12},{12,8},{1,5},{5,1},{9,13},{13,9},{2,6},{6,2},{1... | collective-permute-start | bytes 860168 | tf_op jit(solution)/shard_map/ppermute | solution.py:496
  31.2 4.8 %base.5 = (bf16[224,768]{1,0:T(8,128)(2,1)S(1)}, bf16[224,640]{1,0:T(8,128)(2,1)S(1)}, bf16[224,640]{1,0:T(8,128)(2,1)S(1)}, bf16[224,768]{1,0:T(8,128)(2,1)S(1)...) custom-call(bf16[224,1024]{1,0:T(8,128)(2,1)S(1)} %copy-done.2, ...), custom_call_target="tpu_custom_call", output_to_operand_aliasing={{5}: (2, {})} | custom-call | flops 172800000 | bytes 6912 | tf_op jit(solution)/shard_map/base/pallas_call | solution.py:180
  38.0 2.8 %collective-permute-start.14 = (bf16[224,768]{1,0:T(8,128)(2,1)S(1)}, bf16[224,768]{1,0:T(8,128)(2,1)S(1)}, u32[]{:S(2)}, u32[]{:S(2)}) collective-permute-start(bf16[224,768]{1,0:T(8,128)(2,1)S(1)} %get-tuple-element.150), channel_id=1, source_target_pairs={{0,4},{4,0},{8,12},{12,8},{1,5},{5,1},{9,13},{13,9},{2,6},{6,2},{1... | collective-permute-start | bytes 1032200 | tf_op jit(solution)/shard_map/ppermute | solution.py:496
  43.4 4.0 %collective-permute-done.14.got.refs_2_ = bf16[224,768]{1,0:T(8,128)(2,1)S(1)} collective-permute-done((bf16[224,768]{1,0:T(8,128)(2,1)S(1)}, bf16[224,768]{1,0:T(8,128)(2,1)S(1)}, u32[]{:S(2)}, u32[]{:S(2)}) %collective-permute-start.14) | collective-permute-done | bytes 344096 | tf_op jit(solution)/shard_map/ppermute | solution.py:496
  47.4 1.7 %collective-permute-start.17 = (bf16[224,640]{1,0:T(8,128)(2,1)S(1)}, bf16[224,640]{1,0:T(8,128)(2,1)S(1)}, u32[]{:S(2)}, u32[]{:S(2)}) collective-permute-start(bf16[224,640]{1,0:T(8,128)(2,1)S(1)} %get-tuple-element.162), channel_id=1, source_target_pairs={{0,4},{4,0},{8,12},{12,8},{1,5},{5,1},{9,13},{13,9},{2,6},{6,2},{1... | collective-permute-start | bytes 860168 | tf_op jit(solution)/shard_map/ppermute | solution.py:496
  49.9 5.1 %collective-permute-done.11.refs_8_ = bf16[64,2048]{1,0:T(8,128)(2,1)S(1)} collective-permute-done((bf16[64,2048]{1,0:T(8,128)(2,1)S(1)}, bf16[64,2048]{1,0:T(8,128)(2,1)S(1)}, u32[]{:S(2)}, u32[]{:S(2)}) %collective-permute-start.11) | collective-permute-done | bytes 262176 | tf_op jit(solution)/shard_map/ppermute | solution.py:428
  56.7 5.9 %collective-permute-start.24 = (bf16[224,768]{1,0:T(8,128)(2,1)S(1)}, bf16[224,768]{1,0:T(8,128)(2,1)S(1)}, u32[]{:S(2)}, u32[]{:S(2)}) collective-permute-start(bf16[224,768]{1,0:T(8,128)(2,1)S(1)} %get-tuple-element.177), channel_id=1, source_target_pairs={{0,4},{4,0},{8,12},{12,8},{1,5},{5,1},{9,13},{13,9},{2,6},{6,2},{1... | collective-permute-start | bytes 1032200 | tf_op jit(solution)/shard_map/ppermute | solution.py:496
  64.0 5.6 %collective-permute-start.22 = (bf16[224,640]{1,0:T(8,128)(2,1)S(1)}, bf16[224,640]{1,0:T(8,128)(2,1)S(1)}, u32[]{:S(2)}, u32[]{:S(2)}) collective-permute-start(bf16[224,640]{1,0:T(8,128)(2,1)S(1)} %get-tuple-element.173), channel_id=1, source_target_pairs={{0,4},{4,0},{8,12},{12,8},{1,5},{5,1},{9,13},{13,9},{2,6},{6,2},{1... | collective-permute-start | bytes 860168 | tf_op jit(solution)/shard_map/ppermute | solution.py:496
  73.4 4.3 %collective-permute-start.26 = (bf16[224,640]{1,0:T(8,128)(2,1)S(1)}, bf16[224,640]{1,0:T(8,128)(2,1)S(1)}, u32[]{:S(2)}, u32[]{:S(2)}) collective-permute-start(bf16[224,640]{1,0:T(8,128)(2,1)S(1)} %get-tuple-element.187), channel_id=1, source_target_pairs={{0,4},{4,0},{8,12},{12,8},{1,5},{5,1},{9,13},{13,9},{2,6},{6,2},{1... | collective-permute-start | bytes 860168 | tf_op jit(solution)/shard_map/ppermute | solution.py:496
  80.5 4.9 %collective-permute-start.30 = (bf16[224,768]{1,0:T(8,128)(2,1)S(1)}, bf16[224,768]{1,0:T(8,128)(2,1)S(1)}, u32[]{:S(2)}, u32[]{:S(2)}) collective-permute-start(bf16[224,768]{1,0:T(8,128)(2,1)S(1)} %get-tuple-element.201), channel_id=1, source_target_pairs={{0,4},{4,0},{8,12},{12,8},{1,5},{5,1},{9,13},{13,9},{2,6},{6,2},{1... | collective-permute-start | bytes 1032200 | tf_op jit(solution)/shard_map/ppermute | solution.py:496
  88.3 3.3 %collective-permute-start.28 = (bf16[224,640]{1,0:T(8,128)(2,1)S(1)}, bf16[224,640]{1,0:T(8,128)(2,1)S(1)}, u32[]{:S(2)}, u32[]{:S(2)}) collective-permute-start(bf16[224,640]{1,0:T(8,128)(2,1)S(1)} %get-tuple-element.199), channel_id=1, source_target_pairs={{0,4},{4,0},{8,12},{12,8},{1,5},{5,1},{9,13},{13,9},{2,6},{6,2},{1... | collective-permute-start | bytes 860168 | tf_op jit(solution)/shard_map/ppermute | solution.py:496
  96.0 3.7 %collective-permute-start.32 = (bf16[224,640]{1,0:T(8,128)(2,1)S(1)}, bf16[224,640]{1,0:T(8,128)(2,1)S(1)}, u32[]{:S(2)}, u32[]{:S(2)}) collective-permute-start(bf16[224,640]{1,0:T(8,128)(2,1)S(1)} %get-tuple-element.212), channel_id=1, source_target_pairs={{0,4},{4,0},{8,12},{12,8},{1,5},{5,1},{9,13},{13,9},{2,6},{6,2},{1... | collective-permute-start | bytes 860168 | tf_op jit(solution)/shard_map/ppermute | solution.py:496
  101.8 5.1 %collective-permute-start.35 = (bf16[224,768]{1,0:T(8,128)(2,1)S(1)}, bf16[224,768]{1,0:T(8,128)(2,1)S(1)}, u32[]{:S(2)}, u32[]{:S(2)}) collective-permute-start(bf16[224,768]{1,0:T(8,128)(2,1)S(1)} %get-tuple-element.223), channel_id=1, source_target_pairs={{0,4},{4,0},{8,12},{12,8},{1,5},{5,1},{9,13},{13,9},{2,6},{6,2},{1... | collective-permute-start | bytes 1032200 | tf_op jit(solution)/shard_map/ppermute | solution.py:496
  108.4 2.4 %collective-permute-start.34 = (bf16[224,640]{1,0:T(8,128)(2,1)S(1)}, bf16[224,640]{1,0:T(8,128)(2,1)S(1)}, u32[]{:S(2)}, u32[]{:S(2)}) collective-permute-start(bf16[224,640]{1,0:T(8,128)(2,1)S(1)} %get-tuple-element.222), channel_id=1, source_target_pairs={{0,4},{4,0},{8,12},{12,8},{1,5},{5,1},{9,13},{13,9},{2,6},{6,2},{1... | collective-permute-start | bytes 860168 | tf_op jit(solution)/shard_map/ppermute | solution.py:496
  110.9 2.6 %collective-permute-done.35.refs_1_ = bf16[224,768]{1,0:T(8,128)(2,1)S(1)} collective-permute-done((bf16[224,768]{1,0:T(8,128)(2,1)S(1)}, bf16[224,768]{1,0:T(8,128)(2,1)S(1)}, u32[]{:S(2)}, u32[]{:S(2)}) %collective-permute-start.35) | collective-permute-done | bytes 344096 | tf_op jit(solution)/shard_map/ppermute | solution.py:496
  114.6 2.0 %collective-permute-done.34.refs_1_ = bf16[224,640]{1,0:T(8,128)(2,1)S(1)} collective-permute-done((bf16[224,640]{1,0:T(8,128)(2,1)S(1)}, bf16[224,640]{1,0:T(8,128)(2,1)S(1)}, u32[]{:S(2)}, u32[]{:S(2)}) %collective-permute-start.34) | collective-permute-done | bytes 286752 | tf_op jit(solution)/shard_map/ppermute | solution.py:496
  (117 shorter events, 33.4 us)
Async XLA Ops:
  3.1 10.9 %collective-permute-start = (bf16[224,640]{1,0:T(8,128)(2,1)}, bf16[224,640]{1,0:T(8,128)(2,1)S(1)}, u32[]{:S(2)}, u32[]{:S(2)}) collective-permute-start(bf16[224,640]{1,0:T(8,128)(2,1)} %get-tuple-element.118.near.base.refs_0_), channel_id=1, source_target_pairs={{0,4},{4,0},{8,12},{12,8},{1,5},{5,1},{9,13},{13,9},{2,6},{6,2},{1... | collective-permute-start | bytes 860168 | tf_op jit(solution)/shard_map/ppermute | solution.py:458
  10.5 12.7 %collective-permute-start.3 = (bf16[224,768]{1,0:T(8,128)(2,1)S(1)}, bf16[224,768]{1,0:T(8,128)(2,1)S(1)}, u32[]{:S(2)}, u32[]{:S(2)}) collective-permute-start(bf16[224,768]{1,0:T(8,128)(2,1)S(1)} %get-tuple-element.129.near.base.refs_0_), channel_id=1, source_target_pairs={{0,4},{4,0},{8,12},{12,8},{1,5},{5,1},{9,13},{13,9},{2,6},{6,2},{1... | collective-permute-start | bytes 1032200 | tf_op jit(solution)/shard_map/ppermute | solution.py:464
  10.7 11.9 %collective-permute-start.5 = (bf16[64,1152]{1,0:T(8,128)(2,1)S(1)}, bf16[64,1152]{1,0:T(8,128)(2,1)S(1)}, u32[]{:S(2)}, u32[]{:S(2)}) collective-permute-start(bf16[64,1152]{1,0:T(8,128)(2,1)S(1)} %copy-done.9), channel_id=1, source_target_pairs={{0,2},{1,3},{2,0},{3,1},{4,6},{5,7},{6,4},{7,5},{8,10},{9,11},{10,... | collective-permute-start | bytes 442376 | tf_op jit(solution)/shard_map/ppermute | solution.py:408
  12.6 10.0 %collective-permute-start.6 = (bf16[64,1152]{1,0:T(8,128)(2,1)S(1)}, bf16[64,1152]{1,0:T(8,128)(2,1)S(1)}, u32[]{:S(2)}, u32[]{:S(2)}) collective-permute-start(bf16[64,1152]{1,0:T(8,128)(2,1)S(1)} %copy-done.8), channel_id=1, source_target_pairs={{0,3},{1,0},{2,1},{3,2},{4,7},{5,4},{6,5},{7,6},{8,11},{9,8},{10,9... | collective-permute-start | bytes 442376 | tf_op jit(solution)/shard_map/ppermute | solution.py:408
  14.1 13.7 %collective-permute-start.2 = (bf16[224,640]{1,0:T(8,128)(2,1)S(1)}, bf16[224,640]{1,0:T(8,128)(2,1)S(1)}, u32[]{:S(2)}, u32[]{:S(2)}) collective-permute-start(bf16[224,640]{1,0:T(8,128)(2,1)S(1)} %get-tuple-element.127), channel_id=1, source_target_pairs={{4,8},{8,4},{5,9},{9,5},{6,10},{10,6},{7,11},{11,7},{20,24},{24,20... | collective-permute-start | bytes 860168 | tf_op jit(solution)/shard_map/ppermute | solution.py:466
  18.1 10.8 %collective-permute-start.1 = (bf16[224,640]{1,0:T(8,128)(2,1)S(1)}, bf16[224,640]{1,0:T(8,128)(2,1)S(1)}, u32[]{:S(2)}, u32[]{:S(2)}) collective-permute-start(bf16[224,640]{1,0:T(8,128)(2,1)S(1)} %get-tuple-element.126.near.base.refs_0_), channel_id=1, source_target_pairs={{0,4},{4,0},{8,12},{12,8},{1,5},{5,1},{9,13},{13,9},{2,6},{6,2},{1... | collective-permute-start | bytes 860168 | tf_op jit(solution)/shard_map/ppermute | solution.py:464
  23.3 14.6 %collective-permute-start.13 = (bf16[224,768]{1,0:T(8,128)(2,1)S(1)}, bf16[224,768]{1,0:T(8,128)(2,1)S(1)}, u32[]{:S(2)}, u32[]{:S(2)}) collective-permute-start(bf16[224,768]{1,0:T(8,128)(2,1)S(1)} %get-tuple-element.148), channel_id=1, source_target_pairs={{4,8},{8,4},{5,9},{9,5},{6,10},{10,6},{7,11},{11,7},{20,24},{24,20... | collective-permute-start | bytes 1032200 | tf_op jit(solution)/shard_map/ppermute | solution.py:501
  24.0 12.0 %collective-permute-start.9 = (bf16[128,128]{1,0:T(8,128)(2,1)S(1)}, bf16[128,128]{1,0:T(8,128)(2,1)S(1)}, u32[]{:S(2)}, u32[]{:S(2)}) collective-permute-start(bf16[128,128]{1,0:T(8,128)(2,1)S(1)} %get-tuple-element.141.refs_4_), channel_id=1, source_target_pairs={{0,12},{4,0},{8,4},{12,8},{1,13},{5,1},{9,5},{13,9},{2,14},{6,2},{... | collective-permute-start | bytes 98312 | tf_op jit(solution)/shard_map/ppermute | solution.py:419
  25.9 11.1 %collective-permute-start.8 = (bf16[128,128]{1,0:T(8,128)(2,1)S(1)}, bf16[128,128]{1,0:T(8,128)(2,1)S(1)}, u32[]{:S(2)}, u32[]{:S(2)}) collective-permute-start(bf16[128,128]{1,0:T(8,128)(2,1)S(1)} %get-tuple-element.141.refs_4_), channel_id=1, source_target_pairs={{0,8},{4,12},{8,0},{12,4},{1,9},{5,13},{9,1},{13,5},{2,10},{6,14},... | collective-permute-start | bytes 98312 | tf_op jit(solution)/shard_map/ppermute | solution.py:419
  28.9 13.5 %collective-permute-start.16 = (bf16[224,640]{1,0:T(8,128)(2,1)S(1)}, bf16[224,640]{1,0:T(8,128)(2,1)S(1)}, u32[]{:S(2)}, u32[]{:S(2)}) collective-permute-start(bf16[224,640]{1,0:T(8,128)(2,1)S(1)} %get-tuple-element.153), channel_id=1, source_target_pairs={{0,4},{4,0},{8,12},{12,8},{1,5},{5,1},{9,13},{13,9},{2,6},{6,2},{1... | collective-permute-start | bytes 860168 | tf_op jit(solution)/shard_map/ppermute | solution.py:496
  38.0 9.4 %collective-permute-start.14 = (bf16[224,768]{1,0:T(8,128)(2,1)S(1)}, bf16[224,768]{1,0:T(8,128)(2,1)S(1)}, u32[]{:S(2)}, u32[]{:S(2)}) collective-permute-start(bf16[224,768]{1,0:T(8,128)(2,1)S(1)} %get-tuple-element.150), channel_id=1, source_target_pairs={{0,4},{4,0},{8,12},{12,8},{1,5},{5,1},{9,13},{13,9},{2,6},{6,2},{1... | collective-permute-start | bytes 1032200 | tf_op jit(solution)/shard_map/ppermute | solution.py:496
  40.9 14.2 %collective-permute-start.11 = (bf16[64,2048]{1,0:T(8,128)(2,1)S(1)}, bf16[64,2048]{1,0:T(8,128)(2,1)S(1)}, u32[]{:S(2)}, u32[]{:S(2)}) collective-permute-start(bf16[64,2048]{1,0:T(8,128)(2,1)S(1)} %get-tuple-element.145), channel_id=1, source_target_pairs={{0,2},{1,3},{2,0},{3,1},{4,6},{5,7},{6,4},{7,5},{8,10},{9,11},{10,... | collective-permute-start | bytes 786440 | tf_op jit(solution)/shard_map/ppermute | solution.py:428
  42.3 12.8 %collective-permute-start.12 = (bf16[64,2048]{1,0:T(8,128)(2,1)S(1)}, bf16[64,2048]{1,0:T(8,128)(2,1)S(1)}, u32[]{:S(2)}, u32[]{:S(2)}) collective-permute-start(bf16[64,2048]{1,0:T(8,128)(2,1)S(1)} %get-tuple-element.146), channel_id=1, source_target_pairs={{0,1},{1,2},{2,3},{3,0},{4,5},{5,6},{6,7},{7,4},{8,9},{9,10},{10,1... | collective-permute-start | bytes 786440 | tf_op jit(solution)/shard_map/ppermute | solution.py:428
  42.7 12.9 %collective-permute-start.18 = (bf16[224,640]{1,0:T(8,128)(2,1)S(1)}, bf16[224,640]{1,0:T(8,128)(2,1)S(1)}, u32[]{:S(2)}, u32[]{:S(2)}) collective-permute-start(bf16[224,640]{1,0:T(8,128)(2,1)S(1)} %get-tuple-element.163), channel_id=1, source_target_pairs={{4,8},{8,4},{5,9},{9,5},{6,10},{10,6},{7,11},{11,7},{20,24},{24,20... | collective-permute-start | bytes 860168 | tf_op jit(solution)/shard_map/ppermute | solution.py:501
  56.7 14.9 %collective-permute-start.24 = (bf16[224,768]{1,0:T(8,128)(2,1)S(1)}, bf16[224,768]{1,0:T(8,128)(2,1)S(1)}, u32[]{:S(2)}, u32[]{:S(2)}) collective-permute-start(bf16[224,768]{1,0:T(8,128)(2,1)S(1)} %get-tuple-element.177), channel_id=1, source_target_pairs={{0,4},{4,0},{8,12},{12,8},{1,5},{5,1},{9,13},{13,9},{2,6},{6,2},{1... | collective-permute-start | bytes 1032200 | tf_op jit(solution)/shard_map/ppermute | solution.py:496
  63.1 10.3 %collective-permute-start.23 = (bf16[224,640]{1,0:T(8,128)(2,1)S(1)}, bf16[224,640]{1,0:T(8,128)(2,1)S(1)}, u32[]{:S(2)}, u32[]{:S(2)}) collective-permute-start(bf16[224,640]{1,0:T(8,128)(2,1)S(1)} %get-tuple-element.175), channel_id=1, source_target_pairs={{4,8},{8,4},{5,9},{9,5},{6,10},{10,6},{7,11},{11,7},{20,24},{24,20... | collective-permute-start | bytes 860168 | tf_op jit(solution)/shard_map/ppermute | solution.py:501
  64.0 14.7 %collective-permute-start.22 = (bf16[224,640]{1,0:T(8,128)(2,1)S(1)}, bf16[224,640]{1,0:T(8,128)(2,1)S(1)}, u32[]{:S(2)}, u32[]{:S(2)}) collective-permute-start(bf16[224,640]{1,0:T(8,128)(2,1)S(1)} %get-tuple-element.173), channel_id=1, source_target_pairs={{0,4},{4,0},{8,12},{12,8},{1,5},{5,1},{9,13},{13,9},{2,6},{6,2},{1... | collective-permute-start | bytes 860168 | tf_op jit(solution)/shard_map/ppermute | solution.py:496
  73.4 13.1 %collective-permute-start.26 = (bf16[224,640]{1,0:T(8,128)(2,1)S(1)}, bf16[224,640]{1,0:T(8,128)(2,1)S(1)}, u32[]{:S(2)}, u32[]{:S(2)}) collective-permute-start(bf16[224,640]{1,0:T(8,128)(2,1)S(1)} %get-tuple-element.187), channel_id=1, source_target_pairs={{0,4},{4,0},{8,12},{12,8},{1,5},{5,1},{9,13},{13,9},{2,6},{6,2},{1... | collective-permute-start | bytes 860168 | tf_op jit(solution)/shard_map/ppermute | solution.py:496
  78.8 9.5 %collective-permute-start.25 = (bf16[224,640]{1,0:T(8,128)(2,1)S(1)}, bf16[224,640]{1,0:T(8,128)(2,1)S(1)}, u32[]{:S(2)}, u32[]{:S(2)}) collective-permute-start(bf16[224,640]{1,0:T(8,128)(2,1)S(1)} %get-tuple-element.186), channel_id=1, source_target_pairs={{4,8},{8,4},{5,9},{9,5},{6,10},{10,6},{7,11},{11,7},{20,24},{24,20... | collective-permute-start | bytes 860168 | tf_op jit(solution)/shard_map/ppermute | solution.py:501
  80.5 13.6 %collective-permute-start.30 = (bf16[224,768]{1,0:T(8,128)(2,1)S(1)}, bf16[224,768]{1,0:T(8,128)(2,1)S(1)}, u32[]{:S(2)}, u32[]{:S(2)}) collective-permute-start(bf16[224,768]{1,0:T(8,128)(2,1)S(1)} %get-tuple-element.201), channel_id=1, source_target_pairs={{0,4},{4,0},{8,12},{12,8},{1,5},{5,1},{9,13},{13,9},{2,6},{6,2},{1... | collective-permute-start | bytes 1032200 | tf_op jit(solution)/shard_map/ppermute | solution.py:496
  86.6 9.3 %collective-permute-start.29 = (bf16[224,640]{1,0:T(8,128)(2,1)S(1)}, bf16[224,640]{1,0:T(8,128)(2,1)S(1)}, u32[]{:S(2)}, u32[]{:S(2)}) collective-permute-start(bf16[224,640]{1,0:T(8,128)(2,1)S(1)} %get-tuple-element.200), channel_id=1, source_target_pairs={{4,8},{8,4},{5,9},{9,5},{6,10},{10,6},{7,11},{11,7},{20,24},{24,20... | collective-permute-start | bytes 860168 | tf_op jit(solution)/shard_map/ppermute | solution.py:501
  88.3 11.6 %collective-permute-start.28 = (bf16[224,640]{1,0:T(8,128)(2,1)S(1)}, bf16[224,640]{1,0:T(8,128)(2,1)S(1)}, u32[]{:S(2)}, u32[]{:S(2)}) collective-permute-start(bf16[224,640]{1,0:T(8,128)(2,1)S(1)} %get-tuple-element.199), channel_id=1, source_target_pairs={{0,4},{4,0},{8,12},{12,8},{1,5},{5,1},{9,13},{13,9},{2,6},{6,2},{1... | collective-permute-start | bytes 860168 | tf_op jit(solution)/shard_map/ppermute | solution.py:496
  96.0 11.4 %collective-permute-start.32 = (bf16[224,640]{1,0:T(8,128)(2,1)S(1)}, bf16[224,640]{1,0:T(8,128)(2,1)S(1)}, u32[]{:S(2)}, u32[]{:S(2)}) collective-permute-start(bf16[224,640]{1,0:T(8,128)(2,1)S(1)} %get-tuple-element.212), channel_id=1, source_target_pairs={{0,4},{4,0},{8,12},{12,8},{1,5},{5,1},{9,13},{13,9},{2,6},{6,2},{1... | collective-permute-start | bytes 860168 | tf_op jit(solution)/shard_map/ppermute | solution.py:496
  101.8 11.8 %collective-permute-start.35 = (bf16[224,768]{1,0:T(8,128)(2,1)S(1)}, bf16[224,768]{1,0:T(8,128)(2,1)S(1)}, u32[]{:S(2)}, u32[]{:S(2)}) collective-permute-start(bf16[224,768]{1,0:T(8,128)(2,1)S(1)} %get-tuple-element.223), channel_id=1, source_target_pairs={{0,4},{4,0},{8,12},{12,8},{1,5},{5,1},{9,13},{13,9},{2,6},{6,2},{1... | collective-permute-start | bytes 1032200 | tf_op jit(solution)/shard_map/ppermute | solution.py:496
  (23 other events, 163.9 us)
